TPU v7x, 32 devices: a whole 2x2x4 slice. The times are simulated.
32 devices in a mesh: row: 4 (over x, core), col: 8 (over z, y).
Axes of the slice: x: 2, y: 2, z: 4, core: 2. Of those that a mesh axis runs over, the one named last changes fastest.
Arguments:
- ham: bfloat16 [3072, 3072], P('row', 'col'), may hold values from -0.109375 to 0.109375
- deriv: bfloat16 [3072, 3072], P('row', 'col'), may hold values from -6 to 6
- band: int32 [24], replicated, may hold values from 1 to 12, as said below
- frag_of: int32 [24], replicated, may hold values from 0 to 15
Outputs:
- sign_iterate: bfloat16 [3072, 3072], P('row', 'col')
- energy_density: bfloat16 [3072, 3072], P('row', 'col')
- pulay_terms: float32 [16, 128], P('col')
Inputs may be any that keep to these rules, and one draw needn't show every extreme that they name: Some block row has band half-width exactly 12.
All inputs are finite; a program needn't handle non-finite values.
Results may differ from a plain program's by a relative error of at most 0.006.
Values may be sent and summed in bfloat16 or wider, within the bound.
No kernel may reach another device: no remote copies, remote signals or barrier semaphores. Data moves between devices by JAX's collectives and lax.ppermute only.
A program may use at most 64 MiB of HBM per device.

v0:
```python
import jax
import jax.numpy as jnp
from jax import lax
from jax.sharding import PartitionSpec as P

BLK = 128
FRAG_DEV = 2


def passed_along(value, axis, steps):
    count = lax.axis_size(axis)
    first, last = (max(0, -steps), min(count, count - steps))
    return lax.ppermute(value, axis, [(source, source + steps) for source in range(first, last)])


def reach_of(rows_here):
    block_rows = rows_here // BLK
    widest_band = block_rows * lax.axis_size("row") // 2
    return min((widest_band + block_rows - 1) // block_rows, lax.axis_size("row") - 1)


def shifted_rows(right_matrix, offset):
    return passed_along(right_matrix, "row", offset)


def near_window(right_matrix):
    reach = reach_of(right_matrix.shape[0])
    lower = []
    upper = []
    for offset in range(1, reach + 1):
        lower.append(shifted_rows(right_matrix, offset))
        upper.append(shifted_rows(right_matrix, -offset))
    pieces = lower[::-1] + [right_matrix] + upper
    return jnp.concatenate(pieces, axis=0)


def window_product(slab, right_matrix):
    rows_here = right_matrix.shape[0]
    reach = reach_of(rows_here)
    margin = reach * rows_here
    padded = jnp.pad(slab, ((0, 0), (margin, margin)))
    begin = lax.axis_index("row") * rows_here
    left_window = lax.dynamic_slice_in_dim(padded, begin, (2 * reach + 1) * rows_here, 1)
    return jnp.dot(left_window, near_window(right_matrix), preferred_element_type=jnp.float32)


def folded_product(left_matrix, right_matrix):
    slab = lax.all_gather(left_matrix, "col", axis=1, tiled=True)
    return window_product(slab, right_matrix)


def body(ham, deriv, band, frag_of):
    rows_here = ham.shape[0]
    cols_here = ham.shape[1]
    block_rows = rows_here // BLK
    block_cols = cols_here // BLK
    row_index = lax.axis_index("row")
    col_index = lax.axis_index("col")
    row_blocks = row_index * block_rows + jnp.arange(block_rows, dtype=jnp.int32)
    col_blocks = col_index * block_cols + jnp.arange(block_cols, dtype=jnp.int32)
    row_band = lax.dynamic_slice_in_dim(band, row_index * block_rows, block_rows)
    col_band = lax.dynamic_slice_in_dim(band, col_index * block_cols, block_cols)
    widest = jnp.maximum(row_band[:, None], col_band[None, :])
    inside = jnp.abs(row_blocks[:, None] - col_blocks[None, :]) <= widest
    pattern = jnp.repeat(jnp.repeat(inside.astype(jnp.float32), BLK, axis=0), BLK, axis=1)
    global_rows = row_index * rows_here + jnp.arange(rows_here, dtype=jnp.int32)
    global_cols = col_index * cols_here + jnp.arange(cols_here, dtype=jnp.int32)
    identity = (global_rows[:, None] == global_cols[None, :]).astype(jnp.float32)
    start = (ham.astype(jnp.float32) * pattern).astype(jnp.bfloat16)

    def start_times(right_matrix):
        return folded_product(start, right_matrix)

    square = (start_times(start) * pattern).astype(jnp.bfloat16)
    cubic = start_times(square)
    sign_iterate = (pattern * (1.5 * start.astype(jnp.float32) - 0.5 * cubic)).astype(jnp.bfloat16)
    density = (0.5 * (identity - sign_iterate.astype(jnp.float32))).astype(jnp.bfloat16)
    weighted = (start_times(density) * pattern).astype(jnp.bfloat16)
    energy_density = (folded_product(density, weighted) * pattern).astype(jnp.bfloat16)
    column_terms = jnp.sum(energy_density.astype(jnp.float32) * deriv.astype(jnp.float32), axis=0)
    column_terms = column_terms.reshape(block_cols, BLK)
    local_frags = lax.dynamic_slice_in_dim(frag_of, col_index * block_cols, block_cols)
    fragment_count = FRAG_DEV * lax.axis_size("col")
    fragments = jnp.arange(fragment_count, dtype=jnp.int32)
    onehot = (local_frags[None, :] == fragments[:, None]).astype(jnp.float32)
    partial_value = jnp.dot(onehot, column_terms, precision=lax.Precision.HIGHEST)
    grand_total = lax.psum(partial_value, ("row", "col"))
    pulay_terms = lax.dynamic_slice_in_dim(grand_total, col_index * FRAG_DEV, FRAG_DEV, 0)
    return (sign_iterate, energy_density, pulay_terms)


def solution(mesh):
    placed = (P("row", "col"), P("row", "col"), P(), P())
    return jax.shard_map(
        body,
        mesh=mesh,
        in_specs=placed,
        out_specs=(P("row", "col"), P("row", "col"), P("col", None)),
        check_vma=False,
    )
```

profile of v0, /device:TPU:0, one launch (start us, length us, event | category | flops | bytes accessed | tf_op | source)
XLA Modules:
  0.0 265.9 jit_solution(5142577407391692170)
XLA Ops:
  7.2 0.0 all-gather.3.cloned.1.call-start
  7.3 0.8 dynamic_slice.21
  8.0 0.7 dynamic_slice.20
  8.8 0.1 fusion.17
  8.8 0.1 broadcast_bitcast_fusion
  8.9 0.1 broadcast_in_dim.5
  9.0 0.4 copy.9
  9.4 0.9 multiply_convert_fusion.1
  10.3 0.0 all-gather.3.cloned.1.call-update
  10.4 0.0 all-gather.5.cloned.1.call-start
  10.4 5.9 %collective-permute-start = (bf16[768,384]{1,0:T(8,128)(2,1)}, bf16[768,384]{1,0:T(8,128)(2,1)}, u32[]{:S(2)}, u32[]{:S(2)}) collective-permute-start(bf16[768,384]{1,0:T(8,128)(2,1)} %multiply_convert_fusion.1), channel_id=1, source_target_pairs={{0,16},{8,24},{1,17},{9,25},{2,18},{10,26},{3,19},{11,27},{4,20},{... | collective-permute-start | bytes 1769480 | tf_op jit(solution)/shard_map/ppermute | solution.py:13
  16.3 1.5 collective-permute-start.1
  17.8 1.3 collective-permute-start.2
  19.1 1.3 collective-permute-start.3
  20.4 9.1 %collective-permute-done = bf16[768,384]{1,0:T(8,128)(2,1)} collective-permute-done((bf16[768,384]{1,0:T(8,128)(2,1)}, bf16[768,384]{1,0:T(8,128)(2,1)}, u32[]{:S(2)}, u32[]{:S(2)}) %collective-permute-start) | collective-permute-done | bytes 589856 | tf_op jit(solution)/shard_map/ppermute | solution.py:13
  29.4 1.9 constant_dynamic-update-slice_fusion.4
  31.4 0.9 constant_dynamic-update-slice_fusion.3
  32.3 0.9 constant_dynamic-update-slice_fusion.2
  33.2 0.9 constant_dynamic-update-slice_fusion.1
  34.0 7.9 %collective-permute-done.3 = bf16[768,384]{1,0:T(8,128)(2,1)S(1)} collective-permute-done((bf16[768,384]{1,0:T(8,128)(2,1)}, bf16[768,384]{1,0:T(8,128)(2,1)S(1)}, u32[]{:S(2)}, u32[]{:S(2)}) %collective-permute-start.3) | collective-permute-done | bytes 589856 | tf_op jit(solution)/shard_map/ppermute | solution.py:13
  42.0 0.9 constant_dynamic-update-slice_fusion
  42.8 51.5 %all-gather.3.cloned.1.call-done = bf16[768,3072]{1,0:T(8,128)(2,1)} async-done(((bf16[768,384]{1,0:T(8,128)(2,1)}), bf16[768,3072]{1,0:T(8,128)(2,1)}) %all-gather.3.cloned.1.call-update) | async-done | bytes 4718608 | tf_op jit(solution)/shard_map/all_gather | solution.py:48
  94.4 6.1 %fusion.13 = bf16[768,384]{1,0:T(8,128)(2,1)S(1)} fusion(f32[768,384]{1,0:T(8,128)S(1)} %copy.9, bf16[3840,384]{1,0:T(8,128)(2,1)} %constant_dynamic-update-slice_fusion, s32[]{:T(128)S(6)} %select_n.18, bf16[768,3072]{1,0:T(8,128)(2,1)} %all-gather.3.cloned.1.call-done), kind=kOutput, calls=%fused_computation.15 | convolution fusion | flops 2265513984 | bytes 9437188 | tf_op jit(solution)/shard_map/dot_general | solution.py:44
  100.5 3.8 %collective-permute-start.4 = (bf16[768,384]{1,0:T(8,128)(2,1)S(1)}, bf16[768,384]{1,0:T(8,128)(2,1)S(1)}, u32[]{:S(2)}, u32[]{:S(2)}) collective-permute-start(bf16[768,384]{1,0:T(8,128)(2,1)S(1)} %fusion.13), channel_id=1, source_target_pairs={{0,16},{8,24},{1,17},{9,25},{2,18},{10,26},{3,19},{11,27},{4,20},{... | collective-permute-start | bytes 1769480 | tf_op jit(solution)/shard_map/ppermute | solution.py:13
  104.3 1.3 collective-permute-start.5
  105.6 1.3 collective-permute-start.6
  106.9 1.3 collective-permute-start.7
  108.2 9.8 %collective-permute-done.4 = bf16[768,384]{1,0:T(8,128)(2,1)S(1)} collective-permute-done((bf16[768,384]{1,0:T(8,128)(2,1)S(1)}, bf16[768,384]{1,0:T(8,128)(2,1)S(1)}, u32[]{:S(2)}, u32[]{:S(2)}) %collective-permute-start.4) | collective-permute-done | bytes 589856 | tf_op jit(solution)/shard_map/ppermute | solution.py:13
  118.0 0.1 constant_dynamic-update-slice_fusion.9
  118.1 0.1 constant_dynamic-update-slice_fusion.8
  118.2 0.1 constant_dynamic-update-slice_fusion.7
  118.3 0.1 constant_dynamic-update-slice_fusion.6
  118.4 11.3 %collective-permute-done.7 = bf16[768,384]{1,0:T(8,128)(2,1)S(1)} collective-permute-done((bf16[768,384]{1,0:T(8,128)(2,1)S(1)}, bf16[768,384]{1,0:T(8,128)(2,1)S(1)}, u32[]{:S(2)}, u32[]{:S(2)}) %collective-permute-start.7) | collective-permute-done | bytes 589856 | tf_op jit(solution)/shard_map/ppermute | solution.py:13
  129.7 0.1 constant_dynamic-update-slice_fusion.5
  129.8 4.4 %multiply_convert_fusion = (bf16[768,384]{1,0:T(8,128)(2,1)}, bf16[768,384]{1,0:T(8,128)(2,1)}) fusion(s32[384]{0:T(512)S(1)} %iota_add_fusion.1, s32[768]{0:T(1024)S(1)} %iota_add_fusion, f32[768,384]{1,0:T(8,128)S(1)} %copy.9, bf16[3840,384]{1,0:T(8,128)(2,1)S(1)} %constant_dynamic-update-slice_fusion.5, s32[]{:T(128)S(6)} %select_n.18, ...), kind=kOutput, calls=%fused_computation.17 | convolution fusion | flops 2268463104 | bytes 10621444 | tf_op jit(solution)/shard_map/dot_general | solution.py:44
  134.2 1.6 collective-permute-start.8
  135.8 1.3 collective-permute-start.9
  137.2 1.3 collective-permute-start.10
  138.5 1.3 collective-permute-start.11
  139.8 10.1 %collective-permute-done.8 = bf16[768,384]{1,0:T(8,128)(2,1)S(1)} collective-permute-done((bf16[768,384]{1,0:T(8,128)(2,1)}, bf16[768,384]{1,0:T(8,128)(2,1)S(1)}, u32[]{:S(2)}, u32[]{:S(2)}) %collective-permute-start.8) | collective-permute-done | bytes 589856 | tf_op jit(solution)/shard_map/ppermute | solution.py:13
  149.9 0.1 constant_dynamic-update-slice_fusion.14
  149.9 0.1 constant_dynamic-update-slice_fusion.13
  150.1 0.1 constant_dynamic-update-slice_fusion.12
  150.2 0.1 constant_dynamic-update-slice_fusion.11
  150.3 11.2 %collective-permute-done.11 = bf16[768,384]{1,0:T(8,128)(2,1)S(1)} collective-permute-done((bf16[768,384]{1,0:T(8,128)(2,1)}, bf16[768,384]{1,0:T(8,128)(2,1)S(1)}, u32[]{:S(2)}, u32[]{:S(2)}) %collective-permute-start.11) | collective-permute-done | bytes 589856 | tf_op jit(solution)/shard_map/ppermute | solution.py:13
  161.4 0.1 constant_dynamic-update-slice_fusion.10
  161.5 5.2 %fusion.12 = bf16[768,384]{1,0:T(8,128)(2,1)S(1)} fusion(f32[768,384]{1,0:T(8,128)S(1)} %copy.9, bf16[3840,384]{1,0:T(8,128)(2,1)S(1)} %constant_dynamic-update-slice_fusion.10, s32[]{:T(128)S(6)} %select_n.18, bf16[768,3072]{1,0:T(8,128)(2,1)} %all-gather.3.cloned.1.call-done), kind=kOutput, calls=%fused_computation.14 | convolution fusion | flops 2265513984 | bytes 9437188 | tf_op jit(solution)/shard_map/dot_general | solution.py:44
  166.8 2.8 %collective-permute-start.12 = (bf16[768,384]{1,0:T(8,128)(2,1)S(1)}, bf16[768,384]{1,0:T(8,128)(2,1)}, u32[]{:S(2)}, u32[]{:S(2)}) collective-permute-start(bf16[768,384]{1,0:T(8,128)(2,1)S(1)} %fusion.12), channel_id=1, source_target_pairs={{0,16},{8,24},{1,17},{9,25},{2,18},{10,26},{3,19},{11,27},{4,20},{... | collective-permute-start | bytes 1769480 | tf_op jit(solution)/shard_map/ppermute | solution.py:13
  169.5 1.3 collective-permute-start.13
  170.8 1.3 collective-permute-start.14
  172.1 1.3 collective-permute-start.15
  173.4 0.1 dynamic_slice.24
  173.5 8.9 %collective-permute-done.12 = bf16[768,384]{1,0:T(8,128)(2,1)} collective-permute-done((bf16[768,384]{1,0:T(8,128)(2,1)S(1)}, bf16[768,384]{1,0:T(8,128)(2,1)}, u32[]{:S(2)}, u32[]{:S(2)}) %collective-permute-start.12) | collective-permute-done | bytes 589856 | tf_op jit(solution)/shard_map/ppermute | solution.py:13
  182.5 1.9 constant_dynamic-update-slice_fusion.19
  184.4 0.9 constant_dynamic-update-slice_fusion.18
  185.3 0.9 constant_dynamic-update-slice_fusion.17
  186.2 0.9 constant_dynamic-update-slice_fusion.16
  187.1 7.1 %collective-permute-done.15 = bf16[768,384]{1,0:T(8,128)(2,1)S(1)} collective-permute-done((bf16[768,384]{1,0:T(8,128)(2,1)S(1)}, bf16[768,384]{1,0:T(8,128)(2,1)S(1)}, u32[]{:S(2)}, u32[]{:S(2)}) %collective-permute-start.15) | collective-permute-done | bytes 589856 | tf_op jit(solution)/shard_map/ppermute | solution.py:13
  194.1 0.9 constant_dynamic-update-slice_fusion.15
  195.0 17.6 %all-gather.5.cloned.1.call-done = bf16[768,3072]{1,0:T(8,128)(2,1)} async-done(((bf16[768,384]{1,0:T(8,128)(2,1)}), bf16[768,3072]{1,0:T(8,128)(2,1)}) %all-gather.5.cloned.1.call-update) | async-done | bytes 4718608 | tf_op jit(solution)/shard_map/all_gather | solution.py:48
  212.6 6.9 %multiply_reduce_fusion = (f32[384]{0:T(512)S(1)}, bf16[768,384]{1,0:T(8,128)(2,1)}) fusion(bf16[768,384]{1,0:T(8,128)(2,1)S(1)} %copy-done.4, f32[768,384]{1,0:T(8,128)S(1)} %copy.9, bf16[3840,384]{1,0:T(8,128)(2,1)} %constant_dynamic-update-slice_fusion.15, s32[]{:T(128)S(6)} %select_n.18, bf16[768,3072]{1,0:T(8,128)(2,1)} %all-gather.5.cloned.1.call-done), kind=kOutput, calls=%fused_computation.16 | convolution fusion | flops 2266693120 | bytes 10028548 | tf_op jit(solution)/shard_map/dot_general | solution.py:44
  219.6 0.1 fusion.14
  219.7 38.8 %psum.7 = f32[16,128]{1,0:T(8,128)S(1)} all-reduce(f32[16,128]{1,0:T(8,128)S(1)} %fusion.14), channel_id=1, replica_groups=mesh['row'=4,'col'=8] {'row','col'}, use_global_device_ids=true, to_apply=%region_1.2 | all-reduce | flops 2048 | bytes 16384 | tf_op jit(solution)/shard_map/psum | solution.py:87
  258.5 0.6 constant_dynamic-slice_fusion
  (26 shorter events, 0.1 us)
Async XLA Ops:
  7.2 2.2 copy-start.2
  7.2 87.2 %all-gather.3.cloned.1.call-start = ((), (), s32[]{:S(2)}) async-start(), calls=%async_computation | async-start | bytes 5308416 | tf_op jit(solution)/shard_map/all_gather | solution.py:48
  10.3 21.9 %copy-start = (bf16[768,384]{1,0:T(8,128)(2,1)S(1)}, bf16[768,384]{1,0:T(8,128)(2,1)}, u32[]{:S(2)}) copy-start(bf16[768,384]{1,0:T(8,128)(2,1)} %multiply_convert_fusion.1) | copy-start | bytes 1769476
  10.4 202.3 %all-gather.5.cloned.1.call-start = ((), (), s32[]{:S(2)}) async-start(), calls=%async_computation.1 | async-start | bytes 5308416 | tf_op jit(solution)/shard_map/all_gather | solution.py:48
  10.4 19.0 %collective-permute-start = (bf16[768,384]{1,0:T(8,128)(2,1)}, bf16[768,384]{1,0:T(8,128)(2,1)}, u32[]{:S(2)}, u32[]{:S(2)}) collective-permute-start(bf16[768,384]{1,0:T(8,128)(2,1)} %multiply_convert_fusion.1), channel_id=1, source_target_pairs={{0,16},{8,24},{1,17},{9,25},{2,18},{10,26},{3,19},{11,27},{4,20},{... | collective-permute-start | bytes 1769480 | tf_op jit(solution)/shard_map/ppermute | solution.py:13
  16.3 15.1 %collective-permute-start.1 = (bf16[768,384]{1,0:T(8,128)(2,1)}, bf16[768,384]{1,0:T(8,128)(2,1)S(1)}, u32[]{:S(2)}, u32[]{:S(2)}) collective-permute-start(bf16[768,384]{1,0:T(8,128)(2,1)} %multiply_convert_fusion.1), channel_id=1, source_target_pairs={{0,8},{8,16},{16,24},{1,9},{9,17},{17,25},{2,10},{10,18},{18,26},{... | collective-permute-start | bytes 1769480 | tf_op jit(solution)/shard_map/ppermute | solution.py:13
  17.8 15.4 %collective-permute-start.2 = (bf16[768,384]{1,0:T(8,128)(2,1)}, bf16[768,384]{1,0:T(8,128)(2,1)S(1)}, u32[]{:S(2)}, u32[]{:S(2)}) collective-permute-start(bf16[768,384]{1,0:T(8,128)(2,1)} %multiply_convert_fusion.1), channel_id=1, source_target_pairs={{8,0},{16,8},{24,16},{9,1},{17,9},{25,17},{10,2},{18,10},{26,18},{... | collective-permute-start | bytes 1769480 | tf_op jit(solution)/shard_map/ppermute | solution.py:13
  19.1 22.9 %collective-permute-start.3 = (bf16[768,384]{1,0:T(8,128)(2,1)}, bf16[768,384]{1,0:T(8,128)(2,1)S(1)}, u32[]{:S(2)}, u32[]{:S(2)}) collective-permute-start(bf16[768,384]{1,0:T(8,128)(2,1)} %multiply_convert_fusion.1), channel_id=1, source_target_pairs={{16,0},{24,8},{17,1},{25,9},{18,2},{26,10},{19,3},{27,11},{20,4},{... | collective-permute-start | bytes 1769480 | tf_op jit(solution)/shard_map/ppermute | solution.py:13
  100.5 17.5 %collective-permute-start.4 = (bf16[768,384]{1,0:T(8,128)(2,1)S(1)}, bf16[768,384]{1,0:T(8,128)(2,1)S(1)}, u32[]{:S(2)}, u32[]{:S(2)}) collective-permute-start(bf16[768,384]{1,0:T(8,128)(2,1)S(1)} %fusion.13), channel_id=1, source_target_pairs={{0,16},{8,24},{1,17},{9,25},{2,18},{10,26},{3,19},{11,27},{4,20},{... | collective-permute-start | bytes 1769480 | tf_op jit(solution)/shard_map/ppermute | solution.py:13
  104.3 13.8 %collective-permute-start.5 = (bf16[768,384]{1,0:T(8,128)(2,1)S(1)}, bf16[768,384]{1,0:T(8,128)(2,1)S(1)}, u32[]{:S(2)}, u32[]{:S(2)}) collective-permute-start(bf16[768,384]{1,0:T(8,128)(2,1)S(1)} %fusion.13), channel_id=1, source_target_pairs={{0,8},{8,16},{16,24},{1,9},{9,17},{17,25},{2,10},{10,18},{18,26},{... | collective-permute-start | bytes 1769480 | tf_op jit(solution)/shard_map/ppermute | solution.py:13
  105.6 12.7 %collective-permute-start.6 = (bf16[768,384]{1,0:T(8,128)(2,1)S(1)}, bf16[768,384]{1,0:T(8,128)(2,1)S(1)}, u32[]{:S(2)}, u32[]{:S(2)}) collective-permute-start(bf16[768,384]{1,0:T(8,128)(2,1)S(1)} %fusion.13), channel_id=1, source_target_pairs={{8,0},{16,8},{24,16},{9,1},{17,9},{25,17},{10,2},{18,10},{26,18},{... | collective-permute-start | bytes 1769480 | tf_op jit(solution)/shard_map/ppermute | solution.py:13
  106.9 22.8 %collective-permute-start.7 = (bf16[768,384]{1,0:T(8,128)(2,1)S(1)}, bf16[768,384]{1,0:T(8,128)(2,1)S(1)}, u32[]{:S(2)}, u32[]{:S(2)}) collective-permute-start(bf16[768,384]{1,0:T(8,128)(2,1)S(1)} %fusion.13), channel_id=1, source_target_pairs={{16,0},{24,8},{17,1},{25,9},{18,2},{26,10},{19,3},{27,11},{20,4},{... | collective-permute-start | bytes 1769480 | tf_op jit(solution)/shard_map/ppermute | solution.py:13
  108.2 21.5 %copy-start.3 = (bf16[768,3072]{1,0:T(8,128)(2,1)S(1)}, bf16[768,3072]{1,0:T(8,128)(2,1)}, u32[]{:S(2)}) copy-start(bf16[768,3072]{1,0:T(8,128)(2,1)} %all-gather.3.cloned.1.call-done) | copy-start | bytes 14155780
  134.2 15.9 %copy-start.1 = (bf16[768,384]{1,0:T(8,128)(2,1)S(1)}, bf16[768,384]{1,0:T(8,128)(2,1)}, u32[]{:S(2)}) copy-start(bf16[768,384]{1,0:T(8,128)(2,1)} %get-tuple-element.3) | copy-start | bytes 1769476
  134.2 15.7 %collective-permute-start.8 = (bf16[768,384]{1,0:T(8,128)(2,1)}, bf16[768,384]{1,0:T(8,128)(2,1)S(1)}, u32[]{:S(2)}, u32[]{:S(2)}) collective-permute-start(bf16[768,384]{1,0:T(8,128)(2,1)} %get-tuple-element.3), channel_id=1, source_target_pairs={{0,16},{8,24},{1,17},{9,25},{2,18},{10,26},{3,19},{11,27},{4,20},{... | collective-permute-start | bytes 1769480 | tf_op jit(solution)/shard_map/ppermute | solution.py:13
  135.8 14.1 %collective-permute-start.9 = (bf16[768,384]{1,0:T(8,128)(2,1)}, bf16[768,384]{1,0:T(8,128)(2,1)S(1)}, u32[]{:S(2)}, u32[]{:S(2)}) collective-permute-start(bf16[768,384]{1,0:T(8,128)(2,1)} %get-tuple-element.3), channel_id=1, source_target_pairs={{0,8},{8,16},{16,24},{1,9},{9,17},{17,25},{2,10},{10,18},{18,26},{... | collective-permute-start | bytes 1769480 | tf_op jit(solution)/shard_map/ppermute | solution.py:13
  137.2 13.0 %collective-permute-start.10 = (bf16[768,384]{1,0:T(8,128)(2,1)}, bf16[768,384]{1,0:T(8,128)(2,1)S(1)}, u32[]{:S(2)}, u32[]{:S(2)}) collective-permute-start(bf16[768,384]{1,0:T(8,128)(2,1)} %get-tuple-element.3), channel_id=1, source_target_pairs={{8,0},{16,8},{24,16},{9,1},{17,9},{25,17},{10,2},{18,10},{26,18},{... | collective-permute-start | bytes 1769480 | tf_op jit(solution)/shard_map/ppermute | solution.py:13
  138.5 23.0 %collective-permute-start.11 = (bf16[768,384]{1,0:T(8,128)(2,1)}, bf16[768,384]{1,0:T(8,128)(2,1)S(1)}, u32[]{:S(2)}, u32[]{:S(2)}) collective-permute-start(bf16[768,384]{1,0:T(8,128)(2,1)} %get-tuple-element.3), channel_id=1, source_target_pairs={{16,0},{24,8},{17,1},{25,9},{18,2},{26,10},{19,3},{27,11},{20,4},{... | collective-permute-start | bytes 1769480 | tf_op jit(solution)/shard_map/ppermute | solution.py:13
  161.5 11.9 %copy-start.5 = (s32[24]{0:T(128)S(1)}, s32[24]{0:T(128)}, u32[]{:S(2)}) copy-start(s32[24]{0:T(128)} %param.7) | copy-start | bytes 292
  166.8 15.7 %collective-permute-start.12 = (bf16[768,384]{1,0:T(8,128)(2,1)S(1)}, bf16[768,384]{1,0:T(8,128)(2,1)}, u32[]{:S(2)}, u32[]{:S(2)}) collective-permute-start(bf16[768,384]{1,0:T(8,128)(2,1)S(1)} %fusion.12), channel_id=1, source_target_pairs={{0,16},{8,24},{1,17},{9,25},{2,18},{10,26},{3,19},{11,27},{4,20},{... | collective-permute-start | bytes 1769480 | tf_op jit(solution)/shard_map/ppermute | solution.py:13
  169.5 14.9 %collective-permute-start.13 = (bf16[768,384]{1,0:T(8,128)(2,1)S(1)}, bf16[768,384]{1,0:T(8,128)(2,1)S(1)}, u32[]{:S(2)}, u32[]{:S(2)}) collective-permute-start(bf16[768,384]{1,0:T(8,128)(2,1)S(1)} %fusion.12), channel_id=1, source_target_pairs={{0,8},{8,16},{16,24},{1,9},{9,17},{17,25},{2,10},{10,18},{18,26},{... | collective-permute-start | bytes 1769480 | tf_op jit(solution)/shard_map/ppermute | solution.py:13
  170.8 15.3 %collective-permute-start.14 = (bf16[768,384]{1,0:T(8,128)(2,1)S(1)}, bf16[768,384]{1,0:T(8,128)(2,1)S(1)}, u32[]{:S(2)}, u32[]{:S(2)}) collective-permute-start(bf16[768,384]{1,0:T(8,128)(2,1)S(1)} %fusion.12), channel_id=1, source_target_pairs={{8,0},{16,8},{24,16},{9,1},{17,9},{25,17},{10,2},{18,10},{26,18},{... | collective-permute-start | bytes 1769480 | tf_op jit(solution)/shard_map/ppermute | solution.py:13
  172.1 22.0 %collective-permute-start.15 = (bf16[768,384]{1,0:T(8,128)(2,1)S(1)}, bf16[768,384]{1,0:T(8,128)(2,1)S(1)}, u32[]{:S(2)}, u32[]{:S(2)}) collective-permute-start(bf16[768,384]{1,0:T(8,128)(2,1)S(1)} %fusion.12), channel_id=1, source_target_pairs={{16,0},{24,8},{17,1},{25,9},{18,2},{26,10},{19,3},{27,11},{20,4},{... | collective-permute-start | bytes 1769480 | tf_op jit(solution)/shard_map/ppermute | solution.py:13
  185.3 27.3 %copy-start.4 = (bf16[768,384]{1,0:T(8,128)(2,1)S(1)}, bf16[768,384]{1,0:T(8,128)(2,1)}, u32[]{:S(2)}) copy-start(bf16[768,384]{1,0:T(8,128)(2,1)} %param.5) | copy-start | bytes 1769476
Sparse Core Ops, SparseCore 0:
  10.6 83.6 all-gather.2
  134.3 78.2 all-gather.4
where the time goes:
time: 267 us; the launch traced here: 266 us
  waiting for transfers between devices  144 us (54%)
  blocking collectives  38.8 us (15%)
  starting transfers between devices  29.9 us (11%)
  matrix products  22.8 us (9%)
  local copies, waits for them, and re-layouts  14.6 us (5%)
  between operations  14.4 us (5%)
    ppermute x16, waiting for transfers between devices, passed_along(): lax.ppermute(value, axis, [(source, source + steps) for source in range(f...  75.3 us
    all_gather x2, waiting for transfers between devices, folded_product(): slab = lax.all_gather(left_matrix, 'col', axis=1, tiled=True)  69.1 us
    psum x1, blocking collectives, body(): grand_total = lax.psum(partial_value, ('row', 'col'))  38.8 us
    ppermute x16, starting transfers between devices, passed_along(): lax.ppermute(value, axis, [(source, source + steps) for source in range(f...  29.8 us
    dot_general x4, matrix products, window_product(): jnp.dot(left_window, near_window(right_matrix), preferred_element_type=jn...  22.6 us
    unnamed x30, local copies, waits for them, and re-layouts  10 us
  transfers between devices with their start and end apart: 18, of which 10 were waited for; matrix products, arithmetic and copies ran while one was open for 6% of the time, Pallas kernels for 0%

commit v1 on v0

v1 whole, which is shorter than its diff:
```python
import functools

import jax
import jax.numpy as jnp
from jax import lax
from jax.experimental import pallas as pl
from jax.experimental.pallas import tpu as pltpu
from jax.sharding import PartitionSpec as P

BLK = 128
FRAG_DEV = 2
AXES = ("row", "col")
VMEM_LIMIT = 48 * 1024 * 1024


def cycle_of(count):
    width = 1
    while (2 * width) ** 2 <= count:
        width *= 2
    depth = count // width
    walk = [(step, 0) for step in range(depth)]
    for turn, step in enumerate(range(depth - 1, -1, -1)):
        across = list(range(1, width))
        walk += [(step, place) for place in (across[::-1] if turn % 2 else across)]
    return [step * width + place for step, place in walk]


class Plan:
    def __init__(self, rows_here, cols_here):
        self.rows = lax.axis_size("row")
        self.cols = lax.axis_size("col")
        self.rows_here = rows_here
        self.cols_here = cols_here
        self.parts = rows_here // cols_here
        self.block_rows = rows_here // BLK
        self.block_cols = cols_here // BLK
        self.widest = self.rows * self.block_rows // 2
        self.cycle = cycle_of(self.cols)
        self.schedule = []
        half = self.cols // 2
        for distance in range(1, half + 1):
            for part in range(self.parts):
                for direction in (1, -1):
                    if distance < half or direction == (1 if part % 2 == 0 else -1):
                        self.schedule.append((part, distance, direction))

    def piece_is_zero(self, row, part, col):
        first_row = row * self.block_rows + part * self.block_cols
        first_col = col * self.block_cols
        gap = abs(first_row - first_col) - (self.block_cols - 1)
        return gap > self.widest

    def ring_pairs(self, part, distance, direction):
        pairs = []
        for row in range(self.rows):
            for place in range(self.cols):
                origin = self.cycle[(place - direction * (distance - 1)) % self.cols]
                if self.piece_is_zero(row, part, origin):
                    continue
                source = self.cycle[place]
                target = self.cycle[(place + direction) % self.cols]
                pairs.append((row * self.cols + source, row * self.cols + target))
        return pairs

    def left_order(self):
        return [(part, 0, 1) for part in range(self.parts)] + self.schedule

    def origin_col(self, distance, direction):
        col = lax.axis_index("col")
        result = col
        if distance:
            result = jnp.int32(0)
            for place in range(self.cols):
                origin = self.cycle[(place - direction * distance) % self.cols]
                result = jnp.where(col == self.cycle[place], jnp.int32(origin), result)
        return result


def ring_gather(plan, pieces):
    held = {(part, direction): pieces[part] for part in range(plan.parts) for direction in (1, -1)}
    received = []
    for part, distance, direction in plan.schedule:
        value = lax.ppermute(held[part, direction], AXES, plan.ring_pairs(part, distance, direction))
        held[part, direction] = value
        received.append(value)
    return list(pieces) + received


def row_exchange(plan, pieces):
    found = {}
    for part, piece in enumerate(pieces):
        found[0, part] = piece
        for other in range(2, plan.rows, 2):
            found[other, part] = lax.ppermute(piece, "row", [(i, i ^ other) for i in range(plan.rows)])
    for part in range(plan.parts):
        for other in range(0, plan.rows, 2):
            found[other + 1, part] = lax.ppermute(found[other, part], "row", [(i, i ^ 1) for i in range(plan.rows)])
    return [found[other, part] for other in range(plan.rows) for part in range(plan.parts)]


def block_inside(plan, band_ref, block_row, block_col):
    row = lax.axis_index("row") * plan.block_rows + block_row
    col = lax.axis_index("col") * plan.block_cols + block_col
    return jnp.abs(row - col) <= jnp.maximum(band_ref[row], band_ref[col])


def masked(plan, band_ref, value, part, fill=0.0):
    lines = []
    for i in range(plan.block_cols):
        line = []
        for j in range(plan.block_cols):
            keep = block_inside(plan, band_ref, part * plan.block_cols + i, j)
            block = value[i * BLK : (i + 1) * BLK, j * BLK : (j + 1) * BLK]
            line.append(block * keep.astype(jnp.float32))
        lines.append(jnp.concatenate(line, axis=1))
    return jnp.concatenate(lines, axis=0)


def kernel_call(plan, kernel, outs, band, arrays, flops):
    vmem = pl.BlockSpec(memory_space=pltpu.VMEM)
    smem = pl.BlockSpec(memory_space=pltpu.SMEM)
    moved = sum(a.size * a.dtype.itemsize for a in arrays) + sum(o.size * o.dtype.itemsize for o in outs)
    scratch = [pltpu.VMEM((plan.rows * plan.rows_here, plan.cols_here), jnp.bfloat16)]
    return pl.pallas_call(
        kernel,
        out_shape=outs,
        in_specs=[smem] + [vmem] * len(arrays),
        out_specs=[vmem] * len(outs),
        scratch_shapes=scratch,
        compiler_params=pltpu.CompilerParams(vmem_limit_bytes=VMEM_LIMIT),
        cost_estimate=pl.CostEstimate(flops=flops, bytes_accessed=moved, transcendentals=0),
    )(band, *arrays)


def piece_shape(plan, dtype=jnp.bfloat16):
    return jax.ShapeDtypeStruct((plan.cols_here, plan.cols_here), dtype)


def mask_kernel(plan, band_ref, ham_ref, *refs):
    for part in range(plan.parts):
        lines = pl.ds(part * plan.cols_here, plan.cols_here)
        value = ham_ref[lines, :].astype(jnp.float32)
        refs[part][...] = masked(plan, band_ref, value, part).astype(jnp.bfloat16)


def product(plan, left_refs, right_refs, right_all, part):
    if part == 0:
        row = lax.axis_index("row")
        for other in range(plan.rows):
            for piece in range(plan.parts):
                first = (row ^ other) * plan.rows_here + piece * plan.cols_here
                lines = pl.ds(pl.multiple_of(first, plan.cols_here), plan.cols_here)
                right_all[lines, :] = right_refs[other * plan.parts + piece][...]
    total = None
    for place, (of_part, distance, direction) in enumerate(plan.left_order()):
        if of_part != part:
            continue
        first = plan.origin_col(distance, direction) * plan.cols_here
        lines = pl.ds(pl.multiple_of(first, plan.cols_here), plan.cols_here)
        term = jnp.dot(left_refs[place][...], right_all[lines, :], preferred_element_type=jnp.float32)
        total = term if total is None else total + term
    return total


def split_refs(plan, refs):
    lefts = plan.parts * plan.cols
    rights = plan.parts * plan.rows
    return refs[:lefts], refs[lefts : lefts + rights], refs[lefts + rights :]


def product_kernel(plan, band_ref, *refs):
    left_refs, right_refs, (*out_refs, right_all) = split_refs(plan, refs)
    for part in range(plan.parts):
        total = product(plan, left_refs, right_refs, right_all, part)
        out_refs[part][...] = masked(plan, band_ref, total, part).astype(jnp.bfloat16)


def sign_kernel(plan, band_ref, *refs):
    left_refs, right_refs, (sign_ref, *out_refs, right_all) = split_refs(plan, refs)
    n = plan.cols_here
    for part in range(plan.parts):
        total = product(plan, left_refs, right_refs, right_all, part)
        start = left_refs[part][...].astype(jnp.float32)
        sign = masked(plan, band_ref, 1.5 * start - 0.5 * total, part).astype(jnp.bfloat16)
        sign_ref[part * n : (part + 1) * n, :] = sign
        first_row = lax.axis_index("row") * plan.rows_here + part * n
        first_col = lax.axis_index("col") * n
        rows = first_row + lax.broadcasted_iota(jnp.int32, (n, n), 0)
        cols = first_col + lax.broadcasted_iota(jnp.int32, (n, n), 1)
        identity = (rows == cols).astype(jnp.float32)
        out_refs[part][...] = (0.5 * (identity - sign.astype(jnp.float32))).astype(jnp.bfloat16)


def energy_kernel(plan, band_ref, frag_ref, deriv_ref, *refs):
    left_refs, right_refs, (energy_ref, sums_ref, right_all) = split_refs(plan, refs)
    n = plan.cols_here
    terms = None
    for part in range(plan.parts):
        total = product(plan, left_refs, right_refs, right_all, part)
        energy = masked(plan, band_ref, total, part).astype(jnp.bfloat16)
        lines = pl.ds(part * n, n)
        energy_ref[lines, :] = energy
        weighed = energy.astype(jnp.float32) * deriv_ref[lines, :].astype(jnp.float32)
        term = jnp.sum(weighed, axis=0, keepdims=True)
        terms = term if terms is None else terms + term
    count = FRAG_DEV * plan.cols
    fragment = lax.broadcasted_iota(jnp.int32, (count, BLK), 0)
    sums = jnp.zeros((count, BLK), jnp.float32)
    for j in range(plan.block_cols):
        owner = frag_ref[lax.axis_index("col") * plan.block_cols + j]
        line = jnp.broadcast_to(terms[:, j * BLK : (j + 1) * BLK], (count, BLK))
        sums = sums + jnp.where(fragment == owner, line, 0.0)
    sums_ref[...] = sums


def body(ham, deriv, band, frag_of):
    plan = Plan(*ham.shape)
    flops = 2 * plan.rows_here * plan.rows * plan.rows_here * plan.cols_here
    pieces = [piece_shape(plan)] * plan.parts
    whole = jax.ShapeDtypeStruct(ham.shape, jnp.bfloat16)
    count = FRAG_DEV * plan.cols

    start = kernel_call(plan, functools.partial(mask_kernel, plan), pieces, band, [ham], 0)
    slab = ring_gather(plan, start)
    column = row_exchange(plan, start)
    square = kernel_call(plan, functools.partial(product_kernel, plan), pieces, band, slab + column, flops)
    column = row_exchange(plan, square)
    sign_iterate, *density = kernel_call(
        plan, functools.partial(sign_kernel, plan), [whole] + pieces, band, slab + column, flops
    )
    column = row_exchange(plan, density)
    density_slab = ring_gather(plan, density)
    weighted = kernel_call(plan, functools.partial(product_kernel, plan), pieces, band, slab + column, flops)
    column = row_exchange(plan, weighted)

    vmem = pl.BlockSpec(memory_space=pltpu.VMEM)
    smem = pl.BlockSpec(memory_space=pltpu.SMEM)
    arrays = [deriv] + density_slab + column
    energy_density, sums = pl.pallas_call(
        functools.partial(energy_kernel, plan),
        out_shape=[whole, jax.ShapeDtypeStruct((count, BLK), jnp.float32)],
        in_specs=[smem, smem] + [vmem] * len(arrays),
        out_specs=[vmem, vmem],
        scratch_shapes=[pltpu.VMEM((plan.rows * plan.rows_here, plan.cols_here), jnp.bfloat16)],
        compiler_params=pltpu.CompilerParams(vmem_limit_bytes=VMEM_LIMIT),
        cost_estimate=pl.CostEstimate(flops=flops, bytes_accessed=8 * ham.size, transcendentals=0),
    )(band, frag_of, *arrays)

    sums = sums.reshape(1, plan.cols, FRAG_DEV, BLK)
    sums = jnp.broadcast_to(sums, (plan.rows, plan.cols, FRAG_DEV, BLK))
    sums = sums.reshape(plan.rows * plan.cols, FRAG_DEV, BLK)
    pulay_terms = jnp.sum(lax.all_to_all(sums, AXES, 0, 0), axis=0)
    return (sign_iterate, energy_density, pulay_terms)


def solution(mesh):
    placed = (P("row", "col"), P("row", "col"), P(), P())
    return jax.shard_map(
        body,
        mesh=mesh,
        in_specs=placed,
        out_specs=(P("row", "col"), P("row", "col"), P("col", None)),
        check_vma=False,
    )
```

time: 267 us -> 181 us (0.68)
  waiting for transfers between devices: 144 us -> 45.2 us
  starting transfers between devices: 29.9 us -> 88.3 us
  matrix products: 22.8 us -> 0 us
  Pallas kernels: 0 us -> 20.9 us
  blocking collectives: 38.8 us -> 19.8 us
  between operations: 14.4 us -> 1.29 us
  local copies, waits for them, and re-layouts: 14.6 us -> 4.05 us
    all_gather x2 -> x0, waiting for transfers between devices: 69.1 us -> none  [folded_product(): slab = lax.all_gather(left_matrix, 'col', axis=1, tiled=True)]
    ppermute x16 -> x52, starting transfers between devices: 29.8 us -> 88.3 us  [the longest x28 69.8 us: ring_gather(): lax.ppermute(held[part, direction], AXES, plan.ring_pairs(part, distance,...]
    psum x1 -> x0, blocking collectives: 38.8 us -> none  [body(): grand_total = lax.psum(partial_value, ('row', 'col'))]
    ppermute x16 -> x52, waiting for transfers between devices: 75.3 us -> 45.2 us  [the longest x8 23.7 us: row_exchange(): lax.ppermute(piece, 'row', [(i, i ^ other) for i in range(plan.rows)])]
    dot_general x5 -> x0, matrix products: 22.8 us -> none  [the longest x4 22.6 us: window_product(): jnp.dot(left_window, near_window(right_matrix), preferred_element_type=jn...]
    pallas_call x0 -> x5, Pallas kernels: none -> 20.9 us  [the longest x4 15.3 us: kernel_call(): pl.pallas_call(kernel, out_shape=outs, in_specs=[smem] + [vmem] * len(arr...]
    all_to_all x0 -> x1, blocking collectives: none -> 19.8 us  [body(): pulay_terms = jnp.sum(lax.all_to_all(sums, AXES, 0, 0), axis=0)]
    unnamed x30 -> x38, local copies, waits for them, and re-layouts: 10 us -> 4.04 us
  transfers between devices with their start and end apart: 18 -> 52, of which waited for: 10 -> 17; matrix products, arithmetic and copies ran while one was open for 6% -> 0% of each run, Pallas kernels for 0% -> 3%
where the time goes in v1:
time: 181 us; the launch traced here: 180 us
  starting transfers between devices  88.3 us (49%)
  waiting for transfers between devices  45.2 us (25%)
  Pallas kernels  20.9 us (12%)
  blocking collectives  19.8 us (11%)
  local copies, waits for them, and re-layouts  4.05 us (2%)
    ppermute x28, starting transfers between devices, ring_gather(): lax.ppermute(held[part, direction], AXES, plan.ring_pairs(part, distance,...  69.8 us
    ppermute x8, waiting for transfers between devices, row_exchange(): lax.ppermute(piece, 'row', [(i, i ^ other) for i in range(plan.rows)])  23.7 us
    ppermute x28, waiting for transfers between devices, ring_gather(): lax.ppermute(held[part, direction], AXES, plan.ring_pairs(part, distance,...  20 us
    all_to_all x1, blocking collectives, body(): pulay_terms = jnp.sum(lax.all_to_all(sums, AXES, 0, 0), axis=0)  19.8 us
    pallas_call x4, Pallas kernels, kernel_call(): pl.pallas_call(kernel, out_shape=outs, in_specs=[smem] + [vmem] * len(arr...  15.3 us
    ppermute x8, starting transfers between devices, row_exchange(): lax.ppermute(piece, 'row', [(i, i ^ other) for i in range(plan.rows)])  14.8 us
    pallas_call x1, Pallas kernels, body(): pl.pallas_call(functools.partial(energy_kernel, plan), out_shape=[whole,...  5.53 us
    unnamed x38, local copies, waits for them, and re-layouts  4.04 us
  transfers between devices with their start and end apart: 52, of which 17 were waited for; matrix products, arithmetic and copies ran while one was open for 0% of the time, Pallas kernels for 3%

profile of v1, /device:TPU:0, one launch (start us, length us, event | category | flops | bytes accessed | tf_op | source)
XLA Modules:
  0.0 180.2 jit_solution(9772101681852929698)
XLA Ops:
  0.6 1.1 copy-done
  1.7 0.7 copy-done.1
  2.4 0.7 shard_map.67
  3.0 4.9 %collective-permute-start = (bf16[384,384]{1,0:T(8,128)(2,1)S(1)}, bf16[384,384]{1,0:T(8,128)(2,1)S(1)}, u32[]{:S(2)}, u32[]{:S(2)}) collective-permute-start(bf16[384,384]{1,0:T(8,128)(2,1)S(1)} %get-tuple-element.14.refs_0_.refs_16_), channel_id=1, source_target_pairs={{0,2},{2,4},{4,6},{3,1},{1,0},{8,10},{10,12},{12,14},{14,15},{13,1... | collective-permute-start | bytes 884744 | tf_op jit(solution)/shard_map/ppermute | solution.py:83
  8.0 1.9 %collective-permute-start.3 = (bf16[384,384]{1,0:T(8,128)(2,1)S(1)}, bf16[384,384]{1,0:T(8,128)(2,1)S(1)}, u32[]{:S(2)}, u32[]{:S(2)}) collective-permute-start(bf16[384,384]{1,0:T(8,128)(2,1)S(1)} %get-tuple-element.15.refs_1_.refs_17_), channel_id=1, source_target_pairs={{0,1},{2,0},{4,2},{5,7},{3,5},{1,3},{8,9},{10,8},{12,10},{14,12},{... | collective-permute-start | bytes 884744 | tf_op jit(solution)/shard_map/ppermute | solution.py:83
  9.9 3.9 %collective-permute-start.2 = (bf16[384,384]{1,0:T(8,128)(2,1)S(1)}, bf16[384,384]{1,0:T(8,128)(2,1)S(1)}, u32[]{:S(2)}, u32[]{:S(2)}) collective-permute-start(bf16[384,384]{1,0:T(8,128)(2,1)S(1)} %get-tuple-element.15.refs_1_.refs_17_), channel_id=1, source_target_pairs={{0,2},{2,4},{4,6},{5,3},{3,1},{1,0},{8,10},{10,12},{12,14},{14,15}... | collective-permute-start | bytes 884744 | tf_op jit(solution)/shard_map/ppermute | solution.py:83
  13.8 1.9 %collective-permute-start.1 = (bf16[384,384]{1,0:T(8,128)(2,1)S(1)}, bf16[384,384]{1,0:T(8,128)(2,1)S(1)}, u32[]{:S(2)}, u32[]{:S(2)}) collective-permute-start(bf16[384,384]{1,0:T(8,128)(2,1)S(1)} %get-tuple-element.14.refs_0_.refs_16_), channel_id=1, source_target_pairs={{0,1},{2,0},{4,2},{3,5},{1,3},{8,9},{10,8},{12,10},{14,12},{13,15}... | collective-permute-start | bytes 884744 | tf_op jit(solution)/shard_map/ppermute | solution.py:83
  15.7 1.5 collective-permute-start.16
  17.3 0.6 collective-permute-start.17
  17.8 1.4 collective-permute-done.3.refs_5_
  19.3 1.9 %collective-permute-done.2.refs_4_ = bf16[384,384]{1,0:T(8,128)(2,1)S(1)} collective-permute-done((bf16[384,384]{1,0:T(8,128)(2,1)S(1)}, bf16[384,384]{1,0:T(8,128)(2,1)S(1)}, u32[]{:S(2)}, u32[]{:S(2)}) %collective-permute-start.2) | collective-permute-done | bytes 294944 | tf_op jit(solution)/shard_map/ppermute | solution.py:83
  21.2 3.4 %collective-permute-done.1.refs_3_ = bf16[384,384]{1,0:T(8,128)(2,1)S(1)} collective-permute-done((bf16[384,384]{1,0:T(8,128)(2,1)S(1)}, bf16[384,384]{1,0:T(8,128)(2,1)S(1)}, u32[]{:S(2)}, u32[]{:S(2)}) %collective-permute-start.1) | collective-permute-done | bytes 294944 | tf_op jit(solution)/shard_map/ppermute | solution.py:83
  24.6 3.5 %collective-permute-start.4 = (bf16[384,384]{1,0:T(8,128)(2,1)S(1)}, bf16[384,384]{1,0:T(8,128)(2,1)S(1)}, u32[]{:S(2)}, u32[]{:S(2)}) collective-permute-start(bf16[384,384]{1,0:T(8,128)(2,1)S(1)} %collective-permute-done.refs_2_), channel_id=1, source_target_pairs={{0,2},{2,4},{4,6},{6,7},{1,0},{8,10},{10,12},{12,14},{14,15},{15,1... | collective-permute-start | bytes 884744 | tf_op jit(solution)/shard_map/ppermute | solution.py:83
  28.1 2.4 %collective-permute-start.7 = (bf16[384,384]{1,0:T(8,128)(2,1)S(1)}, bf16[384,384]{1,0:T(8,128)(2,1)S(1)}, u32[]{:S(2)}, u32[]{:S(2)}) collective-permute-start(bf16[384,384]{1,0:T(8,128)(2,1)S(1)} %collective-permute-done.3.refs_5_), channel_id=1, source_target_pairs={{0,1},{2,0},{7,6},{5,7},{3,5},{1,3},{8,9},{10,8},{12,10},{14,12},{... | collective-permute-start | bytes 884744 | tf_op jit(solution)/shard_map/ppermute | solution.py:83
  30.5 3.5 %collective-permute-start.6 = (bf16[384,384]{1,0:T(8,128)(2,1)S(1)}, bf16[384,384]{1,0:T(8,128)(2,1)S(1)}, u32[]{:S(2)}, u32[]{:S(2)}) collective-permute-start(bf16[384,384]{1,0:T(8,128)(2,1)S(1)} %collective-permute-done.2.refs_4_), channel_id=1, source_target_pairs={{0,2},{2,4},{4,6},{6,7},{3,1},{1,0},{8,10},{10,12},{12,14},{14,15}... | collective-permute-start | bytes 884744 | tf_op jit(solution)/shard_map/ppermute | solution.py:83
  34.0 2.4 %collective-permute-start.5 = (bf16[384,384]{1,0:T(8,128)(2,1)S(1)}, bf16[384,384]{1,0:T(8,128)(2,1)S(1)}, u32[]{:S(2)}, u32[]{:S(2)}) collective-permute-start(bf16[384,384]{1,0:T(8,128)(2,1)S(1)} %collective-permute-done.1.refs_3_), channel_id=1, source_target_pairs={{0,1},{2,0},{5,7},{3,5},{1,3},{8,9},{10,8},{12,10},{15,14},{13,15}... | collective-permute-start | bytes 884744 | tf_op jit(solution)/shard_map/ppermute | solution.py:83
  36.5 3.5 %collective-permute-start.8 = (bf16[384,384]{1,0:T(8,128)(2,1)S(1)}, bf16[384,384]{1,0:T(8,128)(2,1)S(1)}, u32[]{:S(2)}, u32[]{:S(2)}) collective-permute-start(bf16[384,384]{1,0:T(8,128)(2,1)S(1)} %collective-permute-done.4.refs_6_), channel_id=1, source_target_pairs={{0,2},{2,4},{4,6},{6,7},{7,5},{8,10},{10,12},{12,14},{14,15},{15,1... | collective-permute-start | bytes 884744 | tf_op jit(solution)/shard_map/ppermute | solution.py:83
  40.0 1.3 collective-permute-start.11
  41.4 1.0 collective-permute-start.19
  42.4 1.7 collective-permute-done.5.refs_7_
  44.1 1.9 %collective-permute-start.10 = (bf16[384,384]{1,0:T(8,128)(2,1)S(1)}, bf16[384,384]{1,0:T(8,128)(2,1)S(1)}, u32[]{:S(2)}, u32[]{:S(2)}) collective-permute-start(bf16[384,384]{1,0:T(8,128)(2,1)S(1)} %collective-permute-done.6.refs_8_), channel_id=1, source_target_pairs={{0,2},{2,4},{4,6},{6,7},{7,5},{1,0},{8,10},{10,12},{12,14},{14,15}... | collective-permute-start | bytes 884744 | tf_op jit(solution)/shard_map/ppermute | solution.py:83
  46.0 3.9 %collective-permute-start.9 = (bf16[384,384]{1,0:T(8,128)(2,1)S(1)}, bf16[384,384]{1,0:T(8,128)(2,1)S(1)}, u32[]{:S(2)}, u32[]{:S(2)}) collective-permute-start(bf16[384,384]{1,0:T(8,128)(2,1)S(1)} %collective-permute-done.5.refs_7_), channel_id=1, source_target_pairs={{0,1},{7,6},{5,7},{3,5},{1,3},{8,9},{10,8},{14,12},{15,14},{13,15}... | collective-permute-start | bytes 884744 | tf_op jit(solution)/shard_map/ppermute | solution.py:83
  50.0 0.7 collective-permute-start.12
  50.7 0.7 collective-permute-start.13
  51.4 2.3 %collective-permute-done.10.refs_12_ = bf16[384,384]{1,0:T(8,128)(2,1)S(1)} collective-permute-done((bf16[384,384]{1,0:T(8,128)(2,1)S(1)}, bf16[384,384]{1,0:T(8,128)(2,1)S(1)}, u32[]{:S(2)}, u32[]{:S(2)}) %collective-permute-start.10) | collective-permute-done | bytes 294944 | tf_op jit(solution)/shard_map/ppermute | solution.py:83
  53.6 3.1 %collective-permute-done.9.refs_11_ = bf16[384,384]{1,0:T(8,128)(2,1)S(1)} collective-permute-done((bf16[384,384]{1,0:T(8,128)(2,1)S(1)}, bf16[384,384]{1,0:T(8,128)(2,1)S(1)}, u32[]{:S(2)}, u32[]{:S(2)}) %collective-permute-start.9) | collective-permute-done | bytes 294944 | tf_op jit(solution)/shard_map/ppermute | solution.py:83
  56.8 4.5 %shard_map.68 = (bf16[384,384]{1,0:T(8,128)(2,1)S(1)}, bf16[384,384]{1,0:T(8,128)(2,1)S(1)}) custom-call(s32[24]{0:T(128)S(1)} %copy-done.1, bf16[384,384]{1,0:T(8,128)(2,1)S(1)} %get-tuple-element.14.refs_0_.refs_16_, bf16[384,384]{1,0:T(8,128)(2,1)S(1)} %get-tuple-element.15.refs_1_.refs_17_, bf16[384,384]{1,0:T(8,128)(2,1)S(1)} %collective-permute-done.refs_2_, ...), custom_call_target="tpu_custom_call" | custom-call | flops 1811939328 | bytes 7667712 | tf_op jit(solution)/shard_map/pallas_call | solution.py:124
  61.2 8.5 %collective-permute-start.22 = (bf16[384,384]{1,0:T(8,128)(2,1)S(1)}, bf16[384,384]{1,0:T(8,128)(2,1)S(1)}, u32[]{:S(2)}, u32[]{:S(2)}) collective-permute-start(bf16[384,384]{1,0:T(8,128)(2,1)S(1)} %get-tuple-element.16.refs_16_), channel_id=1, source_target_pairs={{0,16},{8,24},{16,0},{24,8},{1,17},{9,25},{17,1},{25,9},{2,18},{10... | collective-permute-start | bytes 884744 | tf_op jit(solution)/shard_map/ppermute | solution.py:94
  69.8 0.5 collective-permute-start.21
  70.3 7.3 %collective-permute-done.22.refs_20_ = bf16[384,384]{1,0:T(8,128)(2,1)S(1)} collective-permute-done((bf16[384,384]{1,0:T(8,128)(2,1)S(1)}, bf16[384,384]{1,0:T(8,128)(2,1)S(1)}, u32[]{:S(2)}, u32[]{:S(2)}) %collective-permute-start.22) | collective-permute-done | bytes 294944 | tf_op jit(solution)/shard_map/ppermute | solution.py:94
  77.5 3.2 %collective-permute-done.23.refs_21_ = bf16[384,384]{1,0:T(8,128)(2,1)S(1)} collective-permute-done((bf16[384,384]{1,0:T(8,128)(2,1)S(1)}, bf16[384,384]{1,0:T(8,128)(2,1)S(1)}, u32[]{:S(2)}, u32[]{:S(2)}) %collective-permute-start.23) | collective-permute-done | bytes 294944 | tf_op jit(solution)/shard_map/ppermute | solution.py:94
  80.8 1.5 collective-permute-done.25.refs_23_
  82.3 0.7 copy-done.15
  83.1 5.6 %shard_map.69 = (bf16[768,384]{1,0:T(8,128)(2,1)}, bf16[384,384]{1,0:T(8,128)(2,1)S(1)}, bf16[384,384]{1,0:T(8,128)(2,1)S(1)}) custom-call(s32[24]{0:T(128)S(1)} %copy-done.1, bf16[384,384]{1,0:T(8,128)(2,1)S(1)} %get-tuple-element.14.refs_0_.refs_16_, bf16[384,384]{1,0:T(8,128)(2,1)S(1)} %get-tuple-element.15.refs_1_.refs_17_, ...), custom_call_target="tpu_custom_call" | custom-call | flops 1811939328 | bytes 8257536 | tf_op jit(solution)/shard_map/pallas_call | solution.py:124
  88.6 1.7 collective-permute-start.42
  91.2 2.9 %collective-permute-start.26 = (bf16[384,384]{1,0:T(8,128)(2,1)S(1)}, bf16[384,384]{1,0:T(8,128)(2,1)S(1)}, u32[]{:S(2)}, u32[]{:S(2)}) collective-permute-start(bf16[384,384]{1,0:T(8,128)(2,1)S(1)} %get-tuple-element.19.refs_16_.refs_0_), channel_id=1, source_target_pairs={{0,2},{2,4},{4,6},{3,1},{1,0},{8,10},{10,12},{12,14},{14,15},{13,1... | collective-permute-start | bytes 884744 | tf_op jit(solution)/shard_map/ppermute | solution.py:83
  94.1 4.4 %collective-permute-done.42.refs_20_ = bf16[384,384]{1,0:T(8,128)(2,1)S(1)} collective-permute-done((bf16[384,384]{1,0:T(8,128)(2,1)S(1)}, bf16[384,384]{1,0:T(8,128)(2,1)S(1)}, u32[]{:S(2)}, u32[]{:S(2)}) %collective-permute-start.42) | collective-permute-done | bytes 294944 | tf_op jit(solution)/shard_map/ppermute | solution.py:94
  98.5 2.5 %collective-permute-start.29 = (bf16[384,384]{1,0:T(8,128)(2,1)S(1)}, bf16[384,384]{1,0:T(8,128)(2,1)S(1)}, u32[]{:S(2)}, u32[]{:S(2)}) collective-permute-start(bf16[384,384]{1,0:T(8,128)(2,1)S(1)} %get-tuple-element.20.refs_17_.refs_1_), channel_id=1, source_target_pairs={{0,1},{2,0},{4,2},{5,7},{3,5},{1,3},{8,9},{10,8},{12,10},{14,12},{... | collective-permute-start | bytes 884744 | tf_op jit(solution)/shard_map/ppermute | solution.py:83
  101.0 3.0 %collective-permute-done.43.refs_21_ = bf16[384,384]{1,0:T(8,128)(2,1)S(1)} collective-permute-done((bf16[384,384]{1,0:T(8,128)(2,1)S(1)}, bf16[384,384]{1,0:T(8,128)(2,1)S(1)}, u32[]{:S(2)}, u32[]{:S(2)}) %collective-permute-start.43) | collective-permute-done | bytes 294944 | tf_op jit(solution)/shard_map/ppermute | solution.py:94
  104.0 2.5 %collective-permute-start.27 = (bf16[384,384]{1,0:T(8,128)(2,1)S(1)}, bf16[384,384]{1,0:T(8,128)(2,1)S(1)}, u32[]{:S(2)}, u32[]{:S(2)}) collective-permute-start(bf16[384,384]{1,0:T(8,128)(2,1)S(1)} %get-tuple-element.19.refs_16_.refs_0_), channel_id=1, source_target_pairs={{0,1},{2,0},{4,2},{3,5},{1,3},{8,9},{10,8},{12,10},{14,12},{13,15}... | collective-permute-start | bytes 884744 | tf_op jit(solution)/shard_map/ppermute | solution.py:83
  106.5 3.4 %collective-permute-start.28 = (bf16[384,384]{1,0:T(8,128)(2,1)S(1)}, bf16[384,384]{1,0:T(8,128)(2,1)S(1)}, u32[]{:S(2)}, u32[]{:S(2)}) collective-permute-start(bf16[384,384]{1,0:T(8,128)(2,1)S(1)} %get-tuple-element.20.refs_17_.refs_1_), channel_id=1, source_target_pairs={{0,2},{2,4},{4,6},{5,3},{3,1},{1,0},{8,10},{10,12},{12,14},{14,15}... | collective-permute-start | bytes 884744 | tf_op jit(solution)/shard_map/ppermute | solution.py:83
  110.5 3.2 %collective-permute-start.30 = (bf16[384,384]{1,0:T(8,128)(2,1)S(1)}, bf16[384,384]{1,0:T(8,128)(2,1)S(1)}, u32[]{:S(2)}, u32[]{:S(2)}) collective-permute-start(bf16[384,384]{1,0:T(8,128)(2,1)S(1)} %collective-permute-done.26.refs_2_), channel_id=1, source_target_pairs={{0,2},{2,4},{4,6},{6,7},{1,0},{8,10},{10,12},{12,14},{14,15},{15,1... | collective-permute-start | bytes 884744 | tf_op jit(solution)/shard_map/ppermute | solution.py:83
  114.1 2.5 %collective-permute-start.33 = (bf16[384,384]{1,0:T(8,128)(2,1)S(1)}, bf16[384,384]{1,0:T(8,128)(2,1)S(1)}, u32[]{:S(2)}, u32[]{:S(2)}) collective-permute-start(bf16[384,384]{1,0:T(8,128)(2,1)S(1)} %collective-permute-done.29.refs_5_), channel_id=1, source_target_pairs={{0,1},{2,0},{7,6},{5,7},{3,5},{1,3},{8,9},{10,8},{12,10},{14,12},{... | collective-permute-start | bytes 884744 | tf_op jit(solution)/shard_map/ppermute | solution.py:83
  116.6 1.0 collective-permute-done.28.refs_4_
  117.5 4.1 %collective-permute-start.31 = (bf16[384,384]{1,0:T(8,128)(2,1)S(1)}, bf16[384,384]{1,0:T(8,128)(2,1)S(1)}, u32[]{:S(2)}, u32[]{:S(2)}) collective-permute-start(bf16[384,384]{1,0:T(8,128)(2,1)S(1)} %collective-permute-done.27.refs_3_), channel_id=1, source_target_pairs={{0,1},{2,0},{5,7},{3,5},{1,3},{8,9},{10,8},{12,10},{15,14},{13,15}... | collective-permute-start | bytes 884744 | tf_op jit(solution)/shard_map/ppermute | solution.py:83
  121.7 2.1 %collective-permute-start.32 = (bf16[384,384]{1,0:T(8,128)(2,1)S(1)}, bf16[384,384]{1,0:T(8,128)(2,1)S(1)}, u32[]{:S(2)}, u32[]{:S(2)}) collective-permute-start(bf16[384,384]{1,0:T(8,128)(2,1)S(1)} %collective-permute-done.28.refs_4_), channel_id=1, source_target_pairs={{0,2},{2,4},{4,6},{6,7},{3,1},{1,0},{8,10},{10,12},{12,14},{14,15}... | collective-permute-start | bytes 884744 | tf_op jit(solution)/shard_map/ppermute | solution.py:83
  123.9 0.7 copy-done.9
  124.6 4.6 %shard_map.70 = (bf16[384,384]{1,0:T(8,128)(2,1)S(1)}, bf16[384,384]{1,0:T(8,128)(2,1)S(1)}) custom-call(s32[24]{0:T(128)S(1)} %copy-done.1, bf16[384,384]{1,0:T(8,128)(2,1)S(1)} %get-tuple-element.14.refs_0_.refs_16_, bf16[384,384]{1,0:T(8,128)(2,1)S(1)} %get-tuple-element.15.refs_1_.refs_17_, bf16[384,384]{1,0:T(8,128)(2,1)S(1)} %collective-permute-done.refs_2_, ...), custom_call_target="tpu_custom_call" | custom-call | flops 1811939328 | bytes 7667712 | tf_op jit(solution)/shard_map/pallas_call | solution.py:124
  129.2 1.3 collective-permute-start.48
  130.6 0.8 collective-permute-start.49
  131.9 1.9 %collective-permute-start.34 = (bf16[384,384]{1,0:T(8,128)(2,1)S(1)}, bf16[384,384]{1,0:T(8,128)(2,1)S(1)}, u32[]{:S(2)}, u32[]{:S(2)}) collective-permute-start(bf16[384,384]{1,0:T(8,128)(2,1)S(1)} %collective-permute-done.30.refs_6_), channel_id=1, source_target_pairs={{0,2},{2,4},{4,6},{6,7},{7,5},{8,10},{10,12},{12,14},{14,15},{15,1... | collective-permute-start | bytes 884744 | tf_op jit(solution)/shard_map/ppermute | solution.py:83
  133.8 5.2 %collective-permute-done.48.refs_20_ = bf16[384,384]{1,0:T(8,128)(2,1)S(1)} collective-permute-done((bf16[384,384]{1,0:T(8,128)(2,1)S(1)}, bf16[384,384]{1,0:T(8,128)(2,1)S(1)}, u32[]{:S(2)}, u32[]{:S(2)}) %collective-permute-start.48) | collective-permute-done | bytes 294944 | tf_op jit(solution)/shard_map/ppermute | solution.py:94
  138.9 2.5 %collective-permute-start.37 = (bf16[384,384]{1,0:T(8,128)(2,1)S(1)}, bf16[384,384]{1,0:T(8,128)(2,1)S(1)}, u32[]{:S(2)}, u32[]{:S(2)}) collective-permute-start(bf16[384,384]{1,0:T(8,128)(2,1)S(1)} %collective-permute-done.33.refs_9_), channel_id=1, source_target_pairs={{0,1},{6,4},{7,6},{5,7},{3,5},{1,3},{8,9},{10,8},{12,10},{14,12},{... | collective-permute-start | bytes 884744 | tf_op jit(solution)/shard_map/ppermute | solution.py:83
  141.5 0.6 collective-permute-done.49.refs_21_
  142.1 2.7 %collective-permute-start.35 = (bf16[384,384]{1,0:T(8,128)(2,1)S(1)}, bf16[384,384]{1,0:T(8,128)(2,1)S(1)}, u32[]{:S(2)}, u32[]{:S(2)}) collective-permute-start(bf16[384,384]{1,0:T(8,128)(2,1)S(1)} %collective-permute-done.31.refs_7_), channel_id=1, source_target_pairs={{0,1},{7,6},{5,7},{3,5},{1,3},{8,9},{10,8},{14,12},{15,14},{13,15}... | collective-permute-start | bytes 884744 | tf_op jit(solution)/shard_map/ppermute | solution.py:83
  144.8 1.9 %collective-permute-start.36 = (bf16[384,384]{1,0:T(8,128)(2,1)S(1)}, bf16[384,384]{1,0:T(8,128)(2,1)S(1)}, u32[]{:S(2)}, u32[]{:S(2)}) collective-permute-start(bf16[384,384]{1,0:T(8,128)(2,1)S(1)} %collective-permute-done.32.refs_8_), channel_id=1, source_target_pairs={{0,2},{2,4},{4,6},{6,7},{7,5},{1,0},{8,10},{10,12},{12,14},{14,15}... | collective-permute-start | bytes 884744 | tf_op jit(solution)/shard_map/ppermute | solution.py:83
  147.3 0.7 collective-permute-start.38
  148.0 2.5 %collective-permute-done.35.refs_11_ = bf16[384,384]{1,0:T(8,128)(2,1)S(1)} collective-permute-done((bf16[384,384]{1,0:T(8,128)(2,1)S(1)}, bf16[384,384]{1,0:T(8,128)(2,1)S(1)}, u32[]{:S(2)}, u32[]{:S(2)}) %collective-permute-start.35) | collective-permute-done | bytes 294944 | tf_op jit(solution)/shard_map/ppermute | solution.py:83
  150.5 0.7 collective-permute-start.39
  151.2 2.2 %collective-permute-done.36.refs_12_ = bf16[384,384]{1,0:T(8,128)(2,1)S(1)} collective-permute-done((bf16[384,384]{1,0:T(8,128)(2,1)S(1)}, bf16[384,384]{1,0:T(8,128)(2,1)S(1)}, u32[]{:S(2)}, u32[]{:S(2)}) %collective-permute-start.36) | collective-permute-done | bytes 294944 | tf_op jit(solution)/shard_map/ppermute | solution.py:83
  153.5 0.7 copy-done.17
  154.3 5.5 %shard_map.71 = (bf16[768,384]{1,0:T(8,128)(2,1)}, f32[16,128]{1,0:T(8,128)S(1)}) custom-call(s32[24]{0:T(128)S(1)} %copy-done.1, s32[24]{0:T(128)S(1)} %copy-done.2, bf16[768,384]{1,0:T(8,128)(2,1)} %deriv_ref.1, bf16[384,384]{1,0:T(8,128)(2,1)S(1)} %get-tuple-element.19.refs_16_.refs_0_, bf16[384,384]{1,0:T(8,128)(2,1)S(1)} %get-tuple-element.20.refs_17_.refs_1_, ...), custom_call_target="tpu_custom_call" | custom-call | flops 1811939328 | bytes 2359296 | tf_op jit(solution)/shard_map/pallas_call | solution.py:239
  159.8 19.8 %all_to_all.5 = f32[32,2,128]{2,1,0:T(2,128)S(1)} all-to-all(f32[32,2,128]{2,1,0:T(2,128)S(1)} %bitcast.3), channel_id=1, replica_groups=mesh['row'=4,'col'=8] {'row','col'}, dimensions={0} | all-to-all | bytes 65536 | tf_op jit(solution)/shard_map/all_to_all | solution.py:252
  179.6 0.6 reduce_sum.9
  (86 shorter events, 3.4 us)
Async XLA Ops:
  3.0 14.2 %collective-permute-start = (bf16[384,384]{1,0:T(8,128)(2,1)S(1)}, bf16[384,384]{1,0:T(8,128)(2,1)S(1)}, u32[]{:S(2)}, u32[]{:S(2)}) collective-permute-start(bf16[384,384]{1,0:T(8,128)(2,1)S(1)} %get-tuple-element.14.refs_0_.refs_16_), channel_id=1, source_target_pairs={{0,2},{2,4},{4,6},{3,1},{1,0},{8,10},{10,12},{12,14},{14,15},{13,1... | collective-permute-start | bytes 884744 | tf_op jit(solution)/shard_map/ppermute | solution.py:83
  8.0 11.3 %collective-permute-start.3 = (bf16[384,384]{1,0:T(8,128)(2,1)S(1)}, bf16[384,384]{1,0:T(8,128)(2,1)S(1)}, u32[]{:S(2)}, u32[]{:S(2)}) collective-permute-start(bf16[384,384]{1,0:T(8,128)(2,1)S(1)} %get-tuple-element.15.refs_1_.refs_17_), channel_id=1, source_target_pairs={{0,1},{2,0},{4,2},{5,7},{3,5},{1,3},{8,9},{10,8},{12,10},{14,12},{... | collective-permute-start | bytes 884744 | tf_op jit(solution)/shard_map/ppermute | solution.py:83
  9.9 11.3 %collective-permute-start.2 = (bf16[384,384]{1,0:T(8,128)(2,1)S(1)}, bf16[384,384]{1,0:T(8,128)(2,1)S(1)}, u32[]{:S(2)}, u32[]{:S(2)}) collective-permute-start(bf16[384,384]{1,0:T(8,128)(2,1)S(1)} %get-tuple-element.15.refs_1_.refs_17_), channel_id=1, source_target_pairs={{0,2},{2,4},{4,6},{5,3},{3,1},{1,0},{8,10},{10,12},{12,14},{14,15}... | collective-permute-start | bytes 884744 | tf_op jit(solution)/shard_map/ppermute | solution.py:83
  13.8 10.8 %collective-permute-start.1 = (bf16[384,384]{1,0:T(8,128)(2,1)S(1)}, bf16[384,384]{1,0:T(8,128)(2,1)S(1)}, u32[]{:S(2)}, u32[]{:S(2)}) collective-permute-start(bf16[384,384]{1,0:T(8,128)(2,1)S(1)} %get-tuple-element.14.refs_0_.refs_16_), channel_id=1, source_target_pairs={{0,1},{2,0},{4,2},{3,5},{1,3},{8,9},{10,8},{12,10},{14,12},{13,15}... | collective-permute-start | bytes 884744 | tf_op jit(solution)/shard_map/ppermute | solution.py:83
  15.7 12.4 %collective-permute-start.16 = (bf16[384,384]{1,0:T(8,128)(2,1)S(1)}, bf16[384,384]{1,0:T(8,128)(2,1)S(1)}, u32[]{:S(2)}, u32[]{:S(2)}) collective-permute-start(bf16[384,384]{1,0:T(8,128)(2,1)S(1)} %get-tuple-element.14.refs_0_.refs_16_), channel_id=1, source_target_pairs={{0,16},{8,24},{16,0},{24,8},{1,17},{9,25},{17,1},{25,9},{2,18},{10... | collective-permute-start | bytes 884744 | tf_op jit(solution)/shard_map/ppermute | solution.py:94
  17.3 13.3 %collective-permute-start.17 = (bf16[384,384]{1,0:T(8,128)(2,1)S(1)}, bf16[384,384]{1,0:T(8,128)(2,1)S(1)}, u32[]{:S(2)}, u32[]{:S(2)}) collective-permute-start(bf16[384,384]{1,0:T(8,128)(2,1)S(1)} %get-tuple-element.15.refs_1_.refs_17_), channel_id=1, source_target_pairs={{0,16},{8,24},{16,0},{24,8},{1,17},{9,25},{17,1},{25,9},{2,18},{10... | collective-permute-start | bytes 884744 | tf_op jit(solution)/shard_map/ppermute | solution.py:94
  19.3 14.8 %collective-permute-start.14 = (bf16[384,384]{1,0:T(8,128)(2,1)S(1)}, bf16[384,384]{1,0:T(8,128)(2,1)S(1)}, u32[]{:S(2)}, u32[]{:S(2)}) collective-permute-start(bf16[384,384]{1,0:T(8,128)(2,1)S(1)} %get-tuple-element.14.refs_0_.refs_16_), channel_id=1, source_target_pairs={{0,8},{8,0},{16,24},{24,16},{1,9},{9,1},{17,25},{25,17},{2,10},{10... | collective-permute-start | bytes 884744 | tf_op jit(solution)/shard_map/ppermute | solution.py:97
  21.2 15.2 %collective-permute-start.15 = (bf16[384,384]{1,0:T(8,128)(2,1)S(1)}, bf16[384,384]{1,0:T(8,128)(2,1)S(1)}, u32[]{:S(2)}, u32[]{:S(2)}) collective-permute-start(bf16[384,384]{1,0:T(8,128)(2,1)S(1)} %get-tuple-element.15.refs_1_.refs_17_), channel_id=1, source_target_pairs={{0,8},{8,0},{16,24},{24,16},{1,9},{9,1},{17,25},{25,17},{2,10},{10... | collective-permute-start | bytes 884744 | tf_op jit(solution)/shard_map/ppermute | solution.py:97
  24.6 11.9 %collective-permute-start.4 = (bf16[384,384]{1,0:T(8,128)(2,1)S(1)}, bf16[384,384]{1,0:T(8,128)(2,1)S(1)}, u32[]{:S(2)}, u32[]{:S(2)}) collective-permute-start(bf16[384,384]{1,0:T(8,128)(2,1)S(1)} %collective-permute-done.refs_2_), channel_id=1, source_target_pairs={{0,2},{2,4},{4,6},{6,7},{1,0},{8,10},{10,12},{12,14},{14,15},{15,1... | collective-permute-start | bytes 884744 | tf_op jit(solution)/shard_map/ppermute | solution.py:83
  28.1 11.9 %collective-permute-start.7 = (bf16[384,384]{1,0:T(8,128)(2,1)S(1)}, bf16[384,384]{1,0:T(8,128)(2,1)S(1)}, u32[]{:S(2)}, u32[]{:S(2)}) collective-permute-start(bf16[384,384]{1,0:T(8,128)(2,1)S(1)} %collective-permute-done.3.refs_5_), channel_id=1, source_target_pairs={{0,1},{2,0},{7,6},{5,7},{3,5},{1,3},{8,9},{10,8},{12,10},{14,12},{... | collective-permute-start | bytes 884744 | tf_op jit(solution)/shard_map/ppermute | solution.py:83
  30.5 26.2 %copy-start.3 = (bf16[384,384]{1,0:T(8,128)(2,1)}, bf16[384,384]{1,0:T(8,128)(2,1)S(1)}, u32[]{:S(2)}) copy-start(bf16[384,384]{1,0:T(8,128)(2,1)S(1)} %collective-permute-done.17.refs_21_) | copy-start | bytes 884740
  30.5 10.8 %collective-permute-start.6 = (bf16[384,384]{1,0:T(8,128)(2,1)S(1)}, bf16[384,384]{1,0:T(8,128)(2,1)S(1)}, u32[]{:S(2)}, u32[]{:S(2)}) collective-permute-start(bf16[384,384]{1,0:T(8,128)(2,1)S(1)} %collective-permute-done.2.refs_4_), channel_id=1, source_target_pairs={{0,2},{2,4},{4,6},{6,7},{3,1},{1,0},{8,10},{10,12},{12,14},{14,15}... | collective-permute-start | bytes 884744 | tf_op jit(solution)/shard_map/ppermute | solution.py:83
  34.0 10.0 %collective-permute-start.5 = (bf16[384,384]{1,0:T(8,128)(2,1)S(1)}, bf16[384,384]{1,0:T(8,128)(2,1)S(1)}, u32[]{:S(2)}, u32[]{:S(2)}) collective-permute-start(bf16[384,384]{1,0:T(8,128)(2,1)S(1)} %collective-permute-done.1.refs_3_), channel_id=1, source_target_pairs={{0,1},{2,0},{5,7},{3,5},{1,3},{8,9},{10,8},{12,10},{15,14},{13,15}... | collective-permute-start | bytes 884744 | tf_op jit(solution)/shard_map/ppermute | solution.py:83
  36.4 9.6 %collective-permute-start.18 = (bf16[384,384]{1,0:T(8,128)(2,1)S(1)}, bf16[384,384]{1,0:T(8,128)(2,1)S(1)}, u32[]{:S(2)}, u32[]{:S(2)}) collective-permute-start(bf16[384,384]{1,0:T(8,128)(2,1)S(1)} %collective-permute-done.16.refs_20_), channel_id=1, source_target_pairs={{0,8},{8,0},{16,24},{24,16},{1,9},{9,1},{17,25},{25,17},{2,10},{10... | collective-permute-start | bytes 884744 | tf_op jit(solution)/shard_map/ppermute | solution.py:97
  36.5 13.5 %collective-permute-start.8 = (bf16[384,384]{1,0:T(8,128)(2,1)S(1)}, bf16[384,384]{1,0:T(8,128)(2,1)S(1)}, u32[]{:S(2)}, u32[]{:S(2)}) collective-permute-start(bf16[384,384]{1,0:T(8,128)(2,1)S(1)} %collective-permute-done.4.refs_6_), channel_id=1, source_target_pairs={{0,2},{2,4},{4,6},{6,7},{7,5},{8,10},{10,12},{12,14},{14,15},{15,1... | collective-permute-start | bytes 884744 | tf_op jit(solution)/shard_map/ppermute | solution.py:83
  40.0 10.6 %collective-permute-start.11 = (bf16[384,384]{1,0:T(8,128)(2,1)S(1)}, bf16[384,384]{1,0:T(8,128)(2,1)S(1)}, u32[]{:S(2)}, u32[]{:S(2)}) collective-permute-start(bf16[384,384]{1,0:T(8,128)(2,1)S(1)} %collective-permute-done.7.refs_9_), channel_id=1, source_target_pairs={{0,1},{6,4},{7,6},{5,7},{3,5},{1,3},{8,9},{10,8},{12,10},{14,12},{... | collective-permute-start | bytes 884744 | tf_op jit(solution)/shard_map/ppermute | solution.py:83
  41.4 10.0 %collective-permute-start.19 = (bf16[384,384]{1,0:T(8,128)(2,1)S(1)}, bf16[384,384]{1,0:T(8,128)(2,1)S(1)}, u32[]{:S(2)}, u32[]{:S(2)}) collective-permute-start(bf16[384,384]{1,0:T(8,128)(2,1)S(1)} %collective-permute-done.17.refs_21_), channel_id=1, source_target_pairs={{0,8},{8,0},{16,24},{24,16},{1,9},{9,1},{17,25},{25,17},{2,10},{10... | collective-permute-start | bytes 884744 | tf_op jit(solution)/shard_map/ppermute | solution.py:97
  44.1 9.6 %collective-permute-start.10 = (bf16[384,384]{1,0:T(8,128)(2,1)S(1)}, bf16[384,384]{1,0:T(8,128)(2,1)S(1)}, u32[]{:S(2)}, u32[]{:S(2)}) collective-permute-start(bf16[384,384]{1,0:T(8,128)(2,1)S(1)} %collective-permute-done.6.refs_8_), channel_id=1, source_target_pairs={{0,2},{2,4},{4,6},{6,7},{7,5},{1,0},{8,10},{10,12},{12,14},{14,15}... | collective-permute-start | bytes 884744 | tf_op jit(solution)/shard_map/ppermute | solution.py:83
  46.0 10.7 %copy-start.7 = (bf16[384,384]{1,0:T(8,128)(2,1)}, bf16[384,384]{1,0:T(8,128)(2,1)S(1)}, u32[]{:S(2)}) copy-start(bf16[384,384]{1,0:T(8,128)(2,1)S(1)} %collective-permute-done.18.refs_22_) | copy-start | bytes 884740
  46.0 10.7 %collective-permute-start.9 = (bf16[384,384]{1,0:T(8,128)(2,1)S(1)}, bf16[384,384]{1,0:T(8,128)(2,1)S(1)}, u32[]{:S(2)}, u32[]{:S(2)}) collective-permute-start(bf16[384,384]{1,0:T(8,128)(2,1)S(1)} %collective-permute-done.5.refs_7_), channel_id=1, source_target_pairs={{0,1},{7,6},{5,7},{3,5},{1,3},{8,9},{10,8},{14,12},{15,14},{13,15}... | collective-permute-start | bytes 884744 | tf_op jit(solution)/shard_map/ppermute | solution.py:83
  50.0 6.8 %collective-permute-start.12 = (bf16[384,384]{1,0:T(8,128)(2,1)S(1)}, bf16[384,384]{1,0:T(8,128)(2,1)S(1)}, u32[]{:S(2)}, u32[]{:S(2)}) collective-permute-start(bf16[384,384]{1,0:T(8,128)(2,1)S(1)} %collective-permute-done.8.refs_10_), channel_id=1, source_target_pairs={{2,4},{4,6},{6,7},{7,5},{5,3},{8,10},{10,12},{12,14},{14,15},{15,1... | collective-permute-start | bytes 884744 | tf_op jit(solution)/shard_map/ppermute | solution.py:83
  50.7 6.1 %collective-permute-start.13 = (bf16[384,384]{1,0:T(8,128)(2,1)S(1)}, bf16[384,384]{1,0:T(8,128)(2,1)S(1)}, u32[]{:S(2)}, u32[]{:S(2)}) collective-permute-start(bf16[384,384]{1,0:T(8,128)(2,1)S(1)} %collective-permute-done.11.refs_13_), channel_id=1, source_target_pairs={{4,2},{6,4},{7,6},{5,7},{3,5},{1,3},{8,9},{10,8},{12,10},{14,12},{... | collective-permute-start | bytes 884744 | tf_op jit(solution)/shard_map/ppermute | solution.py:83
  51.4 5.4 %copy-start.10 = (bf16[384,384]{1,0:T(8,128)(2,1)}, bf16[384,384]{1,0:T(8,128)(2,1)S(1)}, u32[]{:S(2)}) copy-start(bf16[384,384]{1,0:T(8,128)(2,1)S(1)} %collective-permute-done.19.refs_23_) | copy-start | bytes 884740
  61.2 16.3 %collective-permute-start.22 = (bf16[384,384]{1,0:T(8,128)(2,1)S(1)}, bf16[384,384]{1,0:T(8,128)(2,1)S(1)}, u32[]{:S(2)}, u32[]{:S(2)}) collective-permute-start(bf16[384,384]{1,0:T(8,128)(2,1)S(1)} %get-tuple-element.16.refs_16_), channel_id=1, source_target_pairs={{0,16},{8,24},{16,0},{24,8},{1,17},{9,25},{17,1},{25,9},{2,18},{10... | collective-permute-start | bytes 884744 | tf_op jit(solution)/shard_map/ppermute | solution.py:94
  69.7 11.0 %collective-permute-start.23 = (bf16[384,384]{1,0:T(8,128)(2,1)S(1)}, bf16[384,384]{1,0:T(8,128)(2,1)S(1)}, u32[]{:S(2)}, u32[]{:S(2)}) collective-permute-start(bf16[384,384]{1,0:T(8,128)(2,1)S(1)} %get-tuple-element.17.refs_17_), channel_id=1, source_target_pairs={{0,16},{8,24},{16,0},{24,8},{1,17},{9,25},{17,1},{25,9},{2,18},{10... | collective-permute-start | bytes 884744 | tf_op jit(solution)/shard_map/ppermute | solution.py:94
  69.8 10.9 %collective-permute-start.20 = (bf16[384,384]{1,0:T(8,128)(2,1)S(1)}, bf16[384,384]{1,0:T(8,128)(2,1)S(1)}, u32[]{:S(2)}, u32[]{:S(2)}) collective-permute-start(bf16[384,384]{1,0:T(8,128)(2,1)S(1)} %get-tuple-element.16.refs_16_), channel_id=1, source_target_pairs={{0,8},{8,0},{16,24},{24,16},{1,9},{9,1},{17,25},{25,17},{2,10},{10... | collective-permute-start | bytes 884744 | tf_op jit(solution)/shard_map/ppermute | solution.py:97
  69.8 10.9 %collective-permute-start.21 = (bf16[384,384]{1,0:T(8,128)(2,1)S(1)}, bf16[384,384]{1,0:T(8,128)(2,1)S(1)}, u32[]{:S(2)}, u32[]{:S(2)}) collective-permute-start(bf16[384,384]{1,0:T(8,128)(2,1)S(1)} %get-tuple-element.17.refs_17_), channel_id=1, source_target_pairs={{0,8},{8,0},{16,24},{24,16},{1,9},{9,1},{17,25},{25,17},{2,10},{10... | collective-permute-start | bytes 884744 | tf_op jit(solution)/shard_map/ppermute | solution.py:97
  77.5 4.7 %copy-start.11 = (bf16[384,384]{1,0:T(8,128)(2,1)}, bf16[384,384]{1,0:T(8,128)(2,1)S(1)}, u32[]{:S(2)}) copy-start(bf16[384,384]{1,0:T(8,128)(2,1)S(1)} %collective-permute-done.22.refs_20_) | copy-start | bytes 884740
  77.5 3.2 %collective-permute-start.24 = (bf16[384,384]{1,0:T(8,128)(2,1)S(1)}, bf16[384,384]{1,0:T(8,128)(2,1)S(1)}, u32[]{:S(2)}, u32[]{:S(2)}) collective-permute-start(bf16[384,384]{1,0:T(8,128)(2,1)S(1)} %collective-permute-done.22.refs_20_), channel_id=1, source_target_pairs={{0,8},{8,0},{16,24},{24,16},{1,9},{9,1},{17,25},{25,17},{2,10},{10... | collective-permute-start | bytes 884744 | tf_op jit(solution)/shard_map/ppermute | solution.py:97
  80.7 1.6 copy-start.12
  80.7 1.6 collective-permute-start.25
  80.7 1.6 copy-start.13
  88.6 9.9 %collective-permute-start.42 = (bf16[384,384]{1,0:T(8,128)(2,1)S(1)}, bf16[384,384]{1,0:T(8,128)(2,1)S(1)}, u32[]{:S(2)}, u32[]{:S(2)}) collective-permute-start(bf16[384,384]{1,0:T(8,128)(2,1)S(1)} %get-tuple-element.19.refs_16_.refs_0_), channel_id=1, source_target_pairs={{0,16},{8,24},{16,0},{24,8},{1,17},{9,25},{17,1},{25,9},{2,18},{10... | collective-permute-start | bytes 884744 | tf_op jit(solution)/shard_map/ppermute | solution.py:94
  90.4 13.6 %collective-permute-start.43 = (bf16[384,384]{1,0:T(8,128)(2,1)S(1)}, bf16[384,384]{1,0:T(8,128)(2,1)S(1)}, u32[]{:S(2)}, u32[]{:S(2)}) collective-permute-start(bf16[384,384]{1,0:T(8,128)(2,1)S(1)} %get-tuple-element.20.refs_17_.refs_1_), channel_id=1, source_target_pairs={{0,16},{8,24},{16,0},{24,8},{1,17},{9,25},{17,1},{25,9},{2,18},{10... | collective-permute-start | bytes 884744 | tf_op jit(solution)/shard_map/ppermute | solution.py:94
  90.7 15.8 %collective-permute-start.40 = (bf16[384,384]{1,0:T(8,128)(2,1)S(1)}, bf16[384,384]{1,0:T(8,128)(2,1)S(1)}, u32[]{:S(2)}, u32[]{:S(2)}) collective-permute-start(bf16[384,384]{1,0:T(8,128)(2,1)S(1)} %get-tuple-element.19.refs_16_.refs_0_), channel_id=1, source_target_pairs={{0,8},{8,0},{16,24},{24,16},{1,9},{9,1},{17,25},{25,17},{2,10},{10... | collective-permute-start | bytes 884744 | tf_op jit(solution)/shard_map/ppermute | solution.py:97
  90.7 19.2 %collective-permute-start.41 = (bf16[384,384]{1,0:T(8,128)(2,1)S(1)}, bf16[384,384]{1,0:T(8,128)(2,1)S(1)}, u32[]{:S(2)}, u32[]{:S(2)}) collective-permute-start(bf16[384,384]{1,0:T(8,128)(2,1)S(1)} %get-tuple-element.20.refs_17_.refs_1_), channel_id=1, source_target_pairs={{0,8},{8,0},{16,24},{24,16},{1,9},{9,1},{17,25},{25,17},{2,10},{10... | collective-permute-start | bytes 884744 | tf_op jit(solution)/shard_map/ppermute | solution.py:97
  91.2 18.8 %collective-permute-start.26 = (bf16[384,384]{1,0:T(8,128)(2,1)S(1)}, bf16[384,384]{1,0:T(8,128)(2,1)S(1)}, u32[]{:S(2)}, u32[]{:S(2)}) collective-permute-start(bf16[384,384]{1,0:T(8,128)(2,1)S(1)} %get-tuple-element.19.refs_16_.refs_0_), channel_id=1, source_target_pairs={{0,2},{2,4},{4,6},{3,1},{1,0},{8,10},{10,12},{12,14},{14,15},{13,1... | collective-permute-start | bytes 884744 | tf_op jit(solution)/shard_map/ppermute | solution.py:83
  98.5 25.3 %copy-start.4 = (bf16[384,384]{1,0:T(8,128)(2,1)}, bf16[384,384]{1,0:T(8,128)(2,1)S(1)}, u32[]{:S(2)}) copy-start(bf16[384,384]{1,0:T(8,128)(2,1)S(1)} %collective-permute-done.42.refs_20_) | copy-start | bytes 884740
  98.5 12.0 %collective-permute-start.29 = (bf16[384,384]{1,0:T(8,128)(2,1)S(1)}, bf16[384,384]{1,0:T(8,128)(2,1)S(1)}, u32[]{:S(2)}, u32[]{:S(2)}) collective-permute-start(bf16[384,384]{1,0:T(8,128)(2,1)S(1)} %get-tuple-element.20.refs_17_.refs_1_), channel_id=1, source_target_pairs={{0,1},{2,0},{4,2},{5,7},{3,5},{1,3},{8,9},{10,8},{12,10},{14,12},{... | collective-permute-start | bytes 884744 | tf_op jit(solution)/shard_map/ppermute | solution.py:83
  104.0 19.8 %copy-start.5 = (bf16[384,384]{1,0:T(8,128)(2,1)}, bf16[384,384]{1,0:T(8,128)(2,1)S(1)}, u32[]{:S(2)}) copy-start(bf16[384,384]{1,0:T(8,128)(2,1)S(1)} %collective-permute-done.43.refs_21_) | copy-start | bytes 884740
  104.0 10.1 %collective-permute-start.27 = (bf16[384,384]{1,0:T(8,128)(2,1)S(1)}, bf16[384,384]{1,0:T(8,128)(2,1)S(1)}, u32[]{:S(2)}, u32[]{:S(2)}) collective-permute-start(bf16[384,384]{1,0:T(8,128)(2,1)S(1)} %get-tuple-element.19.refs_16_.refs_0_), channel_id=1, source_target_pairs={{0,1},{2,0},{4,2},{3,5},{1,3},{8,9},{10,8},{12,10},{14,12},{13,15}... | collective-permute-start | bytes 884744 | tf_op jit(solution)/shard_map/ppermute | solution.py:83
  106.5 11.0 %collective-permute-start.28 = (bf16[384,384]{1,0:T(8,128)(2,1)S(1)}, bf16[384,384]{1,0:T(8,128)(2,1)S(1)}, u32[]{:S(2)}, u32[]{:S(2)}) collective-permute-start(bf16[384,384]{1,0:T(8,128)(2,1)S(1)} %get-tuple-element.20.refs_17_.refs_1_), channel_id=1, source_target_pairs={{0,2},{2,4},{4,6},{5,3},{3,1},{1,0},{8,10},{10,12},{12,14},{14,15}... | collective-permute-start | bytes 884744 | tf_op jit(solution)/shard_map/ppermute | solution.py:83
  109.9 14.0 %copy-start.6 = (bf16[384,384]{1,0:T(8,128)(2,1)}, bf16[384,384]{1,0:T(8,128)(2,1)S(1)}, u32[]{:S(2)}) copy-start(bf16[384,384]{1,0:T(8,128)(2,1)S(1)} %collective-permute-done.41.refs_19_) | copy-start | bytes 884740
  109.9 11.8 %collective-permute-start.44 = (bf16[384,384]{1,0:T(8,128)(2,1)S(1)}, bf16[384,384]{1,0:T(8,128)(2,1)S(1)}, u32[]{:S(2)}, u32[]{:S(2)}) collective-permute-start(bf16[384,384]{1,0:T(8,128)(2,1)S(1)} %collective-permute-done.42.refs_20_), channel_id=1, source_target_pairs={{0,8},{8,0},{16,24},{24,16},{1,9},{9,1},{17,25},{25,17},{2,10},{10... | collective-permute-start | bytes 884744 | tf_op jit(solution)/shard_map/ppermute | solution.py:97
  110.0 13.8 %collective-permute-start.45 = (bf16[384,384]{1,0:T(8,128)(2,1)S(1)}, bf16[384,384]{1,0:T(8,128)(2,1)S(1)}, u32[]{:S(2)}, u32[]{:S(2)}) collective-permute-start(bf16[384,384]{1,0:T(8,128)(2,1)S(1)} %collective-permute-done.43.refs_21_), channel_id=1, source_target_pairs={{0,8},{8,0},{16,24},{24,16},{1,9},{9,1},{17,25},{25,17},{2,10},{10... | collective-permute-start | bytes 884744 | tf_op jit(solution)/shard_map/ppermute | solution.py:97
  110.5 20.1 %collective-permute-start.30 = (bf16[384,384]{1,0:T(8,128)(2,1)S(1)}, bf16[384,384]{1,0:T(8,128)(2,1)S(1)}, u32[]{:S(2)}, u32[]{:S(2)}) collective-permute-start(bf16[384,384]{1,0:T(8,128)(2,1)S(1)} %collective-permute-done.26.refs_2_), channel_id=1, source_target_pairs={{0,2},{2,4},{4,6},{6,7},{1,0},{8,10},{10,12},{12,14},{14,15},{15,1... | collective-permute-start | bytes 884744 | tf_op jit(solution)/shard_map/ppermute | solution.py:83
  114.1 17.2 %collective-permute-start.33 = (bf16[384,384]{1,0:T(8,128)(2,1)S(1)}, bf16[384,384]{1,0:T(8,128)(2,1)S(1)}, u32[]{:S(2)}, u32[]{:S(2)}) collective-permute-start(bf16[384,384]{1,0:T(8,128)(2,1)S(1)} %collective-permute-done.29.refs_5_), channel_id=1, source_target_pairs={{0,1},{2,0},{7,6},{5,7},{3,5},{1,3},{8,9},{10,8},{12,10},{14,12},{... | collective-permute-start | bytes 884744 | tf_op jit(solution)/shard_map/ppermute | solution.py:83
  117.5 13.8 %collective-permute-start.31 = (bf16[384,384]{1,0:T(8,128)(2,1)S(1)}, bf16[384,384]{1,0:T(8,128)(2,1)S(1)}, u32[]{:S(2)}, u32[]{:S(2)}) collective-permute-start(bf16[384,384]{1,0:T(8,128)(2,1)S(1)} %collective-permute-done.27.refs_3_), channel_id=1, source_target_pairs={{0,1},{2,0},{5,7},{3,5},{1,3},{8,9},{10,8},{12,10},{15,14},{13,15}... | collective-permute-start | bytes 884744 | tf_op jit(solution)/shard_map/ppermute | solution.py:83
  121.7 2.2 %copy-start.8 = (bf16[384,384]{1,0:T(8,128)(2,1)}, bf16[384,384]{1,0:T(8,128)(2,1)S(1)}, u32[]{:S(2)}) copy-start(bf16[384,384]{1,0:T(8,128)(2,1)S(1)} %collective-permute-done.44.refs_22_) | copy-start | bytes 884740
  121.7 10.2 %collective-permute-start.32 = (bf16[384,384]{1,0:T(8,128)(2,1)S(1)}, bf16[384,384]{1,0:T(8,128)(2,1)S(1)}, u32[]{:S(2)}, u32[]{:S(2)}) collective-permute-start(bf16[384,384]{1,0:T(8,128)(2,1)S(1)} %collective-permute-done.28.refs_4_), channel_id=1, source_target_pairs={{0,2},{2,4},{4,6},{6,7},{3,1},{1,0},{8,10},{10,12},{12,14},{14,15}... | collective-permute-start | bytes 884744 | tf_op jit(solution)/shard_map/ppermute | solution.py:83
  129.2 25.0 %copy-start.2 = (s32[24]{0:T(128)S(1)}, s32[24]{0:T(128)}, u32[]{:S(2)}) copy-start(s32[24]{0:T(128)} %frag_ref.1) | copy-start | bytes 292
  129.2 9.7 %collective-permute-start.48 = (bf16[384,384]{1,0:T(8,128)(2,1)S(1)}, bf16[384,384]{1,0:T(8,128)(2,1)S(1)}, u32[]{:S(2)}, u32[]{:S(2)}) collective-permute-start(bf16[384,384]{1,0:T(8,128)(2,1)S(1)} %get-tuple-element.21.refs_16_), channel_id=1, source_target_pairs={{0,16},{8,24},{16,0},{24,8},{1,17},{9,25},{17,1},{25,9},{2,18},{10... | collective-permute-start | bytes 884744 | tf_op jit(solution)/shard_map/ppermute | solution.py:94
  130.6 11.6 %collective-permute-start.49 = (bf16[384,384]{1,0:T(8,128)(2,1)S(1)}, bf16[384,384]{1,0:T(8,128)(2,1)S(1)}, u32[]{:S(2)}, u32[]{:S(2)}) collective-permute-start(bf16[384,384]{1,0:T(8,128)(2,1)S(1)} %get-tuple-element.22.refs_17_), channel_id=1, source_target_pairs={{0,16},{8,24},{16,0},{24,8},{1,17},{9,25},{17,1},{25,9},{2,18},{10... | collective-permute-start | bytes 884744 | tf_op jit(solution)/shard_map/ppermute | solution.py:94
  131.3 13.4 %collective-permute-start.46 = (bf16[384,384]{1,0:T(8,128)(2,1)S(1)}, bf16[384,384]{1,0:T(8,128)(2,1)S(1)}, u32[]{:S(2)}, u32[]{:S(2)}) collective-permute-start(bf16[384,384]{1,0:T(8,128)(2,1)S(1)} %get-tuple-element.21.refs_16_), channel_id=1, source_target_pairs={{0,8},{8,0},{16,24},{24,16},{1,9},{9,1},{17,25},{25,17},{2,10},{10... | collective-permute-start | bytes 884744 | tf_op jit(solution)/shard_map/ppermute | solution.py:97
  131.4 15.4 %collective-permute-start.47 = (bf16[384,384]{1,0:T(8,128)(2,1)S(1)}, bf16[384,384]{1,0:T(8,128)(2,1)S(1)}, u32[]{:S(2)}, u32[]{:S(2)}) collective-permute-start(bf16[384,384]{1,0:T(8,128)(2,1)S(1)} %get-tuple-element.22.refs_17_), channel_id=1, source_target_pairs={{0,8},{8,0},{16,24},{24,16},{1,9},{9,1},{17,25},{25,17},{2,10},{10... | collective-permute-start | bytes 884744 | tf_op jit(solution)/shard_map/ppermute | solution.py:97
  131.9 15.0 %collective-permute-start.34 = (bf16[384,384]{1,0:T(8,128)(2,1)S(1)}, bf16[384,384]{1,0:T(8,128)(2,1)S(1)}, u32[]{:S(2)}, u32[]{:S(2)}) collective-permute-start(bf16[384,384]{1,0:T(8,128)(2,1)S(1)} %collective-permute-done.30.refs_6_), channel_id=1, source_target_pairs={{0,2},{2,4},{4,6},{6,7},{7,5},{8,10},{10,12},{12,14},{14,15},{15,1... | collective-permute-start | bytes 884744 | tf_op jit(solution)/shard_map/ppermute | solution.py:83
  138.9 8.4 %collective-permute-start.37 = (bf16[384,384]{1,0:T(8,128)(2,1)S(1)}, bf16[384,384]{1,0:T(8,128)(2,1)S(1)}, u32[]{:S(2)}, u32[]{:S(2)}) collective-permute-start(bf16[384,384]{1,0:T(8,128)(2,1)S(1)} %collective-permute-done.33.refs_9_), channel_id=1, source_target_pairs={{0,1},{6,4},{7,6},{5,7},{3,5},{1,3},{8,9},{10,8},{12,10},{14,12},{... | collective-permute-start | bytes 884744 | tf_op jit(solution)/shard_map/ppermute | solution.py:83
  142.1 11.4 %copy-start.16 = (bf16[384,384]{1,0:T(8,128)(2,1)}, bf16[384,384]{1,0:T(8,128)(2,1)S(1)}, u32[]{:S(2)}) copy-start(bf16[384,384]{1,0:T(8,128)(2,1)S(1)} %collective-permute-done.49.refs_21_) | copy-start | bytes 884740
  142.1 8.4 %collective-permute-start.35 = (bf16[384,384]{1,0:T(8,128)(2,1)S(1)}, bf16[384,384]{1,0:T(8,128)(2,1)S(1)}, u32[]{:S(2)}, u32[]{:S(2)}) collective-permute-start(bf16[384,384]{1,0:T(8,128)(2,1)S(1)} %collective-permute-done.31.refs_7_), channel_id=1, source_target_pairs={{0,1},{7,6},{5,7},{3,5},{1,3},{8,9},{10,8},{14,12},{15,14},{13,15}... | collective-permute-start | bytes 884744 | tf_op jit(solution)/shard_map/ppermute | solution.py:83
  144.8 8.6 %collective-permute-start.36 = (bf16[384,384]{1,0:T(8,128)(2,1)S(1)}, bf16[384,384]{1,0:T(8,128)(2,1)S(1)}, u32[]{:S(2)}, u32[]{:S(2)}) collective-permute-start(bf16[384,384]{1,0:T(8,128)(2,1)S(1)} %collective-permute-done.32.refs_8_), channel_id=1, source_target_pairs={{0,2},{2,4},{4,6},{6,7},{7,5},{1,0},{8,10},{10,12},{12,14},{14,15}... | collective-permute-start | bytes 884744 | tf_op jit(solution)/shard_map/ppermute | solution.py:83
  146.7 6.7 %collective-permute-start.50 = (bf16[384,384]{1,0:T(8,128)(2,1)S(1)}, bf16[384,384]{1,0:T(8,128)(2,1)S(1)}, u32[]{:S(2)}, u32[]{:S(2)}) collective-permute-start(bf16[384,384]{1,0:T(8,128)(2,1)S(1)} %collective-permute-done.48.refs_20_), channel_id=1, source_target_pairs={{0,8},{8,0},{16,24},{24,16},{1,9},{9,1},{17,25},{25,17},{2,10},{10... | collective-permute-start | bytes 884744 | tf_op jit(solution)/shard_map/ppermute | solution.py:97
  146.8 6.6 %collective-permute-start.51 = (bf16[384,384]{1,0:T(8,128)(2,1)S(1)}, bf16[384,384]{1,0:T(8,128)(2,1)S(1)}, u32[]{:S(2)}, u32[]{:S(2)}) collective-permute-start(bf16[384,384]{1,0:T(8,128)(2,1)S(1)} %collective-permute-done.49.refs_21_), channel_id=1, source_target_pairs={{0,8},{8,0},{16,24},{24,16},{1,9},{9,1},{17,25},{25,17},{2,10},{10... | collective-permute-start | bytes 884744 | tf_op jit(solution)/shard_map/ppermute | solution.py:97
  147.3 6.1 %collective-permute-start.38 = (bf16[384,384]{1,0:T(8,128)(2,1)S(1)}, bf16[384,384]{1,0:T(8,128)(2,1)S(1)}, u32[]{:S(2)}, u32[]{:S(2)}) collective-permute-start(bf16[384,384]{1,0:T(8,128)(2,1)S(1)} %collective-permute-done.34.refs_10_), channel_id=1, source_target_pairs={{2,4},{4,6},{6,7},{7,5},{5,3},{8,10},{10,12},{12,14},{14,15},{15,1... | collective-permute-start | bytes 884744 | tf_op jit(solution)/shard_map/ppermute | solution.py:83
  150.5 2.9 %collective-permute-start.39 = (bf16[384,384]{1,0:T(8,128)(2,1)S(1)}, bf16[384,384]{1,0:T(8,128)(2,1)S(1)}, u32[]{:S(2)}, u32[]{:S(2)}) collective-permute-start(bf16[384,384]{1,0:T(8,128)(2,1)S(1)} %collective-permute-done.37.refs_13_), channel_id=1, source_target_pairs={{4,2},{6,4},{7,6},{5,7},{3,5},{1,3},{8,9},{10,8},{12,10},{14,12},{... | collective-permute-start | bytes 884744 | tf_op jit(solution)/shard_map/ppermute | solution.py:83
  (7 other events, 6.3 us)

commit v2 on v0

v2 whole, which is shorter than its diff:
```python
import functools

import jax
import jax.numpy as jnp
from jax import lax
from jax.experimental import pallas as pl
from jax.experimental.pallas import tpu as pltpu
from jax.sharding import PartitionSpec as P

BLK = 128
FRAG_DEV = 2
AXES = ("row", "col")
SPARE_VMEM = 10 * 1024 * 1024


def cycle_of(count):
    width = 1
    while (2 * width) ** 2 <= count:
        width *= 2
    depth = count // width
    walk = [(step, 0) for step in range(depth)]
    for turn, step in enumerate(range(depth - 1, -1, -1)):
        across = list(range(1, width))
        walk += [(step, place) for place in (across[::-1] if turn % 2 else across)]
    return [step * width + place for step, place in walk]


class Plan:
    def __init__(self, rows_here, cols_here):
        self.rows = lax.axis_size("row")
        self.cols = lax.axis_size("col")
        self.rows_here = rows_here
        self.cols_here = cols_here
        self.order = self.rows * rows_here
        self.block_rows = rows_here // BLK
        self.block_cols = cols_here // BLK
        self.cycle = cycle_of(self.cols)
        self.far = self.cols // 2

    def ring(self, value):
        pairs = []
        for row in range(self.rows):
            direction = -1 if row % 2 else 1
            for place in range(self.cols):
                target = self.cycle[(place + direction) % self.cols]
                pairs.append((row * self.cols + self.cycle[place], row * self.cols + target))
        return lax.ppermute(value, AXES, pairs)

    def across(self, value, other):
        return lax.ppermute(value, "row", [(i, i ^ other) for i in range(self.rows)])

    def origin_first(self, distance, behind):
        col = lax.axis_index("col")
        forward = (lax.axis_index("row") % 2 == 0) == behind
        origin = jnp.int32(0)
        for place in range(self.cols):
            before = self.cycle[(place - distance) % self.cols]
            after = self.cycle[(place + distance) % self.cols]
            source = jnp.where(forward, jnp.int32(before), jnp.int32(after))
            origin = jnp.where(col == self.cycle[place], source, origin)
        return pl.multiple_of(origin * self.cols_here, self.cols_here)

    def row_first(self, other):
        return pl.multiple_of((lax.axis_index("row") ^ other) * self.rows_here, self.rows_here)


def masked(plan, band_ref, value):
    lines = []
    for i in range(plan.block_rows):
        line = []
        for j in range(plan.block_cols):
            row = lax.axis_index("row") * plan.block_rows + i
            col = lax.axis_index("col") * plan.block_cols + j
            keep = jnp.abs(row - col) <= jnp.maximum(band_ref[row], band_ref[col])
            block = value[i * BLK : (i + 1) * BLK, j * BLK : (j + 1) * BLK]
            line.append(block * keep.astype(jnp.float32))
        lines.append(jnp.concatenate(line, axis=1))
    return jnp.concatenate(lines, axis=0)


def dot(left, right):
    return jnp.dot(left, right, preferred_element_type=jnp.float32)


def call(kernel, outs, scalars, arrays, flops, aliases=None):
    vmem = pl.BlockSpec(memory_space=pltpu.VMEM)
    smem = pl.BlockSpec(memory_space=pltpu.SMEM)
    moved = sum(a.size * a.dtype.itemsize for a in list(arrays) + list(outs))
    return pl.pallas_call(
        kernel,
        out_shape=outs,
        in_specs=[smem] * len(scalars) + [vmem] * len(arrays),
        out_specs=[vmem] * len(outs),
        input_output_aliases=aliases or {},
        compiler_params=pltpu.CompilerParams(vmem_limit_bytes=moved + SPARE_VMEM),
        cost_estimate=pl.CostEstimate(flops=flops, bytes_accessed=moved, transcendentals=0),
    )(*scalars, *arrays)


def mask_kernel(plan, band_ref, ham_ref, out_ref):
    out_ref[...] = masked(plan, band_ref, ham_ref[...].astype(jnp.float32)).astype(jnp.bfloat16)


def near_kernel(plan, keep_slab, *refs):
    rights, refs = refs[: plan.rows], refs[plan.rows :]
    count = 2 * plan.far - 1
    lefts, (total_ref, right_ref, *slab_ref) = refs[:count], refs[count:]
    for other in range(plan.rows):
        right_ref[pl.ds(plan.row_first(other), plan.rows_here), :] = rights[other][...]
    total = None
    for place, left in enumerate(lefts):
        first = plan.origin_first((place + 1) // 2, place % 2 == 1)
        if keep_slab:
            slab_ref[0][:, pl.ds(first, plan.cols_here)] = left[...]
        term = dot(left[...], right_ref[pl.ds(first, plan.cols_here), :])
        total = term if total is None else total + term
    total_ref[...] = total


def far_terms(plan, total_ref, right_ref, far_ref):
    first = plan.origin_first(plan.far, True)
    return total_ref[...] + dot(far_ref[...], right_ref[pl.ds(first, plan.cols_here), :])


def square_kernel(plan, band_ref, total_ref, right_ref, far_ref, _, out_ref, slab_ref):
    total = far_terms(plan, total_ref, right_ref, far_ref)
    slab_ref[:, pl.ds(plan.origin_first(plan.far, True), plan.cols_here)] = far_ref[...]
    out_ref[...] = masked(plan, band_ref, total).astype(jnp.bfloat16)


def slab_terms(plan, slab_ref, pieces):
    total = None
    for other, piece in pieces:
        term = dot(slab_ref[:, pl.ds(plan.row_first(other), plan.rows_here)], piece[...])
        total = term if total is None else total + term
    return total


def some_kernel(plan, others, slab_ref, *refs):
    *pieces, total_ref = refs
    total_ref[...] = slab_terms(plan, slab_ref, list(zip(others, pieces)))


def sign_kernel(plan, others, band_ref, slab_ref, total_ref, start_ref, *refs):
    *pieces, sign_ref, density_ref = refs
    cubic = total_ref[...] + slab_terms(plan, slab_ref, list(zip(others, pieces)))
    sign = masked(plan, band_ref, 1.5 * start_ref[...].astype(jnp.float32) - 0.5 * cubic).astype(jnp.bfloat16)
    sign_ref[...] = sign
    first_row = lax.axis_index("row") * plan.rows_here
    first_col = lax.axis_index("col") * plan.cols_here
    rows = first_row + lax.broadcasted_iota(jnp.int32, sign.shape, 0)
    cols = first_col + lax.broadcasted_iota(jnp.int32, sign.shape, 1)
    identity = (rows == cols).astype(jnp.float32)
    density_ref[...] = (0.5 * (identity - sign.astype(jnp.float32))).astype(jnp.bfloat16)


def weighted_kernel(plan, others, band_ref, slab_ref, *refs):
    *pieces, out_ref = refs
    total = slab_terms(plan, slab_ref, list(zip(others, pieces)))
    out_ref[...] = masked(plan, band_ref, total).astype(jnp.bfloat16)


def energy_kernel(plan, band_ref, frag_ref, total_ref, right_ref, far_ref, deriv_ref, energy_ref, sums_ref):
    total = far_terms(plan, total_ref, right_ref, far_ref)
    energy = masked(plan, band_ref, total).astype(jnp.bfloat16)
    energy_ref[...] = energy
    weighed = energy.astype(jnp.float32) * deriv_ref[...].astype(jnp.float32)
    terms = jnp.sum(weighed, axis=0, keepdims=True)
    count = FRAG_DEV * plan.cols
    fragment = lax.broadcasted_iota(jnp.int32, (count, BLK), 0)
    sums = jnp.zeros((count, BLK), jnp.float32)
    for j in range(plan.block_cols):
        owner = frag_ref[lax.axis_index("col") * plan.block_cols + j]
        line = jnp.broadcast_to(terms[:, j * BLK : (j + 1) * BLK], (count, BLK))
        sums = sums + jnp.where(fragment == owner, line, 0.0)
    sums_ref[...] = sums


def body(ham, deriv, band, frag_of):
    plan = Plan(*ham.shape)
    bind = functools.partial
    flops = 2 * plan.rows_here * plan.order * plan.cols_here
    block = jax.ShapeDtypeStruct(ham.shape, jnp.bfloat16)
    total_type = jax.ShapeDtypeStruct(ham.shape, jnp.float32)
    slab_type = jax.ShapeDtypeStruct((plan.rows_here, plan.order), jnp.bfloat16)
    column_type = jax.ShapeDtypeStruct((plan.order, plan.cols_here), jnp.bfloat16)
    others = range(plan.rows)

    def exchange_start(value):
        return [plan.across(value, other) for other in range(2, plan.rows, 2)]

    def exchange_end(first_two, crossed):
        return list(first_two) + [piece for value in crossed for piece in (value, plan.across(value, 1))]

    def gather(mine, partner):
        shards = [mine]
        for distance in range(1, plan.far):
            mine = plan.ring(mine)
            partner = plan.ring(partner)
            shards += [mine, plan.across(partner, 1)]
        return shards, plan.ring(mine)

    (start,) = call(bind(mask_kernel, plan), [block], [band], [ham], 0)
    partner = plan.across(start, 1)
    shards, far = gather(start, partner)
    column = exchange_end([start, partner], exchange_start(start))
    total, right, slab = call(
        bind(near_kernel, plan, True), [total_type, column_type, slab_type], [], column + shards, flops
    )
    square, slab = call(
        bind(square_kernel, plan), [block, slab_type], [band], [total, right, far, slab], flops // 8, {4: 1}
    )

    crossed = exchange_start(square)
    partner = plan.across(square, 1)
    (total,) = call(bind(some_kernel, plan, [0, 1]), [total_type], [], [slab, square, partner], flops // 2)
    column = exchange_end([square, partner], crossed)
    sign_iterate, density = call(
        bind(sign_kernel, plan, list(others)[2:]), [block, block], [band], [slab, total, start] + column[2:], flops // 2
    )

    partner = plan.across(density, 1)
    shards, far = gather(density, partner)
    column = exchange_end([density, partner], exchange_start(density))
    (weighted,) = call(bind(weighted_kernel, plan, others), [block], [band], [slab] + column, flops)
    column = exchange_end([weighted, plan.across(weighted, 1)], exchange_start(weighted))
    total, right = call(bind(near_kernel, plan, False), [total_type, column_type], [], column + shards, flops)
    energy_density, sums = call(
        bind(energy_kernel, plan),
        [block, jax.ShapeDtypeStruct((FRAG_DEV * plan.cols, BLK), jnp.float32)],
        [band, frag_of],
        [total, right, far, deriv],
        flops // 8,
    )
    sums = sums.reshape(1, plan.cols, FRAG_DEV, BLK)
    sums = jnp.broadcast_to(sums, (plan.rows, plan.cols, FRAG_DEV, BLK))
    sums = sums.reshape(plan.rows * plan.cols, FRAG_DEV, BLK)
    pulay_terms = jnp.sum(lax.all_to_all(sums, AXES, 0, 0), axis=0)
    return (sign_iterate, energy_density, pulay_terms)


def solution(mesh):
    placed = (P("row", "col"), P("row", "col"), P(), P())
    return jax.shard_map(
        body,
        mesh=mesh,
        in_specs=placed,
        out_specs=(P("row", "col"), P("row", "col"), P("col", None)),
        check_vma=False,
    )
```

time: 267 us -> 145 us (0.54)
  waiting for transfers between devices: 144 us -> 78.3 us
  blocking collectives: 38.8 us -> 12.1 us
  matrix products: 22.8 us -> 0 us
  Pallas kernels: 0 us -> 17.4 us
  between operations: 14.4 us -> 0.76 us
  local copies, waits for them, and re-layouts: 14.6 us -> 1.74 us
  starting transfers between devices: 29.9 us -> 33.9 us
    all_gather x2 -> x0, waiting for transfers between devices: 69.1 us -> none  [folded_product(): slab = lax.all_gather(left_matrix, 'col', axis=1, tiled=True)]
    psum x1 -> x0, blocking collectives: 38.8 us -> none  [body(): grand_total = lax.psum(partial_value, ('row', 'col'))]
    dot_general x5 -> x0, matrix products: 22.8 us -> none  [the longest x4 22.6 us: window_product(): jnp.dot(left_window, near_window(right_matrix), preferred_element_type=jn...]
    pallas_call x0 -> x8, Pallas kernels: none -> 17.4 us  [call(): pl.pallas_call(kernel, out_shape=outs, in_specs=[smem] * len(scalars) + [...]
    all_to_all x0 -> x1, blocking collectives: none -> 12.1 us  [body(): pulay_terms = jnp.sum(lax.all_to_all(sums, AXES, 0, 0), axis=0)]
    unnamed x30 -> x10, local copies, waits for them, and re-layouts: 10 us -> 1.73 us
    ppermute x16 -> x32, starting transfers between devices: 29.8 us -> 33.9 us  [the longest x14 25.1 us: ring(): return lax.ppermute(value, AXES, pairs)]
    ppermute x16 -> x32, waiting for transfers between devices: 75.3 us -> 78.3 us  [the longest x14 48.8 us: ring(): return lax.ppermute(value, AXES, pairs)]
  transfers between devices with their start and end apart: 18 -> 32, of which waited for: 10 -> 19; matrix products, arithmetic and copies ran while one was open for 6% -> 0% of each run, Pallas kernels for 0% -> 7%
where the time goes in v2:
time: 145 us
  waiting for transfers between devices  78.3 us (54%)
  starting transfers between devices  33.9 us (23%)
  Pallas kernels  17.4 us (12%)
  blocking collectives  12.1 us (8%)
  local copies, waits for them, and re-layouts  1.74 us (1%)
    ppermute x14, waiting for transfers between devices, ring(): return lax.ppermute(value, AXES, pairs)  48.8 us
    ppermute x18, waiting for transfers between devices, across(): lax.ppermute(value, 'row', [(i, i ^ other) for i in range(self.rows)])  29.4 us
    ppermute x14, starting transfers between devices, ring(): return lax.ppermute(value, AXES, pairs)  25.1 us
    pallas_call x8, Pallas kernels, call(): pl.pallas_call(kernel, out_shape=outs, in_specs=[smem] * len(scalars) + [...  17.4 us
    all_to_all x1, blocking collectives, body(): pulay_terms = jnp.sum(lax.all_to_all(sums, AXES, 0, 0), axis=0)  12.1 us
    ppermute x18, starting transfers between devices, across(): lax.ppermute(value, 'row', [(i, i ^ other) for i in range(self.rows)])  8.81 us
  transfers between devices with their start and end apart: 32, of which 19 were waited for; matrix products, arithmetic and copies ran while one was open for 0% of the time, Pallas kernels for 7%

profile of v2, /device:TPU:0, one launch (start us, length us, event | category | flops | bytes accessed | tf_op | source)
XLA Modules:
  0.0 144.8 jit_solution(7950009101216811203)
XLA Ops:
  0.6 1.1 copy-done.1
  1.7 0.7 copy-done.2
  2.4 0.7 shard_map.67.refs_0_.refs_4_.start_ref
  3.0 0.0 copy-start.3
  3.0 0.5 collective-permute-start
  3.6 1.6 %collective-permute-done.refs_1_ = bf16[768,384]{1,0:T(8,128)(2,1)S(1)} collective-permute-done((bf16[768,384]{1,0:T(8,128)(2,1)S(1)}, bf16[768,384]{1,0:T(8,128)(2,1)S(1)}, u32[]{:S(2)}, u32[]{:S(2)}) %collective-permute-start) | collective-permute-done | bytes 589856 | tf_op jit(solution)/shard_map/ppermute | solution.py:50
  5.2 2.9 %collective-permute-start.4 = (bf16[768,384]{1,0:T(8,128)(2,1)S(1)}, bf16[768,384]{1,0:T(8,128)(2,1)S(1)}, u32[]{:S(2)}, u32[]{:S(2)}) collective-permute-start(bf16[768,384]{1,0:T(8,128)(2,1)S(1)} %collective-permute-done.refs_1_), channel_id=1, source_target_pairs={{0,2},{2,4},{4,6},{6,7},{7,5},{5,3},{3,1},{1,0},{8,9},{10,8},{12,1... | collective-permute-start | bytes 1769480 | tf_op jit(solution)/shard_map/ppermute | solution.py:47
  8.1 1.6 %collective-permute-start.3 = (bf16[768,384]{1,0:T(8,128)(2,1)S(1)}, bf16[768,384]{1,0:T(8,128)(2,1)S(1)}, u32[]{:S(2)}, u32[]{:S(2)}) collective-permute-start(bf16[768,384]{1,0:T(8,128)(2,1)S(1)} %shard_map.67.refs_0_.refs_4_.start_ref), channel_id=1, source_target_pairs={{0,2},{2,4},{4,6},{6,7},{7,5},{5,3},{3,1},{1,0},{8,9},{10,8},{12,1... | collective-permute-start | bytes 1769480 | tf_op jit(solution)/shard_map/ppermute | solution.py:47
  9.7 6.2 %collective-permute-done.4 = bf16[768,384]{1,0:T(8,128)(2,1)S(1)} collective-permute-done((bf16[768,384]{1,0:T(8,128)(2,1)S(1)}, bf16[768,384]{1,0:T(8,128)(2,1)S(1)}, u32[]{:S(2)}, u32[]{:S(2)}) %collective-permute-start.4) | collective-permute-done | bytes 589856 | tf_op jit(solution)/shard_map/ppermute | solution.py:47
  15.9 2.1 %collective-permute-start.7 = (bf16[768,384]{1,0:T(8,128)(2,1)S(1)}, bf16[768,384]{1,0:T(8,128)(2,1)S(1)}, u32[]{:S(2)}, u32[]{:S(2)}) collective-permute-start(bf16[768,384]{1,0:T(8,128)(2,1)S(1)} %collective-permute-done.4), channel_id=1, source_target_pairs={{0,2},{2,4},{4,6},{6,7},{7,5},{5,3},{3,1},{1,0},{8,9},{10,8},{12,1... | collective-permute-start | bytes 1769480 | tf_op jit(solution)/shard_map/ppermute | solution.py:47
  18.0 4.2 %collective-permute-done.3.refs_5_ = bf16[768,384]{1,0:T(8,128)(2,1)S(1)} collective-permute-done((bf16[768,384]{1,0:T(8,128)(2,1)S(1)}, bf16[768,384]{1,0:T(8,128)(2,1)S(1)}, u32[]{:S(2)}, u32[]{:S(2)}) %collective-permute-start.3) | collective-permute-done | bytes 589856 | tf_op jit(solution)/shard_map/ppermute | solution.py:47
  22.3 2.1 %collective-permute-start.6 = (bf16[768,384]{1,0:T(8,128)(2,1)S(1)}, bf16[768,384]{1,0:T(8,128)(2,1)S(1)}, u32[]{:S(2)}, u32[]{:S(2)}) collective-permute-start(bf16[768,384]{1,0:T(8,128)(2,1)S(1)} %collective-permute-done.3.refs_5_), channel_id=1, source_target_pairs={{0,2},{2,4},{4,6},{6,7},{7,5},{5,3},{3,1},{1,0},{8,9},{10,8},{12,1... | collective-permute-start | bytes 1769480 | tf_op jit(solution)/shard_map/ppermute | solution.py:47
  24.3 1.5 %collective-permute-start.1 = (bf16[768,384]{1,0:T(8,128)(2,1)S(1)}, bf16[768,384]{1,0:T(8,128)(2,1)S(1)}, u32[]{:S(2)}, u32[]{:S(2)}) collective-permute-start(bf16[768,384]{1,0:T(8,128)(2,1)S(1)} %shard_map.67.refs_0_.refs_4_.start_ref), channel_id=1, source_target_pairs={{0,16},{8,24},{16,0},{24,8},{1,17},{9,25},{17,1},{25,9},{2,18},{10... | collective-permute-start | bytes 1769480 | tf_op jit(solution)/shard_map/ppermute | solution.py:50
  25.8 2.7 %collective-permute-done.7 = bf16[768,384]{1,0:T(8,128)(2,1)S(1)} collective-permute-done((bf16[768,384]{1,0:T(8,128)(2,1)S(1)}, bf16[768,384]{1,0:T(8,128)(2,1)S(1)}, u32[]{:S(2)}, u32[]{:S(2)}) %collective-permute-start.7) | collective-permute-done | bytes 589856 | tf_op jit(solution)/shard_map/ppermute | solution.py:47
  28.6 2.1 %collective-permute-start.10 = (bf16[768,384]{1,0:T(8,128)(2,1)S(1)}, bf16[768,384]{1,0:T(8,128)(2,1)S(1)}, u32[]{:S(2)}, u32[]{:S(2)}) collective-permute-start(bf16[768,384]{1,0:T(8,128)(2,1)S(1)} %collective-permute-done.7), channel_id=1, source_target_pairs={{0,2},{2,4},{4,6},{6,7},{7,5},{5,3},{3,1},{1,0},{8,9},{10,8},{12,1... | collective-permute-start | bytes 1769480 | tf_op jit(solution)/shard_map/ppermute | solution.py:47
  30.7 4.2 %collective-permute-done.6.refs_7_ = bf16[768,384]{1,0:T(8,128)(2,1)S(1)} collective-permute-done((bf16[768,384]{1,0:T(8,128)(2,1)S(1)}, bf16[768,384]{1,0:T(8,128)(2,1)S(1)}, u32[]{:S(2)}, u32[]{:S(2)}) %collective-permute-start.6) | collective-permute-done | bytes 589856 | tf_op jit(solution)/shard_map/ppermute | solution.py:47
  34.9 2.1 %collective-permute-start.9 = (bf16[768,384]{1,0:T(8,128)(2,1)S(1)}, bf16[768,384]{1,0:T(8,128)(2,1)S(1)}, u32[]{:S(2)}, u32[]{:S(2)}) collective-permute-start(bf16[768,384]{1,0:T(8,128)(2,1)S(1)} %collective-permute-done.6.refs_7_), channel_id=1, source_target_pairs={{0,2},{2,4},{4,6},{6,7},{7,5},{5,3},{3,1},{1,0},{8,9},{10,8},{12,1... | collective-permute-start | bytes 1769480 | tf_op jit(solution)/shard_map/ppermute | solution.py:47
  37.0 1.5 %collective-permute-done.1.refs_2_ = bf16[768,384]{1,0:T(8,128)(2,1)S(1)} collective-permute-done((bf16[768,384]{1,0:T(8,128)(2,1)S(1)}, bf16[768,384]{1,0:T(8,128)(2,1)S(1)}, u32[]{:S(2)}, u32[]{:S(2)}) %collective-permute-start.1) | collective-permute-done | bytes 589856 | tf_op jit(solution)/shard_map/ppermute | solution.py:50
  38.5 0.5 collective-permute-start.5
  39.0 0.0 collective-permute-start.8
  39.0 2.2 %collective-permute-done.10 = bf16[768,384]{1,0:T(8,128)(2,1)S(1)} collective-permute-done((bf16[768,384]{1,0:T(8,128)(2,1)S(1)}, bf16[768,384]{1,0:T(8,128)(2,1)S(1)}, u32[]{:S(2)}, u32[]{:S(2)}) %collective-permute-start.10) | collective-permute-done | bytes 589856 | tf_op jit(solution)/shard_map/ppermute | solution.py:47
  41.2 0.0 collective-permute-start.11
  41.2 6.3 %collective-permute-done.9.refs_9_ = bf16[768,384]{1,0:T(8,128)(2,1)S(1)} collective-permute-done((bf16[768,384]{1,0:T(8,128)(2,1)S(1)}, bf16[768,384]{1,0:T(8,128)(2,1)S(1)}, u32[]{:S(2)}, u32[]{:S(2)}) %collective-permute-start.9) | collective-permute-done | bytes 589856 | tf_op jit(solution)/shard_map/ppermute | solution.py:47
  47.5 2.1 %collective-permute-start.12 = (bf16[768,384]{1,0:T(8,128)(2,1)S(1)}, bf16[768,384]{1,0:T(8,128)(2,1)S(1)}, u32[]{:S(2)}, u32[]{:S(2)}) collective-permute-start(bf16[768,384]{1,0:T(8,128)(2,1)S(1)} %collective-permute-done.9.refs_9_), channel_id=1, source_target_pairs={{0,2},{2,4},{4,6},{6,7},{7,5},{5,3},{3,1},{1,0},{8,9},{10,8},{12,1... | collective-permute-start | bytes 1769480 | tf_op jit(solution)/shard_map/ppermute | solution.py:47
  49.6 0.0 collective-permute-done.2.refs_3_
  49.6 0.0 collective-permute-done.5.refs_6_
  49.6 0.0 collective-permute-done.11.refs_10_
  49.6 3.3 %shard_map.68 = (f32[768,384]{1,0:T(8,128)S(1)}, bf16[3072,384]{1,0:T(8,128)(2,1)S(1)}, bf16[768,3072]{1,0:T(8,128)(2,1)S(1)}) custom-call(bf16[768,384]{1,0:T(8,128)(2,1)S(1)} %shard_map.67.refs_0_.refs_4_.start_ref, bf16[768,384]{1,0:T(8,128)(2,1)S(1)} %collective-permute-done.refs_1_, bf16[768,384]{1,0:T(8,128)(2,1)S(1)} %collective-permute-done.1.refs_2_, ...), custom_call_target="tpu_custom_call" | custom-call | flops 1811939328 | bytes 14745600 | tf_op jit(solution)/shard_map/pallas_call | solution.py:89
  52.9 4.5 %collective-permute-done.12.far_ref = bf16[768,384]{1,0:T(8,128)(2,1)S(1)} collective-permute-done((bf16[768,384]{1,0:T(8,128)(2,1)S(1)}, bf16[768,384]{1,0:T(8,128)(2,1)S(1)}, u32[]{:S(2)}, u32[]{:S(2)}) %collective-permute-start.12) | collective-permute-done | bytes 589856 | tf_op jit(solution)/shard_map/ppermute | solution.py:47
  57.4 1.1 shard_map.69
  58.5 2.1 %collective-permute-start.14 = (bf16[768,384]{1,0:T(8,128)(2,1)S(1)}, bf16[768,384]{1,0:T(8,128)(2,1)S(1)}, u32[]{:S(2)}, u32[]{:S(2)}) collective-permute-start(bf16[768,384]{1,0:T(8,128)(2,1)S(1)} %get-tuple-element.18.refs_0_), channel_id=1, source_target_pairs={{0,16},{8,24},{16,0},{24,8},{1,17},{9,25},{17,1},{25,9},{2,18},{10... | collective-permute-start | bytes 1769480 | tf_op jit(solution)/shard_map/ppermute | solution.py:50
  60.6 12.0 %collective-permute-done.14.refs_0_ = bf16[768,384]{1,0:T(8,128)(2,1)S(1)} collective-permute-done((bf16[768,384]{1,0:T(8,128)(2,1)S(1)}, bf16[768,384]{1,0:T(8,128)(2,1)S(1)}, u32[]{:S(2)}, u32[]{:S(2)}) %collective-permute-start.14) | collective-permute-done | bytes 589856 | tf_op jit(solution)/shard_map/ppermute | solution.py:50
  72.6 0.0 collective-permute-start.15
  72.6 1.4 shard_map.70.total_ref
  73.9 0.6 collective-permute-done.15.refs_1_
  74.6 3.1 %shard_map.71 = (bf16[768,384]{1,0:T(8,128)(2,1)}, bf16[768,384]{1,0:T(8,128)(2,1)S(1)}) custom-call(s32[24]{0:T(128)S(1)} %copy-done.3, bf16[768,3072]{1,0:T(8,128)(2,1)S(1)} %get-tuple-element.17.slab_ref, f32[768,384]{1,0:T(8,128)S(1)} %shard_map.70.total_ref, bf16[768,384]{1,0:T(8,128)(2,1)S(1)} %shard_map.67.refs_0_.refs_4_.start_ref, ...), custom_call_target="tpu_custom_call" | custom-call | flops 905969664 | bytes 8847360 | tf_op jit(solution)/shard_map/pallas_call | solution.py:89
  77.6 0.1 collective-permute-start.16
  77.8 1.7 %collective-permute-start.22 = (bf16[768,384]{1,0:T(8,128)(2,1)S(1)}, bf16[768,384]{1,0:T(8,128)(2,1)S(1)}, u32[]{:S(2)}, u32[]{:S(2)}) collective-permute-start(bf16[768,384]{1,0:T(8,128)(2,1)S(1)} %get-tuple-element.20.refs_0_.refs_4_), channel_id=1, source_target_pairs={{0,2},{2,4},{4,6},{6,7},{7,5},{5,3},{3,1},{1,0},{8,9},{10,8},{12,1... | collective-permute-start | bytes 1769480 | tf_op jit(solution)/shard_map/ppermute | solution.py:47
  79.5 1.5 %collective-permute-start.17 = (bf16[768,384]{1,0:T(8,128)(2,1)S(1)}, bf16[768,384]{1,0:T(8,128)(2,1)S(1)}, u32[]{:S(2)}, u32[]{:S(2)}) collective-permute-start(bf16[768,384]{1,0:T(8,128)(2,1)S(1)} %get-tuple-element.20.refs_0_.refs_4_), channel_id=1, source_target_pairs={{0,16},{8,24},{16,0},{24,8},{1,17},{9,25},{17,1},{25,9},{2,18},{10... | collective-permute-start | bytes 1769480 | tf_op jit(solution)/shard_map/ppermute | solution.py:50
  81.0 1.6 %collective-permute-start.23 = (bf16[768,384]{1,0:T(8,128)(2,1)S(1)}, bf16[768,384]{1,0:T(8,128)(2,1)S(1)}, u32[]{:S(2)}, u32[]{:S(2)}) collective-permute-start(bf16[768,384]{1,0:T(8,128)(2,1)S(1)} %collective-permute-done.16.refs_1_), channel_id=1, source_target_pairs={{0,2},{2,4},{4,6},{6,7},{7,5},{5,3},{3,1},{1,0},{8,9},{10,8},{12,1... | collective-permute-start | bytes 1769480 | tf_op jit(solution)/shard_map/ppermute | solution.py:47
  82.6 5.1 %collective-permute-done.22.refs_5_ = bf16[768,384]{1,0:T(8,128)(2,1)S(1)} collective-permute-done((bf16[768,384]{1,0:T(8,128)(2,1)S(1)}, bf16[768,384]{1,0:T(8,128)(2,1)S(1)}, u32[]{:S(2)}, u32[]{:S(2)}) %collective-permute-start.22) | collective-permute-done | bytes 589856 | tf_op jit(solution)/shard_map/ppermute | solution.py:47
  87.6 1.7 %collective-permute-start.25 = (bf16[768,384]{1,0:T(8,128)(2,1)S(1)}, bf16[768,384]{1,0:T(8,128)(2,1)S(1)}, u32[]{:S(2)}, u32[]{:S(2)}) collective-permute-start(bf16[768,384]{1,0:T(8,128)(2,1)S(1)} %collective-permute-done.22.refs_5_), channel_id=1, source_target_pairs={{0,2},{2,4},{4,6},{6,7},{7,5},{5,3},{3,1},{1,0},{8,9},{10,8},{12,1... | collective-permute-start | bytes 1769480 | tf_op jit(solution)/shard_map/ppermute | solution.py:47
  89.4 5.4 %collective-permute-done.17.refs_2_ = bf16[768,384]{1,0:T(8,128)(2,1)S(1)} collective-permute-done((bf16[768,384]{1,0:T(8,128)(2,1)S(1)}, bf16[768,384]{1,0:T(8,128)(2,1)S(1)}, u32[]{:S(2)}, u32[]{:S(2)}) %collective-permute-start.17) | collective-permute-done | bytes 589856 | tf_op jit(solution)/shard_map/ppermute | solution.py:50
  94.8 0.9 collective-permute-start.26
  95.7 4.6 %collective-permute-done.25.refs_7_ = bf16[768,384]{1,0:T(8,128)(2,1)S(1)} collective-permute-done((bf16[768,384]{1,0:T(8,128)(2,1)S(1)}, bf16[768,384]{1,0:T(8,128)(2,1)S(1)}, u32[]{:S(2)}, u32[]{:S(2)}) %collective-permute-start.25) | collective-permute-done | bytes 589856 | tf_op jit(solution)/shard_map/ppermute | solution.py:47
  100.3 1.7 %collective-permute-start.28 = (bf16[768,384]{1,0:T(8,128)(2,1)S(1)}, bf16[768,384]{1,0:T(8,128)(2,1)S(1)}, u32[]{:S(2)}, u32[]{:S(2)}) collective-permute-start(bf16[768,384]{1,0:T(8,128)(2,1)S(1)} %collective-permute-done.25.refs_7_), channel_id=1, source_target_pairs={{0,2},{2,4},{4,6},{6,7},{7,5},{5,3},{3,1},{1,0},{8,9},{10,8},{12,1... | collective-permute-start | bytes 1769480 | tf_op jit(solution)/shard_map/ppermute | solution.py:47
  102.0 0.0 collective-permute-done.18.refs_3_
  102.0 3.1 %shard_map.72.refs_0_ = bf16[768,384]{1,0:T(8,128)(2,1)S(1)} custom-call(s32[24]{0:T(128)S(1)} %copy-done.3, bf16[768,3072]{1,0:T(8,128)(2,1)S(1)} %get-tuple-element.17.slab_ref, bf16[768,384]{1,0:T(8,128)(2,1)S(1)} %get-tuple-element.20.refs_0_.refs_4_, bf16[768,384]{1,0:T(8,128)(2,1)S(1)} %collective-permute-done.16.refs_1_, ...), custom_call_target="tpu_custom_call" | custom-call | flops 1811939328 | bytes 7667712 | tf_op jit(solution)/shard_map/pallas_call | solution.py:89
  105.2 0.0 copy-start
  105.2 0.0 copy-start.4
  105.2 1.6 %collective-permute-start.20 = (bf16[768,384]{1,0:T(8,128)(2,1)S(1)}, bf16[768,384]{1,0:T(8,128)(2,1)S(1)}, u32[]{:S(2)}, u32[]{:S(2)}) collective-permute-start(bf16[768,384]{1,0:T(8,128)(2,1)S(1)} %shard_map.72.refs_0_), channel_id=1, source_target_pairs={{0,16},{8,24},{16,0},{24,8},{1,17},{9,25},{17,1},{25,9},{2,18},{10... | collective-permute-start | bytes 1769480 | tf_op jit(solution)/shard_map/ppermute | solution.py:50
  106.8 1.6 %collective-permute-start.29 = (bf16[768,384]{1,0:T(8,128)(2,1)S(1)}, bf16[768,384]{1,0:T(8,128)(2,1)S(1)}, u32[]{:S(2)}, u32[]{:S(2)}) collective-permute-start(bf16[768,384]{1,0:T(8,128)(2,1)S(1)} %collective-permute-done.26), channel_id=1, source_target_pairs={{0,2},{2,4},{4,6},{6,7},{7,5},{5,3},{3,1},{1,0},{8,9},{10,8},{12,1... | collective-permute-start | bytes 1769480 | tf_op jit(solution)/shard_map/ppermute | solution.py:47
  108.4 0.5 collective-permute-start.24
  108.9 4.1 %collective-permute-done.28.refs_9_ = bf16[768,384]{1,0:T(8,128)(2,1)S(1)} collective-permute-done((bf16[768,384]{1,0:T(8,128)(2,1)S(1)}, bf16[768,384]{1,0:T(8,128)(2,1)S(1)}, u32[]{:S(2)}, u32[]{:S(2)}) %collective-permute-start.28) | collective-permute-done | bytes 589856 | tf_op jit(solution)/shard_map/ppermute | solution.py:47
  112.9 6.7 %collective-permute-done.20.refs_2_ = bf16[768,384]{1,0:T(8,128)(2,1)S(1)} collective-permute-done((bf16[768,384]{1,0:T(8,128)(2,1)S(1)}, bf16[768,384]{1,0:T(8,128)(2,1)S(1)}, u32[]{:S(2)}, u32[]{:S(2)}) %collective-permute-start.20) | collective-permute-done | bytes 589856 | tf_op jit(solution)/shard_map/ppermute | solution.py:50
  119.7 0.5 collective-permute-start.30
  120.2 0.8 collective-permute-start.31
  121.0 0.7 collective-permute-done.21.refs_3_
  121.7 0.8 collective-permute-done.30.refs_10_
  122.5 2.9 %shard_map.73 = (f32[768,384]{1,0:T(8,128)S(1)}, bf16[3072,384]{1,0:T(8,128)(2,1)S(1)}) custom-call(bf16[768,384]{1,0:T(8,128)(2,1)S(1)} %shard_map.72.refs_0_, bf16[768,384]{1,0:T(8,128)(2,1)S(1)} %collective-permute-done.19.refs_1_, bf16[768,384]{1,0:T(8,128)(2,1)S(1)} %collective-permute-done.20.refs_2_, ...), custom_call_target="tpu_custom_call" | custom-call | flops 1811939328 | bytes 10027008 | tf_op jit(solution)/shard_map/pallas_call | solution.py:89
  125.4 4.7 %collective-permute-done.31.far_ref = bf16[768,384]{1,0:T(8,128)(2,1)S(1)} collective-permute-done((bf16[768,384]{1,0:T(8,128)(2,1)S(1)}, bf16[768,384]{1,0:T(8,128)(2,1)S(1)}, u32[]{:S(2)}, u32[]{:S(2)}) %collective-permute-start.31) | collective-permute-done | bytes 589856 | tf_op jit(solution)/shard_map/ppermute | solution.py:47
  130.1 2.0 %shard_map.74 = (bf16[768,384]{1,0:T(8,128)(2,1)}, f32[16,128]{1,0:T(8,128)S(1)}) custom-call(s32[24]{0:T(128)S(1)} %copy-done.3, s32[24]{0:T(128)S(1)} %copy-done.4, f32[768,384]{1,0:T(8,128)S(1)} %get-tuple-element.21.total_ref, bf16[3072,384]{1,0:T(8,128)(2,1)S(1)} %get-tuple-element.22.right_ref, bf16[768,384]{1,0:T(8,128)(2,1)S(1)} %collective-permute-done.31.far_ref, ...), custom_call_target="tpu_custom_call" | custom-call | flops 226492416 | bytes 5316608 | tf_op jit(solution)/shard_map/pallas_call | solution.py:89
  132.1 12.1 %all_to_all.5 = f32[32,2,128]{2,1,0:T(2,128)S(1)} all-to-all(f32[32,2,128]{2,1,0:T(2,128)S(1)} %bitcast.3), channel_id=1, replica_groups=mesh['row'=4,'col'=8] {'row','col'}, dimensions={0} | all-to-all | bytes 65536 | tf_op jit(solution)/shard_map/all_to_all | solution.py:238
  144.2 0.6 reduce_sum.9
  (21 shorter events, 0.1 us)
Async XLA Ops:
  0.6 1.1 copy-start.1
  1.7 0.7 copy-start.2
  3.0 54.4 %copy-start.3 = (s32[24]{0:T(128)S(1)}, s32[24]{0:T(128)}, u32[]{:S(2)}) copy-start(s32[24]{0:T(128)} %band_ref.9) | copy-start | bytes 292
  3.0 2.1 %collective-permute-start = (bf16[768,384]{1,0:T(8,128)(2,1)S(1)}, bf16[768,384]{1,0:T(8,128)(2,1)S(1)}, u32[]{:S(2)}, u32[]{:S(2)}) collective-permute-start(bf16[768,384]{1,0:T(8,128)(2,1)S(1)} %shard_map.67.refs_0_.refs_4_.start_ref), channel_id=1, source_target_pairs={{0,8},{8,0},{16,24},{24,16},{1,9},{9,1},{17,25},{25,17},{2,10},{10... | collective-permute-start | bytes 1769480 | tf_op jit(solution)/shard_map/ppermute | solution.py:50
  5.2 10.7 %collective-permute-start.4 = (bf16[768,384]{1,0:T(8,128)(2,1)S(1)}, bf16[768,384]{1,0:T(8,128)(2,1)S(1)}, u32[]{:S(2)}, u32[]{:S(2)}) collective-permute-start(bf16[768,384]{1,0:T(8,128)(2,1)S(1)} %collective-permute-done.refs_1_), channel_id=1, source_target_pairs={{0,2},{2,4},{4,6},{6,7},{7,5},{5,3},{3,1},{1,0},{8,9},{10,8},{12,1... | collective-permute-start | bytes 1769480 | tf_op jit(solution)/shard_map/ppermute | solution.py:47
  8.1 14.1 %collective-permute-start.3 = (bf16[768,384]{1,0:T(8,128)(2,1)S(1)}, bf16[768,384]{1,0:T(8,128)(2,1)S(1)}, u32[]{:S(2)}, u32[]{:S(2)}) collective-permute-start(bf16[768,384]{1,0:T(8,128)(2,1)S(1)} %shard_map.67.refs_0_.refs_4_.start_ref), channel_id=1, source_target_pairs={{0,2},{2,4},{4,6},{6,7},{7,5},{5,3},{3,1},{1,0},{8,9},{10,8},{12,1... | collective-permute-start | bytes 1769480 | tf_op jit(solution)/shard_map/ppermute | solution.py:47
  15.9 12.6 %collective-permute-start.7 = (bf16[768,384]{1,0:T(8,128)(2,1)S(1)}, bf16[768,384]{1,0:T(8,128)(2,1)S(1)}, u32[]{:S(2)}, u32[]{:S(2)}) collective-permute-start(bf16[768,384]{1,0:T(8,128)(2,1)S(1)} %collective-permute-done.4), channel_id=1, source_target_pairs={{0,2},{2,4},{4,6},{6,7},{7,5},{5,3},{3,1},{1,0},{8,9},{10,8},{12,1... | collective-permute-start | bytes 1769480 | tf_op jit(solution)/shard_map/ppermute | solution.py:47
  22.3 12.6 %collective-permute-start.6 = (bf16[768,384]{1,0:T(8,128)(2,1)S(1)}, bf16[768,384]{1,0:T(8,128)(2,1)S(1)}, u32[]{:S(2)}, u32[]{:S(2)}) collective-permute-start(bf16[768,384]{1,0:T(8,128)(2,1)S(1)} %collective-permute-done.3.refs_5_), channel_id=1, source_target_pairs={{0,2},{2,4},{4,6},{6,7},{7,5},{5,3},{3,1},{1,0},{8,9},{10,8},{12,1... | collective-permute-start | bytes 1769480 | tf_op jit(solution)/shard_map/ppermute | solution.py:47
  24.3 14.2 %collective-permute-start.1 = (bf16[768,384]{1,0:T(8,128)(2,1)S(1)}, bf16[768,384]{1,0:T(8,128)(2,1)S(1)}, u32[]{:S(2)}, u32[]{:S(2)}) collective-permute-start(bf16[768,384]{1,0:T(8,128)(2,1)S(1)} %shard_map.67.refs_0_.refs_4_.start_ref), channel_id=1, source_target_pairs={{0,16},{8,24},{16,0},{24,8},{1,17},{9,25},{17,1},{25,9},{2,18},{10... | collective-permute-start | bytes 1769480 | tf_op jit(solution)/shard_map/ppermute | solution.py:50
  28.6 12.6 %collective-permute-start.10 = (bf16[768,384]{1,0:T(8,128)(2,1)S(1)}, bf16[768,384]{1,0:T(8,128)(2,1)S(1)}, u32[]{:S(2)}, u32[]{:S(2)}) collective-permute-start(bf16[768,384]{1,0:T(8,128)(2,1)S(1)} %collective-permute-done.7), channel_id=1, source_target_pairs={{0,2},{2,4},{4,6},{6,7},{7,5},{5,3},{3,1},{1,0},{8,9},{10,8},{12,1... | collective-permute-start | bytes 1769480 | tf_op jit(solution)/shard_map/ppermute | solution.py:47
  34.9 12.6 %collective-permute-start.9 = (bf16[768,384]{1,0:T(8,128)(2,1)S(1)}, bf16[768,384]{1,0:T(8,128)(2,1)S(1)}, u32[]{:S(2)}, u32[]{:S(2)}) collective-permute-start(bf16[768,384]{1,0:T(8,128)(2,1)S(1)} %collective-permute-done.6.refs_7_), channel_id=1, source_target_pairs={{0,2},{2,4},{4,6},{6,7},{7,5},{5,3},{3,1},{1,0},{8,9},{10,8},{12,1... | collective-permute-start | bytes 1769480 | tf_op jit(solution)/shard_map/ppermute | solution.py:47
  38.5 11.1 %collective-permute-start.2 = (bf16[768,384]{1,0:T(8,128)(2,1)S(1)}, bf16[768,384]{1,0:T(8,128)(2,1)S(1)}, u32[]{:S(2)}, u32[]{:S(2)}) collective-permute-start(bf16[768,384]{1,0:T(8,128)(2,1)S(1)} %collective-permute-done.1.refs_2_), channel_id=1, source_target_pairs={{0,8},{8,0},{16,24},{24,16},{1,9},{9,1},{17,25},{25,17},{2,10},{10... | collective-permute-start | bytes 1769480 | tf_op jit(solution)/shard_map/ppermute | solution.py:50
  38.5 11.1 %collective-permute-start.5 = (bf16[768,384]{1,0:T(8,128)(2,1)S(1)}, bf16[768,384]{1,0:T(8,128)(2,1)S(1)}, u32[]{:S(2)}, u32[]{:S(2)}) collective-permute-start(bf16[768,384]{1,0:T(8,128)(2,1)S(1)} %collective-permute-done.4), channel_id=1, source_target_pairs={{0,8},{8,0},{16,24},{24,16},{1,9},{9,1},{17,25},{25,17},{2,10},{10... | collective-permute-start | bytes 1769480 | tf_op jit(solution)/shard_map/ppermute | solution.py:50
  39.0 10.6 %collective-permute-start.8 = (bf16[768,384]{1,0:T(8,128)(2,1)S(1)}, bf16[768,384]{1,0:T(8,128)(2,1)S(1)}, u32[]{:S(2)}, u32[]{:S(2)}) collective-permute-start(bf16[768,384]{1,0:T(8,128)(2,1)S(1)} %collective-permute-done.7), channel_id=1, source_target_pairs={{0,8},{8,0},{16,24},{24,16},{1,9},{9,1},{17,25},{25,17},{2,10},{10... | collective-permute-start | bytes 1769480 | tf_op jit(solution)/shard_map/ppermute | solution.py:50
  41.2 8.4 %collective-permute-start.11 = (bf16[768,384]{1,0:T(8,128)(2,1)S(1)}, bf16[768,384]{1,0:T(8,128)(2,1)S(1)}, u32[]{:S(2)}, u32[]{:S(2)}) collective-permute-start(bf16[768,384]{1,0:T(8,128)(2,1)S(1)} %collective-permute-done.10), channel_id=1, source_target_pairs={{0,8},{8,0},{16,24},{24,16},{1,9},{9,1},{17,25},{25,17},{2,10},{10... | collective-permute-start | bytes 1769480 | tf_op jit(solution)/shard_map/ppermute | solution.py:50
  47.5 9.9 %collective-permute-start.12 = (bf16[768,384]{1,0:T(8,128)(2,1)S(1)}, bf16[768,384]{1,0:T(8,128)(2,1)S(1)}, u32[]{:S(2)}, u32[]{:S(2)}) collective-permute-start(bf16[768,384]{1,0:T(8,128)(2,1)S(1)} %collective-permute-done.9.refs_9_), channel_id=1, source_target_pairs={{0,2},{2,4},{4,6},{6,7},{7,5},{5,3},{3,1},{1,0},{8,9},{10,8},{12,1... | collective-permute-start | bytes 1769480 | tf_op jit(solution)/shard_map/ppermute | solution.py:47
  58.5 14.1 %collective-permute-start.14 = (bf16[768,384]{1,0:T(8,128)(2,1)S(1)}, bf16[768,384]{1,0:T(8,128)(2,1)S(1)}, u32[]{:S(2)}, u32[]{:S(2)}) collective-permute-start(bf16[768,384]{1,0:T(8,128)(2,1)S(1)} %get-tuple-element.18.refs_0_), channel_id=1, source_target_pairs={{0,16},{8,24},{16,0},{24,8},{1,17},{9,25},{17,1},{25,9},{2,18},{10... | collective-permute-start | bytes 1769480 | tf_op jit(solution)/shard_map/ppermute | solution.py:50
  60.6 12.0 %collective-permute-start.13 = (bf16[768,384]{1,0:T(8,128)(2,1)S(1)}, bf16[768,384]{1,0:T(8,128)(2,1)S(1)}, u32[]{:S(2)}, u32[]{:S(2)}) collective-permute-start(bf16[768,384]{1,0:T(8,128)(2,1)S(1)} %get-tuple-element.18.refs_0_), channel_id=1, source_target_pairs={{0,8},{8,0},{16,24},{24,16},{1,9},{9,1},{17,25},{25,17},{2,10},{10... | collective-permute-start | bytes 1769480 | tf_op jit(solution)/shard_map/ppermute | solution.py:50
  72.6 2.0 %collective-permute-start.15 = (bf16[768,384]{1,0:T(8,128)(2,1)S(1)}, bf16[768,384]{1,0:T(8,128)(2,1)S(1)}, u32[]{:S(2)}, u32[]{:S(2)}) collective-permute-start(bf16[768,384]{1,0:T(8,128)(2,1)S(1)} %collective-permute-done.14.refs_0_), channel_id=1, source_target_pairs={{0,8},{8,0},{16,24},{24,16},{1,9},{9,1},{17,25},{25,17},{2,10},{10... | collective-permute-start | bytes 1769480 | tf_op jit(solution)/shard_map/ppermute | solution.py:50
  77.6 3.4 %collective-permute-start.16 = (bf16[768,384]{1,0:T(8,128)(2,1)S(1)}, bf16[768,384]{1,0:T(8,128)(2,1)S(1)}, u32[]{:S(2)}, u32[]{:S(2)}) collective-permute-start(bf16[768,384]{1,0:T(8,128)(2,1)S(1)} %get-tuple-element.20.refs_0_.refs_4_), channel_id=1, source_target_pairs={{0,8},{8,0},{16,24},{24,16},{1,9},{9,1},{17,25},{25,17},{2,10},{10... | collective-permute-start | bytes 1769480 | tf_op jit(solution)/shard_map/ppermute | solution.py:50
  77.8 9.9 %collective-permute-start.22 = (bf16[768,384]{1,0:T(8,128)(2,1)S(1)}, bf16[768,384]{1,0:T(8,128)(2,1)S(1)}, u32[]{:S(2)}, u32[]{:S(2)}) collective-permute-start(bf16[768,384]{1,0:T(8,128)(2,1)S(1)} %get-tuple-element.20.refs_0_.refs_4_), channel_id=1, source_target_pairs={{0,2},{2,4},{4,6},{6,7},{7,5},{5,3},{3,1},{1,0},{8,9},{10,8},{12,1... | collective-permute-start | bytes 1769480 | tf_op jit(solution)/shard_map/ppermute | solution.py:47
  79.5 15.3 %collective-permute-start.17 = (bf16[768,384]{1,0:T(8,128)(2,1)S(1)}, bf16[768,384]{1,0:T(8,128)(2,1)S(1)}, u32[]{:S(2)}, u32[]{:S(2)}) collective-permute-start(bf16[768,384]{1,0:T(8,128)(2,1)S(1)} %get-tuple-element.20.refs_0_.refs_4_), channel_id=1, source_target_pairs={{0,16},{8,24},{16,0},{24,8},{1,17},{9,25},{17,1},{25,9},{2,18},{10... | collective-permute-start | bytes 1769480 | tf_op jit(solution)/shard_map/ppermute | solution.py:50
  81.0 13.8 %collective-permute-start.23 = (bf16[768,384]{1,0:T(8,128)(2,1)S(1)}, bf16[768,384]{1,0:T(8,128)(2,1)S(1)}, u32[]{:S(2)}, u32[]{:S(2)}) collective-permute-start(bf16[768,384]{1,0:T(8,128)(2,1)S(1)} %collective-permute-done.16.refs_1_), channel_id=1, source_target_pairs={{0,2},{2,4},{4,6},{6,7},{7,5},{5,3},{3,1},{1,0},{8,9},{10,8},{12,1... | collective-permute-start | bytes 1769480 | tf_op jit(solution)/shard_map/ppermute | solution.py:47
  87.6 12.6 %collective-permute-start.25 = (bf16[768,384]{1,0:T(8,128)(2,1)S(1)}, bf16[768,384]{1,0:T(8,128)(2,1)S(1)}, u32[]{:S(2)}, u32[]{:S(2)}) collective-permute-start(bf16[768,384]{1,0:T(8,128)(2,1)S(1)} %collective-permute-done.22.refs_5_), channel_id=1, source_target_pairs={{0,2},{2,4},{4,6},{6,7},{7,5},{5,3},{3,1},{1,0},{8,9},{10,8},{12,1... | collective-permute-start | bytes 1769480 | tf_op jit(solution)/shard_map/ppermute | solution.py:47
  94.8 7.3 %collective-permute-start.18 = (bf16[768,384]{1,0:T(8,128)(2,1)S(1)}, bf16[768,384]{1,0:T(8,128)(2,1)S(1)}, u32[]{:S(2)}, u32[]{:S(2)}) collective-permute-start(bf16[768,384]{1,0:T(8,128)(2,1)S(1)} %collective-permute-done.17.refs_2_), channel_id=1, source_target_pairs={{0,8},{8,0},{16,24},{24,16},{1,9},{9,1},{17,25},{25,17},{2,10},{10... | collective-permute-start | bytes 1769480 | tf_op jit(solution)/shard_map/ppermute | solution.py:50
  94.8 12.0 %collective-permute-start.26 = (bf16[768,384]{1,0:T(8,128)(2,1)S(1)}, bf16[768,384]{1,0:T(8,128)(2,1)S(1)}, u32[]{:S(2)}, u32[]{:S(2)}) collective-permute-start(bf16[768,384]{1,0:T(8,128)(2,1)S(1)} %collective-permute-done.23), channel_id=1, source_target_pairs={{0,2},{2,4},{4,6},{6,7},{7,5},{5,3},{3,1},{1,0},{8,9},{10,8},{12,1... | collective-permute-start | bytes 1769480 | tf_op jit(solution)/shard_map/ppermute | solution.py:47
  100.3 12.6 %collective-permute-start.28 = (bf16[768,384]{1,0:T(8,128)(2,1)S(1)}, bf16[768,384]{1,0:T(8,128)(2,1)S(1)}, u32[]{:S(2)}, u32[]{:S(2)}) collective-permute-start(bf16[768,384]{1,0:T(8,128)(2,1)S(1)} %collective-permute-done.25.refs_7_), channel_id=1, source_target_pairs={{0,2},{2,4},{4,6},{6,7},{7,5},{5,3},{3,1},{1,0},{8,9},{10,8},{12,1... | collective-permute-start | bytes 1769480 | tf_op jit(solution)/shard_map/ppermute | solution.py:47
  105.2 24.9 %copy-start = (bf16[768,384]{1,0:T(8,128)(2,1)S(1)}, bf16[768,384]{1,0:T(8,128)(2,1)}, u32[]{:S(2)}) copy-start(bf16[768,384]{1,0:T(8,128)(2,1)} %deriv_ref.1) | copy-start | bytes 1769476
  105.2 24.9 %copy-start.4 = (s32[24]{0:T(128)S(1)}, s32[24]{0:T(128)}, u32[]{:S(2)}) copy-start(s32[24]{0:T(128)} %frag_ref.1) | copy-start | bytes 292
  105.2 14.5 %collective-permute-start.20 = (bf16[768,384]{1,0:T(8,128)(2,1)S(1)}, bf16[768,384]{1,0:T(8,128)(2,1)S(1)}, u32[]{:S(2)}, u32[]{:S(2)}) collective-permute-start(bf16[768,384]{1,0:T(8,128)(2,1)S(1)} %shard_map.72.refs_0_), channel_id=1, source_target_pairs={{0,16},{8,24},{16,0},{24,8},{1,17},{9,25},{17,1},{25,9},{2,18},{10... | collective-permute-start | bytes 1769480 | tf_op jit(solution)/shard_map/ppermute | solution.py:50
  106.8 12.9 %collective-permute-start.29 = (bf16[768,384]{1,0:T(8,128)(2,1)S(1)}, bf16[768,384]{1,0:T(8,128)(2,1)S(1)}, u32[]{:S(2)}, u32[]{:S(2)}) collective-permute-start(bf16[768,384]{1,0:T(8,128)(2,1)S(1)} %collective-permute-done.26), channel_id=1, source_target_pairs={{0,2},{2,4},{4,6},{6,7},{7,5},{5,3},{3,1},{1,0},{8,9},{10,8},{12,1... | collective-permute-start | bytes 1769480 | tf_op jit(solution)/shard_map/ppermute | solution.py:47
  108.4 11.8 %collective-permute-start.19 = (bf16[768,384]{1,0:T(8,128)(2,1)S(1)}, bf16[768,384]{1,0:T(8,128)(2,1)S(1)}, u32[]{:S(2)}, u32[]{:S(2)}) collective-permute-start(bf16[768,384]{1,0:T(8,128)(2,1)S(1)} %shard_map.72.refs_0_), channel_id=1, source_target_pairs={{0,8},{8,0},{16,24},{24,16},{1,9},{9,1},{17,25},{25,17},{2,10},{10... | collective-permute-start | bytes 1769480 | tf_op jit(solution)/shard_map/ppermute | solution.py:50
  108.4 12.6 %collective-permute-start.24 = (bf16[768,384]{1,0:T(8,128)(2,1)S(1)}, bf16[768,384]{1,0:T(8,128)(2,1)S(1)}, u32[]{:S(2)}, u32[]{:S(2)}) collective-permute-start(bf16[768,384]{1,0:T(8,128)(2,1)S(1)} %collective-permute-done.23), channel_id=1, source_target_pairs={{0,8},{8,0},{16,24},{24,16},{1,9},{9,1},{17,25},{25,17},{2,10},{10... | collective-permute-start | bytes 1769480 | tf_op jit(solution)/shard_map/ppermute | solution.py:50
  112.9 8.8 %collective-permute-start.27 = (bf16[768,384]{1,0:T(8,128)(2,1)S(1)}, bf16[768,384]{1,0:T(8,128)(2,1)S(1)}, u32[]{:S(2)}, u32[]{:S(2)}) collective-permute-start(bf16[768,384]{1,0:T(8,128)(2,1)S(1)} %collective-permute-done.26), channel_id=1, source_target_pairs={{0,8},{8,0},{16,24},{24,16},{1,9},{9,1},{17,25},{25,17},{2,10},{10... | collective-permute-start | bytes 1769480 | tf_op jit(solution)/shard_map/ppermute | solution.py:50
  119.7 2.0 %collective-permute-start.21 = (bf16[768,384]{1,0:T(8,128)(2,1)S(1)}, bf16[768,384]{1,0:T(8,128)(2,1)S(1)}, u32[]{:S(2)}, u32[]{:S(2)}) collective-permute-start(bf16[768,384]{1,0:T(8,128)(2,1)S(1)} %collective-permute-done.20.refs_2_), channel_id=1, source_target_pairs={{0,8},{8,0},{16,24},{24,16},{1,9},{9,1},{17,25},{25,17},{2,10},{10... | collective-permute-start | bytes 1769480 | tf_op jit(solution)/shard_map/ppermute | solution.py:50
  119.7 2.8 %collective-permute-start.30 = (bf16[768,384]{1,0:T(8,128)(2,1)S(1)}, bf16[768,384]{1,0:T(8,128)(2,1)S(1)}, u32[]{:S(2)}, u32[]{:S(2)}) collective-permute-start(bf16[768,384]{1,0:T(8,128)(2,1)S(1)} %collective-permute-done.29), channel_id=1, source_target_pairs={{0,8},{8,0},{16,24},{24,16},{1,9},{9,1},{17,25},{25,17},{2,10},{10... | collective-permute-start | bytes 1769480 | tf_op jit(solution)/shard_map/ppermute | solution.py:50
  120.2 9.9 %collective-permute-start.31 = (bf16[768,384]{1,0:T(8,128)(2,1)S(1)}, bf16[768,384]{1,0:T(8,128)(2,1)S(1)}, u32[]{:S(2)}, u32[]{:S(2)}) collective-permute-start(bf16[768,384]{1,0:T(8,128)(2,1)S(1)} %collective-permute-done.28.refs_9_), channel_id=1, source_target_pairs={{0,2},{2,4},{4,6},{6,7},{7,5},{5,3},{3,1},{1,0},{8,9},{10,8},{12,1... | collective-permute-start | bytes 1769480 | tf_op jit(solution)/shard_map/ppermute | solution.py:47

commit v3 on v2

--- a/solution.py
+++ b/solution.py
@@ -37,13 +37,15 @@
         self.cycle = cycle_of(self.cols)
         self.far = self.cols // 2
 
-    def ring(self, value):
+    def ring(self, value, to_partner=False):
         pairs = []
         for row in range(self.rows):
             direction = -1 if row % 2 else 1
+            target_row = row ^ 1 if to_partner else row
             for place in range(self.cols):
+                source = self.cycle[place]
                 target = self.cycle[(place + direction) % self.cols]
-                pairs.append((row * self.cols + self.cycle[place], row * self.cols + target))
+                pairs.append((row * self.cols + source, target_row * self.cols + target))
         return lax.ppermute(value, AXES, pairs)
 
     def across(self, value, other):
@@ -82,7 +84,7 @@
     return jnp.dot(left, right, preferred_element_type=jnp.float32)
 
 
-def call(kernel, outs, scalars, arrays, flops, aliases=None):
+def call(kernel, outs, scalars, arrays, aliases=None):
     vmem = pl.BlockSpec(memory_space=pltpu.VMEM)
     smem = pl.BlockSpec(memory_space=pltpu.SMEM)
     moved = sum(a.size * a.dtype.itemsize for a in list(arrays) + list(outs))
@@ -93,39 +95,67 @@
         out_specs=[vmem] * len(outs),
         input_output_aliases=aliases or {},
         compiler_params=pltpu.CompilerParams(vmem_limit_bytes=moved + SPARE_VMEM),
-        cost_estimate=pl.CostEstimate(flops=flops, bytes_accessed=moved, transcendentals=0),
+        cost_estimate=pl.CostEstimate(flops=0, bytes_accessed=0, transcendentals=0),
     )(*scalars, *arrays)
 
 
-def mask_kernel(plan, band_ref, ham_ref, out_ref):
-    out_ref[...] = masked(plan, band_ref, ham_ref[...].astype(jnp.float32)).astype(jnp.bfloat16)
-
-
-def near_kernel(plan, keep_slab, *refs):
+def lay_masked(plan, band_ref, to_ref, from_ref, row_first, col_first, to_row, to_col):
+    for i in range(plan.block_rows):
+        for j in range(plan.block_cols):
+            row, col = row_first // BLK + i, col_first // BLK + j
+            keep = jnp.abs(row - col) <= jnp.maximum(band_ref[row], band_ref[col])
+            block = from_ref[i * BLK : (i + 1) * BLK, j * BLK : (j + 1) * BLK]
+            lines = pl.ds(pl.multiple_of(to_row + i * BLK, BLK), BLK)
+            lanes = pl.ds(pl.multiple_of(to_col + j * BLK, BLK), BLK)
+            to_ref[lines, lanes] = block * keep.astype(jnp.bfloat16)
+
+
+def near_places(plan, first, last):
+    return [(distance, behind) for distance in range(first, last) for behind in ((True, False) if distance else (True,))]
+
+
+def start_terms(plan, places, band_ref, right_ref, slab_ref, lefts):
+    total = None
+    for (distance, behind), left in zip(places, lefts):
+        first = plan.origin_first(distance, behind)
+        lay_masked(plan, band_ref, slab_ref, left, plan.row_first(0), first, 0, first)
+        lanes = pl.ds(first, plan.cols_here)
+        term = dot(slab_ref[:, lanes], right_ref[lanes, :])
+        total = term if total is None else total + term
+    return total
+
+
+def start_kernel(plan, places, band_ref, *refs):
     rights, refs = refs[: plan.rows], refs[plan.rows :]
-    count = 2 * plan.far - 1
-    lefts, (total_ref, right_ref, *slab_ref) = refs[:count], refs[count:]
+    *lefts, total_ref, right_ref, slab_ref = refs
+    col_first = plan.origin_first(0, True)
+    for other in range(plan.rows):
+        row_first = plan.row_first(other)
+        lay_masked(plan, band_ref, right_ref, rights[other], row_first, col_first, row_first, 0)
+    total_ref[...] = start_terms(plan, places, band_ref, right_ref, slab_ref, lefts)
+
+
+def square_kernel(plan, places, band_ref, before_ref, right_ref, _, far_ref, out_ref, slab_ref):
+    total = before_ref[...] + start_terms(plan, places, band_ref, right_ref, slab_ref, [far_ref])
+    out_ref[...] = masked(plan, band_ref, total).astype(jnp.bfloat16)
+
+
+def pass_kernel(*refs):
+    for from_ref, to_ref in zip(refs, refs[len(refs) // 2 :]):
+        to_ref[:16, :BLK] = from_ref[:16, :BLK]
+
+
+def near_kernel(plan, places, *refs):
+    rights, refs = refs[: plan.rows], refs[plan.rows :]
+    *lefts, total_ref, right_ref = refs
     for other in range(plan.rows):
         right_ref[pl.ds(plan.row_first(other), plan.rows_here), :] = rights[other][...]
     total = None
-    for place, left in enumerate(lefts):
-        first = plan.origin_first((place + 1) // 2, place % 2 == 1)
-        if keep_slab:
-            slab_ref[0][:, pl.ds(first, plan.cols_here)] = left[...]
+    for (distance, behind), left in zip(places, lefts):
+        first = plan.origin_first(distance, behind)
         term = dot(left[...], right_ref[pl.ds(first, plan.cols_here), :])
         total = term if total is None else total + term
     total_ref[...] = total
-
-
-def far_terms(plan, total_ref, right_ref, far_ref):
-    first = plan.origin_first(plan.far, True)
-    return total_ref[...] + dot(far_ref[...], right_ref[pl.ds(first, plan.cols_here), :])
-
-
-def square_kernel(plan, band_ref, total_ref, right_ref, far_ref, _, out_ref, slab_ref):
-    total = far_terms(plan, total_ref, right_ref, far_ref)
-    slab_ref[:, pl.ds(plan.origin_first(plan.far, True), plan.cols_here)] = far_ref[...]
-    out_ref[...] = masked(plan, band_ref, total).astype(jnp.bfloat16)
 
 
 def slab_terms(plan, slab_ref, pieces):
@@ -141,10 +171,16 @@
     total_ref[...] = slab_terms(plan, slab_ref, list(zip(others, pieces)))
 
 
-def sign_kernel(plan, others, band_ref, slab_ref, total_ref, start_ref, *refs):
+def more_kernel(plan, others, slab_ref, before_ref, *refs):
+    *pieces, total_ref = refs
+    total_ref[...] = before_ref[...] + slab_terms(plan, slab_ref, list(zip(others, pieces)))
+
+
+def sign_kernel(plan, others, band_ref, slab_ref, total_ref, *refs):
     *pieces, sign_ref, density_ref = refs
     cubic = total_ref[...] + slab_terms(plan, slab_ref, list(zip(others, pieces)))
-    sign = masked(plan, band_ref, 1.5 * start_ref[...].astype(jnp.float32) - 0.5 * cubic).astype(jnp.bfloat16)
+    start = slab_ref[:, pl.ds(plan.origin_first(0, True), plan.cols_here)].astype(jnp.float32)
+    sign = masked(plan, band_ref, 1.5 * start - 0.5 * cubic).astype(jnp.bfloat16)
     sign_ref[...] = sign
     first_row = lax.axis_index("row") * plan.rows_here
     first_col = lax.axis_index("col") * plan.cols_here
@@ -160,8 +196,12 @@
     out_ref[...] = masked(plan, band_ref, total).astype(jnp.bfloat16)
 
 
-def energy_kernel(plan, band_ref, frag_ref, total_ref, right_ref, far_ref, deriv_ref, energy_ref, sums_ref):
-    total = far_terms(plan, total_ref, right_ref, far_ref)
+def energy_kernel(plan, places, band_ref, frag_ref, total_ref, right_ref, deriv_ref, *refs):
+    *lefts, energy_ref, sums_ref = refs
+    total = total_ref[...]
+    for (distance, behind), left in zip(places, lefts):
+        first = plan.origin_first(distance, behind)
+        total = total + dot(left[...], right_ref[pl.ds(first, plan.cols_here), :])
     energy = masked(plan, band_ref, total).astype(jnp.bfloat16)
     energy_ref[...] = energy
     weighed = energy.astype(jnp.float32) * deriv_ref[...].astype(jnp.float32)
@@ -179,7 +219,6 @@
 def body(ham, deriv, band, frag_of):
     plan = Plan(*ham.shape)
     bind = functools.partial
-    flops = 2 * plan.rows_here * plan.order * plan.cols_here
     block = jax.ShapeDtypeStruct(ham.shape, jnp.bfloat16)
     total_type = jax.ShapeDtypeStruct(ham.shape, jnp.float32)
     slab_type = jax.ShapeDtypeStruct((plan.rows_here, plan.order), jnp.bfloat16)
@@ -192,45 +231,52 @@
     def exchange_end(first_two, crossed):
         return list(first_two) + [piece for value in crossed for piece in (value, plan.across(value, 1))]
 
-    def gather(mine, partner):
+    def gather(mine, partner, hand_over):
         shards = [mine]
         for distance in range(1, plan.far):
             mine = plan.ring(mine)
-            partner = plan.ring(partner)
-            shards += [mine, plan.across(partner, 1)]
+            last = distance == plan.far - 1 and not hand_over
+            partner = plan.ring(partner, last)
+            shards += [mine, partner if last else plan.across(partner, 1)]
         return shards, plan.ring(mine)
 
-    (start,) = call(bind(mask_kernel, plan), [block], [band], [ham], 0)
-    partner = plan.across(start, 1)
-    shards, far = gather(start, partner)
-    column = exchange_end([start, partner], exchange_start(start))
+    partner = plan.across(ham, 1)
+    shards, far = gather(ham, partner, False)
+    column = exchange_end([ham, partner], exchange_start(ham))
     total, right, slab = call(
-        bind(near_kernel, plan, True), [total_type, column_type, slab_type], [], column + shards, flops
+        bind(start_kernel, plan, near_places(plan, 0, plan.far)),
+        [total_type, column_type, slab_type],
+        [band],
+        column + shards,
     )
     square, slab = call(
-        bind(square_kernel, plan), [block, slab_type], [band], [total, right, far, slab], flops // 8, {4: 1}
+        bind(square_kernel, plan, [(plan.far, True)]), [block, slab_type], [band], [total, right, slab, far], {3: 1}
     )
 
     crossed = exchange_start(square)
     partner = plan.across(square, 1)
-    (total,) = call(bind(some_kernel, plan, [0, 1]), [total_type], [], [slab, square, partner], flops // 2)
+    (total,) = call(bind(some_kernel, plan, [0, 1]), [total_type], [], [slab, square, partner])
+    *crossed, total = lax.optimization_barrier((*crossed, total))
     column = exchange_end([square, partner], crossed)
+    even, odd = list(others)[2::2], list(others)[3::2]
+    (total,) = call(bind(more_kernel, plan, even), [total_type], [], [slab, total] + column[2::2])
     sign_iterate, density = call(
-        bind(sign_kernel, plan, list(others)[2:]), [block, block], [band], [slab, total, start] + column[2:], flops // 2
+        bind(sign_kernel, plan, odd), [block, block], [band], [slab, total] + column[3::2]
     )
 
     partner = plan.across(density, 1)
-    shards, far = gather(density, partner)
+    shards, far = gather(density, partner, True)
     column = exchange_end([density, partner], exchange_start(density))
-    (weighted,) = call(bind(weighted_kernel, plan, others), [block], [band], [slab] + column, flops)
+    (weighted,) = call(bind(weighted_kernel, plan, others), [block], [band], [slab] + column)
     column = exchange_end([weighted, plan.across(weighted, 1)], exchange_start(weighted))
-    total, right = call(bind(near_kernel, plan, False), [total_type, column_type], [], column + shards, flops)
+    places = near_places(plan, 0, plan.far)
+    late = [shards[-1], far]
+    total, right = call(bind(near_kernel, plan, places[:-1]), [total_type, column_type], [], column + shards[:-1])
     energy_density, sums = call(
-        bind(energy_kernel, plan),
+        bind(energy_kernel, plan, places[-1:] + [(plan.far, True)]),
         [block, jax.ShapeDtypeStruct((FRAG_DEV * plan.cols, BLK), jnp.float32)],
         [band, frag_of],
-        [total, right, far, deriv],
-        flops // 8,
+        [total, right, deriv] + late,
     )
     sums = sums.reshape(1, plan.cols, FRAG_DEV, BLK)
     sums = jnp.broadcast_to(sums, (plan.rows, plan.cols, FRAG_DEV, BLK))

time: 145 us -> 138 us (0.952)
  waiting for transfers between devices: 78.3 us -> 70.5 us
    ppermute x14, waiting for transfers between devices: 48.8 us -> 42.2 us  [ring(): return lax.ppermute(value, AXES, pairs)]
    ppermute x18 -> x17, starting transfers between devices: 8.81 us -> 10.2 us  [across(): lax.ppermute(value, 'row', [(i, i ^ other) for i in range(self.rows)])]
    ppermute x18 -> x17, waiting for transfers between devices: 29.4 us -> 28.3 us  [across(): lax.ppermute(value, 'row', [(i, i ^ other) for i in range(self.rows)])]
  transfers between devices with their start and end apart: 32 -> 31, of which waited for: 19 -> 17; matrix products, arithmetic and copies ran while one was open for 0% -> 0% of each run, Pallas kernels for 7% -> 9%
where the time goes in v3:
time: 138 us
  waiting for transfers between devices  70.5 us (51%)
  starting transfers between devices  34.4 us (25%)
  Pallas kernels  18.4 us (13%)
  blocking collectives  11.9 us (9%)
  local copies, waits for them, and re-layouts  1.75 us (1%)
    ppermute x14, waiting for transfers between devices, ring(): return lax.ppermute(value, AXES, pairs)  42.2 us
    ppermute x17, waiting for transfers between devices, across(): lax.ppermute(value, 'row', [(i, i ^ other) for i in range(self.rows)])  28.3 us
    ppermute x14, starting transfers between devices, ring(): return lax.ppermute(value, AXES, pairs)  24.2 us
    pallas_call x8, Pallas kernels, call(): pl.pallas_call(kernel, out_shape=outs, in_specs=[smem] * len(scalars) + [...  18.4 us
    all_to_all x1, blocking collectives, body(): pulay_terms = jnp.sum(lax.all_to_all(sums, AXES, 0, 0), axis=0)  11.9 us
    ppermute x17, starting transfers between devices, across(): lax.ppermute(value, 'row', [(i, i ^ other) for i in range(self.rows)])  10.2 us
  transfers between devices with their start and end apart: 31, of which 17 were waited for; matrix products, arithmetic and copies ran while one was open for 0% of the time, Pallas kernels for 9%

profile of v3, /device:TPU:0, one launch (start us, length us, event | category | flops | bytes accessed | tf_op | source)
XLA Modules:
  0.0 138.3 jit_solution(14381647549166257855)
XLA Ops:
  0.6 0.5 collective-permute-start
  1.1 2.6 %collective-permute-start.3 = (bf16[768,384]{1,0:T(8,128)(2,1)}, bf16[768,384]{1,0:T(8,128)(2,1)S(1)}, u32[]{:S(2)}, u32[]{:S(2)}) collective-permute-start(bf16[768,384]{1,0:T(8,128)(2,1)} %refs_4_.1), channel_id=1, source_target_pairs={{0,2},{2,4},{4,6},{6,7},{7,5},{5,3},{3,1},{1,0},{8,9},{10,8},{12,1... | collective-permute-start | bytes 1769480 | tf_op jit(solution)/shard_map/ppermute | solution.py:49
  3.8 0.0 collective-permute-done.refs_1_
  3.8 2.1 %collective-permute-start.4 = (bf16[768,384]{1,0:T(8,128)(2,1)S(1)}, bf16[768,384]{1,0:T(8,128)(2,1)S(1)}, u32[]{:S(2)}, u32[]{:S(2)}) collective-permute-start(bf16[768,384]{1,0:T(8,128)(2,1)S(1)} %collective-permute-done.refs_1_), channel_id=1, source_target_pairs={{0,2},{2,4},{4,6},{6,7},{7,5},{5,3},{3,1},{1,0},{8,9},{10,8},{12,1... | collective-permute-start | bytes 1769480 | tf_op jit(solution)/shard_map/ppermute | solution.py:49
  5.9 5.9 %collective-permute-done.3.refs_5_ = bf16[768,384]{1,0:T(8,128)(2,1)S(1)} collective-permute-done((bf16[768,384]{1,0:T(8,128)(2,1)}, bf16[768,384]{1,0:T(8,128)(2,1)S(1)}, u32[]{:S(2)}, u32[]{:S(2)}) %collective-permute-start.3) | collective-permute-done | bytes 589856 | tf_op jit(solution)/shard_map/ppermute | solution.py:49
  11.8 2.1 %collective-permute-start.6 = (bf16[768,384]{1,0:T(8,128)(2,1)S(1)}, bf16[768,384]{1,0:T(8,128)(2,1)S(1)}, u32[]{:S(2)}, u32[]{:S(2)}) collective-permute-start(bf16[768,384]{1,0:T(8,128)(2,1)S(1)} %collective-permute-done.3.refs_5_), channel_id=1, source_target_pairs={{0,2},{2,4},{4,6},{6,7},{7,5},{5,3},{3,1},{1,0},{8,9},{10,8},{12,1... | collective-permute-start | bytes 1769480 | tf_op jit(solution)/shard_map/ppermute | solution.py:49
  13.9 1.5 %collective-permute-start.1 = (bf16[768,384]{1,0:T(8,128)(2,1)}, bf16[768,384]{1,0:T(8,128)(2,1)S(1)}, u32[]{:S(2)}, u32[]{:S(2)}) collective-permute-start(bf16[768,384]{1,0:T(8,128)(2,1)} %refs_4_.1), channel_id=1, source_target_pairs={{0,16},{8,24},{16,0},{24,8},{1,17},{9,25},{17,1},{25,9},{2,18},{10... | collective-permute-start | bytes 1769480 | tf_op jit(solution)/shard_map/ppermute | solution.py:52
  15.4 2.8 %collective-permute-done.4 = bf16[768,384]{1,0:T(8,128)(2,1)S(1)} collective-permute-done((bf16[768,384]{1,0:T(8,128)(2,1)S(1)}, bf16[768,384]{1,0:T(8,128)(2,1)S(1)}, u32[]{:S(2)}, u32[]{:S(2)}) %collective-permute-start.4) | collective-permute-done | bytes 589856 | tf_op jit(solution)/shard_map/ppermute | solution.py:49
  18.1 2.1 %collective-permute-start.7 = (bf16[768,384]{1,0:T(8,128)(2,1)S(1)}, bf16[768,384]{1,0:T(8,128)(2,1)S(1)}, u32[]{:S(2)}, u32[]{:S(2)}) collective-permute-start(bf16[768,384]{1,0:T(8,128)(2,1)S(1)} %collective-permute-done.4), channel_id=1, source_target_pairs={{0,2},{2,4},{4,6},{6,7},{7,5},{5,3},{3,1},{1,0},{8,9},{10,8},{12,1... | collective-permute-start | bytes 1769480 | tf_op jit(solution)/shard_map/ppermute | solution.py:49
  20.2 4.2 %collective-permute-done.6.refs_7_ = bf16[768,384]{1,0:T(8,128)(2,1)S(1)} collective-permute-done((bf16[768,384]{1,0:T(8,128)(2,1)S(1)}, bf16[768,384]{1,0:T(8,128)(2,1)S(1)}, u32[]{:S(2)}, u32[]{:S(2)}) %collective-permute-start.6) | collective-permute-done | bytes 589856 | tf_op jit(solution)/shard_map/ppermute | solution.py:49
  24.4 2.1 %collective-permute-start.9 = (bf16[768,384]{1,0:T(8,128)(2,1)S(1)}, bf16[768,384]{1,0:T(8,128)(2,1)S(1)}, u32[]{:S(2)}, u32[]{:S(2)}) collective-permute-start(bf16[768,384]{1,0:T(8,128)(2,1)S(1)} %collective-permute-done.6.refs_7_), channel_id=1, source_target_pairs={{0,2},{2,4},{4,6},{6,7},{7,5},{5,3},{3,1},{1,0},{8,9},{10,8},{12,1... | collective-permute-start | bytes 1769480 | tf_op jit(solution)/shard_map/ppermute | solution.py:49
  26.5 2.1 %collective-permute-done.1.refs_2_ = bf16[768,384]{1,0:T(8,128)(2,1)S(1)} collective-permute-done((bf16[768,384]{1,0:T(8,128)(2,1)}, bf16[768,384]{1,0:T(8,128)(2,1)S(1)}, u32[]{:S(2)}, u32[]{:S(2)}) %collective-permute-start.1) | collective-permute-done | bytes 589856 | tf_op jit(solution)/shard_map/ppermute | solution.py:52
  28.6 0.5 collective-permute-start.5
  29.1 1.7 %collective-permute-done.7 = bf16[768,384]{1,0:T(8,128)(2,1)S(1)} collective-permute-done((bf16[768,384]{1,0:T(8,128)(2,1)S(1)}, bf16[768,384]{1,0:T(8,128)(2,1)S(1)}, u32[]{:S(2)}, u32[]{:S(2)}) %collective-permute-start.7) | collective-permute-done | bytes 589856 | tf_op jit(solution)/shard_map/ppermute | solution.py:49
  30.8 1.3 collective-permute-start.10
  32.0 0.9 collective-permute-start.8
  32.9 4.2 %collective-permute-done.9.refs_9_ = bf16[768,384]{1,0:T(8,128)(2,1)S(1)} collective-permute-done((bf16[768,384]{1,0:T(8,128)(2,1)S(1)}, bf16[768,384]{1,0:T(8,128)(2,1)S(1)}, u32[]{:S(2)}, u32[]{:S(2)}) %collective-permute-start.9) | collective-permute-done | bytes 589856 | tf_op jit(solution)/shard_map/ppermute | solution.py:49
  37.1 2.1 %collective-permute-start.11 = (bf16[768,384]{1,0:T(8,128)(2,1)S(1)}, bf16[768,384]{1,0:T(8,128)(2,1)S(1)}, u32[]{:S(2)}, u32[]{:S(2)}) collective-permute-start(bf16[768,384]{1,0:T(8,128)(2,1)S(1)} %collective-permute-done.9.refs_9_), channel_id=1, source_target_pairs={{0,2},{2,4},{4,6},{6,7},{7,5},{5,3},{3,1},{1,0},{8,9},{10,8},{12,1... | collective-permute-start | bytes 1769480 | tf_op jit(solution)/shard_map/ppermute | solution.py:49
  39.2 4.0 %collective-permute-done.10.refs_10_ = bf16[768,384]{1,0:T(8,128)(2,1)S(1)} collective-permute-done((bf16[768,384]{1,0:T(8,128)(2,1)S(1)}, bf16[768,384]{1,0:T(8,128)(2,1)S(1)}, u32[]{:S(2)}, u32[]{:S(2)}) %collective-permute-start.10) | collective-permute-done | bytes 589856 | tf_op jit(solution)/shard_map/ppermute | solution.py:49
  43.2 0.0 collective-permute-done.8.refs_8_
  43.2 1.1 copy-done
  44.3 0.7 copy-done.2
  44.9 4.7 %shard_map.67 = (f32[768,384]{1,0:T(8,128)S(1)}, bf16[3072,384]{1,0:T(8,128)(2,1)S(1)}, bf16[768,3072]{1,0:T(8,128)(2,1)S(1)}) custom-call(s32[24]{0:T(128)S(1)} %copy-done.2, bf16[768,384]{1,0:T(8,128)(2,1)S(1)} %copy-done, bf16[768,384]{1,0:T(8,128)(2,1)S(1)} %collective-permute-done.refs_1_, bf16[768,384]{1,0:T(8,128)(2,1)S(1)} %collective-permute-done.1.refs_2_, ...), custom_call_target="tpu_custom_call" | custom-call | tf_op jit(solution)/shard_map/pallas_call | solution.py:91
  49.6 0.1 collective-permute-done.11.far_ref
  49.7 1.1 shard_map.68
  50.9 0.1 collective-permute-start.13
  50.9 2.0 %collective-permute-start.12 = (bf16[768,384]{1,0:T(8,128)(2,1)S(1)}, bf16[768,384]{1,0:T(8,128)(2,1)S(1)}, u32[]{:S(2)}, u32[]{:S(2)}) collective-permute-start(bf16[768,384]{1,0:T(8,128)(2,1)S(1)} %get-tuple-element.20.refs_0_), channel_id=1, source_target_pairs={{0,16},{8,24},{16,0},{24,8},{1,17},{9,25},{17,1},{25,9},{2,18},{10... | collective-permute-start | bytes 1769480 | tf_op jit(solution)/shard_map/ppermute | solution.py:52
  53.0 0.0 collective-permute-done.13.refs_1_
  53.0 1.4 shard_map.69.before_ref
  54.4 12.5 %collective-permute-done.12.refs_0_ = bf16[768,384]{1,0:T(8,128)(2,1)S(1)} collective-permute-done((bf16[768,384]{1,0:T(8,128)(2,1)S(1)}, bf16[768,384]{1,0:T(8,128)(2,1)S(1)}, u32[]{:S(2)}, u32[]{:S(2)}) %collective-permute-start.12) | collective-permute-done | bytes 589856 | tf_op jit(solution)/shard_map/ppermute | solution.py:52
  66.9 0.0 collective-permute-start.14
  66.9 0.8 shard_map.70.total_ref
  67.7 1.2 collective-permute-done.14.refs_0_
  68.9 2.5 %shard_map.71 = (bf16[768,384]{1,0:T(8,128)(2,1)}, bf16[768,384]{1,0:T(8,128)(2,1)S(1)}) custom-call(s32[24]{0:T(128)S(1)} %copy-done.2, bf16[768,3072]{1,0:T(8,128)(2,1)S(1)} %get-tuple-element.19.slab_ref, f32[768,384]{1,0:T(8,128)S(1)} %shard_map.70.total_ref, bf16[768,384]{1,0:T(8,128)(2,1)S(1)} %collective-permute-done.14.refs_0_), custom_call_target="tpu_custom_call" | custom-call | tf_op jit(solution)/shard_map/pallas_call | solution.py:91
  71.4 0.1 collective-permute-start.15
  71.5 1.8 %collective-permute-start.21 = (bf16[768,384]{1,0:T(8,128)(2,1)S(1)}, bf16[768,384]{1,0:T(8,128)(2,1)S(1)}, u32[]{:S(2)}, u32[]{:S(2)}) collective-permute-start(bf16[768,384]{1,0:T(8,128)(2,1)S(1)} %get-tuple-element.24.refs_0_.refs_4_), channel_id=1, source_target_pairs={{0,2},{2,4},{4,6},{6,7},{7,5},{5,3},{3,1},{1,0},{8,9},{10,8},{12,1... | collective-permute-start | bytes 1769480 | tf_op jit(solution)/shard_map/ppermute | solution.py:49
  73.3 1.5 %collective-permute-start.16 = (bf16[768,384]{1,0:T(8,128)(2,1)S(1)}, bf16[768,384]{1,0:T(8,128)(2,1)S(1)}, u32[]{:S(2)}, u32[]{:S(2)}) collective-permute-start(bf16[768,384]{1,0:T(8,128)(2,1)S(1)} %get-tuple-element.24.refs_0_.refs_4_), channel_id=1, source_target_pairs={{0,16},{8,24},{16,0},{24,8},{1,17},{9,25},{17,1},{25,9},{2,18},{10... | collective-permute-start | bytes 1769480 | tf_op jit(solution)/shard_map/ppermute | solution.py:52
  74.8 1.6 %collective-permute-start.22 = (bf16[768,384]{1,0:T(8,128)(2,1)S(1)}, bf16[768,384]{1,0:T(8,128)(2,1)S(1)}, u32[]{:S(2)}, u32[]{:S(2)}) collective-permute-start(bf16[768,384]{1,0:T(8,128)(2,1)S(1)} %collective-permute-done.15.refs_1_), channel_id=1, source_target_pairs={{0,2},{2,4},{4,6},{6,7},{7,5},{5,3},{3,1},{1,0},{8,9},{10,8},{12,1... | collective-permute-start | bytes 1769480 | tf_op jit(solution)/shard_map/ppermute | solution.py:49
  76.4 5.0 %collective-permute-done.21.refs_5_ = bf16[768,384]{1,0:T(8,128)(2,1)S(1)} collective-permute-done((bf16[768,384]{1,0:T(8,128)(2,1)S(1)}, bf16[768,384]{1,0:T(8,128)(2,1)S(1)}, u32[]{:S(2)}, u32[]{:S(2)}) %collective-permute-start.21) | collective-permute-done | bytes 589856 | tf_op jit(solution)/shard_map/ppermute | solution.py:49
  81.4 1.8 %collective-permute-start.24 = (bf16[768,384]{1,0:T(8,128)(2,1)S(1)}, bf16[768,384]{1,0:T(8,128)(2,1)S(1)}, u32[]{:S(2)}, u32[]{:S(2)}) collective-permute-start(bf16[768,384]{1,0:T(8,128)(2,1)S(1)} %collective-permute-done.21.refs_5_), channel_id=1, source_target_pairs={{0,2},{2,4},{4,6},{6,7},{7,5},{5,3},{3,1},{1,0},{8,9},{10,8},{12,1... | collective-permute-start | bytes 1769480 | tf_op jit(solution)/shard_map/ppermute | solution.py:49
  83.2 5.4 %collective-permute-done.16.refs_2_ = bf16[768,384]{1,0:T(8,128)(2,1)S(1)} collective-permute-done((bf16[768,384]{1,0:T(8,128)(2,1)S(1)}, bf16[768,384]{1,0:T(8,128)(2,1)S(1)}, u32[]{:S(2)}, u32[]{:S(2)}) %collective-permute-start.16) | collective-permute-done | bytes 589856 | tf_op jit(solution)/shard_map/ppermute | solution.py:52
  88.6 0.9 collective-permute-start.25
  89.5 4.5 %collective-permute-done.24.refs_7_ = bf16[768,384]{1,0:T(8,128)(2,1)S(1)} collective-permute-done((bf16[768,384]{1,0:T(8,128)(2,1)S(1)}, bf16[768,384]{1,0:T(8,128)(2,1)S(1)}, u32[]{:S(2)}, u32[]{:S(2)}) %collective-permute-start.24) | collective-permute-done | bytes 589856 | tf_op jit(solution)/shard_map/ppermute | solution.py:49
  94.0 1.8 %collective-permute-start.27 = (bf16[768,384]{1,0:T(8,128)(2,1)S(1)}, bf16[768,384]{1,0:T(8,128)(2,1)S(1)}, u32[]{:S(2)}, u32[]{:S(2)}) collective-permute-start(bf16[768,384]{1,0:T(8,128)(2,1)S(1)} %collective-permute-done.24.refs_7_), channel_id=1, source_target_pairs={{0,2},{2,4},{4,6},{6,7},{7,5},{5,3},{3,1},{1,0},{8,9},{10,8},{12,1... | collective-permute-start | bytes 1769480 | tf_op jit(solution)/shard_map/ppermute | solution.py:49
  95.9 0.0 collective-permute-done.17.refs_3_
  95.9 3.1 %shard_map.72.refs_0_ = bf16[768,384]{1,0:T(8,128)(2,1)S(1)} custom-call(s32[24]{0:T(128)S(1)} %copy-done.2, bf16[768,3072]{1,0:T(8,128)(2,1)S(1)} %get-tuple-element.19.slab_ref, bf16[768,384]{1,0:T(8,128)(2,1)S(1)} %get-tuple-element.24.refs_0_.refs_4_, bf16[768,384]{1,0:T(8,128)(2,1)S(1)} %collective-permute-done.15.refs_1_, ...), custom_call_target="tpu_custom_call" | custom-call | tf_op jit(solution)/shard_map/pallas_call | solution.py:91
  99.0 0.0 copy-start.1
  99.0 0.0 copy-start.3
  99.0 0.0 copy-start.4
  99.0 1.5 %collective-permute-start.19 = (bf16[768,384]{1,0:T(8,128)(2,1)S(1)}, bf16[768,384]{1,0:T(8,128)(2,1)S(1)}, u32[]{:S(2)}, u32[]{:S(2)}) collective-permute-start(bf16[768,384]{1,0:T(8,128)(2,1)S(1)} %shard_map.72.refs_0_), channel_id=1, source_target_pairs={{0,16},{8,24},{16,0},{24,8},{1,17},{9,25},{17,1},{25,9},{2,18},{10... | collective-permute-start | bytes 1769480 | tf_op jit(solution)/shard_map/ppermute | solution.py:52
  100.6 0.0 collective-permute-start.18
  100.6 0.0 collective-permute-done.25
  100.6 1.6 %collective-permute-start.28 = (bf16[768,384]{1,0:T(8,128)(2,1)S(1)}, bf16[768,384]{1,0:T(8,128)(2,1)S(1)}, u32[]{:S(2)}, u32[]{:S(2)}) collective-permute-start(bf16[768,384]{1,0:T(8,128)(2,1)S(1)} %collective-permute-done.25), channel_id=1, source_target_pairs={{0,2},{2,4},{4,6},{6,7},{7,5},{5,3},{3,1},{1,0},{8,9},{10,8},{12,1... | collective-permute-start | bytes 1769480 | tf_op jit(solution)/shard_map/ppermute | solution.py:49
  102.2 0.0 collective-permute-start.23
  102.2 4.5 %collective-permute-done.27.refs_9_ = bf16[768,384]{1,0:T(8,128)(2,1)S(1)} collective-permute-done((bf16[768,384]{1,0:T(8,128)(2,1)S(1)}, bf16[768,384]{1,0:T(8,128)(2,1)S(1)}, u32[]{:S(2)}, u32[]{:S(2)}) %collective-permute-start.27) | collective-permute-done | bytes 589856 | tf_op jit(solution)/shard_map/ppermute | solution.py:49
  106.7 6.9 %collective-permute-done.19.refs_2_ = bf16[768,384]{1,0:T(8,128)(2,1)S(1)} collective-permute-done((bf16[768,384]{1,0:T(8,128)(2,1)S(1)}, bf16[768,384]{1,0:T(8,128)(2,1)S(1)}, u32[]{:S(2)}, u32[]{:S(2)}) %collective-permute-start.19) | collective-permute-done | bytes 589856 | tf_op jit(solution)/shard_map/ppermute | solution.py:52
  113.5 0.3 collective-permute-start.30
  113.9 1.5 %collective-permute-start.29 = (bf16[768,384]{1,0:T(8,128)(2,1)S(1)}, bf16[768,384]{1,0:T(8,128)(2,1)S(1)}, u32[]{:S(2)}, u32[]{:S(2)}) collective-permute-start(bf16[768,384]{1,0:T(8,128)(2,1)S(1)} %collective-permute-done.28), channel_id=1, source_target_pairs={{0,8},{8,0},{16,24},{24,16},{1,9},{9,1},{17,25},{25,17},{2,10},{10... | collective-permute-start | bytes 1769480 | tf_op jit(solution)/shard_map/ppermute | solution.py:52
  115.3 0.2 collective-permute-done.20.refs_3_
  115.5 2.5 %shard_map.73 = (f32[768,384]{1,0:T(8,128)S(1)}, bf16[3072,384]{1,0:T(8,128)(2,1)S(1)}) custom-call(bf16[768,384]{1,0:T(8,128)(2,1)S(1)} %shard_map.72.refs_0_, bf16[768,384]{1,0:T(8,128)(2,1)S(1)} %collective-permute-done.18.refs_1_, bf16[768,384]{1,0:T(8,128)(2,1)S(1)} %collective-permute-done.19.refs_2_, ...), custom_call_target="tpu_custom_call" | custom-call | tf_op jit(solution)/shard_map/pallas_call | solution.py:91
  118.1 5.4 %collective-permute-done.30.refs_1_ = bf16[768,384]{1,0:T(8,128)(2,1)S(1)} collective-permute-done((bf16[768,384]{1,0:T(8,128)(2,1)S(1)}, bf16[768,384]{1,0:T(8,128)(2,1)S(1)}, u32[]{:S(2)}, u32[]{:S(2)}) %collective-permute-start.30) | collective-permute-done | bytes 589856 | tf_op jit(solution)/shard_map/ppermute | solution.py:49
  123.5 2.4 %shard_map.74 = (bf16[768,384]{1,0:T(8,128)(2,1)}, f32[16,128]{1,0:T(8,128)S(1)}) custom-call(s32[24]{0:T(128)S(1)} %copy-done.3, s32[24]{0:T(128)S(1)} %copy-done.4, f32[768,384]{1,0:T(8,128)S(1)} %get-tuple-element.25.total_ref, bf16[3072,384]{1,0:T(8,128)(2,1)S(1)} %get-tuple-element.26.right_ref, bf16[768,384]{1,0:T(8,128)(2,1)S(1)} %copy-done.1, ...), custom_call_target="tpu_custom_call" | custom-call | tf_op jit(solution)/shard_map/pallas_call | solution.py:91
  125.8 11.9 %all_to_all.5 = f32[32,2,128]{2,1,0:T(2,128)S(1)} all-to-all(f32[32,2,128]{2,1,0:T(2,128)S(1)} %bitcast.3), channel_id=1, replica_groups=mesh['row'=4,'col'=8] {'row','col'}, dimensions={0} | all-to-all | bytes 65536 | tf_op jit(solution)/shard_map/all_to_all | solution.py:284
  137.7 0.6 reduce_sum.9
  (19 shorter events, 0.1 us)
Async XLA Ops:
  0.6 3.2 %collective-permute-start = (bf16[768,384]{1,0:T(8,128)(2,1)}, bf16[768,384]{1,0:T(8,128)(2,1)S(1)}, u32[]{:S(2)}, u32[]{:S(2)}) collective-permute-start(bf16[768,384]{1,0:T(8,128)(2,1)} %refs_4_.1), channel_id=1, source_target_pairs={{0,8},{8,0},{16,24},{24,16},{1,9},{9,1},{17,25},{25,17},{2,10},{10... | collective-permute-start | bytes 1769480 | tf_op jit(solution)/shard_map/ppermute | solution.py:52
  1.1 10.7 %collective-permute-start.3 = (bf16[768,384]{1,0:T(8,128)(2,1)}, bf16[768,384]{1,0:T(8,128)(2,1)S(1)}, u32[]{:S(2)}, u32[]{:S(2)}) collective-permute-start(bf16[768,384]{1,0:T(8,128)(2,1)} %refs_4_.1), channel_id=1, source_target_pairs={{0,2},{2,4},{4,6},{6,7},{7,5},{5,3},{3,1},{1,0},{8,9},{10,8},{12,1... | collective-permute-start | bytes 1769480 | tf_op jit(solution)/shard_map/ppermute | solution.py:49
  3.8 14.3 %collective-permute-start.4 = (bf16[768,384]{1,0:T(8,128)(2,1)S(1)}, bf16[768,384]{1,0:T(8,128)(2,1)S(1)}, u32[]{:S(2)}, u32[]{:S(2)}) collective-permute-start(bf16[768,384]{1,0:T(8,128)(2,1)S(1)} %collective-permute-done.refs_1_), channel_id=1, source_target_pairs={{0,2},{2,4},{4,6},{6,7},{7,5},{5,3},{3,1},{1,0},{8,9},{10,8},{12,1... | collective-permute-start | bytes 1769480 | tf_op jit(solution)/shard_map/ppermute | solution.py:49
  11.8 12.6 %collective-permute-start.6 = (bf16[768,384]{1,0:T(8,128)(2,1)S(1)}, bf16[768,384]{1,0:T(8,128)(2,1)S(1)}, u32[]{:S(2)}, u32[]{:S(2)}) collective-permute-start(bf16[768,384]{1,0:T(8,128)(2,1)S(1)} %collective-permute-done.3.refs_5_), channel_id=1, source_target_pairs={{0,2},{2,4},{4,6},{6,7},{7,5},{5,3},{3,1},{1,0},{8,9},{10,8},{12,1... | collective-permute-start | bytes 1769480 | tf_op jit(solution)/shard_map/ppermute | solution.py:49
  13.9 14.7 %collective-permute-start.1 = (bf16[768,384]{1,0:T(8,128)(2,1)}, bf16[768,384]{1,0:T(8,128)(2,1)S(1)}, u32[]{:S(2)}, u32[]{:S(2)}) collective-permute-start(bf16[768,384]{1,0:T(8,128)(2,1)} %refs_4_.1), channel_id=1, source_target_pairs={{0,16},{8,24},{16,0},{24,8},{1,17},{9,25},{17,1},{25,9},{2,18},{10... | collective-permute-start | bytes 1769480 | tf_op jit(solution)/shard_map/ppermute | solution.py:52
  18.1 12.6 %collective-permute-start.7 = (bf16[768,384]{1,0:T(8,128)(2,1)S(1)}, bf16[768,384]{1,0:T(8,128)(2,1)S(1)}, u32[]{:S(2)}, u32[]{:S(2)}) collective-permute-start(bf16[768,384]{1,0:T(8,128)(2,1)S(1)} %collective-permute-done.4), channel_id=1, source_target_pairs={{0,2},{2,4},{4,6},{6,7},{7,5},{5,3},{3,1},{1,0},{8,9},{10,8},{12,1... | collective-permute-start | bytes 1769480 | tf_op jit(solution)/shard_map/ppermute | solution.py:49
  24.4 12.6 %collective-permute-start.9 = (bf16[768,384]{1,0:T(8,128)(2,1)S(1)}, bf16[768,384]{1,0:T(8,128)(2,1)S(1)}, u32[]{:S(2)}, u32[]{:S(2)}) collective-permute-start(bf16[768,384]{1,0:T(8,128)(2,1)S(1)} %collective-permute-done.6.refs_7_), channel_id=1, source_target_pairs={{0,2},{2,4},{4,6},{6,7},{7,5},{5,3},{3,1},{1,0},{8,9},{10,8},{12,1... | collective-permute-start | bytes 1769480 | tf_op jit(solution)/shard_map/ppermute | solution.py:49
  28.6 10.6 %collective-permute-start.2 = (bf16[768,384]{1,0:T(8,128)(2,1)S(1)}, bf16[768,384]{1,0:T(8,128)(2,1)S(1)}, u32[]{:S(2)}, u32[]{:S(2)}) collective-permute-start(bf16[768,384]{1,0:T(8,128)(2,1)S(1)} %collective-permute-done.1.refs_2_), channel_id=1, source_target_pairs={{0,8},{8,0},{16,24},{24,16},{1,9},{9,1},{17,25},{25,17},{2,10},{10... | collective-permute-start | bytes 1769480 | tf_op jit(solution)/shard_map/ppermute | solution.py:52
  28.6 10.6 %collective-permute-start.5 = (bf16[768,384]{1,0:T(8,128)(2,1)S(1)}, bf16[768,384]{1,0:T(8,128)(2,1)S(1)}, u32[]{:S(2)}, u32[]{:S(2)}) collective-permute-start(bf16[768,384]{1,0:T(8,128)(2,1)S(1)} %collective-permute-done.4), channel_id=1, source_target_pairs={{0,8},{8,0},{16,24},{24,16},{1,9},{9,1},{17,25},{25,17},{2,10},{10... | collective-permute-start | bytes 1769480 | tf_op jit(solution)/shard_map/ppermute | solution.py:52
  30.8 12.4 %collective-permute-start.10 = (bf16[768,384]{1,0:T(8,128)(2,1)S(1)}, bf16[768,384]{1,0:T(8,128)(2,1)S(1)}, u32[]{:S(2)}, u32[]{:S(2)}) collective-permute-start(bf16[768,384]{1,0:T(8,128)(2,1)S(1)} %collective-permute-done.7), channel_id=1, source_target_pairs={{0,10},{2,12},{4,14},{6,15},{7,13},{5,11},{3,9},{1,8},{8,1},{10,0}... | collective-permute-start | bytes 1769480 | tf_op jit(solution)/shard_map/ppermute | solution.py:49
  32.0 11.2 %collective-permute-start.8 = (bf16[768,384]{1,0:T(8,128)(2,1)S(1)}, bf16[768,384]{1,0:T(8,128)(2,1)S(1)}, u32[]{:S(2)}, u32[]{:S(2)}) collective-permute-start(bf16[768,384]{1,0:T(8,128)(2,1)S(1)} %collective-permute-done.7), channel_id=1, source_target_pairs={{0,8},{8,0},{16,24},{24,16},{1,9},{9,1},{17,25},{25,17},{2,10},{10... | collective-permute-start | bytes 1769480 | tf_op jit(solution)/shard_map/ppermute | solution.py:52
  37.1 12.6 %collective-permute-start.11 = (bf16[768,384]{1,0:T(8,128)(2,1)S(1)}, bf16[768,384]{1,0:T(8,128)(2,1)S(1)}, u32[]{:S(2)}, u32[]{:S(2)}) collective-permute-start(bf16[768,384]{1,0:T(8,128)(2,1)S(1)} %collective-permute-done.9.refs_9_), channel_id=1, source_target_pairs={{0,2},{2,4},{4,6},{6,7},{7,5},{5,3},{3,1},{1,0},{8,9},{10,8},{12,1... | collective-permute-start | bytes 1769480 | tf_op jit(solution)/shard_map/ppermute | solution.py:49
  43.2 1.1 copy-start
  44.3 0.7 copy-start.2
  50.9 2.1 %collective-permute-start.13 = (bf16[768,384]{1,0:T(8,128)(2,1)S(1)}, bf16[768,384]{1,0:T(8,128)(2,1)S(1)}, u32[]{:S(2)}, u32[]{:S(2)}) collective-permute-start(bf16[768,384]{1,0:T(8,128)(2,1)S(1)} %get-tuple-element.20.refs_0_), channel_id=1, source_target_pairs={{0,8},{8,0},{16,24},{24,16},{1,9},{9,1},{17,25},{25,17},{2,10},{10... | collective-permute-start | bytes 1769480 | tf_op jit(solution)/shard_map/ppermute | solution.py:52
  50.9 16.0 %collective-permute-start.12 = (bf16[768,384]{1,0:T(8,128)(2,1)S(1)}, bf16[768,384]{1,0:T(8,128)(2,1)S(1)}, u32[]{:S(2)}, u32[]{:S(2)}) collective-permute-start(bf16[768,384]{1,0:T(8,128)(2,1)S(1)} %get-tuple-element.20.refs_0_), channel_id=1, source_target_pairs={{0,16},{8,24},{16,0},{24,8},{1,17},{9,25},{17,1},{25,9},{2,18},{10... | collective-permute-start | bytes 1769480 | tf_op jit(solution)/shard_map/ppermute | solution.py:52
  66.9 2.0 %collective-permute-start.14 = (bf16[768,384]{1,0:T(8,128)(2,1)S(1)}, bf16[768,384]{1,0:T(8,128)(2,1)S(1)}, u32[]{:S(2)}, u32[]{:S(2)}) collective-permute-start(bf16[768,384]{1,0:T(8,128)(2,1)S(1)} %collective-permute-done.12.refs_0_), channel_id=1, source_target_pairs={{0,8},{8,0},{16,24},{24,16},{1,9},{9,1},{17,25},{25,17},{2,10},{10... | collective-permute-start | bytes 1769480 | tf_op jit(solution)/shard_map/ppermute | solution.py:52
  71.4 3.5 %collective-permute-start.15 = (bf16[768,384]{1,0:T(8,128)(2,1)S(1)}, bf16[768,384]{1,0:T(8,128)(2,1)S(1)}, u32[]{:S(2)}, u32[]{:S(2)}) collective-permute-start(bf16[768,384]{1,0:T(8,128)(2,1)S(1)} %get-tuple-element.24.refs_0_.refs_4_), channel_id=1, source_target_pairs={{0,8},{8,0},{16,24},{24,16},{1,9},{9,1},{17,25},{25,17},{2,10},{10... | collective-permute-start | bytes 1769480 | tf_op jit(solution)/shard_map/ppermute | solution.py:52
  71.5 9.9 %collective-permute-start.21 = (bf16[768,384]{1,0:T(8,128)(2,1)S(1)}, bf16[768,384]{1,0:T(8,128)(2,1)S(1)}, u32[]{:S(2)}, u32[]{:S(2)}) collective-permute-start(bf16[768,384]{1,0:T(8,128)(2,1)S(1)} %get-tuple-element.24.refs_0_.refs_4_), channel_id=1, source_target_pairs={{0,2},{2,4},{4,6},{6,7},{7,5},{5,3},{3,1},{1,0},{8,9},{10,8},{12,1... | collective-permute-start | bytes 1769480 | tf_op jit(solution)/shard_map/ppermute | solution.py:49
  73.3 15.3 %collective-permute-start.16 = (bf16[768,384]{1,0:T(8,128)(2,1)S(1)}, bf16[768,384]{1,0:T(8,128)(2,1)S(1)}, u32[]{:S(2)}, u32[]{:S(2)}) collective-permute-start(bf16[768,384]{1,0:T(8,128)(2,1)S(1)} %get-tuple-element.24.refs_0_.refs_4_), channel_id=1, source_target_pairs={{0,16},{8,24},{16,0},{24,8},{1,17},{9,25},{17,1},{25,9},{2,18},{10... | collective-permute-start | bytes 1769480 | tf_op jit(solution)/shard_map/ppermute | solution.py:52
  74.8 13.8 %collective-permute-start.22 = (bf16[768,384]{1,0:T(8,128)(2,1)S(1)}, bf16[768,384]{1,0:T(8,128)(2,1)S(1)}, u32[]{:S(2)}, u32[]{:S(2)}) collective-permute-start(bf16[768,384]{1,0:T(8,128)(2,1)S(1)} %collective-permute-done.15.refs_1_), channel_id=1, source_target_pairs={{0,2},{2,4},{4,6},{6,7},{7,5},{5,3},{3,1},{1,0},{8,9},{10,8},{12,1... | collective-permute-start | bytes 1769480 | tf_op jit(solution)/shard_map/ppermute | solution.py:49
  81.4 12.6 %collective-permute-start.24 = (bf16[768,384]{1,0:T(8,128)(2,1)S(1)}, bf16[768,384]{1,0:T(8,128)(2,1)S(1)}, u32[]{:S(2)}, u32[]{:S(2)}) collective-permute-start(bf16[768,384]{1,0:T(8,128)(2,1)S(1)} %collective-permute-done.21.refs_5_), channel_id=1, source_target_pairs={{0,2},{2,4},{4,6},{6,7},{7,5},{5,3},{3,1},{1,0},{8,9},{10,8},{12,1... | collective-permute-start | bytes 1769480 | tf_op jit(solution)/shard_map/ppermute | solution.py:49
  88.6 7.2 %collective-permute-start.17 = (bf16[768,384]{1,0:T(8,128)(2,1)S(1)}, bf16[768,384]{1,0:T(8,128)(2,1)S(1)}, u32[]{:S(2)}, u32[]{:S(2)}) collective-permute-start(bf16[768,384]{1,0:T(8,128)(2,1)S(1)} %collective-permute-done.16.refs_2_), channel_id=1, source_target_pairs={{0,8},{8,0},{16,24},{24,16},{1,9},{9,1},{17,25},{25,17},{2,10},{10... | collective-permute-start | bytes 1769480 | tf_op jit(solution)/shard_map/ppermute | solution.py:52
  88.6 12.0 %collective-permute-start.25 = (bf16[768,384]{1,0:T(8,128)(2,1)S(1)}, bf16[768,384]{1,0:T(8,128)(2,1)S(1)}, u32[]{:S(2)}, u32[]{:S(2)}) collective-permute-start(bf16[768,384]{1,0:T(8,128)(2,1)S(1)} %collective-permute-done.22), channel_id=1, source_target_pairs={{0,2},{2,4},{4,6},{6,7},{7,5},{5,3},{3,1},{1,0},{8,9},{10,8},{12,1... | collective-permute-start | bytes 1769480 | tf_op jit(solution)/shard_map/ppermute | solution.py:49
  94.0 12.6 %collective-permute-start.27 = (bf16[768,384]{1,0:T(8,128)(2,1)S(1)}, bf16[768,384]{1,0:T(8,128)(2,1)S(1)}, u32[]{:S(2)}, u32[]{:S(2)}) collective-permute-start(bf16[768,384]{1,0:T(8,128)(2,1)S(1)} %collective-permute-done.24.refs_7_), channel_id=1, source_target_pairs={{0,2},{2,4},{4,6},{6,7},{7,5},{5,3},{3,1},{1,0},{8,9},{10,8},{12,1... | collective-permute-start | bytes 1769480 | tf_op jit(solution)/shard_map/ppermute | solution.py:49
  99.0 24.4 %copy-start.1 = (bf16[768,384]{1,0:T(8,128)(2,1)S(1)}, bf16[768,384]{1,0:T(8,128)(2,1)}, u32[]{:S(2)}) copy-start(bf16[768,384]{1,0:T(8,128)(2,1)} %deriv_ref.1) | copy-start | bytes 1769476
  99.0 24.4 %copy-start.3 = (s32[24]{0:T(128)S(1)}, s32[24]{0:T(128)}, u32[]{:S(2)}) copy-start(s32[24]{0:T(128)} %band_ref.9) | copy-start | bytes 292
  99.0 24.4 %copy-start.4 = (s32[24]{0:T(128)S(1)}, s32[24]{0:T(128)}, u32[]{:S(2)}) copy-start(s32[24]{0:T(128)} %frag_ref.1) | copy-start | bytes 292
  99.0 14.5 %collective-permute-start.19 = (bf16[768,384]{1,0:T(8,128)(2,1)S(1)}, bf16[768,384]{1,0:T(8,128)(2,1)S(1)}, u32[]{:S(2)}, u32[]{:S(2)}) collective-permute-start(bf16[768,384]{1,0:T(8,128)(2,1)S(1)} %shard_map.72.refs_0_), channel_id=1, source_target_pairs={{0,16},{8,24},{16,0},{24,8},{1,17},{9,25},{17,1},{25,9},{2,18},{10... | collective-permute-start | bytes 1769480 | tf_op jit(solution)/shard_map/ppermute | solution.py:52
  100.6 13.0 %collective-permute-start.18 = (bf16[768,384]{1,0:T(8,128)(2,1)S(1)}, bf16[768,384]{1,0:T(8,128)(2,1)S(1)}, u32[]{:S(2)}, u32[]{:S(2)}) collective-permute-start(bf16[768,384]{1,0:T(8,128)(2,1)S(1)} %shard_map.72.refs_0_), channel_id=1, source_target_pairs={{0,8},{8,0},{16,24},{24,16},{1,9},{9,1},{17,25},{25,17},{2,10},{10... | collective-permute-start | bytes 1769480 | tf_op jit(solution)/shard_map/ppermute | solution.py:52
  100.6 13.3 %collective-permute-start.28 = (bf16[768,384]{1,0:T(8,128)(2,1)S(1)}, bf16[768,384]{1,0:T(8,128)(2,1)S(1)}, u32[]{:S(2)}, u32[]{:S(2)}) collective-permute-start(bf16[768,384]{1,0:T(8,128)(2,1)S(1)} %collective-permute-done.25), channel_id=1, source_target_pairs={{0,2},{2,4},{4,6},{6,7},{7,5},{5,3},{3,1},{1,0},{8,9},{10,8},{12,1... | collective-permute-start | bytes 1769480 | tf_op jit(solution)/shard_map/ppermute | solution.py:49
  102.2 13.2 %collective-permute-start.23 = (bf16[768,384]{1,0:T(8,128)(2,1)S(1)}, bf16[768,384]{1,0:T(8,128)(2,1)S(1)}, u32[]{:S(2)}, u32[]{:S(2)}) collective-permute-start(bf16[768,384]{1,0:T(8,128)(2,1)S(1)} %collective-permute-done.22), channel_id=1, source_target_pairs={{0,8},{8,0},{16,24},{24,16},{1,9},{9,1},{17,25},{25,17},{2,10},{10... | collective-permute-start | bytes 1769480 | tf_op jit(solution)/shard_map/ppermute | solution.py:52
  106.7 8.9 %collective-permute-start.26 = (bf16[768,384]{1,0:T(8,128)(2,1)S(1)}, bf16[768,384]{1,0:T(8,128)(2,1)S(1)}, u32[]{:S(2)}, u32[]{:S(2)}) collective-permute-start(bf16[768,384]{1,0:T(8,128)(2,1)S(1)} %collective-permute-done.25), channel_id=1, source_target_pairs={{0,8},{8,0},{16,24},{24,16},{1,9},{9,1},{17,25},{25,17},{2,10},{10... | collective-permute-start | bytes 1769480 | tf_op jit(solution)/shard_map/ppermute | solution.py:52
  113.5 2.0 %collective-permute-start.20 = (bf16[768,384]{1,0:T(8,128)(2,1)S(1)}, bf16[768,384]{1,0:T(8,128)(2,1)S(1)}, u32[]{:S(2)}, u32[]{:S(2)}) collective-permute-start(bf16[768,384]{1,0:T(8,128)(2,1)S(1)} %collective-permute-done.19.refs_2_), channel_id=1, source_target_pairs={{0,8},{8,0},{16,24},{24,16},{1,9},{9,1},{17,25},{25,17},{2,10},{10... | collective-permute-start | bytes 1769480 | tf_op jit(solution)/shard_map/ppermute | solution.py:52
  113.5 9.9 %collective-permute-start.30 = (bf16[768,384]{1,0:T(8,128)(2,1)S(1)}, bf16[768,384]{1,0:T(8,128)(2,1)S(1)}, u32[]{:S(2)}, u32[]{:S(2)}) collective-permute-start(bf16[768,384]{1,0:T(8,128)(2,1)S(1)} %collective-permute-done.27.refs_9_), channel_id=1, source_target_pairs={{0,2},{2,4},{4,6},{6,7},{7,5},{5,3},{3,1},{1,0},{8,9},{10,8},{12,1... | collective-permute-start | bytes 1769480 | tf_op jit(solution)/shard_map/ppermute | solution.py:49
  113.9 9.6 %collective-permute-start.29 = (bf16[768,384]{1,0:T(8,128)(2,1)S(1)}, bf16[768,384]{1,0:T(8,128)(2,1)S(1)}, u32[]{:S(2)}, u32[]{:S(2)}) collective-permute-start(bf16[768,384]{1,0:T(8,128)(2,1)S(1)} %collective-permute-done.28), channel_id=1, source_target_pairs={{0,8},{8,0},{16,24},{24,16},{1,9},{9,1},{17,25},{25,17},{2,10},{10... | collective-permute-start | bytes 1769480 | tf_op jit(solution)/shard_map/ppermute | solution.py:52

commit v4 on v3

--- a/solution.py
+++ b/solution.py
@@ -190,9 +190,9 @@
     density_ref[...] = (0.5 * (identity - sign.astype(jnp.float32))).astype(jnp.bfloat16)
 
 
-def weighted_kernel(plan, others, band_ref, slab_ref, *refs):
+def weighted_kernel(plan, others, band_ref, slab_ref, before_ref, *refs):
     *pieces, out_ref = refs
-    total = slab_terms(plan, slab_ref, list(zip(others, pieces)))
+    total = before_ref[...] + slab_terms(plan, slab_ref, list(zip(others, pieces)))
     out_ref[...] = masked(plan, band_ref, total).astype(jnp.bfloat16)
 
 
@@ -267,7 +267,9 @@
     partner = plan.across(density, 1)
     shards, far = gather(density, partner, True)
     column = exchange_end([density, partner], exchange_start(density))
-    (weighted,) = call(bind(weighted_kernel, plan, others), [block], [band], [slab] + column)
+    (total,) = call(bind(some_kernel, plan, [0, 1]), [total_type], [], [slab] + column[:2])
+    (total,) = call(bind(more_kernel, plan, even), [total_type], [], [slab, total] + column[2::2])
+    (weighted,) = call(bind(weighted_kernel, plan, odd), [block], [band], [slab, total] + column[3::2])
     column = exchange_end([weighted, plan.across(weighted, 1)], exchange_start(weighted))
     places = near_places(plan, 0, plan.far)
     late = [shards[-1], far]

time: 138 us -> 137 us (level)
  waiting for transfers between devices: 70.5 us -> 69 us
    ppermute x17, waiting for transfers between devices: 28.3 us -> 26.5 us  [across(): lax.ppermute(value, 'row', [(i, i ^ other) for i in range(self.rows)])]
    pallas_call x8 -> x10, Pallas kernels: 18.4 us -> 18.8 us  [call(): pl.pallas_call(kernel, out_shape=outs, in_specs=[smem] * len(scalars) + [...]
  transfers between devices with their start and end apart: 31 -> 31, of which waited for: 17 -> 19; matrix products, arithmetic and copies ran while one was open for 0% -> 0% of each run, Pallas kernels for 9% -> 9%
where the time goes in v4:
time: 137 us; the launch traced here: 136 us
  waiting for transfers between devices  69 us (50%)
  starting transfers between devices  33.7 us (25%)
  Pallas kernels  18.8 us (14%)
  blocking collectives  11.9 us (9%)
  local copies, waits for them, and re-layouts  1.75 us (1%)
    ppermute x14, waiting for transfers between devices, ring(): return lax.ppermute(value, AXES, pairs)  42.5 us
    ppermute x17, waiting for transfers between devices, across(): lax.ppermute(value, 'row', [(i, i ^ other) for i in range(self.rows)])  26.5 us
    ppermute x14, starting transfers between devices, ring(): return lax.ppermute(value, AXES, pairs)  24.5 us
    pallas_call x10, Pallas kernels, call(): pl.pallas_call(kernel, out_shape=outs, in_specs=[smem] * len(scalars) + [...  18.8 us
    all_to_all x1, blocking collectives, body(): pulay_terms = jnp.sum(lax.all_to_all(sums, AXES, 0, 0), axis=0)  11.9 us
    ppermute x17, starting transfers between devices, across(): lax.ppermute(value, 'row', [(i, i ^ other) for i in range(self.rows)])  9.25 us
  transfers between devices with their start and end apart: 31, of which 19 were waited for; matrix products, arithmetic and copies ran while one was open for 0% of the time, Pallas kernels for 9%

profile of v4, /device:TPU:0, one launch (start us, length us, event | category | flops | bytes accessed | tf_op | source)
XLA Modules:
  0.0 136.5 jit_solution(9719276850150473061)
XLA Ops:
  0.6 0.5 collective-permute-start
  1.1 2.6 %collective-permute-start.3 = (bf16[768,384]{1,0:T(8,128)(2,1)}, bf16[768,384]{1,0:T(8,128)(2,1)S(1)}, u32[]{:S(2)}, u32[]{:S(2)}) collective-permute-start(bf16[768,384]{1,0:T(8,128)(2,1)} %refs_4_.1), channel_id=1, source_target_pairs={{0,2},{2,4},{4,6},{6,7},{7,5},{5,3},{3,1},{1,0},{8,9},{10,8},{12,1... | collective-permute-start | bytes 1769480 | tf_op jit(solution)/shard_map/ppermute | solution.py:49
  3.8 0.0 collective-permute-done.refs_1_
  3.8 2.1 %collective-permute-start.4 = (bf16[768,384]{1,0:T(8,128)(2,1)S(1)}, bf16[768,384]{1,0:T(8,128)(2,1)S(1)}, u32[]{:S(2)}, u32[]{:S(2)}) collective-permute-start(bf16[768,384]{1,0:T(8,128)(2,1)S(1)} %collective-permute-done.refs_1_), channel_id=1, source_target_pairs={{0,2},{2,4},{4,6},{6,7},{7,5},{5,3},{3,1},{1,0},{8,9},{10,8},{12,1... | collective-permute-start | bytes 1769480 | tf_op jit(solution)/shard_map/ppermute | solution.py:49
  5.9 5.9 %collective-permute-done.3.refs_5_ = bf16[768,384]{1,0:T(8,128)(2,1)S(1)} collective-permute-done((bf16[768,384]{1,0:T(8,128)(2,1)}, bf16[768,384]{1,0:T(8,128)(2,1)S(1)}, u32[]{:S(2)}, u32[]{:S(2)}) %collective-permute-start.3) | collective-permute-done | bytes 589856 | tf_op jit(solution)/shard_map/ppermute | solution.py:49
  11.8 2.1 %collective-permute-start.6 = (bf16[768,384]{1,0:T(8,128)(2,1)S(1)}, bf16[768,384]{1,0:T(8,128)(2,1)S(1)}, u32[]{:S(2)}, u32[]{:S(2)}) collective-permute-start(bf16[768,384]{1,0:T(8,128)(2,1)S(1)} %collective-permute-done.3.refs_5_), channel_id=1, source_target_pairs={{0,2},{2,4},{4,6},{6,7},{7,5},{5,3},{3,1},{1,0},{8,9},{10,8},{12,1... | collective-permute-start | bytes 1769480 | tf_op jit(solution)/shard_map/ppermute | solution.py:49
  13.9 1.5 %collective-permute-start.1 = (bf16[768,384]{1,0:T(8,128)(2,1)}, bf16[768,384]{1,0:T(8,128)(2,1)S(1)}, u32[]{:S(2)}, u32[]{:S(2)}) collective-permute-start(bf16[768,384]{1,0:T(8,128)(2,1)} %refs_4_.1), channel_id=1, source_target_pairs={{0,16},{8,24},{16,0},{24,8},{1,17},{9,25},{17,1},{25,9},{2,18},{10... | collective-permute-start | bytes 1769480 | tf_op jit(solution)/shard_map/ppermute | solution.py:52
  15.4 2.8 %collective-permute-done.4 = bf16[768,384]{1,0:T(8,128)(2,1)S(1)} collective-permute-done((bf16[768,384]{1,0:T(8,128)(2,1)S(1)}, bf16[768,384]{1,0:T(8,128)(2,1)S(1)}, u32[]{:S(2)}, u32[]{:S(2)}) %collective-permute-start.4) | collective-permute-done | bytes 589856 | tf_op jit(solution)/shard_map/ppermute | solution.py:49
  18.1 2.1 %collective-permute-start.7 = (bf16[768,384]{1,0:T(8,128)(2,1)S(1)}, bf16[768,384]{1,0:T(8,128)(2,1)S(1)}, u32[]{:S(2)}, u32[]{:S(2)}) collective-permute-start(bf16[768,384]{1,0:T(8,128)(2,1)S(1)} %collective-permute-done.4), channel_id=1, source_target_pairs={{0,2},{2,4},{4,6},{6,7},{7,5},{5,3},{3,1},{1,0},{8,9},{10,8},{12,1... | collective-permute-start | bytes 1769480 | tf_op jit(solution)/shard_map/ppermute | solution.py:49
  20.2 4.2 %collective-permute-done.6.refs_7_ = bf16[768,384]{1,0:T(8,128)(2,1)S(1)} collective-permute-done((bf16[768,384]{1,0:T(8,128)(2,1)S(1)}, bf16[768,384]{1,0:T(8,128)(2,1)S(1)}, u32[]{:S(2)}, u32[]{:S(2)}) %collective-permute-start.6) | collective-permute-done | bytes 589856 | tf_op jit(solution)/shard_map/ppermute | solution.py:49
  24.4 2.1 %collective-permute-start.9 = (bf16[768,384]{1,0:T(8,128)(2,1)S(1)}, bf16[768,384]{1,0:T(8,128)(2,1)S(1)}, u32[]{:S(2)}, u32[]{:S(2)}) collective-permute-start(bf16[768,384]{1,0:T(8,128)(2,1)S(1)} %collective-permute-done.6.refs_7_), channel_id=1, source_target_pairs={{0,2},{2,4},{4,6},{6,7},{7,5},{5,3},{3,1},{1,0},{8,9},{10,8},{12,1... | collective-permute-start | bytes 1769480 | tf_op jit(solution)/shard_map/ppermute | solution.py:49
  26.5 2.1 %collective-permute-done.1.refs_2_ = bf16[768,384]{1,0:T(8,128)(2,1)S(1)} collective-permute-done((bf16[768,384]{1,0:T(8,128)(2,1)}, bf16[768,384]{1,0:T(8,128)(2,1)S(1)}, u32[]{:S(2)}, u32[]{:S(2)}) %collective-permute-start.1) | collective-permute-done | bytes 589856 | tf_op jit(solution)/shard_map/ppermute | solution.py:52
  28.6 0.5 collective-permute-start.5
  29.1 1.7 %collective-permute-done.7 = bf16[768,384]{1,0:T(8,128)(2,1)S(1)} collective-permute-done((bf16[768,384]{1,0:T(8,128)(2,1)S(1)}, bf16[768,384]{1,0:T(8,128)(2,1)S(1)}, u32[]{:S(2)}, u32[]{:S(2)}) %collective-permute-start.7) | collective-permute-done | bytes 589856 | tf_op jit(solution)/shard_map/ppermute | solution.py:49
  30.8 1.3 collective-permute-start.10
  32.0 0.9 collective-permute-start.8
  32.9 4.2 %collective-permute-done.9.refs_9_ = bf16[768,384]{1,0:T(8,128)(2,1)S(1)} collective-permute-done((bf16[768,384]{1,0:T(8,128)(2,1)S(1)}, bf16[768,384]{1,0:T(8,128)(2,1)S(1)}, u32[]{:S(2)}, u32[]{:S(2)}) %collective-permute-start.9) | collective-permute-done | bytes 589856 | tf_op jit(solution)/shard_map/ppermute | solution.py:49
  37.1 2.1 %collective-permute-start.11 = (bf16[768,384]{1,0:T(8,128)(2,1)S(1)}, bf16[768,384]{1,0:T(8,128)(2,1)S(1)}, u32[]{:S(2)}, u32[]{:S(2)}) collective-permute-start(bf16[768,384]{1,0:T(8,128)(2,1)S(1)} %collective-permute-done.9.refs_9_), channel_id=1, source_target_pairs={{0,2},{2,4},{4,6},{6,7},{7,5},{5,3},{3,1},{1,0},{8,9},{10,8},{12,1... | collective-permute-start | bytes 1769480 | tf_op jit(solution)/shard_map/ppermute | solution.py:49
  39.2 4.0 %collective-permute-done.10.refs_10_ = bf16[768,384]{1,0:T(8,128)(2,1)S(1)} collective-permute-done((bf16[768,384]{1,0:T(8,128)(2,1)S(1)}, bf16[768,384]{1,0:T(8,128)(2,1)S(1)}, u32[]{:S(2)}, u32[]{:S(2)}) %collective-permute-start.10) | collective-permute-done | bytes 589856 | tf_op jit(solution)/shard_map/ppermute | solution.py:49
  43.2 0.0 collective-permute-done.8.refs_8_
  43.2 1.1 copy-done
  44.3 0.7 copy-done.2
  44.9 4.7 %shard_map.67 = (f32[768,384]{1,0:T(8,128)S(1)}, bf16[3072,384]{1,0:T(8,128)(2,1)S(1)}, bf16[768,3072]{1,0:T(8,128)(2,1)S(1)}) custom-call(s32[24]{0:T(128)S(1)} %copy-done.2, bf16[768,384]{1,0:T(8,128)(2,1)S(1)} %copy-done, bf16[768,384]{1,0:T(8,128)(2,1)S(1)} %collective-permute-done.refs_1_, bf16[768,384]{1,0:T(8,128)(2,1)S(1)} %collective-permute-done.1.refs_2_, ...), custom_call_target="tpu_custom_call" | custom-call | tf_op jit(solution)/shard_map/pallas_call | solution.py:91
  49.6 0.1 collective-permute-done.11.far_ref
  49.7 1.1 shard_map.68
  50.9 0.1 collective-permute-start.13
  50.9 2.0 %collective-permute-start.12 = (bf16[768,384]{1,0:T(8,128)(2,1)S(1)}, bf16[768,384]{1,0:T(8,128)(2,1)S(1)}, u32[]{:S(2)}, u32[]{:S(2)}) collective-permute-start(bf16[768,384]{1,0:T(8,128)(2,1)S(1)} %get-tuple-element.20.refs_0_), channel_id=1, source_target_pairs={{0,16},{8,24},{16,0},{24,8},{1,17},{9,25},{17,1},{25,9},{2,18},{10... | collective-permute-start | bytes 1769480 | tf_op jit(solution)/shard_map/ppermute | solution.py:52
  53.0 0.0 collective-permute-done.13.refs_1_
  53.0 1.4 %shard_map.69.before_ref = f32[768,384]{1,0:T(8,128)S(1)} custom-call(bf16[768,3072]{1,0:T(8,128)(2,1)S(1)} %get-tuple-element.19.slab_ref, bf16[768,384]{1,0:T(8,128)(2,1)S(1)} %get-tuple-element.20.refs_0_, bf16[768,384]{1,0:T(8,128)(2,1)S(1)} %collective-permute-done.13.refs_1_), custom_call_target="tpu_custom_call" | custom-call | tf_op jit(solution)/shard_map/pallas_call | solution.py:91
  54.4 12.5 %collective-permute-done.12.refs_0_ = bf16[768,384]{1,0:T(8,128)(2,1)S(1)} collective-permute-done((bf16[768,384]{1,0:T(8,128)(2,1)S(1)}, bf16[768,384]{1,0:T(8,128)(2,1)S(1)}, u32[]{:S(2)}, u32[]{:S(2)}) %collective-permute-start.12) | collective-permute-done | bytes 589856 | tf_op jit(solution)/shard_map/ppermute | solution.py:52
  66.9 0.0 collective-permute-start.14
  66.9 0.8 shard_map.70.total_ref
  67.7 1.2 collective-permute-done.14.refs_0_
  68.9 2.5 %shard_map.71 = (bf16[768,384]{1,0:T(8,128)(2,1)}, bf16[768,384]{1,0:T(8,128)(2,1)S(1)}) custom-call(s32[24]{0:T(128)S(1)} %copy-done.2, bf16[768,3072]{1,0:T(8,128)(2,1)S(1)} %get-tuple-element.19.slab_ref, f32[768,384]{1,0:T(8,128)S(1)} %shard_map.70.total_ref, bf16[768,384]{1,0:T(8,128)(2,1)S(1)} %collective-permute-done.14.refs_0_), custom_call_target="tpu_custom_call" | custom-call | tf_op jit(solution)/shard_map/pallas_call | solution.py:91
  71.4 0.1 collective-permute-start.15
  71.5 1.8 %collective-permute-start.21 = (bf16[768,384]{1,0:T(8,128)(2,1)S(1)}, bf16[768,384]{1,0:T(8,128)(2,1)S(1)}, u32[]{:S(2)}, u32[]{:S(2)}) collective-permute-start(bf16[768,384]{1,0:T(8,128)(2,1)S(1)} %get-tuple-element.24.refs_0_.refs_4_), channel_id=1, source_target_pairs={{0,2},{2,4},{4,6},{6,7},{7,5},{5,3},{3,1},{1,0},{8,9},{10,8},{12,1... | collective-permute-start | bytes 1769480 | tf_op jit(solution)/shard_map/ppermute | solution.py:49
  73.3 1.5 %collective-permute-start.16 = (bf16[768,384]{1,0:T(8,128)(2,1)S(1)}, bf16[768,384]{1,0:T(8,128)(2,1)S(1)}, u32[]{:S(2)}, u32[]{:S(2)}) collective-permute-start(bf16[768,384]{1,0:T(8,128)(2,1)S(1)} %get-tuple-element.24.refs_0_.refs_4_), channel_id=1, source_target_pairs={{0,16},{8,24},{16,0},{24,8},{1,17},{9,25},{17,1},{25,9},{2,18},{10... | collective-permute-start | bytes 1769480 | tf_op jit(solution)/shard_map/ppermute | solution.py:52
  74.8 1.6 %collective-permute-start.22 = (bf16[768,384]{1,0:T(8,128)(2,1)S(1)}, bf16[768,384]{1,0:T(8,128)(2,1)S(1)}, u32[]{:S(2)}, u32[]{:S(2)}) collective-permute-start(bf16[768,384]{1,0:T(8,128)(2,1)S(1)} %collective-permute-done.15.refs_1_), channel_id=1, source_target_pairs={{0,2},{2,4},{4,6},{6,7},{7,5},{5,3},{3,1},{1,0},{8,9},{10,8},{12,1... | collective-permute-start | bytes 1769480 | tf_op jit(solution)/shard_map/ppermute | solution.py:49
  76.4 5.0 %collective-permute-done.21.refs_5_ = bf16[768,384]{1,0:T(8,128)(2,1)S(1)} collective-permute-done((bf16[768,384]{1,0:T(8,128)(2,1)S(1)}, bf16[768,384]{1,0:T(8,128)(2,1)S(1)}, u32[]{:S(2)}, u32[]{:S(2)}) %collective-permute-start.21) | collective-permute-done | bytes 589856 | tf_op jit(solution)/shard_map/ppermute | solution.py:49
  81.4 1.8 %collective-permute-start.24 = (bf16[768,384]{1,0:T(8,128)(2,1)S(1)}, bf16[768,384]{1,0:T(8,128)(2,1)S(1)}, u32[]{:S(2)}, u32[]{:S(2)}) collective-permute-start(bf16[768,384]{1,0:T(8,128)(2,1)S(1)} %collective-permute-done.21.refs_5_), channel_id=1, source_target_pairs={{0,2},{2,4},{4,6},{6,7},{7,5},{5,3},{3,1},{1,0},{8,9},{10,8},{12,1... | collective-permute-start | bytes 1769480 | tf_op jit(solution)/shard_map/ppermute | solution.py:49
  83.2 5.4 %collective-permute-done.16.refs_0_ = bf16[768,384]{1,0:T(8,128)(2,1)S(1)} collective-permute-done((bf16[768,384]{1,0:T(8,128)(2,1)S(1)}, bf16[768,384]{1,0:T(8,128)(2,1)S(1)}, u32[]{:S(2)}, u32[]{:S(2)}) %collective-permute-start.16) | collective-permute-done | bytes 589856 | tf_op jit(solution)/shard_map/ppermute | solution.py:52
  88.6 0.9 collective-permute-start.25
  89.5 1.4 %shard_map.72.before_ref = f32[768,384]{1,0:T(8,128)S(1)} custom-call(bf16[768,3072]{1,0:T(8,128)(2,1)S(1)} %get-tuple-element.19.slab_ref, bf16[768,384]{1,0:T(8,128)(2,1)S(1)} %get-tuple-element.24.refs_0_.refs_4_, bf16[768,384]{1,0:T(8,128)(2,1)S(1)} %collective-permute-done.15.refs_1_), custom_call_target="tpu_custom_call" | custom-call | tf_op jit(solution)/shard_map/pallas_call | solution.py:91
  90.9 0.8 shard_map.73.before_ref
  91.7 2.3 %collective-permute-done.24.refs_7_ = bf16[768,384]{1,0:T(8,128)(2,1)S(1)} collective-permute-done((bf16[768,384]{1,0:T(8,128)(2,1)S(1)}, bf16[768,384]{1,0:T(8,128)(2,1)S(1)}, u32[]{:S(2)}, u32[]{:S(2)}) %collective-permute-start.24) | collective-permute-done | bytes 589856 | tf_op jit(solution)/shard_map/ppermute | solution.py:49
  94.0 1.8 %collective-permute-start.27 = (bf16[768,384]{1,0:T(8,128)(2,1)S(1)}, bf16[768,384]{1,0:T(8,128)(2,1)S(1)}, u32[]{:S(2)}, u32[]{:S(2)}) collective-permute-start(bf16[768,384]{1,0:T(8,128)(2,1)S(1)} %collective-permute-done.24.refs_7_), channel_id=1, source_target_pairs={{0,2},{2,4},{4,6},{6,7},{7,5},{5,3},{3,1},{1,0},{8,9},{10,8},{12,1... | collective-permute-start | bytes 1769480 | tf_op jit(solution)/shard_map/ppermute | solution.py:49
  95.9 1.3 shard_map.74.refs_0_
  97.2 0.0 copy-start.1
  97.2 0.0 copy-start.3
  97.2 0.0 copy-start.4
  97.2 1.5 %collective-permute-start.19 = (bf16[768,384]{1,0:T(8,128)(2,1)S(1)}, bf16[768,384]{1,0:T(8,128)(2,1)S(1)}, u32[]{:S(2)}, u32[]{:S(2)}) collective-permute-start(bf16[768,384]{1,0:T(8,128)(2,1)S(1)} %shard_map.74.refs_0_), channel_id=1, source_target_pairs={{0,16},{8,24},{16,0},{24,8},{1,17},{9,25},{17,1},{25,9},{2,18},{10... | collective-permute-start | bytes 1769480 | tf_op jit(solution)/shard_map/ppermute | solution.py:52
  98.8 1.6 %collective-permute-done.25 = bf16[768,384]{1,0:T(8,128)(2,1)S(1)} collective-permute-done((bf16[768,384]{1,0:T(8,128)(2,1)S(1)}, bf16[768,384]{1,0:T(8,128)(2,1)S(1)}, u32[]{:S(2)}, u32[]{:S(2)}) %collective-permute-start.25) | collective-permute-done | bytes 589856 | tf_op jit(solution)/shard_map/ppermute | solution.py:49
  100.3 1.8 %collective-permute-start.28 = (bf16[768,384]{1,0:T(8,128)(2,1)S(1)}, bf16[768,384]{1,0:T(8,128)(2,1)S(1)}, u32[]{:S(2)}, u32[]{:S(2)}) collective-permute-start(bf16[768,384]{1,0:T(8,128)(2,1)S(1)} %collective-permute-done.25), channel_id=1, source_target_pairs={{0,2},{2,4},{4,6},{6,7},{7,5},{5,3},{3,1},{1,0},{8,9},{10,8},{12,1... | collective-permute-start | bytes 1769480 | tf_op jit(solution)/shard_map/ppermute | solution.py:49
  102.2 4.5 %collective-permute-done.27.refs_9_ = bf16[768,384]{1,0:T(8,128)(2,1)S(1)} collective-permute-done((bf16[768,384]{1,0:T(8,128)(2,1)S(1)}, bf16[768,384]{1,0:T(8,128)(2,1)S(1)}, u32[]{:S(2)}, u32[]{:S(2)}) %collective-permute-start.27) | collective-permute-done | bytes 589856 | tf_op jit(solution)/shard_map/ppermute | solution.py:49
  106.7 5.1 %collective-permute-done.19.refs_2_ = bf16[768,384]{1,0:T(8,128)(2,1)S(1)} collective-permute-done((bf16[768,384]{1,0:T(8,128)(2,1)S(1)}, bf16[768,384]{1,0:T(8,128)(2,1)S(1)}, u32[]{:S(2)}, u32[]{:S(2)}) %collective-permute-start.19) | collective-permute-done | bytes 589856 | tf_op jit(solution)/shard_map/ppermute | solution.py:52
  111.7 0.3 collective-permute-start.30
  112.1 0.9 collective-permute-done.28
  113.0 0.5 collective-permute-start.29
  113.5 0.2 collective-permute-done.20.refs_3_
  113.7 2.5 %shard_map.75 = (f32[768,384]{1,0:T(8,128)S(1)}, bf16[3072,384]{1,0:T(8,128)(2,1)S(1)}) custom-call(bf16[768,384]{1,0:T(8,128)(2,1)S(1)} %shard_map.74.refs_0_, bf16[768,384]{1,0:T(8,128)(2,1)S(1)} %collective-permute-done.18.refs_1_, bf16[768,384]{1,0:T(8,128)(2,1)S(1)} %collective-permute-done.19.refs_2_, ...), custom_call_target="tpu_custom_call" | custom-call | tf_op jit(solution)/shard_map/pallas_call | solution.py:91
  116.3 5.4 %collective-permute-done.30.refs_1_ = bf16[768,384]{1,0:T(8,128)(2,1)S(1)} collective-permute-done((bf16[768,384]{1,0:T(8,128)(2,1)S(1)}, bf16[768,384]{1,0:T(8,128)(2,1)S(1)}, u32[]{:S(2)}, u32[]{:S(2)}) %collective-permute-start.30) | collective-permute-done | bytes 589856 | tf_op jit(solution)/shard_map/ppermute | solution.py:49
  121.6 2.4 %shard_map.76 = (bf16[768,384]{1,0:T(8,128)(2,1)}, f32[16,128]{1,0:T(8,128)S(1)}) custom-call(s32[24]{0:T(128)S(1)} %copy-done.3, s32[24]{0:T(128)S(1)} %copy-done.4, f32[768,384]{1,0:T(8,128)S(1)} %get-tuple-element.25.total_ref, bf16[3072,384]{1,0:T(8,128)(2,1)S(1)} %get-tuple-element.26.right_ref, bf16[768,384]{1,0:T(8,128)(2,1)S(1)} %copy-done.1, ...), custom_call_target="tpu_custom_call" | custom-call | tf_op jit(solution)/shard_map/pallas_call | solution.py:91
  124.0 11.9 %all_to_all.5 = f32[32,2,128]{2,1,0:T(2,128)S(1)} all-to-all(f32[32,2,128]{2,1,0:T(2,128)S(1)} %bitcast.3), channel_id=1, replica_groups=mesh['row'=4,'col'=8] {'row','col'}, dimensions={0} | all-to-all | bytes 65536 | tf_op jit(solution)/shard_map/all_to_all | solution.py:286
  135.9 0.6 reduce_sum.9
  (21 shorter events, 0.1 us)
Async XLA Ops:
  0.6 3.2 %collective-permute-start = (bf16[768,384]{1,0:T(8,128)(2,1)}, bf16[768,384]{1,0:T(8,128)(2,1)S(1)}, u32[]{:S(2)}, u32[]{:S(2)}) collective-permute-start(bf16[768,384]{1,0:T(8,128)(2,1)} %refs_4_.1), channel_id=1, source_target_pairs={{0,8},{8,0},{16,24},{24,16},{1,9},{9,1},{17,25},{25,17},{2,10},{10... | collective-permute-start | bytes 1769480 | tf_op jit(solution)/shard_map/ppermute | solution.py:52
  1.1 10.7 %collective-permute-start.3 = (bf16[768,384]{1,0:T(8,128)(2,1)}, bf16[768,384]{1,0:T(8,128)(2,1)S(1)}, u32[]{:S(2)}, u32[]{:S(2)}) collective-permute-start(bf16[768,384]{1,0:T(8,128)(2,1)} %refs_4_.1), channel_id=1, source_target_pairs={{0,2},{2,4},{4,6},{6,7},{7,5},{5,3},{3,1},{1,0},{8,9},{10,8},{12,1... | collective-permute-start | bytes 1769480 | tf_op jit(solution)/shard_map/ppermute | solution.py:49
  3.8 14.3 %collective-permute-start.4 = (bf16[768,384]{1,0:T(8,128)(2,1)S(1)}, bf16[768,384]{1,0:T(8,128)(2,1)S(1)}, u32[]{:S(2)}, u32[]{:S(2)}) collective-permute-start(bf16[768,384]{1,0:T(8,128)(2,1)S(1)} %collective-permute-done.refs_1_), channel_id=1, source_target_pairs={{0,2},{2,4},{4,6},{6,7},{7,5},{5,3},{3,1},{1,0},{8,9},{10,8},{12,1... | collective-permute-start | bytes 1769480 | tf_op jit(solution)/shard_map/ppermute | solution.py:49
  11.8 12.6 %collective-permute-start.6 = (bf16[768,384]{1,0:T(8,128)(2,1)S(1)}, bf16[768,384]{1,0:T(8,128)(2,1)S(1)}, u32[]{:S(2)}, u32[]{:S(2)}) collective-permute-start(bf16[768,384]{1,0:T(8,128)(2,1)S(1)} %collective-permute-done.3.refs_5_), channel_id=1, source_target_pairs={{0,2},{2,4},{4,6},{6,7},{7,5},{5,3},{3,1},{1,0},{8,9},{10,8},{12,1... | collective-permute-start | bytes 1769480 | tf_op jit(solution)/shard_map/ppermute | solution.py:49
  13.9 14.7 %collective-permute-start.1 = (bf16[768,384]{1,0:T(8,128)(2,1)}, bf16[768,384]{1,0:T(8,128)(2,1)S(1)}, u32[]{:S(2)}, u32[]{:S(2)}) collective-permute-start(bf16[768,384]{1,0:T(8,128)(2,1)} %refs_4_.1), channel_id=1, source_target_pairs={{0,16},{8,24},{16,0},{24,8},{1,17},{9,25},{17,1},{25,9},{2,18},{10... | collective-permute-start | bytes 1769480 | tf_op jit(solution)/shard_map/ppermute | solution.py:52
  18.1 12.6 %collective-permute-start.7 = (bf16[768,384]{1,0:T(8,128)(2,1)S(1)}, bf16[768,384]{1,0:T(8,128)(2,1)S(1)}, u32[]{:S(2)}, u32[]{:S(2)}) collective-permute-start(bf16[768,384]{1,0:T(8,128)(2,1)S(1)} %collective-permute-done.4), channel_id=1, source_target_pairs={{0,2},{2,4},{4,6},{6,7},{7,5},{5,3},{3,1},{1,0},{8,9},{10,8},{12,1... | collective-permute-start | bytes 1769480 | tf_op jit(solution)/shard_map/ppermute | solution.py:49
  24.4 12.6 %collective-permute-start.9 = (bf16[768,384]{1,0:T(8,128)(2,1)S(1)}, bf16[768,384]{1,0:T(8,128)(2,1)S(1)}, u32[]{:S(2)}, u32[]{:S(2)}) collective-permute-start(bf16[768,384]{1,0:T(8,128)(2,1)S(1)} %collective-permute-done.6.refs_7_), channel_id=1, source_target_pairs={{0,2},{2,4},{4,6},{6,7},{7,5},{5,3},{3,1},{1,0},{8,9},{10,8},{12,1... | collective-permute-start | bytes 1769480 | tf_op jit(solution)/shard_map/ppermute | solution.py:49
  28.6 10.6 %collective-permute-start.2 = (bf16[768,384]{1,0:T(8,128)(2,1)S(1)}, bf16[768,384]{1,0:T(8,128)(2,1)S(1)}, u32[]{:S(2)}, u32[]{:S(2)}) collective-permute-start(bf16[768,384]{1,0:T(8,128)(2,1)S(1)} %collective-permute-done.1.refs_2_), channel_id=1, source_target_pairs={{0,8},{8,0},{16,24},{24,16},{1,9},{9,1},{17,25},{25,17},{2,10},{10... | collective-permute-start | bytes 1769480 | tf_op jit(solution)/shard_map/ppermute | solution.py:52
  28.6 10.6 %collective-permute-start.5 = (bf16[768,384]{1,0:T(8,128)(2,1)S(1)}, bf16[768,384]{1,0:T(8,128)(2,1)S(1)}, u32[]{:S(2)}, u32[]{:S(2)}) collective-permute-start(bf16[768,384]{1,0:T(8,128)(2,1)S(1)} %collective-permute-done.4), channel_id=1, source_target_pairs={{0,8},{8,0},{16,24},{24,16},{1,9},{9,1},{17,25},{25,17},{2,10},{10... | collective-permute-start | bytes 1769480 | tf_op jit(solution)/shard_map/ppermute | solution.py:52
  30.8 12.4 %collective-permute-start.10 = (bf16[768,384]{1,0:T(8,128)(2,1)S(1)}, bf16[768,384]{1,0:T(8,128)(2,1)S(1)}, u32[]{:S(2)}, u32[]{:S(2)}) collective-permute-start(bf16[768,384]{1,0:T(8,128)(2,1)S(1)} %collective-permute-done.7), channel_id=1, source_target_pairs={{0,10},{2,12},{4,14},{6,15},{7,13},{5,11},{3,9},{1,8},{8,1},{10,0}... | collective-permute-start | bytes 1769480 | tf_op jit(solution)/shard_map/ppermute | solution.py:49
  32.0 11.2 %collective-permute-start.8 = (bf16[768,384]{1,0:T(8,128)(2,1)S(1)}, bf16[768,384]{1,0:T(8,128)(2,1)S(1)}, u32[]{:S(2)}, u32[]{:S(2)}) collective-permute-start(bf16[768,384]{1,0:T(8,128)(2,1)S(1)} %collective-permute-done.7), channel_id=1, source_target_pairs={{0,8},{8,0},{16,24},{24,16},{1,9},{9,1},{17,25},{25,17},{2,10},{10... | collective-permute-start | bytes 1769480 | tf_op jit(solution)/shard_map/ppermute | solution.py:52
  37.1 12.6 %collective-permute-start.11 = (bf16[768,384]{1,0:T(8,128)(2,1)S(1)}, bf16[768,384]{1,0:T(8,128)(2,1)S(1)}, u32[]{:S(2)}, u32[]{:S(2)}) collective-permute-start(bf16[768,384]{1,0:T(8,128)(2,1)S(1)} %collective-permute-done.9.refs_9_), channel_id=1, source_target_pairs={{0,2},{2,4},{4,6},{6,7},{7,5},{5,3},{3,1},{1,0},{8,9},{10,8},{12,1... | collective-permute-start | bytes 1769480 | tf_op jit(solution)/shard_map/ppermute | solution.py:49
  43.2 1.1 copy-start
  44.3 0.7 copy-start.2
  50.9 2.1 %collective-permute-start.13 = (bf16[768,384]{1,0:T(8,128)(2,1)S(1)}, bf16[768,384]{1,0:T(8,128)(2,1)S(1)}, u32[]{:S(2)}, u32[]{:S(2)}) collective-permute-start(bf16[768,384]{1,0:T(8,128)(2,1)S(1)} %get-tuple-element.20.refs_0_), channel_id=1, source_target_pairs={{0,8},{8,0},{16,24},{24,16},{1,9},{9,1},{17,25},{25,17},{2,10},{10... | collective-permute-start | bytes 1769480 | tf_op jit(solution)/shard_map/ppermute | solution.py:52
  50.9 16.0 %collective-permute-start.12 = (bf16[768,384]{1,0:T(8,128)(2,1)S(1)}, bf16[768,384]{1,0:T(8,128)(2,1)S(1)}, u32[]{:S(2)}, u32[]{:S(2)}) collective-permute-start(bf16[768,384]{1,0:T(8,128)(2,1)S(1)} %get-tuple-element.20.refs_0_), channel_id=1, source_target_pairs={{0,16},{8,24},{16,0},{24,8},{1,17},{9,25},{17,1},{25,9},{2,18},{10... | collective-permute-start | bytes 1769480 | tf_op jit(solution)/shard_map/ppermute | solution.py:52
  66.9 2.0 %collective-permute-start.14 = (bf16[768,384]{1,0:T(8,128)(2,1)S(1)}, bf16[768,384]{1,0:T(8,128)(2,1)S(1)}, u32[]{:S(2)}, u32[]{:S(2)}) collective-permute-start(bf16[768,384]{1,0:T(8,128)(2,1)S(1)} %collective-permute-done.12.refs_0_), channel_id=1, source_target_pairs={{0,8},{8,0},{16,24},{24,16},{1,9},{9,1},{17,25},{25,17},{2,10},{10... | collective-permute-start | bytes 1769480 | tf_op jit(solution)/shard_map/ppermute | solution.py:52
  71.4 3.5 %collective-permute-start.15 = (bf16[768,384]{1,0:T(8,128)(2,1)S(1)}, bf16[768,384]{1,0:T(8,128)(2,1)S(1)}, u32[]{:S(2)}, u32[]{:S(2)}) collective-permute-start(bf16[768,384]{1,0:T(8,128)(2,1)S(1)} %get-tuple-element.24.refs_0_.refs_4_), channel_id=1, source_target_pairs={{0,8},{8,0},{16,24},{24,16},{1,9},{9,1},{17,25},{25,17},{2,10},{10... | collective-permute-start | bytes 1769480 | tf_op jit(solution)/shard_map/ppermute | solution.py:52
  71.5 9.9 %collective-permute-start.21 = (bf16[768,384]{1,0:T(8,128)(2,1)S(1)}, bf16[768,384]{1,0:T(8,128)(2,1)S(1)}, u32[]{:S(2)}, u32[]{:S(2)}) collective-permute-start(bf16[768,384]{1,0:T(8,128)(2,1)S(1)} %get-tuple-element.24.refs_0_.refs_4_), channel_id=1, source_target_pairs={{0,2},{2,4},{4,6},{6,7},{7,5},{5,3},{3,1},{1,0},{8,9},{10,8},{12,1... | collective-permute-start | bytes 1769480 | tf_op jit(solution)/shard_map/ppermute | solution.py:49
  73.3 15.3 %collective-permute-start.16 = (bf16[768,384]{1,0:T(8,128)(2,1)S(1)}, bf16[768,384]{1,0:T(8,128)(2,1)S(1)}, u32[]{:S(2)}, u32[]{:S(2)}) collective-permute-start(bf16[768,384]{1,0:T(8,128)(2,1)S(1)} %get-tuple-element.24.refs_0_.refs_4_), channel_id=1, source_target_pairs={{0,16},{8,24},{16,0},{24,8},{1,17},{9,25},{17,1},{25,9},{2,18},{10... | collective-permute-start | bytes 1769480 | tf_op jit(solution)/shard_map/ppermute | solution.py:52
  74.8 13.8 %collective-permute-start.22 = (bf16[768,384]{1,0:T(8,128)(2,1)S(1)}, bf16[768,384]{1,0:T(8,128)(2,1)S(1)}, u32[]{:S(2)}, u32[]{:S(2)}) collective-permute-start(bf16[768,384]{1,0:T(8,128)(2,1)S(1)} %collective-permute-done.15.refs_1_), channel_id=1, source_target_pairs={{0,2},{2,4},{4,6},{6,7},{7,5},{5,3},{3,1},{1,0},{8,9},{10,8},{12,1... | collective-permute-start | bytes 1769480 | tf_op jit(solution)/shard_map/ppermute | solution.py:49
  81.4 12.6 %collective-permute-start.24 = (bf16[768,384]{1,0:T(8,128)(2,1)S(1)}, bf16[768,384]{1,0:T(8,128)(2,1)S(1)}, u32[]{:S(2)}, u32[]{:S(2)}) collective-permute-start(bf16[768,384]{1,0:T(8,128)(2,1)S(1)} %collective-permute-done.21.refs_5_), channel_id=1, source_target_pairs={{0,2},{2,4},{4,6},{6,7},{7,5},{5,3},{3,1},{1,0},{8,9},{10,8},{12,1... | collective-permute-start | bytes 1769480 | tf_op jit(solution)/shard_map/ppermute | solution.py:49
  88.6 7.2 %collective-permute-start.17 = (bf16[768,384]{1,0:T(8,128)(2,1)S(1)}, bf16[768,384]{1,0:T(8,128)(2,1)S(1)}, u32[]{:S(2)}, u32[]{:S(2)}) collective-permute-start(bf16[768,384]{1,0:T(8,128)(2,1)S(1)} %collective-permute-done.16.refs_0_), channel_id=1, source_target_pairs={{0,8},{8,0},{16,24},{24,16},{1,9},{9,1},{17,25},{25,17},{2,10},{10... | collective-permute-start | bytes 1769480 | tf_op jit(solution)/shard_map/ppermute | solution.py:52
  88.6 11.7 %collective-permute-start.25 = (bf16[768,384]{1,0:T(8,128)(2,1)S(1)}, bf16[768,384]{1,0:T(8,128)(2,1)S(1)}, u32[]{:S(2)}, u32[]{:S(2)}) collective-permute-start(bf16[768,384]{1,0:T(8,128)(2,1)S(1)} %collective-permute-done.22), channel_id=1, source_target_pairs={{0,2},{2,4},{4,6},{6,7},{7,5},{5,3},{3,1},{1,0},{8,9},{10,8},{12,1... | collective-permute-start | bytes 1769480 | tf_op jit(solution)/shard_map/ppermute | solution.py:49
  94.0 12.6 %collective-permute-start.27 = (bf16[768,384]{1,0:T(8,128)(2,1)S(1)}, bf16[768,384]{1,0:T(8,128)(2,1)S(1)}, u32[]{:S(2)}, u32[]{:S(2)}) collective-permute-start(bf16[768,384]{1,0:T(8,128)(2,1)S(1)} %collective-permute-done.24.refs_7_), channel_id=1, source_target_pairs={{0,2},{2,4},{4,6},{6,7},{7,5},{5,3},{3,1},{1,0},{8,9},{10,8},{12,1... | collective-permute-start | bytes 1769480 | tf_op jit(solution)/shard_map/ppermute | solution.py:49
  97.2 24.4 %copy-start.1 = (bf16[768,384]{1,0:T(8,128)(2,1)S(1)}, bf16[768,384]{1,0:T(8,128)(2,1)}, u32[]{:S(2)}) copy-start(bf16[768,384]{1,0:T(8,128)(2,1)} %deriv_ref.1) | copy-start | bytes 1769476
  97.2 24.4 %copy-start.3 = (s32[24]{0:T(128)S(1)}, s32[24]{0:T(128)}, u32[]{:S(2)}) copy-start(s32[24]{0:T(128)} %band_ref.9) | copy-start | bytes 292
  97.2 24.4 %copy-start.4 = (s32[24]{0:T(128)S(1)}, s32[24]{0:T(128)}, u32[]{:S(2)}) copy-start(s32[24]{0:T(128)} %frag_ref.1) | copy-start | bytes 292
  97.2 14.5 %collective-permute-start.19 = (bf16[768,384]{1,0:T(8,128)(2,1)S(1)}, bf16[768,384]{1,0:T(8,128)(2,1)S(1)}, u32[]{:S(2)}, u32[]{:S(2)}) collective-permute-start(bf16[768,384]{1,0:T(8,128)(2,1)S(1)} %shard_map.74.refs_0_), channel_id=1, source_target_pairs={{0,16},{8,24},{16,0},{24,8},{1,17},{9,25},{17,1},{25,9},{2,18},{10... | collective-permute-start | bytes 1769480 | tf_op jit(solution)/shard_map/ppermute | solution.py:52
  98.8 13.0 %collective-permute-start.23 = (bf16[768,384]{1,0:T(8,128)(2,1)S(1)}, bf16[768,384]{1,0:T(8,128)(2,1)S(1)}, u32[]{:S(2)}, u32[]{:S(2)}) collective-permute-start(bf16[768,384]{1,0:T(8,128)(2,1)S(1)} %collective-permute-done.22), channel_id=1, source_target_pairs={{0,8},{8,0},{16,24},{24,16},{1,9},{9,1},{17,25},{25,17},{2,10},{10... | collective-permute-start | bytes 1769480 | tf_op jit(solution)/shard_map/ppermute | solution.py:52
  100.3 12.6 %collective-permute-start.28 = (bf16[768,384]{1,0:T(8,128)(2,1)S(1)}, bf16[768,384]{1,0:T(8,128)(2,1)S(1)}, u32[]{:S(2)}, u32[]{:S(2)}) collective-permute-start(bf16[768,384]{1,0:T(8,128)(2,1)S(1)} %collective-permute-done.25), channel_id=1, source_target_pairs={{0,2},{2,4},{4,6},{6,7},{7,5},{5,3},{3,1},{1,0},{8,9},{10,8},{12,1... | collective-permute-start | bytes 1769480 | tf_op jit(solution)/shard_map/ppermute | solution.py:49
  102.2 11.4 %collective-permute-start.18 = (bf16[768,384]{1,0:T(8,128)(2,1)S(1)}, bf16[768,384]{1,0:T(8,128)(2,1)S(1)}, u32[]{:S(2)}, u32[]{:S(2)}) collective-permute-start(bf16[768,384]{1,0:T(8,128)(2,1)S(1)} %shard_map.74.refs_0_), channel_id=1, source_target_pairs={{0,8},{8,0},{16,24},{24,16},{1,9},{9,1},{17,25},{25,17},{2,10},{10... | collective-permute-start | bytes 1769480 | tf_op jit(solution)/shard_map/ppermute | solution.py:52
  106.7 6.9 %collective-permute-start.26 = (bf16[768,384]{1,0:T(8,128)(2,1)S(1)}, bf16[768,384]{1,0:T(8,128)(2,1)S(1)}, u32[]{:S(2)}, u32[]{:S(2)}) collective-permute-start(bf16[768,384]{1,0:T(8,128)(2,1)S(1)} %collective-permute-done.25), channel_id=1, source_target_pairs={{0,8},{8,0},{16,24},{24,16},{1,9},{9,1},{17,25},{25,17},{2,10},{10... | collective-permute-start | bytes 1769480 | tf_op jit(solution)/shard_map/ppermute | solution.py:52
  111.7 2.0 %collective-permute-start.20 = (bf16[768,384]{1,0:T(8,128)(2,1)S(1)}, bf16[768,384]{1,0:T(8,128)(2,1)S(1)}, u32[]{:S(2)}, u32[]{:S(2)}) collective-permute-start(bf16[768,384]{1,0:T(8,128)(2,1)S(1)} %collective-permute-done.19.refs_2_), channel_id=1, source_target_pairs={{0,8},{8,0},{16,24},{24,16},{1,9},{9,1},{17,25},{25,17},{2,10},{10... | collective-permute-start | bytes 1769480 | tf_op jit(solution)/shard_map/ppermute | solution.py:52
  111.7 9.9 %collective-permute-start.30 = (bf16[768,384]{1,0:T(8,128)(2,1)S(1)}, bf16[768,384]{1,0:T(8,128)(2,1)S(1)}, u32[]{:S(2)}, u32[]{:S(2)}) collective-permute-start(bf16[768,384]{1,0:T(8,128)(2,1)S(1)} %collective-permute-done.27.refs_9_), channel_id=1, source_target_pairs={{0,2},{2,4},{4,6},{6,7},{7,5},{5,3},{3,1},{1,0},{8,9},{10,8},{12,1... | collective-permute-start | bytes 1769480 | tf_op jit(solution)/shard_map/ppermute | solution.py:49
  113.0 8.6 %collective-permute-start.29 = (bf16[768,384]{1,0:T(8,128)(2,1)S(1)}, bf16[768,384]{1,0:T(8,128)(2,1)S(1)}, u32[]{:S(2)}, u32[]{:S(2)}) collective-permute-start(bf16[768,384]{1,0:T(8,128)(2,1)S(1)} %collective-permute-done.28), channel_id=1, source_target_pairs={{0,8},{8,0},{16,24},{24,16},{1,9},{9,1},{17,25},{25,17},{2,10},{10... | collective-permute-start | bytes 1769480 | tf_op jit(solution)/shard_map/ppermute | solution.py:52

commit v5 on v4

--- a/solution.py
+++ b/solution.py
@@ -10,6 +10,7 @@
 BLK = 128
 FRAG_DEV = 2
 AXES = ("row", "col")
+SPAN = 1
 SPARE_VMEM = 10 * 1024 * 1024
 
 
@@ -66,12 +67,17 @@
         return pl.multiple_of((lax.axis_index("row") ^ other) * self.rows_here, self.rows_here)
 
 
-def masked(plan, band_ref, value):
+def spans(plan):
+    step = min(SPAN, plan.block_rows)
+    return [(i, slice(i * BLK, min(i + step, plan.block_rows) * BLK)) for i in range(0, plan.block_rows, step)]
+
+
+def masked(plan, band_ref, value, first_block):
     lines = []
-    for i in range(plan.block_rows):
+    for i in range(value.shape[0] // BLK):
         line = []
         for j in range(plan.block_cols):
-            row = lax.axis_index("row") * plan.block_rows + i
+            row = lax.axis_index("row") * plan.block_rows + first_block + i
             col = lax.axis_index("col") * plan.block_cols + j
             keep = jnp.abs(row - col) <= jnp.maximum(band_ref[row], band_ref[col])
             block = value[i * BLK : (i + 1) * BLK, j * BLK : (j + 1) * BLK]
@@ -135,14 +141,13 @@
     total_ref[...] = start_terms(plan, places, band_ref, right_ref, slab_ref, lefts)
 
 
-def square_kernel(plan, places, band_ref, before_ref, right_ref, _, far_ref, out_ref, slab_ref):
-    total = before_ref[...] + start_terms(plan, places, band_ref, right_ref, slab_ref, [far_ref])
-    out_ref[...] = masked(plan, band_ref, total).astype(jnp.bfloat16)
-
-
-def pass_kernel(*refs):
-    for from_ref, to_ref in zip(refs, refs[len(refs) // 2 :]):
-        to_ref[:16, :BLK] = from_ref[:16, :BLK]
+def square_kernel(plan, band_ref, before_ref, right_ref, _, far_ref, out_ref, slab_ref):
+    first = plan.origin_first(plan.far, True)
+    lanes = pl.ds(first, plan.cols_here)
+    lay_masked(plan, band_ref, slab_ref, far_ref, plan.row_first(0), first, 0, first)
+    for block, lines in spans(plan):
+        total = before_ref[lines, :] + dot(slab_ref[lines, lanes], right_ref[lanes, :])
+        out_ref[lines, :] = masked(plan, band_ref, total, block).astype(jnp.bfloat16)
 
 
 def near_kernel(plan, places, *refs):
@@ -158,10 +163,10 @@
     total_ref[...] = total
 
 
-def slab_terms(plan, slab_ref, pieces):
+def slab_terms(plan, slab_ref, pieces, lines=slice(None)):
     total = None
     for other, piece in pieces:
-        term = dot(slab_ref[:, pl.ds(plan.row_first(other), plan.rows_here)], piece[...])
+        term = dot(slab_ref[lines, pl.ds(plan.row_first(other), plan.rows_here)], piece[...])
         total = term if total is None else total + term
     return total
 
@@ -178,34 +183,43 @@
 
 def sign_kernel(plan, others, band_ref, slab_ref, total_ref, *refs):
     *pieces, sign_ref, density_ref = refs
-    cubic = total_ref[...] + slab_terms(plan, slab_ref, list(zip(others, pieces)))
-    start = slab_ref[:, pl.ds(plan.origin_first(0, True), plan.cols_here)].astype(jnp.float32)
-    sign = masked(plan, band_ref, 1.5 * start - 0.5 * cubic).astype(jnp.bfloat16)
-    sign_ref[...] = sign
     first_row = lax.axis_index("row") * plan.rows_here
-    first_col = lax.axis_index("col") * plan.cols_here
-    rows = first_row + lax.broadcasted_iota(jnp.int32, sign.shape, 0)
-    cols = first_col + lax.broadcasted_iota(jnp.int32, sign.shape, 1)
-    identity = (rows == cols).astype(jnp.float32)
-    density_ref[...] = (0.5 * (identity - sign.astype(jnp.float32))).astype(jnp.bfloat16)
+    first_col = plan.origin_first(0, True)
+    for block, lines in spans(plan):
+        cubic = total_ref[lines, :] + slab_terms(plan, slab_ref, list(zip(others, pieces)), lines)
+        start = slab_ref[lines, pl.ds(first_col, plan.cols_here)].astype(jnp.float32)
+        sign = masked(plan, band_ref, 1.5 * start - 0.5 * cubic, block).astype(jnp.bfloat16)
+        sign_ref[lines, :] = sign
+        rows = first_row + block * BLK + lax.broadcasted_iota(jnp.int32, sign.shape, 0)
+        cols = first_col + lax.broadcasted_iota(jnp.int32, sign.shape, 1)
+        identity = (rows == cols).astype(jnp.float32)
+        density_ref[lines, :] = (0.5 * (identity - sign.astype(jnp.float32))).astype(jnp.bfloat16)
+
+
+def copy_kernel(from_ref, to_ref):
+    to_ref[...] = from_ref[...]
 
 
 def weighted_kernel(plan, others, band_ref, slab_ref, before_ref, *refs):
     *pieces, out_ref = refs
-    total = before_ref[...] + slab_terms(plan, slab_ref, list(zip(others, pieces)))
-    out_ref[...] = masked(plan, band_ref, total).astype(jnp.bfloat16)
+    for block, lines in spans(plan):
+        total = before_ref[lines, :] + slab_terms(plan, slab_ref, list(zip(others, pieces)), lines)
+        out_ref[lines, :] = masked(plan, band_ref, total, block).astype(jnp.bfloat16)
 
 
 def energy_kernel(plan, places, band_ref, frag_ref, total_ref, right_ref, deriv_ref, *refs):
     *lefts, energy_ref, sums_ref = refs
-    total = total_ref[...]
-    for (distance, behind), left in zip(places, lefts):
-        first = plan.origin_first(distance, behind)
-        total = total + dot(left[...], right_ref[pl.ds(first, plan.cols_here), :])
-    energy = masked(plan, band_ref, total).astype(jnp.bfloat16)
-    energy_ref[...] = energy
-    weighed = energy.astype(jnp.float32) * deriv_ref[...].astype(jnp.float32)
-    terms = jnp.sum(weighed, axis=0, keepdims=True)
+    terms = jnp.zeros((8, plan.cols_here), jnp.float32)
+    for block, lines in spans(plan):
+        total = total_ref[lines, :]
+        for (distance, behind), left in zip(places, lefts):
+            first = plan.origin_first(distance, behind)
+            total = total + dot(left[lines, :], right_ref[pl.ds(first, plan.cols_here), :])
+        energy = masked(plan, band_ref, total, block).astype(jnp.bfloat16)
+        energy_ref[lines, :] = energy
+        weighed = energy.astype(jnp.float32) * deriv_ref[lines, :].astype(jnp.float32)
+        terms = terms + jnp.sum(weighed.reshape(-1, 8, plan.cols_here), axis=0)
+    terms = jnp.sum(terms, axis=0, keepdims=True)
     count = FRAG_DEV * plan.cols
     fragment = lax.broadcasted_iota(jnp.int32, (count, BLK), 0)
     sums = jnp.zeros((count, BLK), jnp.float32)
@@ -250,7 +264,7 @@
         column + shards,
     )
     square, slab = call(
-        bind(square_kernel, plan, [(plan.far, True)]), [block, slab_type], [band], [total, right, slab, far], {3: 1}
+        bind(square_kernel, plan), [block, slab_type], [band], [total, right, slab, far], {3: 1}
     )
 
     crossed = exchange_start(square)
@@ -260,7 +274,7 @@
     column = exchange_end([square, partner], crossed)
     even, odd = list(others)[2::2], list(others)[3::2]
     (total,) = call(bind(more_kernel, plan, even), [total_type], [], [slab, total] + column[2::2])
-    sign_iterate, density = call(
+    sign, density = call(
         bind(sign_kernel, plan, odd), [block, block], [band], [slab, total] + column[3::2]
     )
 
@@ -271,6 +285,8 @@
     (total,) = call(bind(more_kernel, plan, even), [total_type], [], [slab, total] + column[2::2])
     (weighted,) = call(bind(weighted_kernel, plan, odd), [block], [band], [slab, total] + column[3::2])
     column = exchange_end([weighted, plan.across(weighted, 1)], exchange_start(weighted))
+    (sign_iterate,) = call(copy_kernel, [block], [], [sign])
+    shards[0], sign_iterate = lax.optimization_barrier((shards[0], sign_iterate))
     places = near_places(plan, 0, plan.far)
     late = [shards[-1], far]
     total, right = call(bind(near_kernel, plan, places[:-1]), [total_type, column_type], [], column + shards[:-1])

time: 137 us -> 136 us (level)
    pallas_call x10 -> x11, Pallas kernels: 18.8 us -> 18.6 us  [call(): pl.pallas_call(kernel, out_shape=outs, in_specs=[smem] * len(scalars) + [...]
  transfers between devices with their start and end apart: 31 -> 31, of which waited for: 19 -> 18; matrix products, arithmetic and copies ran while one was open for 0% -> 0% of each run, Pallas kernels for 9% -> 10%
where the time goes in v5:
time: 136 us; the launch traced here: 135 us
  waiting for transfers between devices  68.1 us (50%)
  starting transfers between devices  33.8 us (25%)
  Pallas kernels  18.6 us (14%)
  blocking collectives  11.8 us (9%)
  local copies, waits for them, and re-layouts  1.74 us (1%)
    ppermute x14, waiting for transfers between devices, ring(): return lax.ppermute(value, AXES, pairs)  41.8 us
    ppermute x17, waiting for transfers between devices, across(): lax.ppermute(value, 'row', [(i, i ^ other) for i in range(self.rows)])  26.3 us
    ppermute x14, starting transfers between devices, ring(): return lax.ppermute(value, AXES, pairs)  24.5 us
    pallas_call x11, Pallas kernels, call(): pl.pallas_call(kernel, out_shape=outs, in_specs=[smem] * len(scalars) + [...  18.6 us
    all_to_all x1, blocking collectives, body(): pulay_terms = jnp.sum(lax.all_to_all(sums, AXES, 0, 0), axis=0)  11.8 us
    ppermute x17, starting transfers between devices, across(): lax.ppermute(value, 'row', [(i, i ^ other) for i in range(self.rows)])  9.32 us
  transfers between devices with their start and end apart: 31, of which 18 were waited for; matrix products, arithmetic and copies ran while one was open for 0% of the time, Pallas kernels for 10%

profile of v5, /device:TPU:0, one launch (start us, length us, event | category | flops | bytes accessed | tf_op | source)
XLA Modules:
  0.0 135.5 jit_solution(9939316753929057768)
XLA Ops:
  0.6 0.5 collective-permute-start
  1.1 2.6 %collective-permute-start.3 = (bf16[768,384]{1,0:T(8,128)(2,1)}, bf16[768,384]{1,0:T(8,128)(2,1)S(1)}, u32[]{:S(2)}, u32[]{:S(2)}) collective-permute-start(bf16[768,384]{1,0:T(8,128)(2,1)} %refs_4_.1), channel_id=1, source_target_pairs={{0,2},{2,4},{4,6},{6,7},{7,5},{5,3},{3,1},{1,0},{8,9},{10,8},{12,1... | collective-permute-start | bytes 1769480 | tf_op jit(solution)/shard_map/ppermute | solution.py:50
  3.8 0.0 collective-permute-done.refs_1_
  3.8 2.1 %collective-permute-start.4 = (bf16[768,384]{1,0:T(8,128)(2,1)S(1)}, bf16[768,384]{1,0:T(8,128)(2,1)S(1)}, u32[]{:S(2)}, u32[]{:S(2)}) collective-permute-start(bf16[768,384]{1,0:T(8,128)(2,1)S(1)} %collective-permute-done.refs_1_), channel_id=1, source_target_pairs={{0,2},{2,4},{4,6},{6,7},{7,5},{5,3},{3,1},{1,0},{8,9},{10,8},{12,1... | collective-permute-start | bytes 1769480 | tf_op jit(solution)/shard_map/ppermute | solution.py:50
  5.9 5.9 %collective-permute-done.3.refs_5_ = bf16[768,384]{1,0:T(8,128)(2,1)S(1)} collective-permute-done((bf16[768,384]{1,0:T(8,128)(2,1)}, bf16[768,384]{1,0:T(8,128)(2,1)S(1)}, u32[]{:S(2)}, u32[]{:S(2)}) %collective-permute-start.3) | collective-permute-done | bytes 589856 | tf_op jit(solution)/shard_map/ppermute | solution.py:50
  11.8 2.1 %collective-permute-start.6 = (bf16[768,384]{1,0:T(8,128)(2,1)S(1)}, bf16[768,384]{1,0:T(8,128)(2,1)S(1)}, u32[]{:S(2)}, u32[]{:S(2)}) collective-permute-start(bf16[768,384]{1,0:T(8,128)(2,1)S(1)} %collective-permute-done.3.refs_5_), channel_id=1, source_target_pairs={{0,2},{2,4},{4,6},{6,7},{7,5},{5,3},{3,1},{1,0},{8,9},{10,8},{12,1... | collective-permute-start | bytes 1769480 | tf_op jit(solution)/shard_map/ppermute | solution.py:50
  13.9 1.5 %collective-permute-start.1 = (bf16[768,384]{1,0:T(8,128)(2,1)}, bf16[768,384]{1,0:T(8,128)(2,1)S(1)}, u32[]{:S(2)}, u32[]{:S(2)}) collective-permute-start(bf16[768,384]{1,0:T(8,128)(2,1)} %refs_4_.1), channel_id=1, source_target_pairs={{0,16},{8,24},{16,0},{24,8},{1,17},{9,25},{17,1},{25,9},{2,18},{10... | collective-permute-start | bytes 1769480 | tf_op jit(solution)/shard_map/ppermute | solution.py:53
  15.4 2.8 %collective-permute-done.4 = bf16[768,384]{1,0:T(8,128)(2,1)S(1)} collective-permute-done((bf16[768,384]{1,0:T(8,128)(2,1)S(1)}, bf16[768,384]{1,0:T(8,128)(2,1)S(1)}, u32[]{:S(2)}, u32[]{:S(2)}) %collective-permute-start.4) | collective-permute-done | bytes 589856 | tf_op jit(solution)/shard_map/ppermute | solution.py:50
  18.1 2.1 %collective-permute-start.7 = (bf16[768,384]{1,0:T(8,128)(2,1)S(1)}, bf16[768,384]{1,0:T(8,128)(2,1)S(1)}, u32[]{:S(2)}, u32[]{:S(2)}) collective-permute-start(bf16[768,384]{1,0:T(8,128)(2,1)S(1)} %collective-permute-done.4), channel_id=1, source_target_pairs={{0,2},{2,4},{4,6},{6,7},{7,5},{5,3},{3,1},{1,0},{8,9},{10,8},{12,1... | collective-permute-start | bytes 1769480 | tf_op jit(solution)/shard_map/ppermute | solution.py:50
  20.2 4.2 %collective-permute-done.6.refs_7_ = bf16[768,384]{1,0:T(8,128)(2,1)S(1)} collective-permute-done((bf16[768,384]{1,0:T(8,128)(2,1)S(1)}, bf16[768,384]{1,0:T(8,128)(2,1)S(1)}, u32[]{:S(2)}, u32[]{:S(2)}) %collective-permute-start.6) | collective-permute-done | bytes 589856 | tf_op jit(solution)/shard_map/ppermute | solution.py:50
  24.4 2.1 %collective-permute-start.9 = (bf16[768,384]{1,0:T(8,128)(2,1)S(1)}, bf16[768,384]{1,0:T(8,128)(2,1)S(1)}, u32[]{:S(2)}, u32[]{:S(2)}) collective-permute-start(bf16[768,384]{1,0:T(8,128)(2,1)S(1)} %collective-permute-done.6.refs_7_), channel_id=1, source_target_pairs={{0,2},{2,4},{4,6},{6,7},{7,5},{5,3},{3,1},{1,0},{8,9},{10,8},{12,1... | collective-permute-start | bytes 1769480 | tf_op jit(solution)/shard_map/ppermute | solution.py:50
  26.5 2.1 %collective-permute-done.1.refs_2_ = bf16[768,384]{1,0:T(8,128)(2,1)S(1)} collective-permute-done((bf16[768,384]{1,0:T(8,128)(2,1)}, bf16[768,384]{1,0:T(8,128)(2,1)S(1)}, u32[]{:S(2)}, u32[]{:S(2)}) %collective-permute-start.1) | collective-permute-done | bytes 589856 | tf_op jit(solution)/shard_map/ppermute | solution.py:53
  28.6 0.5 collective-permute-start.5
  29.1 1.7 %collective-permute-done.7 = bf16[768,384]{1,0:T(8,128)(2,1)S(1)} collective-permute-done((bf16[768,384]{1,0:T(8,128)(2,1)S(1)}, bf16[768,384]{1,0:T(8,128)(2,1)S(1)}, u32[]{:S(2)}, u32[]{:S(2)}) %collective-permute-start.7) | collective-permute-done | bytes 589856 | tf_op jit(solution)/shard_map/ppermute | solution.py:50
  30.8 1.3 collective-permute-start.10
  32.0 0.9 collective-permute-start.8
  32.9 4.2 %collective-permute-done.9.refs_9_ = bf16[768,384]{1,0:T(8,128)(2,1)S(1)} collective-permute-done((bf16[768,384]{1,0:T(8,128)(2,1)S(1)}, bf16[768,384]{1,0:T(8,128)(2,1)S(1)}, u32[]{:S(2)}, u32[]{:S(2)}) %collective-permute-start.9) | collective-permute-done | bytes 589856 | tf_op jit(solution)/shard_map/ppermute | solution.py:50
  37.1 2.1 %collective-permute-start.11 = (bf16[768,384]{1,0:T(8,128)(2,1)S(1)}, bf16[768,384]{1,0:T(8,128)(2,1)S(1)}, u32[]{:S(2)}, u32[]{:S(2)}) collective-permute-start(bf16[768,384]{1,0:T(8,128)(2,1)S(1)} %collective-permute-done.9.refs_9_), channel_id=1, source_target_pairs={{0,2},{2,4},{4,6},{6,7},{7,5},{5,3},{3,1},{1,0},{8,9},{10,8},{12,1... | collective-permute-start | bytes 1769480 | tf_op jit(solution)/shard_map/ppermute | solution.py:50
  39.2 4.0 %collective-permute-done.10.refs_10_ = bf16[768,384]{1,0:T(8,128)(2,1)S(1)} collective-permute-done((bf16[768,384]{1,0:T(8,128)(2,1)S(1)}, bf16[768,384]{1,0:T(8,128)(2,1)S(1)}, u32[]{:S(2)}, u32[]{:S(2)}) %collective-permute-start.10) | collective-permute-done | bytes 589856 | tf_op jit(solution)/shard_map/ppermute | solution.py:50
  43.2 0.0 collective-permute-done.8.refs_8_
  43.2 1.1 copy-done
  44.3 0.7 copy-done.2
  44.9 4.7 %shard_map.67 = (f32[768,384]{1,0:T(8,128)S(1)}, bf16[3072,384]{1,0:T(8,128)(2,1)S(1)}, bf16[768,3072]{1,0:T(8,128)(2,1)S(1)}) custom-call(s32[24]{0:T(128)S(1)} %copy-done.2, bf16[768,384]{1,0:T(8,128)(2,1)S(1)} %copy-done, bf16[768,384]{1,0:T(8,128)(2,1)S(1)} %collective-permute-done.refs_1_, bf16[768,384]{1,0:T(8,128)(2,1)S(1)} %collective-permute-done.1.refs_2_, ...), custom_call_target="tpu_custom_call" | custom-call | tf_op jit(solution)/shard_map/pallas_call | solution.py:97
  49.6 0.1 collective-permute-done.11.far_ref
  49.7 1.2 shard_map.68
  50.9 0.1 collective-permute-start.13
  51.0 2.0 %collective-permute-start.12 = (bf16[768,384]{1,0:T(8,128)(2,1)S(1)}, bf16[768,384]{1,0:T(8,128)(2,1)S(1)}, u32[]{:S(2)}, u32[]{:S(2)}) collective-permute-start(bf16[768,384]{1,0:T(8,128)(2,1)S(1)} %get-tuple-element.22.refs_0_), channel_id=1, source_target_pairs={{0,16},{8,24},{16,0},{24,8},{1,17},{9,25},{17,1},{25,9},{2,18},{10... | collective-permute-start | bytes 1769480 | tf_op jit(solution)/shard_map/ppermute | solution.py:53
  53.0 0.0 collective-permute-done.13.refs_1_
  53.0 1.4 %shard_map.69.before_ref = f32[768,384]{1,0:T(8,128)S(1)} custom-call(bf16[768,3072]{1,0:T(8,128)(2,1)S(1)} %get-tuple-element.21.slab_ref, bf16[768,384]{1,0:T(8,128)(2,1)S(1)} %get-tuple-element.22.refs_0_, bf16[768,384]{1,0:T(8,128)(2,1)S(1)} %collective-permute-done.13.refs_1_), custom_call_target="tpu_custom_call" | custom-call | tf_op jit(solution)/shard_map/pallas_call | solution.py:97
  54.4 12.5 %collective-permute-done.12.refs_0_ = bf16[768,384]{1,0:T(8,128)(2,1)S(1)} collective-permute-done((bf16[768,384]{1,0:T(8,128)(2,1)S(1)}, bf16[768,384]{1,0:T(8,128)(2,1)S(1)}, u32[]{:S(2)}, u32[]{:S(2)}) %collective-permute-start.12) | collective-permute-done | bytes 589856 | tf_op jit(solution)/shard_map/ppermute | solution.py:53
  66.9 0.0 collective-permute-start.14
  66.9 0.8 shard_map.70.total_ref
  67.7 1.2 collective-permute-done.14.refs_0_
  69.0 1.4 %shard_map.71 = (bf16[768,384]{1,0:T(8,128)(2,1)S(1)}, bf16[768,384]{1,0:T(8,128)(2,1)S(1)}) custom-call(s32[24]{0:T(128)S(1)} %copy-done.2, bf16[768,3072]{1,0:T(8,128)(2,1)S(1)} %get-tuple-element.21.slab_ref, f32[768,384]{1,0:T(8,128)S(1)} %shard_map.70.total_ref, bf16[768,384]{1,0:T(8,128)(2,1)S(1)} %collective-permute-done.14.refs_0_), custom_call_target="tpu_custom_call" | custom-call | tf_op jit(solution)/shard_map/pallas_call | solution.py:97
  70.4 0.2 collective-permute-start.15
  70.6 1.8 %collective-permute-start.21 = (bf16[768,384]{1,0:T(8,128)(2,1)S(1)}, bf16[768,384]{1,0:T(8,128)(2,1)S(1)}, u32[]{:S(2)}, u32[]{:S(2)}) collective-permute-start(bf16[768,384]{1,0:T(8,128)(2,1)S(1)} %get-tuple-element.28.refs_0_.refs_4_), channel_id=1, source_target_pairs={{0,2},{2,4},{4,6},{6,7},{7,5},{5,3},{3,1},{1,0},{8,9},{10,8},{12,1... | collective-permute-start | bytes 1769480 | tf_op jit(solution)/shard_map/ppermute | solution.py:50
  72.4 1.5 %collective-permute-start.16 = (bf16[768,384]{1,0:T(8,128)(2,1)S(1)}, bf16[768,384]{1,0:T(8,128)(2,1)S(1)}, u32[]{:S(2)}, u32[]{:S(2)}) collective-permute-start(bf16[768,384]{1,0:T(8,128)(2,1)S(1)} %get-tuple-element.28.refs_0_.refs_4_), channel_id=1, source_target_pairs={{0,16},{8,24},{16,0},{24,8},{1,17},{9,25},{17,1},{25,9},{2,18},{10... | collective-permute-start | bytes 1769480 | tf_op jit(solution)/shard_map/ppermute | solution.py:53
  73.9 1.6 %collective-permute-start.22 = (bf16[768,384]{1,0:T(8,128)(2,1)S(1)}, bf16[768,384]{1,0:T(8,128)(2,1)S(1)}, u32[]{:S(2)}, u32[]{:S(2)}) collective-permute-start(bf16[768,384]{1,0:T(8,128)(2,1)S(1)} %collective-permute-done.15.refs_1_), channel_id=1, source_target_pairs={{0,2},{2,4},{4,6},{6,7},{7,5},{5,3},{3,1},{1,0},{8,9},{10,8},{12,1... | collective-permute-start | bytes 1769480 | tf_op jit(solution)/shard_map/ppermute | solution.py:50
  75.5 5.0 %collective-permute-done.21.refs_5_ = bf16[768,384]{1,0:T(8,128)(2,1)S(1)} collective-permute-done((bf16[768,384]{1,0:T(8,128)(2,1)S(1)}, bf16[768,384]{1,0:T(8,128)(2,1)S(1)}, u32[]{:S(2)}, u32[]{:S(2)}) %collective-permute-start.21) | collective-permute-done | bytes 589856 | tf_op jit(solution)/shard_map/ppermute | solution.py:50
  80.5 1.8 %collective-permute-start.24 = (bf16[768,384]{1,0:T(8,128)(2,1)S(1)}, bf16[768,384]{1,0:T(8,128)(2,1)S(1)}, u32[]{:S(2)}, u32[]{:S(2)}) collective-permute-start(bf16[768,384]{1,0:T(8,128)(2,1)S(1)} %collective-permute-done.21.refs_5_), channel_id=1, source_target_pairs={{0,2},{2,4},{4,6},{6,7},{7,5},{5,3},{3,1},{1,0},{8,9},{10,8},{12,1... | collective-permute-start | bytes 1769480 | tf_op jit(solution)/shard_map/ppermute | solution.py:50
  82.3 5.4 %collective-permute-done.16.refs_0_ = bf16[768,384]{1,0:T(8,128)(2,1)S(1)} collective-permute-done((bf16[768,384]{1,0:T(8,128)(2,1)S(1)}, bf16[768,384]{1,0:T(8,128)(2,1)S(1)}, u32[]{:S(2)}, u32[]{:S(2)}) %collective-permute-start.16) | collective-permute-done | bytes 589856 | tf_op jit(solution)/shard_map/ppermute | solution.py:53
  87.7 0.0 collective-permute-start.17
  87.7 0.9 collective-permute-start.25
  88.6 1.4 %shard_map.73.before_ref = f32[768,384]{1,0:T(8,128)S(1)} custom-call(bf16[768,3072]{1,0:T(8,128)(2,1)S(1)} %get-tuple-element.21.slab_ref, bf16[768,384]{1,0:T(8,128)(2,1)S(1)} %get-tuple-element.28.refs_0_.refs_4_, bf16[768,384]{1,0:T(8,128)(2,1)S(1)} %collective-permute-done.15.refs_1_), custom_call_target="tpu_custom_call" | custom-call | tf_op jit(solution)/shard_map/pallas_call | solution.py:97
  90.0 0.8 shard_map.74.before_ref
  90.8 2.3 %collective-permute-done.24.refs_7_ = bf16[768,384]{1,0:T(8,128)(2,1)S(1)} collective-permute-done((bf16[768,384]{1,0:T(8,128)(2,1)S(1)}, bf16[768,384]{1,0:T(8,128)(2,1)S(1)}, u32[]{:S(2)}, u32[]{:S(2)}) %collective-permute-start.24) | collective-permute-done | bytes 589856 | tf_op jit(solution)/shard_map/ppermute | solution.py:50
  93.1 1.8 %collective-permute-start.27 = (bf16[768,384]{1,0:T(8,128)(2,1)S(1)}, bf16[768,384]{1,0:T(8,128)(2,1)S(1)}, u32[]{:S(2)}, u32[]{:S(2)}) collective-permute-start(bf16[768,384]{1,0:T(8,128)(2,1)S(1)} %collective-permute-done.24.refs_7_), channel_id=1, source_target_pairs={{0,2},{2,4},{4,6},{6,7},{7,5},{5,3},{3,1},{1,0},{8,9},{10,8},{12,1... | collective-permute-start | bytes 1769480 | tf_op jit(solution)/shard_map/ppermute | solution.py:50
  94.9 0.0 collective-permute-done.17.refs_0_
  94.9 1.3 shard_map.75.refs_0_
  96.3 1.5 %collective-permute-start.19 = (bf16[768,384]{1,0:T(8,128)(2,1)S(1)}, bf16[768,384]{1,0:T(8,128)(2,1)S(1)}, u32[]{:S(2)}, u32[]{:S(2)}) collective-permute-start(bf16[768,384]{1,0:T(8,128)(2,1)S(1)} %shard_map.75.refs_0_), channel_id=1, source_target_pairs={{0,16},{8,24},{16,0},{24,8},{1,17},{9,25},{17,1},{25,9},{2,18},{10... | collective-permute-start | bytes 1769480 | tf_op jit(solution)/shard_map/ppermute | solution.py:53
  97.8 0.0 collective-permute-start.23
  97.8 1.6 %collective-permute-done.25 = bf16[768,384]{1,0:T(8,128)(2,1)S(1)} collective-permute-done((bf16[768,384]{1,0:T(8,128)(2,1)S(1)}, bf16[768,384]{1,0:T(8,128)(2,1)S(1)}, u32[]{:S(2)}, u32[]{:S(2)}) %collective-permute-start.25) | collective-permute-done | bytes 589856 | tf_op jit(solution)/shard_map/ppermute | solution.py:50
  99.4 1.8 %collective-permute-start.28 = (bf16[768,384]{1,0:T(8,128)(2,1)S(1)}, bf16[768,384]{1,0:T(8,128)(2,1)S(1)}, u32[]{:S(2)}, u32[]{:S(2)}) collective-permute-start(bf16[768,384]{1,0:T(8,128)(2,1)S(1)} %collective-permute-done.25), channel_id=1, source_target_pairs={{0,2},{2,4},{4,6},{6,7},{7,5},{5,3},{3,1},{1,0},{8,9},{10,8},{12,1... | collective-permute-start | bytes 1769480 | tf_op jit(solution)/shard_map/ppermute | solution.py:50
  101.3 4.5 %collective-permute-done.27.refs_9_ = bf16[768,384]{1,0:T(8,128)(2,1)S(1)} collective-permute-done((bf16[768,384]{1,0:T(8,128)(2,1)S(1)}, bf16[768,384]{1,0:T(8,128)(2,1)S(1)}, u32[]{:S(2)}, u32[]{:S(2)}) %collective-permute-start.27) | collective-permute-done | bytes 589856 | tf_op jit(solution)/shard_map/ppermute | solution.py:50
  105.8 5.0 %collective-permute-done.19.refs_2_ = bf16[768,384]{1,0:T(8,128)(2,1)S(1)} collective-permute-done((bf16[768,384]{1,0:T(8,128)(2,1)S(1)}, bf16[768,384]{1,0:T(8,128)(2,1)S(1)}, u32[]{:S(2)}, u32[]{:S(2)}) %collective-permute-start.19) | collective-permute-done | bytes 589856 | tf_op jit(solution)/shard_map/ppermute | solution.py:53
  110.8 0.3 collective-permute-start.30
  111.1 0.9 collective-permute-done.28
  112.1 0.6 collective-permute-start.29
  112.6 0.9 shard_map.72
  113.5 2.5 %shard_map.76 = (f32[768,384]{1,0:T(8,128)S(1)}, bf16[3072,384]{1,0:T(8,128)(2,1)S(1)}) custom-call(bf16[768,384]{1,0:T(8,128)(2,1)S(1)} %shard_map.75.refs_0_, bf16[768,384]{1,0:T(8,128)(2,1)S(1)} %collective-permute-done.18.refs_1_, bf16[768,384]{1,0:T(8,128)(2,1)S(1)} %collective-permute-done.19.refs_2_, ...), custom_call_target="tpu_custom_call" | custom-call | tf_op jit(solution)/shard_map/pallas_call | solution.py:97
  116.1 4.6 %collective-permute-done.30.refs_1_ = bf16[768,384]{1,0:T(8,128)(2,1)S(1)} collective-permute-done((bf16[768,384]{1,0:T(8,128)(2,1)S(1)}, bf16[768,384]{1,0:T(8,128)(2,1)S(1)}, u32[]{:S(2)}, u32[]{:S(2)}) %collective-permute-start.30) | collective-permute-done | bytes 589856 | tf_op jit(solution)/shard_map/ppermute | solution.py:50
  120.7 2.3 %shard_map.77 = (bf16[768,384]{1,0:T(8,128)(2,1)}, f32[16,128]{1,0:T(8,128)S(1)}) custom-call(s32[24]{0:T(128)S(1)} %copy-done.3, s32[24]{0:T(128)S(1)} %copy-done.4, f32[768,384]{1,0:T(8,128)S(1)} %get-tuple-element.29.total_ref, bf16[3072,384]{1,0:T(8,128)(2,1)S(1)} %get-tuple-element.30.right_ref, bf16[768,384]{1,0:T(8,128)(2,1)S(1)} %copy-done.1, ...), custom_call_target="tpu_custom_call" | custom-call | tf_op jit(solution)/shard_map/pallas_call | solution.py:97
  123.0 11.8 %all_to_all.5 = f32[32,2,128]{2,1,0:T(2,128)S(1)} all-to-all(f32[32,2,128]{2,1,0:T(2,128)S(1)} %bitcast.3), channel_id=1, replica_groups=mesh['row'=4,'col'=8] {'row','col'}, dimensions={0} | all-to-all | bytes 65536 | tf_op jit(solution)/shard_map/all_to_all | solution.py:302
  134.9 0.6 reduce_sum.9
  (22 shorter events, 0.1 us)
Async XLA Ops:
  0.6 3.2 %collective-permute-start = (bf16[768,384]{1,0:T(8,128)(2,1)}, bf16[768,384]{1,0:T(8,128)(2,1)S(1)}, u32[]{:S(2)}, u32[]{:S(2)}) collective-permute-start(bf16[768,384]{1,0:T(8,128)(2,1)} %refs_4_.1), channel_id=1, source_target_pairs={{0,8},{8,0},{16,24},{24,16},{1,9},{9,1},{17,25},{25,17},{2,10},{10... | collective-permute-start | bytes 1769480 | tf_op jit(solution)/shard_map/ppermute | solution.py:53
  1.1 10.7 %collective-permute-start.3 = (bf16[768,384]{1,0:T(8,128)(2,1)}, bf16[768,384]{1,0:T(8,128)(2,1)S(1)}, u32[]{:S(2)}, u32[]{:S(2)}) collective-permute-start(bf16[768,384]{1,0:T(8,128)(2,1)} %refs_4_.1), channel_id=1, source_target_pairs={{0,2},{2,4},{4,6},{6,7},{7,5},{5,3},{3,1},{1,0},{8,9},{10,8},{12,1... | collective-permute-start | bytes 1769480 | tf_op jit(solution)/shard_map/ppermute | solution.py:50
  3.8 14.3 %collective-permute-start.4 = (bf16[768,384]{1,0:T(8,128)(2,1)S(1)}, bf16[768,384]{1,0:T(8,128)(2,1)S(1)}, u32[]{:S(2)}, u32[]{:S(2)}) collective-permute-start(bf16[768,384]{1,0:T(8,128)(2,1)S(1)} %collective-permute-done.refs_1_), channel_id=1, source_target_pairs={{0,2},{2,4},{4,6},{6,7},{7,5},{5,3},{3,1},{1,0},{8,9},{10,8},{12,1... | collective-permute-start | bytes 1769480 | tf_op jit(solution)/shard_map/ppermute | solution.py:50
  11.8 12.6 %collective-permute-start.6 = (bf16[768,384]{1,0:T(8,128)(2,1)S(1)}, bf16[768,384]{1,0:T(8,128)(2,1)S(1)}, u32[]{:S(2)}, u32[]{:S(2)}) collective-permute-start(bf16[768,384]{1,0:T(8,128)(2,1)S(1)} %collective-permute-done.3.refs_5_), channel_id=1, source_target_pairs={{0,2},{2,4},{4,6},{6,7},{7,5},{5,3},{3,1},{1,0},{8,9},{10,8},{12,1... | collective-permute-start | bytes 1769480 | tf_op jit(solution)/shard_map/ppermute | solution.py:50
  13.9 14.7 %collective-permute-start.1 = (bf16[768,384]{1,0:T(8,128)(2,1)}, bf16[768,384]{1,0:T(8,128)(2,1)S(1)}, u32[]{:S(2)}, u32[]{:S(2)}) collective-permute-start(bf16[768,384]{1,0:T(8,128)(2,1)} %refs_4_.1), channel_id=1, source_target_pairs={{0,16},{8,24},{16,0},{24,8},{1,17},{9,25},{17,1},{25,9},{2,18},{10... | collective-permute-start | bytes 1769480 | tf_op jit(solution)/shard_map/ppermute | solution.py:53
  18.1 12.6 %collective-permute-start.7 = (bf16[768,384]{1,0:T(8,128)(2,1)S(1)}, bf16[768,384]{1,0:T(8,128)(2,1)S(1)}, u32[]{:S(2)}, u32[]{:S(2)}) collective-permute-start(bf16[768,384]{1,0:T(8,128)(2,1)S(1)} %collective-permute-done.4), channel_id=1, source_target_pairs={{0,2},{2,4},{4,6},{6,7},{7,5},{5,3},{3,1},{1,0},{8,9},{10,8},{12,1... | collective-permute-start | bytes 1769480 | tf_op jit(solution)/shard_map/ppermute | solution.py:50
  24.4 12.6 %collective-permute-start.9 = (bf16[768,384]{1,0:T(8,128)(2,1)S(1)}, bf16[768,384]{1,0:T(8,128)(2,1)S(1)}, u32[]{:S(2)}, u32[]{:S(2)}) collective-permute-start(bf16[768,384]{1,0:T(8,128)(2,1)S(1)} %collective-permute-done.6.refs_7_), channel_id=1, source_target_pairs={{0,2},{2,4},{4,6},{6,7},{7,5},{5,3},{3,1},{1,0},{8,9},{10,8},{12,1... | collective-permute-start | bytes 1769480 | tf_op jit(solution)/shard_map/ppermute | solution.py:50
  28.6 10.6 %collective-permute-start.2 = (bf16[768,384]{1,0:T(8,128)(2,1)S(1)}, bf16[768,384]{1,0:T(8,128)(2,1)S(1)}, u32[]{:S(2)}, u32[]{:S(2)}) collective-permute-start(bf16[768,384]{1,0:T(8,128)(2,1)S(1)} %collective-permute-done.1.refs_2_), channel_id=1, source_target_pairs={{0,8},{8,0},{16,24},{24,16},{1,9},{9,1},{17,25},{25,17},{2,10},{10... | collective-permute-start | bytes 1769480 | tf_op jit(solution)/shard_map/ppermute | solution.py:53
  28.6 10.6 %collective-permute-start.5 = (bf16[768,384]{1,0:T(8,128)(2,1)S(1)}, bf16[768,384]{1,0:T(8,128)(2,1)S(1)}, u32[]{:S(2)}, u32[]{:S(2)}) collective-permute-start(bf16[768,384]{1,0:T(8,128)(2,1)S(1)} %collective-permute-done.4), channel_id=1, source_target_pairs={{0,8},{8,0},{16,24},{24,16},{1,9},{9,1},{17,25},{25,17},{2,10},{10... | collective-permute-start | bytes 1769480 | tf_op jit(solution)/shard_map/ppermute | solution.py:53
  30.8 12.4 %collective-permute-start.10 = (bf16[768,384]{1,0:T(8,128)(2,1)S(1)}, bf16[768,384]{1,0:T(8,128)(2,1)S(1)}, u32[]{:S(2)}, u32[]{:S(2)}) collective-permute-start(bf16[768,384]{1,0:T(8,128)(2,1)S(1)} %collective-permute-done.7), channel_id=1, source_target_pairs={{0,10},{2,12},{4,14},{6,15},{7,13},{5,11},{3,9},{1,8},{8,1},{10,0}... | collective-permute-start | bytes 1769480 | tf_op jit(solution)/shard_map/ppermute | solution.py:50
  32.0 11.2 %collective-permute-start.8 = (bf16[768,384]{1,0:T(8,128)(2,1)S(1)}, bf16[768,384]{1,0:T(8,128)(2,1)S(1)}, u32[]{:S(2)}, u32[]{:S(2)}) collective-permute-start(bf16[768,384]{1,0:T(8,128)(2,1)S(1)} %collective-permute-done.7), channel_id=1, source_target_pairs={{0,8},{8,0},{16,24},{24,16},{1,9},{9,1},{17,25},{25,17},{2,10},{10... | collective-permute-start | bytes 1769480 | tf_op jit(solution)/shard_map/ppermute | solution.py:53
  37.1 12.6 %collective-permute-start.11 = (bf16[768,384]{1,0:T(8,128)(2,1)S(1)}, bf16[768,384]{1,0:T(8,128)(2,1)S(1)}, u32[]{:S(2)}, u32[]{:S(2)}) collective-permute-start(bf16[768,384]{1,0:T(8,128)(2,1)S(1)} %collective-permute-done.9.refs_9_), channel_id=1, source_target_pairs={{0,2},{2,4},{4,6},{6,7},{7,5},{5,3},{3,1},{1,0},{8,9},{10,8},{12,1... | collective-permute-start | bytes 1769480 | tf_op jit(solution)/shard_map/ppermute | solution.py:50
  43.2 1.1 copy-start
  44.3 0.7 copy-start.2
  50.9 2.1 %collective-permute-start.13 = (bf16[768,384]{1,0:T(8,128)(2,1)S(1)}, bf16[768,384]{1,0:T(8,128)(2,1)S(1)}, u32[]{:S(2)}, u32[]{:S(2)}) collective-permute-start(bf16[768,384]{1,0:T(8,128)(2,1)S(1)} %get-tuple-element.22.refs_0_), channel_id=1, source_target_pairs={{0,8},{8,0},{16,24},{24,16},{1,9},{9,1},{17,25},{25,17},{2,10},{10... | collective-permute-start | bytes 1769480 | tf_op jit(solution)/shard_map/ppermute | solution.py:53
  51.0 16.0 %collective-permute-start.12 = (bf16[768,384]{1,0:T(8,128)(2,1)S(1)}, bf16[768,384]{1,0:T(8,128)(2,1)S(1)}, u32[]{:S(2)}, u32[]{:S(2)}) collective-permute-start(bf16[768,384]{1,0:T(8,128)(2,1)S(1)} %get-tuple-element.22.refs_0_), channel_id=1, source_target_pairs={{0,16},{8,24},{16,0},{24,8},{1,17},{9,25},{17,1},{25,9},{2,18},{10... | collective-permute-start | bytes 1769480 | tf_op jit(solution)/shard_map/ppermute | solution.py:53
  66.9 2.0 %collective-permute-start.14 = (bf16[768,384]{1,0:T(8,128)(2,1)S(1)}, bf16[768,384]{1,0:T(8,128)(2,1)S(1)}, u32[]{:S(2)}, u32[]{:S(2)}) collective-permute-start(bf16[768,384]{1,0:T(8,128)(2,1)S(1)} %collective-permute-done.12.refs_0_), channel_id=1, source_target_pairs={{0,8},{8,0},{16,24},{24,16},{1,9},{9,1},{17,25},{25,17},{2,10},{10... | collective-permute-start | bytes 1769480 | tf_op jit(solution)/shard_map/ppermute | solution.py:53
  70.4 3.5 %collective-permute-start.15 = (bf16[768,384]{1,0:T(8,128)(2,1)S(1)}, bf16[768,384]{1,0:T(8,128)(2,1)S(1)}, u32[]{:S(2)}, u32[]{:S(2)}) collective-permute-start(bf16[768,384]{1,0:T(8,128)(2,1)S(1)} %get-tuple-element.28.refs_0_.refs_4_), channel_id=1, source_target_pairs={{0,8},{8,0},{16,24},{24,16},{1,9},{9,1},{17,25},{25,17},{2,10},{10... | collective-permute-start | bytes 1769480 | tf_op jit(solution)/shard_map/ppermute | solution.py:53
  70.6 9.9 %collective-permute-start.21 = (bf16[768,384]{1,0:T(8,128)(2,1)S(1)}, bf16[768,384]{1,0:T(8,128)(2,1)S(1)}, u32[]{:S(2)}, u32[]{:S(2)}) collective-permute-start(bf16[768,384]{1,0:T(8,128)(2,1)S(1)} %get-tuple-element.28.refs_0_.refs_4_), channel_id=1, source_target_pairs={{0,2},{2,4},{4,6},{6,7},{7,5},{5,3},{3,1},{1,0},{8,9},{10,8},{12,1... | collective-permute-start | bytes 1769480 | tf_op jit(solution)/shard_map/ppermute | solution.py:50
  72.4 15.3 %collective-permute-start.16 = (bf16[768,384]{1,0:T(8,128)(2,1)S(1)}, bf16[768,384]{1,0:T(8,128)(2,1)S(1)}, u32[]{:S(2)}, u32[]{:S(2)}) collective-permute-start(bf16[768,384]{1,0:T(8,128)(2,1)S(1)} %get-tuple-element.28.refs_0_.refs_4_), channel_id=1, source_target_pairs={{0,16},{8,24},{16,0},{24,8},{1,17},{9,25},{17,1},{25,9},{2,18},{10... | collective-permute-start | bytes 1769480 | tf_op jit(solution)/shard_map/ppermute | solution.py:53
  73.9 13.8 %collective-permute-start.22 = (bf16[768,384]{1,0:T(8,128)(2,1)S(1)}, bf16[768,384]{1,0:T(8,128)(2,1)S(1)}, u32[]{:S(2)}, u32[]{:S(2)}) collective-permute-start(bf16[768,384]{1,0:T(8,128)(2,1)S(1)} %collective-permute-done.15.refs_1_), channel_id=1, source_target_pairs={{0,2},{2,4},{4,6},{6,7},{7,5},{5,3},{3,1},{1,0},{8,9},{10,8},{12,1... | collective-permute-start | bytes 1769480 | tf_op jit(solution)/shard_map/ppermute | solution.py:50
  80.5 12.6 %collective-permute-start.24 = (bf16[768,384]{1,0:T(8,128)(2,1)S(1)}, bf16[768,384]{1,0:T(8,128)(2,1)S(1)}, u32[]{:S(2)}, u32[]{:S(2)}) collective-permute-start(bf16[768,384]{1,0:T(8,128)(2,1)S(1)} %collective-permute-done.21.refs_5_), channel_id=1, source_target_pairs={{0,2},{2,4},{4,6},{6,7},{7,5},{5,3},{3,1},{1,0},{8,9},{10,8},{12,1... | collective-permute-start | bytes 1769480 | tf_op jit(solution)/shard_map/ppermute | solution.py:50
  87.7 7.2 %collective-permute-start.17 = (bf16[768,384]{1,0:T(8,128)(2,1)S(1)}, bf16[768,384]{1,0:T(8,128)(2,1)S(1)}, u32[]{:S(2)}, u32[]{:S(2)}) collective-permute-start(bf16[768,384]{1,0:T(8,128)(2,1)S(1)} %collective-permute-done.16.refs_0_), channel_id=1, source_target_pairs={{0,8},{8,0},{16,24},{24,16},{1,9},{9,1},{17,25},{25,17},{2,10},{10... | collective-permute-start | bytes 1769480 | tf_op jit(solution)/shard_map/ppermute | solution.py:53
  87.7 11.7 %collective-permute-start.25 = (bf16[768,384]{1,0:T(8,128)(2,1)S(1)}, bf16[768,384]{1,0:T(8,128)(2,1)S(1)}, u32[]{:S(2)}, u32[]{:S(2)}) collective-permute-start(bf16[768,384]{1,0:T(8,128)(2,1)S(1)} %collective-permute-done.22), channel_id=1, source_target_pairs={{0,2},{2,4},{4,6},{6,7},{7,5},{5,3},{3,1},{1,0},{8,9},{10,8},{12,1... | collective-permute-start | bytes 1769480 | tf_op jit(solution)/shard_map/ppermute | solution.py:50
  93.1 12.6 %collective-permute-start.27 = (bf16[768,384]{1,0:T(8,128)(2,1)S(1)}, bf16[768,384]{1,0:T(8,128)(2,1)S(1)}, u32[]{:S(2)}, u32[]{:S(2)}) collective-permute-start(bf16[768,384]{1,0:T(8,128)(2,1)S(1)} %collective-permute-done.24.refs_7_), channel_id=1, source_target_pairs={{0,2},{2,4},{4,6},{6,7},{7,5},{5,3},{3,1},{1,0},{8,9},{10,8},{12,1... | collective-permute-start | bytes 1769480 | tf_op jit(solution)/shard_map/ppermute | solution.py:50
  96.3 14.5 %collective-permute-start.19 = (bf16[768,384]{1,0:T(8,128)(2,1)S(1)}, bf16[768,384]{1,0:T(8,128)(2,1)S(1)}, u32[]{:S(2)}, u32[]{:S(2)}) collective-permute-start(bf16[768,384]{1,0:T(8,128)(2,1)S(1)} %shard_map.75.refs_0_), channel_id=1, source_target_pairs={{0,16},{8,24},{16,0},{24,8},{1,17},{9,25},{17,1},{25,9},{2,18},{10... | collective-permute-start | bytes 1769480 | tf_op jit(solution)/shard_map/ppermute | solution.py:53
  97.8 13.0 %collective-permute-start.23 = (bf16[768,384]{1,0:T(8,128)(2,1)S(1)}, bf16[768,384]{1,0:T(8,128)(2,1)S(1)}, u32[]{:S(2)}, u32[]{:S(2)}) collective-permute-start(bf16[768,384]{1,0:T(8,128)(2,1)S(1)} %collective-permute-done.22), channel_id=1, source_target_pairs={{0,8},{8,0},{16,24},{24,16},{1,9},{9,1},{17,25},{25,17},{2,10},{10... | collective-permute-start | bytes 1769480 | tf_op jit(solution)/shard_map/ppermute | solution.py:53
  99.4 12.6 %collective-permute-start.28 = (bf16[768,384]{1,0:T(8,128)(2,1)S(1)}, bf16[768,384]{1,0:T(8,128)(2,1)S(1)}, u32[]{:S(2)}, u32[]{:S(2)}) collective-permute-start(bf16[768,384]{1,0:T(8,128)(2,1)S(1)} %collective-permute-done.25), channel_id=1, source_target_pairs={{0,2},{2,4},{4,6},{6,7},{7,5},{5,3},{3,1},{1,0},{8,9},{10,8},{12,1... | collective-permute-start | bytes 1769480 | tf_op jit(solution)/shard_map/ppermute | solution.py:50
  101.3 12.2 %collective-permute-start.18 = (bf16[768,384]{1,0:T(8,128)(2,1)S(1)}, bf16[768,384]{1,0:T(8,128)(2,1)S(1)}, u32[]{:S(2)}, u32[]{:S(2)}) collective-permute-start(bf16[768,384]{1,0:T(8,128)(2,1)S(1)} %shard_map.75.refs_0_), channel_id=1, source_target_pairs={{0,8},{8,0},{16,24},{24,16},{1,9},{9,1},{17,25},{25,17},{2,10},{10... | collective-permute-start | bytes 1769480 | tf_op jit(solution)/shard_map/ppermute | solution.py:53
  105.8 7.8 %collective-permute-start.26 = (bf16[768,384]{1,0:T(8,128)(2,1)S(1)}, bf16[768,384]{1,0:T(8,128)(2,1)S(1)}, u32[]{:S(2)}, u32[]{:S(2)}) collective-permute-start(bf16[768,384]{1,0:T(8,128)(2,1)S(1)} %collective-permute-done.25), channel_id=1, source_target_pairs={{0,8},{8,0},{16,24},{24,16},{1,9},{9,1},{17,25},{25,17},{2,10},{10... | collective-permute-start | bytes 1769480 | tf_op jit(solution)/shard_map/ppermute | solution.py:53
  110.8 2.7 %collective-permute-start.20 = (bf16[768,384]{1,0:T(8,128)(2,1)S(1)}, bf16[768,384]{1,0:T(8,128)(2,1)S(1)}, u32[]{:S(2)}, u32[]{:S(2)}) collective-permute-start(bf16[768,384]{1,0:T(8,128)(2,1)S(1)} %collective-permute-done.19.refs_2_), channel_id=1, source_target_pairs={{0,8},{8,0},{16,24},{24,16},{1,9},{9,1},{17,25},{25,17},{2,10},{10... | collective-permute-start | bytes 1769480 | tf_op jit(solution)/shard_map/ppermute | solution.py:53
  110.8 9.9 %collective-permute-start.30 = (bf16[768,384]{1,0:T(8,128)(2,1)S(1)}, bf16[768,384]{1,0:T(8,128)(2,1)S(1)}, u32[]{:S(2)}, u32[]{:S(2)}) collective-permute-start(bf16[768,384]{1,0:T(8,128)(2,1)S(1)} %collective-permute-done.27.refs_9_), channel_id=1, source_target_pairs={{0,2},{2,4},{4,6},{6,7},{7,5},{5,3},{3,1},{1,0},{8,9},{10,8},{12,1... | collective-permute-start | bytes 1769480 | tf_op jit(solution)/shard_map/ppermute | solution.py:50
  112.1 8.6 %collective-permute-start.29 = (bf16[768,384]{1,0:T(8,128)(2,1)S(1)}, bf16[768,384]{1,0:T(8,128)(2,1)S(1)}, u32[]{:S(2)}, u32[]{:S(2)}) collective-permute-start(bf16[768,384]{1,0:T(8,128)(2,1)S(1)} %collective-permute-done.28), channel_id=1, source_target_pairs={{0,8},{8,0},{16,24},{24,16},{1,9},{9,1},{17,25},{25,17},{2,10},{10... | collective-permute-start | bytes 1769480 | tf_op jit(solution)/shard_map/ppermute | solution.py:53
  113.5 7.2 %copy-start.1 = (bf16[768,384]{1,0:T(8,128)(2,1)S(1)}, bf16[768,384]{1,0:T(8,128)(2,1)}, u32[]{:S(2)}) copy-start(bf16[768,384]{1,0:T(8,128)(2,1)} %deriv_ref.1) | copy-start | bytes 1769476
  113.5 7.2 %copy-start.3 = (s32[24]{0:T(128)S(1)}, s32[24]{0:T(128)}, u32[]{:S(2)}) copy-start(s32[24]{0:T(128)} %band_ref.9) | copy-start | bytes 292
  113.5 7.2 %copy-start.4 = (s32[24]{0:T(128)S(1)}, s32[24]{0:T(128)}, u32[]{:S(2)}) copy-start(s32[24]{0:T(128)} %frag_ref.1) | copy-start | bytes 292

commit v6 on v5

--- a/solution.py
+++ b/solution.py
@@ -141,13 +141,17 @@
     total_ref[...] = start_terms(plan, places, band_ref, right_ref, slab_ref, lefts)
 
 
-def square_kernel(plan, band_ref, before_ref, right_ref, _, far_ref, out_ref, slab_ref):
+def square_kernel(plan, band_ref, before_ref, right_ref, _, far_ref, *refs):
+    *out_refs, slab_ref = refs
     first = plan.origin_first(plan.far, True)
     lanes = pl.ds(first, plan.cols_here)
     lay_masked(plan, band_ref, slab_ref, far_ref, plan.row_first(0), first, 0, first)
-    for block, lines in spans(plan):
+    half = plan.block_rows // 2
+    for block in range(plan.block_rows):
+        lines = slice(block * BLK, (block + 1) * BLK)
         total = before_ref[lines, :] + dot(slab_ref[lines, lanes], right_ref[lanes, :])
-        out_ref[lines, :] = masked(plan, band_ref, total, block).astype(jnp.bfloat16)
+        place = slice(block % half * BLK, (block % half + 1) * BLK)
+        out_refs[block // half][place, :] = masked(plan, band_ref, total, block).astype(jnp.bfloat16)
 
 
 def near_kernel(plan, places, *refs):
@@ -165,8 +169,10 @@
 
 def slab_terms(plan, slab_ref, pieces, lines=slice(None)):
     total = None
-    for other, piece in pieces:
-        term = dot(slab_ref[lines, pl.ds(plan.row_first(other), plan.rows_here)], piece[...])
+    for (other, part), piece in pieces:
+        count = piece.shape[0]
+        first = pl.multiple_of(plan.row_first(other) + part * count, count)
+        term = dot(slab_ref[lines, pl.ds(first, count)], piece[...])
         total = term if total is None else total + term
     return total
 
@@ -263,25 +269,30 @@
         [band],
         column + shards,
     )
-    square, slab = call(
-        bind(square_kernel, plan), [block, slab_type], [band], [total, right, slab, far], {3: 1}
+    half_type = jax.ShapeDtypeStruct((plan.rows_here // 2, plan.cols_here), jnp.bfloat16)
+    *square, slab = call(
+        bind(square_kernel, plan), [half_type, half_type, slab_type], [band], [total, right, slab, far], {3: 2}
     )
 
-    crossed = exchange_start(square)
-    partner = plan.across(square, 1)
-    (total,) = call(bind(some_kernel, plan, [0, 1]), [total_type], [], [slab, square, partner])
-    *crossed, total = lax.optimization_barrier((*crossed, total))
-    column = exchange_end([square, partner], crossed)
-    even, odd = list(others)[2::2], list(others)[3::2]
-    (total,) = call(bind(more_kernel, plan, even), [total_type], [], [slab, total] + column[2::2])
-    sign, density = call(
-        bind(sign_kernel, plan, odd), [block, block], [band], [slab, total] + column[3::2]
-    )
+    crossed = [exchange_start(part) for part in square]
+    partner = [plan.across(part, 1) for part in square]
+    keys = [(other, part) for other in (0, 1) for part in (0, 1)]
+    (total,) = call(bind(some_kernel, plan, keys), [total_type], [], [slab] + square + partner)
+    *second, total = lax.optimization_barrier((*crossed[1], total))
+    upper, lower = [[plan.across(value, 1) for value in part] for part in (crossed[0], second)]
+    evens, odds = list(others)[2::2], list(others)[3::2]
+    keys = [(other, 0) for other in evens + odds]
+    (total,) = call(bind(more_kernel, plan, keys), [total_type], [], [slab, total] + crossed[0] + upper)
+    keys = [(other, 1) for other in evens]
+    (total,) = call(bind(more_kernel, plan, keys), [total_type], [], [slab, total] + second)
+    keys = [(other, 1) for other in odds]
+    sign, density = call(bind(sign_kernel, plan, keys), [block, block], [band], [slab, total] + lower)
+    even, odd = [(other, 0) for other in evens], [(other, 0) for other in odds]
 
     partner = plan.across(density, 1)
     shards, far = gather(density, partner, True)
     column = exchange_end([density, partner], exchange_start(density))
-    (total,) = call(bind(some_kernel, plan, [0, 1]), [total_type], [], [slab] + column[:2])
+    (total,) = call(bind(some_kernel, plan, [(0, 0), (1, 0)]), [total_type], [], [slab] + column[:2])
     (total,) = call(bind(more_kernel, plan, even), [total_type], [], [slab, total] + column[2::2])
     (weighted,) = call(bind(weighted_kernel, plan, odd), [block], [band], [slab, total] + column[3::2])
     column = exchange_end([weighted, plan.across(weighted, 1)], exchange_start(weighted))

time: 136 us -> 135 us (level)
  waiting for transfers between devices: 68.1 us -> 65.6 us
    ppermute x17 -> x20, waiting for transfers between devices: 26.3 us -> 23.5 us  [across(): lax.ppermute(value, 'row', [(i, i ^ other) for i in range(self.rows)])]
    pallas_call x11 -> x12, Pallas kernels: 18.6 us -> 19.3 us  [call(): pl.pallas_call(kernel, out_shape=outs, in_specs=[smem] * len(scalars) + [...]
    ppermute x17 -> x20, starting transfers between devices: 9.32 us -> 9.81 us  [across(): lax.ppermute(value, 'row', [(i, i ^ other) for i in range(self.rows)])]
  transfers between devices with their start and end apart: 31 -> 34, of which waited for: 18 -> 19; matrix products, arithmetic and copies ran while one was open for 0% -> 0% of each run, Pallas kernels for 10% -> 11%
where the time goes in v6:
time: 135 us; the launch traced here: 134 us
  waiting for transfers between devices  65.6 us (49%)
  starting transfers between devices  34.5 us (26%)
  Pallas kernels  19.3 us (14%)
  blocking collectives  11.8 us (9%)
  local copies, waits for them, and re-layouts  1.74 us (1%)
    ppermute x14, waiting for transfers between devices, ring(): return lax.ppermute(value, AXES, pairs)  42.1 us
    ppermute x14, starting transfers between devices, ring(): return lax.ppermute(value, AXES, pairs)  24.7 us
    ppermute x20, waiting for transfers between devices, across(): lax.ppermute(value, 'row', [(i, i ^ other) for i in range(self.rows)])  23.5 us
    pallas_call x12, Pallas kernels, call(): pl.pallas_call(kernel, out_shape=outs, in_specs=[smem] * len(scalars) + [...  19.3 us
    all_to_all x1, blocking collectives, body(): pulay_terms = jnp.sum(lax.all_to_all(sums, AXES, 0, 0), axis=0)  11.8 us
    ppermute x20, starting transfers between devices, across(): lax.ppermute(value, 'row', [(i, i ^ other) for i in range(self.rows)])  9.81 us
  transfers between devices with their start and end apart: 34, of which 19 were waited for; matrix products, arithmetic and copies ran while one was open for 0% of the time, Pallas kernels for 11%

profile of v6, /device:TPU:0, one launch (start us, length us, event | category | flops | bytes accessed | tf_op | source)
XLA Modules:
  0.0 134.4 jit_solution(9544823449202913587)
XLA Ops:
  0.6 0.5 collective-permute-start
  1.1 2.6 %collective-permute-start.3 = (bf16[768,384]{1,0:T(8,128)(2,1)}, bf16[768,384]{1,0:T(8,128)(2,1)S(1)}, u32[]{:S(2)}, u32[]{:S(2)}) collective-permute-start(bf16[768,384]{1,0:T(8,128)(2,1)} %refs_4_.1), channel_id=1, source_target_pairs={{0,2},{2,4},{4,6},{6,7},{7,5},{5,3},{3,1},{1,0},{8,9},{10,8},{12,1... | collective-permute-start | bytes 1769480 | tf_op jit(solution)/shard_map/ppermute | solution.py:50
  3.8 0.0 collective-permute-done.refs_1_
  3.8 2.1 %collective-permute-start.4 = (bf16[768,384]{1,0:T(8,128)(2,1)S(1)}, bf16[768,384]{1,0:T(8,128)(2,1)S(1)}, u32[]{:S(2)}, u32[]{:S(2)}) collective-permute-start(bf16[768,384]{1,0:T(8,128)(2,1)S(1)} %collective-permute-done.refs_1_), channel_id=1, source_target_pairs={{0,2},{2,4},{4,6},{6,7},{7,5},{5,3},{3,1},{1,0},{8,9},{10,8},{12,1... | collective-permute-start | bytes 1769480 | tf_op jit(solution)/shard_map/ppermute | solution.py:50
  5.9 5.9 %collective-permute-done.3.refs_5_ = bf16[768,384]{1,0:T(8,128)(2,1)S(1)} collective-permute-done((bf16[768,384]{1,0:T(8,128)(2,1)}, bf16[768,384]{1,0:T(8,128)(2,1)S(1)}, u32[]{:S(2)}, u32[]{:S(2)}) %collective-permute-start.3) | collective-permute-done | bytes 589856 | tf_op jit(solution)/shard_map/ppermute | solution.py:50
  11.8 2.1 %collective-permute-start.6 = (bf16[768,384]{1,0:T(8,128)(2,1)S(1)}, bf16[768,384]{1,0:T(8,128)(2,1)S(1)}, u32[]{:S(2)}, u32[]{:S(2)}) collective-permute-start(bf16[768,384]{1,0:T(8,128)(2,1)S(1)} %collective-permute-done.3.refs_5_), channel_id=1, source_target_pairs={{0,2},{2,4},{4,6},{6,7},{7,5},{5,3},{3,1},{1,0},{8,9},{10,8},{12,1... | collective-permute-start | bytes 1769480 | tf_op jit(solution)/shard_map/ppermute | solution.py:50
  13.9 1.5 %collective-permute-start.1 = (bf16[768,384]{1,0:T(8,128)(2,1)}, bf16[768,384]{1,0:T(8,128)(2,1)S(1)}, u32[]{:S(2)}, u32[]{:S(2)}) collective-permute-start(bf16[768,384]{1,0:T(8,128)(2,1)} %refs_4_.1), channel_id=1, source_target_pairs={{0,16},{8,24},{16,0},{24,8},{1,17},{9,25},{17,1},{25,9},{2,18},{10... | collective-permute-start | bytes 1769480 | tf_op jit(solution)/shard_map/ppermute | solution.py:53
  15.4 2.8 %collective-permute-done.4 = bf16[768,384]{1,0:T(8,128)(2,1)S(1)} collective-permute-done((bf16[768,384]{1,0:T(8,128)(2,1)S(1)}, bf16[768,384]{1,0:T(8,128)(2,1)S(1)}, u32[]{:S(2)}, u32[]{:S(2)}) %collective-permute-start.4) | collective-permute-done | bytes 589856 | tf_op jit(solution)/shard_map/ppermute | solution.py:50
  18.1 2.1 %collective-permute-start.7 = (bf16[768,384]{1,0:T(8,128)(2,1)S(1)}, bf16[768,384]{1,0:T(8,128)(2,1)S(1)}, u32[]{:S(2)}, u32[]{:S(2)}) collective-permute-start(bf16[768,384]{1,0:T(8,128)(2,1)S(1)} %collective-permute-done.4), channel_id=1, source_target_pairs={{0,2},{2,4},{4,6},{6,7},{7,5},{5,3},{3,1},{1,0},{8,9},{10,8},{12,1... | collective-permute-start | bytes 1769480 | tf_op jit(solution)/shard_map/ppermute | solution.py:50
  20.2 4.2 %collective-permute-done.6.refs_7_ = bf16[768,384]{1,0:T(8,128)(2,1)S(1)} collective-permute-done((bf16[768,384]{1,0:T(8,128)(2,1)S(1)}, bf16[768,384]{1,0:T(8,128)(2,1)S(1)}, u32[]{:S(2)}, u32[]{:S(2)}) %collective-permute-start.6) | collective-permute-done | bytes 589856 | tf_op jit(solution)/shard_map/ppermute | solution.py:50
  24.4 2.1 %collective-permute-start.9 = (bf16[768,384]{1,0:T(8,128)(2,1)S(1)}, bf16[768,384]{1,0:T(8,128)(2,1)S(1)}, u32[]{:S(2)}, u32[]{:S(2)}) collective-permute-start(bf16[768,384]{1,0:T(8,128)(2,1)S(1)} %collective-permute-done.6.refs_7_), channel_id=1, source_target_pairs={{0,2},{2,4},{4,6},{6,7},{7,5},{5,3},{3,1},{1,0},{8,9},{10,8},{12,1... | collective-permute-start | bytes 1769480 | tf_op jit(solution)/shard_map/ppermute | solution.py:50
  26.5 2.1 %collective-permute-done.1.refs_2_ = bf16[768,384]{1,0:T(8,128)(2,1)S(1)} collective-permute-done((bf16[768,384]{1,0:T(8,128)(2,1)}, bf16[768,384]{1,0:T(8,128)(2,1)S(1)}, u32[]{:S(2)}, u32[]{:S(2)}) %collective-permute-start.1) | collective-permute-done | bytes 589856 | tf_op jit(solution)/shard_map/ppermute | solution.py:53
  28.6 0.5 collective-permute-start.5
  29.1 1.7 %collective-permute-done.7 = bf16[768,384]{1,0:T(8,128)(2,1)S(1)} collective-permute-done((bf16[768,384]{1,0:T(8,128)(2,1)S(1)}, bf16[768,384]{1,0:T(8,128)(2,1)S(1)}, u32[]{:S(2)}, u32[]{:S(2)}) %collective-permute-start.7) | collective-permute-done | bytes 589856 | tf_op jit(solution)/shard_map/ppermute | solution.py:50
  30.8 1.3 collective-permute-start.10
  32.0 0.9 collective-permute-start.8
  32.9 4.2 %collective-permute-done.9.refs_9_ = bf16[768,384]{1,0:T(8,128)(2,1)S(1)} collective-permute-done((bf16[768,384]{1,0:T(8,128)(2,1)S(1)}, bf16[768,384]{1,0:T(8,128)(2,1)S(1)}, u32[]{:S(2)}, u32[]{:S(2)}) %collective-permute-start.9) | collective-permute-done | bytes 589856 | tf_op jit(solution)/shard_map/ppermute | solution.py:50
  37.1 2.1 %collective-permute-start.11 = (bf16[768,384]{1,0:T(8,128)(2,1)S(1)}, bf16[768,384]{1,0:T(8,128)(2,1)S(1)}, u32[]{:S(2)}, u32[]{:S(2)}) collective-permute-start(bf16[768,384]{1,0:T(8,128)(2,1)S(1)} %collective-permute-done.9.refs_9_), channel_id=1, source_target_pairs={{0,2},{2,4},{4,6},{6,7},{7,5},{5,3},{3,1},{1,0},{8,9},{10,8},{12,1... | collective-permute-start | bytes 1769480 | tf_op jit(solution)/shard_map/ppermute | solution.py:50
  39.2 4.0 %collective-permute-done.10.refs_10_ = bf16[768,384]{1,0:T(8,128)(2,1)S(1)} collective-permute-done((bf16[768,384]{1,0:T(8,128)(2,1)S(1)}, bf16[768,384]{1,0:T(8,128)(2,1)S(1)}, u32[]{:S(2)}, u32[]{:S(2)}) %collective-permute-start.10) | collective-permute-done | bytes 589856 | tf_op jit(solution)/shard_map/ppermute | solution.py:50
  43.2 0.0 collective-permute-done.8.refs_8_
  43.2 1.1 copy-done
  44.3 0.7 copy-done.2
  44.9 4.7 %shard_map.67 = (f32[768,384]{1,0:T(8,128)S(1)}, bf16[3072,384]{1,0:T(8,128)(2,1)S(1)}, bf16[768,3072]{1,0:T(8,128)(2,1)S(1)}) custom-call(s32[24]{0:T(128)S(1)} %copy-done.2, bf16[768,384]{1,0:T(8,128)(2,1)S(1)} %copy-done, bf16[768,384]{1,0:T(8,128)(2,1)S(1)} %collective-permute-done.refs_1_, bf16[768,384]{1,0:T(8,128)(2,1)S(1)} %collective-permute-done.1.refs_2_, ...), custom_call_target="tpu_custom_call" | custom-call | tf_op jit(solution)/shard_map/pallas_call | solution.py:97
  49.6 0.1 collective-permute-done.11.far_ref
  49.7 1.2 shard_map.68
  50.9 2.1 %collective-permute-start.15 = (bf16[384,384]{1,0:T(8,128)(2,1)S(1)}, bf16[384,384]{1,0:T(8,128)(2,1)S(1)}, u32[]{:S(2)}, u32[]{:S(2)}) collective-permute-start(bf16[384,384]{1,0:T(8,128)(2,1)S(1)} %get-tuple-element.24.refs_0_), channel_id=1, source_target_pairs={{0,16},{8,24},{16,0},{24,8},{1,17},{9,25},{17,1},{25,9},{2,18},{10... | collective-permute-start | bytes 884744 | tf_op jit(solution)/shard_map/ppermute | solution.py:53
  52.9 0.0 collective-permute-start.14
  52.9 0.5 collective-permute-start.13
  53.5 0.1 collective-permute-start.12
  53.5 7.3 %collective-permute-done.15.refs_0_ = bf16[384,384]{1,0:T(8,128)(2,1)S(1)} collective-permute-done((bf16[384,384]{1,0:T(8,128)(2,1)S(1)}, bf16[384,384]{1,0:T(8,128)(2,1)S(1)}, u32[]{:S(2)}, u32[]{:S(2)}) %collective-permute-start.15) | collective-permute-done | bytes 294944 | tf_op jit(solution)/shard_map/ppermute | solution.py:53
  60.8 0.0 collective-permute-start.16
  60.8 1.6 %shard_map.69.before_ref = f32[768,384]{1,0:T(8,128)S(1)} custom-call(bf16[768,3072]{1,0:T(8,128)(2,1)S(1)} %get-tuple-element.22.slab_ref, bf16[384,384]{1,0:T(8,128)(2,1)S(1)} %get-tuple-element.24.refs_0_, bf16[384,384]{1,0:T(8,128)(2,1)S(1)} %get-tuple-element.23.refs_1_, bf16[384,384]{1,0:T(8,128)(2,1)S(1)} %collective-permute-done.13.refs_2_, ...), custom_call_target="tpu_custom_call" | custom-call | tf_op jit(solution)/shard_map/pallas_call | solution.py:97
  62.4 3.9 %collective-permute-done.12.refs_0_ = bf16[384,384]{1,0:T(8,128)(2,1)S(1)} collective-permute-done((bf16[384,384]{1,0:T(8,128)(2,1)S(1)}, bf16[384,384]{1,0:T(8,128)(2,1)S(1)}, u32[]{:S(2)}, u32[]{:S(2)}) %collective-permute-start.12) | collective-permute-done | bytes 294944 | tf_op jit(solution)/shard_map/ppermute | solution.py:53
  66.4 0.9 shard_map.70.before_ref
  67.2 0.5 shard_map.71.total_ref
  67.8 0.2 collective-permute-done.17.refs_0_
  67.9 1.3 shard_map.72
  69.3 0.4 collective-permute-start.18
  69.7 1.8 %collective-permute-start.24 = (bf16[768,384]{1,0:T(8,128)(2,1)S(1)}, bf16[768,384]{1,0:T(8,128)(2,1)S(1)}, u32[]{:S(2)}, u32[]{:S(2)}) collective-permute-start(bf16[768,384]{1,0:T(8,128)(2,1)S(1)} %get-tuple-element.30.refs_0_.refs_4_), channel_id=1, source_target_pairs={{0,2},{2,4},{4,6},{6,7},{7,5},{5,3},{3,1},{1,0},{8,9},{10,8},{12,1... | collective-permute-start | bytes 1769480 | tf_op jit(solution)/shard_map/ppermute | solution.py:50
  71.5 1.5 %collective-permute-start.19 = (bf16[768,384]{1,0:T(8,128)(2,1)S(1)}, bf16[768,384]{1,0:T(8,128)(2,1)S(1)}, u32[]{:S(2)}, u32[]{:S(2)}) collective-permute-start(bf16[768,384]{1,0:T(8,128)(2,1)S(1)} %get-tuple-element.30.refs_0_.refs_4_), channel_id=1, source_target_pairs={{0,16},{8,24},{16,0},{24,8},{1,17},{9,25},{17,1},{25,9},{2,18},{10... | collective-permute-start | bytes 1769480 | tf_op jit(solution)/shard_map/ppermute | solution.py:53
  73.0 1.6 %collective-permute-start.25 = (bf16[768,384]{1,0:T(8,128)(2,1)S(1)}, bf16[768,384]{1,0:T(8,128)(2,1)S(1)}, u32[]{:S(2)}, u32[]{:S(2)}) collective-permute-start(bf16[768,384]{1,0:T(8,128)(2,1)S(1)} %collective-permute-done.18.refs_1_), channel_id=1, source_target_pairs={{0,2},{2,4},{4,6},{6,7},{7,5},{5,3},{3,1},{1,0},{8,9},{10,8},{12,1... | collective-permute-start | bytes 1769480 | tf_op jit(solution)/shard_map/ppermute | solution.py:50
  74.6 5.0 %collective-permute-done.24.refs_5_ = bf16[768,384]{1,0:T(8,128)(2,1)S(1)} collective-permute-done((bf16[768,384]{1,0:T(8,128)(2,1)S(1)}, bf16[768,384]{1,0:T(8,128)(2,1)S(1)}, u32[]{:S(2)}, u32[]{:S(2)}) %collective-permute-start.24) | collective-permute-done | bytes 589856 | tf_op jit(solution)/shard_map/ppermute | solution.py:50
  79.6 1.8 %collective-permute-start.27 = (bf16[768,384]{1,0:T(8,128)(2,1)S(1)}, bf16[768,384]{1,0:T(8,128)(2,1)S(1)}, u32[]{:S(2)}, u32[]{:S(2)}) collective-permute-start(bf16[768,384]{1,0:T(8,128)(2,1)S(1)} %collective-permute-done.24.refs_5_), channel_id=1, source_target_pairs={{0,2},{2,4},{4,6},{6,7},{7,5},{5,3},{3,1},{1,0},{8,9},{10,8},{12,1... | collective-permute-start | bytes 1769480 | tf_op jit(solution)/shard_map/ppermute | solution.py:50
  81.4 5.2 %collective-permute-done.19.refs_0_ = bf16[768,384]{1,0:T(8,128)(2,1)S(1)} collective-permute-done((bf16[768,384]{1,0:T(8,128)(2,1)S(1)}, bf16[768,384]{1,0:T(8,128)(2,1)S(1)}, u32[]{:S(2)}, u32[]{:S(2)}) %collective-permute-start.19) | collective-permute-done | bytes 589856 | tf_op jit(solution)/shard_map/ppermute | solution.py:53
  86.6 1.1 collective-permute-start.28
  87.7 1.4 %shard_map.74.before_ref = f32[768,384]{1,0:T(8,128)S(1)} custom-call(bf16[768,3072]{1,0:T(8,128)(2,1)S(1)} %get-tuple-element.22.slab_ref, bf16[768,384]{1,0:T(8,128)(2,1)S(1)} %get-tuple-element.30.refs_0_.refs_4_, bf16[768,384]{1,0:T(8,128)(2,1)S(1)} %collective-permute-done.18.refs_1_), custom_call_target="tpu_custom_call" | custom-call | tf_op jit(solution)/shard_map/pallas_call | solution.py:97
  89.1 0.8 shard_map.75.before_ref
  89.9 2.3 %collective-permute-done.27.refs_7_ = bf16[768,384]{1,0:T(8,128)(2,1)S(1)} collective-permute-done((bf16[768,384]{1,0:T(8,128)(2,1)S(1)}, bf16[768,384]{1,0:T(8,128)(2,1)S(1)}, u32[]{:S(2)}, u32[]{:S(2)}) %collective-permute-start.27) | collective-permute-done | bytes 589856 | tf_op jit(solution)/shard_map/ppermute | solution.py:50
  92.2 1.8 %collective-permute-start.30 = (bf16[768,384]{1,0:T(8,128)(2,1)S(1)}, bf16[768,384]{1,0:T(8,128)(2,1)S(1)}, u32[]{:S(2)}, u32[]{:S(2)}) collective-permute-start(bf16[768,384]{1,0:T(8,128)(2,1)S(1)} %collective-permute-done.27.refs_7_), channel_id=1, source_target_pairs={{0,2},{2,4},{4,6},{6,7},{7,5},{5,3},{3,1},{1,0},{8,9},{10,8},{12,1... | collective-permute-start | bytes 1769480 | tf_op jit(solution)/shard_map/ppermute | solution.py:50
  94.0 1.3 %shard_map.76.refs_0_ = bf16[768,384]{1,0:T(8,128)(2,1)S(1)} custom-call(s32[24]{0:T(128)S(1)} %copy-done.2, bf16[768,3072]{1,0:T(8,128)(2,1)S(1)} %get-tuple-element.22.slab_ref, f32[768,384]{1,0:T(8,128)S(1)} %shard_map.75.before_ref, bf16[768,384]{1,0:T(8,128)(2,1)S(1)} %collective-permute-done.20.refs_0_), custom_call_target="tpu_custom_call" | custom-call | tf_op jit(solution)/shard_map/pallas_call | solution.py:97
  95.4 1.5 %collective-permute-start.22 = (bf16[768,384]{1,0:T(8,128)(2,1)S(1)}, bf16[768,384]{1,0:T(8,128)(2,1)S(1)}, u32[]{:S(2)}, u32[]{:S(2)}) collective-permute-start(bf16[768,384]{1,0:T(8,128)(2,1)S(1)} %shard_map.76.refs_0_), channel_id=1, source_target_pairs={{0,16},{8,24},{16,0},{24,8},{1,17},{9,25},{17,1},{25,9},{2,18},{10... | collective-permute-start | bytes 1769480 | tf_op jit(solution)/shard_map/ppermute | solution.py:53
  96.9 1.6 %collective-permute-done.28 = bf16[768,384]{1,0:T(8,128)(2,1)S(1)} collective-permute-done((bf16[768,384]{1,0:T(8,128)(2,1)S(1)}, bf16[768,384]{1,0:T(8,128)(2,1)S(1)}, u32[]{:S(2)}, u32[]{:S(2)}) %collective-permute-start.28) | collective-permute-done | bytes 589856 | tf_op jit(solution)/shard_map/ppermute | solution.py:50
  98.5 1.8 %collective-permute-start.31 = (bf16[768,384]{1,0:T(8,128)(2,1)S(1)}, bf16[768,384]{1,0:T(8,128)(2,1)S(1)}, u32[]{:S(2)}, u32[]{:S(2)}) collective-permute-start(bf16[768,384]{1,0:T(8,128)(2,1)S(1)} %collective-permute-done.28), channel_id=1, source_target_pairs={{0,2},{2,4},{4,6},{6,7},{7,5},{5,3},{3,1},{1,0},{8,9},{10,8},{12,1... | collective-permute-start | bytes 1769480 | tf_op jit(solution)/shard_map/ppermute | solution.py:50
  100.4 4.5 %collective-permute-done.30.refs_9_ = bf16[768,384]{1,0:T(8,128)(2,1)S(1)} collective-permute-done((bf16[768,384]{1,0:T(8,128)(2,1)S(1)}, bf16[768,384]{1,0:T(8,128)(2,1)S(1)}, u32[]{:S(2)}, u32[]{:S(2)}) %collective-permute-start.30) | collective-permute-done | bytes 589856 | tf_op jit(solution)/shard_map/ppermute | solution.py:50
  104.9 4.8 %collective-permute-done.22.refs_2_ = bf16[768,384]{1,0:T(8,128)(2,1)S(1)} collective-permute-done((bf16[768,384]{1,0:T(8,128)(2,1)S(1)}, bf16[768,384]{1,0:T(8,128)(2,1)S(1)}, u32[]{:S(2)}, u32[]{:S(2)}) %collective-permute-start.22) | collective-permute-done | bytes 589856 | tf_op jit(solution)/shard_map/ppermute | solution.py:53
  109.7 0.3 collective-permute-start.33
  110.0 1.1 collective-permute-done.31
  111.2 0.3 collective-permute-start.32
  111.5 0.9 shard_map.73
  112.4 2.5 %shard_map.77 = (f32[768,384]{1,0:T(8,128)S(1)}, bf16[3072,384]{1,0:T(8,128)(2,1)S(1)}) custom-call(bf16[768,384]{1,0:T(8,128)(2,1)S(1)} %shard_map.76.refs_0_, bf16[768,384]{1,0:T(8,128)(2,1)S(1)} %collective-permute-done.21.refs_1_, bf16[768,384]{1,0:T(8,128)(2,1)S(1)} %collective-permute-done.22.refs_2_, ...), custom_call_target="tpu_custom_call" | custom-call | tf_op jit(solution)/shard_map/pallas_call | solution.py:97
  114.9 4.7 %collective-permute-done.33.refs_1_ = bf16[768,384]{1,0:T(8,128)(2,1)S(1)} collective-permute-done((bf16[768,384]{1,0:T(8,128)(2,1)S(1)}, bf16[768,384]{1,0:T(8,128)(2,1)S(1)}, u32[]{:S(2)}, u32[]{:S(2)}) %collective-permute-start.33) | collective-permute-done | bytes 589856 | tf_op jit(solution)/shard_map/ppermute | solution.py:50
  119.6 2.3 %shard_map.78 = (bf16[768,384]{1,0:T(8,128)(2,1)}, f32[16,128]{1,0:T(8,128)S(1)}) custom-call(s32[24]{0:T(128)S(1)} %copy-done.3, s32[24]{0:T(128)S(1)} %copy-done.4, f32[768,384]{1,0:T(8,128)S(1)} %get-tuple-element.31.total_ref, bf16[3072,384]{1,0:T(8,128)(2,1)S(1)} %get-tuple-element.32.right_ref, bf16[768,384]{1,0:T(8,128)(2,1)S(1)} %copy-done.1, ...), custom_call_target="tpu_custom_call" | custom-call | tf_op jit(solution)/shard_map/pallas_call | solution.py:97
  121.9 11.8 %all_to_all.5 = f32[32,2,128]{2,1,0:T(2,128)S(1)} all-to-all(f32[32,2,128]{2,1,0:T(2,128)S(1)} %bitcast.3), channel_id=1, replica_groups=mesh['row'=4,'col'=8] {'row','col'}, dimensions={0} | all-to-all | bytes 65536 | tf_op jit(solution)/shard_map/all_to_all | solution.py:313
  133.8 0.6 reduce_sum.9
  (29 shorter events, 0.1 us)
Async XLA Ops:
  0.6 3.2 %collective-permute-start = (bf16[768,384]{1,0:T(8,128)(2,1)}, bf16[768,384]{1,0:T(8,128)(2,1)S(1)}, u32[]{:S(2)}, u32[]{:S(2)}) collective-permute-start(bf16[768,384]{1,0:T(8,128)(2,1)} %refs_4_.1), channel_id=1, source_target_pairs={{0,8},{8,0},{16,24},{24,16},{1,9},{9,1},{17,25},{25,17},{2,10},{10... | collective-permute-start | bytes 1769480 | tf_op jit(solution)/shard_map/ppermute | solution.py:53
  1.1 10.7 %collective-permute-start.3 = (bf16[768,384]{1,0:T(8,128)(2,1)}, bf16[768,384]{1,0:T(8,128)(2,1)S(1)}, u32[]{:S(2)}, u32[]{:S(2)}) collective-permute-start(bf16[768,384]{1,0:T(8,128)(2,1)} %refs_4_.1), channel_id=1, source_target_pairs={{0,2},{2,4},{4,6},{6,7},{7,5},{5,3},{3,1},{1,0},{8,9},{10,8},{12,1... | collective-permute-start | bytes 1769480 | tf_op jit(solution)/shard_map/ppermute | solution.py:50
  3.8 14.3 %collective-permute-start.4 = (bf16[768,384]{1,0:T(8,128)(2,1)S(1)}, bf16[768,384]{1,0:T(8,128)(2,1)S(1)}, u32[]{:S(2)}, u32[]{:S(2)}) collective-permute-start(bf16[768,384]{1,0:T(8,128)(2,1)S(1)} %collective-permute-done.refs_1_), channel_id=1, source_target_pairs={{0,2},{2,4},{4,6},{6,7},{7,5},{5,3},{3,1},{1,0},{8,9},{10,8},{12,1... | collective-permute-start | bytes 1769480 | tf_op jit(solution)/shard_map/ppermute | solution.py:50
  11.8 12.6 %collective-permute-start.6 = (bf16[768,384]{1,0:T(8,128)(2,1)S(1)}, bf16[768,384]{1,0:T(8,128)(2,1)S(1)}, u32[]{:S(2)}, u32[]{:S(2)}) collective-permute-start(bf16[768,384]{1,0:T(8,128)(2,1)S(1)} %collective-permute-done.3.refs_5_), channel_id=1, source_target_pairs={{0,2},{2,4},{4,6},{6,7},{7,5},{5,3},{3,1},{1,0},{8,9},{10,8},{12,1... | collective-permute-start | bytes 1769480 | tf_op jit(solution)/shard_map/ppermute | solution.py:50
  13.9 14.7 %collective-permute-start.1 = (bf16[768,384]{1,0:T(8,128)(2,1)}, bf16[768,384]{1,0:T(8,128)(2,1)S(1)}, u32[]{:S(2)}, u32[]{:S(2)}) collective-permute-start(bf16[768,384]{1,0:T(8,128)(2,1)} %refs_4_.1), channel_id=1, source_target_pairs={{0,16},{8,24},{16,0},{24,8},{1,17},{9,25},{17,1},{25,9},{2,18},{10... | collective-permute-start | bytes 1769480 | tf_op jit(solution)/shard_map/ppermute | solution.py:53
  18.1 12.6 %collective-permute-start.7 = (bf16[768,384]{1,0:T(8,128)(2,1)S(1)}, bf16[768,384]{1,0:T(8,128)(2,1)S(1)}, u32[]{:S(2)}, u32[]{:S(2)}) collective-permute-start(bf16[768,384]{1,0:T(8,128)(2,1)S(1)} %collective-permute-done.4), channel_id=1, source_target_pairs={{0,2},{2,4},{4,6},{6,7},{7,5},{5,3},{3,1},{1,0},{8,9},{10,8},{12,1... | collective-permute-start | bytes 1769480 | tf_op jit(solution)/shard_map/ppermute | solution.py:50
  24.4 12.6 %collective-permute-start.9 = (bf16[768,384]{1,0:T(8,128)(2,1)S(1)}, bf16[768,384]{1,0:T(8,128)(2,1)S(1)}, u32[]{:S(2)}, u32[]{:S(2)}) collective-permute-start(bf16[768,384]{1,0:T(8,128)(2,1)S(1)} %collective-permute-done.6.refs_7_), channel_id=1, source_target_pairs={{0,2},{2,4},{4,6},{6,7},{7,5},{5,3},{3,1},{1,0},{8,9},{10,8},{12,1... | collective-permute-start | bytes 1769480 | tf_op jit(solution)/shard_map/ppermute | solution.py:50
  28.6 10.6 %collective-permute-start.2 = (bf16[768,384]{1,0:T(8,128)(2,1)S(1)}, bf16[768,384]{1,0:T(8,128)(2,1)S(1)}, u32[]{:S(2)}, u32[]{:S(2)}) collective-permute-start(bf16[768,384]{1,0:T(8,128)(2,1)S(1)} %collective-permute-done.1.refs_2_), channel_id=1, source_target_pairs={{0,8},{8,0},{16,24},{24,16},{1,9},{9,1},{17,25},{25,17},{2,10},{10... | collective-permute-start | bytes 1769480 | tf_op jit(solution)/shard_map/ppermute | solution.py:53
  28.6 10.6 %collective-permute-start.5 = (bf16[768,384]{1,0:T(8,128)(2,1)S(1)}, bf16[768,384]{1,0:T(8,128)(2,1)S(1)}, u32[]{:S(2)}, u32[]{:S(2)}) collective-permute-start(bf16[768,384]{1,0:T(8,128)(2,1)S(1)} %collective-permute-done.4), channel_id=1, source_target_pairs={{0,8},{8,0},{16,24},{24,16},{1,9},{9,1},{17,25},{25,17},{2,10},{10... | collective-permute-start | bytes 1769480 | tf_op jit(solution)/shard_map/ppermute | solution.py:53
  30.8 12.4 %collective-permute-start.10 = (bf16[768,384]{1,0:T(8,128)(2,1)S(1)}, bf16[768,384]{1,0:T(8,128)(2,1)S(1)}, u32[]{:S(2)}, u32[]{:S(2)}) collective-permute-start(bf16[768,384]{1,0:T(8,128)(2,1)S(1)} %collective-permute-done.7), channel_id=1, source_target_pairs={{0,10},{2,12},{4,14},{6,15},{7,13},{5,11},{3,9},{1,8},{8,1},{10,0}... | collective-permute-start | bytes 1769480 | tf_op jit(solution)/shard_map/ppermute | solution.py:50
  32.0 11.2 %collective-permute-start.8 = (bf16[768,384]{1,0:T(8,128)(2,1)S(1)}, bf16[768,384]{1,0:T(8,128)(2,1)S(1)}, u32[]{:S(2)}, u32[]{:S(2)}) collective-permute-start(bf16[768,384]{1,0:T(8,128)(2,1)S(1)} %collective-permute-done.7), channel_id=1, source_target_pairs={{0,8},{8,0},{16,24},{24,16},{1,9},{9,1},{17,25},{25,17},{2,10},{10... | collective-permute-start | bytes 1769480 | tf_op jit(solution)/shard_map/ppermute | solution.py:53
  37.1 12.6 %collective-permute-start.11 = (bf16[768,384]{1,0:T(8,128)(2,1)S(1)}, bf16[768,384]{1,0:T(8,128)(2,1)S(1)}, u32[]{:S(2)}, u32[]{:S(2)}) collective-permute-start(bf16[768,384]{1,0:T(8,128)(2,1)S(1)} %collective-permute-done.9.refs_9_), channel_id=1, source_target_pairs={{0,2},{2,4},{4,6},{6,7},{7,5},{5,3},{3,1},{1,0},{8,9},{10,8},{12,1... | collective-permute-start | bytes 1769480 | tf_op jit(solution)/shard_map/ppermute | solution.py:50
  43.2 1.1 copy-start
  44.3 0.7 copy-start.2
  50.9 9.9 %collective-permute-start.15 = (bf16[384,384]{1,0:T(8,128)(2,1)S(1)}, bf16[384,384]{1,0:T(8,128)(2,1)S(1)}, u32[]{:S(2)}, u32[]{:S(2)}) collective-permute-start(bf16[384,384]{1,0:T(8,128)(2,1)S(1)} %get-tuple-element.24.refs_0_), channel_id=1, source_target_pairs={{0,16},{8,24},{16,0},{24,8},{1,17},{9,25},{17,1},{25,9},{2,18},{10... | collective-permute-start | bytes 884744 | tf_op jit(solution)/shard_map/ppermute | solution.py:53
  52.9 7.9 %collective-permute-start.14 = (bf16[384,384]{1,0:T(8,128)(2,1)S(1)}, bf16[384,384]{1,0:T(8,128)(2,1)S(1)}, u32[]{:S(2)}, u32[]{:S(2)}) collective-permute-start(bf16[384,384]{1,0:T(8,128)(2,1)S(1)} %get-tuple-element.23.refs_1_), channel_id=1, source_target_pairs={{0,8},{8,0},{16,24},{24,16},{1,9},{9,1},{17,25},{25,17},{2,10},{10... | collective-permute-start | bytes 884744 | tf_op jit(solution)/shard_map/ppermute | solution.py:53
  52.9 7.9 %collective-permute-start.13 = (bf16[384,384]{1,0:T(8,128)(2,1)S(1)}, bf16[384,384]{1,0:T(8,128)(2,1)S(1)}, u32[]{:S(2)}, u32[]{:S(2)}) collective-permute-start(bf16[384,384]{1,0:T(8,128)(2,1)S(1)} %get-tuple-element.24.refs_0_), channel_id=1, source_target_pairs={{0,8},{8,0},{16,24},{24,16},{1,9},{9,1},{17,25},{25,17},{2,10},{10... | collective-permute-start | bytes 884744 | tf_op jit(solution)/shard_map/ppermute | solution.py:53
  53.5 12.9 %collective-permute-start.12 = (bf16[384,384]{1,0:T(8,128)(2,1)S(1)}, bf16[384,384]{1,0:T(8,128)(2,1)S(1)}, u32[]{:S(2)}, u32[]{:S(2)}) collective-permute-start(bf16[384,384]{1,0:T(8,128)(2,1)S(1)} %get-tuple-element.23.refs_1_), channel_id=1, source_target_pairs={{0,16},{8,24},{16,0},{24,8},{1,17},{9,25},{17,1},{25,9},{2,18},{10... | collective-permute-start | bytes 884744 | tf_op jit(solution)/shard_map/ppermute | solution.py:53
  60.8 5.6 %collective-permute-start.16 = (bf16[384,384]{1,0:T(8,128)(2,1)S(1)}, bf16[384,384]{1,0:T(8,128)(2,1)S(1)}, u32[]{:S(2)}, u32[]{:S(2)}) collective-permute-start(bf16[384,384]{1,0:T(8,128)(2,1)S(1)} %collective-permute-done.15.refs_0_), channel_id=1, source_target_pairs={{0,8},{8,0},{16,24},{24,16},{1,9},{9,1},{17,25},{25,17},{2,10},{10... | collective-permute-start | bytes 884744 | tf_op jit(solution)/shard_map/ppermute | solution.py:53
  66.4 1.6 %collective-permute-start.17 = (bf16[384,384]{1,0:T(8,128)(2,1)S(1)}, bf16[384,384]{1,0:T(8,128)(2,1)S(1)}, u32[]{:S(2)}, u32[]{:S(2)}) collective-permute-start(bf16[384,384]{1,0:T(8,128)(2,1)S(1)} %collective-permute-done.12.refs_0_), channel_id=1, source_target_pairs={{0,8},{8,0},{16,24},{24,16},{1,9},{9,1},{17,25},{25,17},{2,10},{10... | collective-permute-start | bytes 884744 | tf_op jit(solution)/shard_map/ppermute | solution.py:53
  69.3 3.7 %collective-permute-start.18 = (bf16[768,384]{1,0:T(8,128)(2,1)S(1)}, bf16[768,384]{1,0:T(8,128)(2,1)S(1)}, u32[]{:S(2)}, u32[]{:S(2)}) collective-permute-start(bf16[768,384]{1,0:T(8,128)(2,1)S(1)} %get-tuple-element.30.refs_0_.refs_4_), channel_id=1, source_target_pairs={{0,8},{8,0},{16,24},{24,16},{1,9},{9,1},{17,25},{25,17},{2,10},{10... | collective-permute-start | bytes 1769480 | tf_op jit(solution)/shard_map/ppermute | solution.py:53
  69.7 9.9 %collective-permute-start.24 = (bf16[768,384]{1,0:T(8,128)(2,1)S(1)}, bf16[768,384]{1,0:T(8,128)(2,1)S(1)}, u32[]{:S(2)}, u32[]{:S(2)}) collective-permute-start(bf16[768,384]{1,0:T(8,128)(2,1)S(1)} %get-tuple-element.30.refs_0_.refs_4_), channel_id=1, source_target_pairs={{0,2},{2,4},{4,6},{6,7},{7,5},{5,3},{3,1},{1,0},{8,9},{10,8},{12,1... | collective-permute-start | bytes 1769480 | tf_op jit(solution)/shard_map/ppermute | solution.py:50
  71.5 15.1 %collective-permute-start.19 = (bf16[768,384]{1,0:T(8,128)(2,1)S(1)}, bf16[768,384]{1,0:T(8,128)(2,1)S(1)}, u32[]{:S(2)}, u32[]{:S(2)}) collective-permute-start(bf16[768,384]{1,0:T(8,128)(2,1)S(1)} %get-tuple-element.30.refs_0_.refs_4_), channel_id=1, source_target_pairs={{0,16},{8,24},{16,0},{24,8},{1,17},{9,25},{17,1},{25,9},{2,18},{10... | collective-permute-start | bytes 1769480 | tf_op jit(solution)/shard_map/ppermute | solution.py:53
  73.0 13.6 %collective-permute-start.25 = (bf16[768,384]{1,0:T(8,128)(2,1)S(1)}, bf16[768,384]{1,0:T(8,128)(2,1)S(1)}, u32[]{:S(2)}, u32[]{:S(2)}) collective-permute-start(bf16[768,384]{1,0:T(8,128)(2,1)S(1)} %collective-permute-done.18.refs_1_), channel_id=1, source_target_pairs={{0,2},{2,4},{4,6},{6,7},{7,5},{5,3},{3,1},{1,0},{8,9},{10,8},{12,1... | collective-permute-start | bytes 1769480 | tf_op jit(solution)/shard_map/ppermute | solution.py:50
  79.6 12.6 %collective-permute-start.27 = (bf16[768,384]{1,0:T(8,128)(2,1)S(1)}, bf16[768,384]{1,0:T(8,128)(2,1)S(1)}, u32[]{:S(2)}, u32[]{:S(2)}) collective-permute-start(bf16[768,384]{1,0:T(8,128)(2,1)S(1)} %collective-permute-done.24.refs_5_), channel_id=1, source_target_pairs={{0,2},{2,4},{4,6},{6,7},{7,5},{5,3},{3,1},{1,0},{8,9},{10,8},{12,1... | collective-permute-start | bytes 1769480 | tf_op jit(solution)/shard_map/ppermute | solution.py:50
  86.6 7.4 %collective-permute-start.20 = (bf16[768,384]{1,0:T(8,128)(2,1)S(1)}, bf16[768,384]{1,0:T(8,128)(2,1)S(1)}, u32[]{:S(2)}, u32[]{:S(2)}) collective-permute-start(bf16[768,384]{1,0:T(8,128)(2,1)S(1)} %collective-permute-done.19.refs_0_), channel_id=1, source_target_pairs={{0,8},{8,0},{16,24},{24,16},{1,9},{9,1},{17,25},{25,17},{2,10},{10... | collective-permute-start | bytes 1769480 | tf_op jit(solution)/shard_map/ppermute | solution.py:53
  86.6 11.9 %collective-permute-start.28 = (bf16[768,384]{1,0:T(8,128)(2,1)S(1)}, bf16[768,384]{1,0:T(8,128)(2,1)S(1)}, u32[]{:S(2)}, u32[]{:S(2)}) collective-permute-start(bf16[768,384]{1,0:T(8,128)(2,1)S(1)} %collective-permute-done.25), channel_id=1, source_target_pairs={{0,2},{2,4},{4,6},{6,7},{7,5},{5,3},{3,1},{1,0},{8,9},{10,8},{12,1... | collective-permute-start | bytes 1769480 | tf_op jit(solution)/shard_map/ppermute | solution.py:50
  92.2 12.6 %collective-permute-start.30 = (bf16[768,384]{1,0:T(8,128)(2,1)S(1)}, bf16[768,384]{1,0:T(8,128)(2,1)S(1)}, u32[]{:S(2)}, u32[]{:S(2)}) collective-permute-start(bf16[768,384]{1,0:T(8,128)(2,1)S(1)} %collective-permute-done.27.refs_7_), channel_id=1, source_target_pairs={{0,2},{2,4},{4,6},{6,7},{7,5},{5,3},{3,1},{1,0},{8,9},{10,8},{12,1... | collective-permute-start | bytes 1769480 | tf_op jit(solution)/shard_map/ppermute | solution.py:50
  95.4 14.3 %collective-permute-start.22 = (bf16[768,384]{1,0:T(8,128)(2,1)S(1)}, bf16[768,384]{1,0:T(8,128)(2,1)S(1)}, u32[]{:S(2)}, u32[]{:S(2)}) collective-permute-start(bf16[768,384]{1,0:T(8,128)(2,1)S(1)} %shard_map.76.refs_0_), channel_id=1, source_target_pairs={{0,16},{8,24},{16,0},{24,8},{1,17},{9,25},{17,1},{25,9},{2,18},{10... | collective-permute-start | bytes 1769480 | tf_op jit(solution)/shard_map/ppermute | solution.py:53
  96.9 12.8 %collective-permute-start.26 = (bf16[768,384]{1,0:T(8,128)(2,1)S(1)}, bf16[768,384]{1,0:T(8,128)(2,1)S(1)}, u32[]{:S(2)}, u32[]{:S(2)}) collective-permute-start(bf16[768,384]{1,0:T(8,128)(2,1)S(1)} %collective-permute-done.25), channel_id=1, source_target_pairs={{0,8},{8,0},{16,24},{24,16},{1,9},{9,1},{17,25},{25,17},{2,10},{10... | collective-permute-start | bytes 1769480 | tf_op jit(solution)/shard_map/ppermute | solution.py:53
  98.5 12.6 %collective-permute-start.31 = (bf16[768,384]{1,0:T(8,128)(2,1)S(1)}, bf16[768,384]{1,0:T(8,128)(2,1)S(1)}, u32[]{:S(2)}, u32[]{:S(2)}) collective-permute-start(bf16[768,384]{1,0:T(8,128)(2,1)S(1)} %collective-permute-done.28), channel_id=1, source_target_pairs={{0,2},{2,4},{4,6},{6,7},{7,5},{5,3},{3,1},{1,0},{8,9},{10,8},{12,1... | collective-permute-start | bytes 1769480 | tf_op jit(solution)/shard_map/ppermute | solution.py:50
  100.3 12.0 %collective-permute-start.21 = (bf16[768,384]{1,0:T(8,128)(2,1)S(1)}, bf16[768,384]{1,0:T(8,128)(2,1)S(1)}, u32[]{:S(2)}, u32[]{:S(2)}) collective-permute-start(bf16[768,384]{1,0:T(8,128)(2,1)S(1)} %shard_map.76.refs_0_), channel_id=1, source_target_pairs={{0,8},{8,0},{16,24},{24,16},{1,9},{9,1},{17,25},{25,17},{2,10},{10... | collective-permute-start | bytes 1769480 | tf_op jit(solution)/shard_map/ppermute | solution.py:53
  104.8 7.5 %collective-permute-start.29 = (bf16[768,384]{1,0:T(8,128)(2,1)S(1)}, bf16[768,384]{1,0:T(8,128)(2,1)S(1)}, u32[]{:S(2)}, u32[]{:S(2)}) collective-permute-start(bf16[768,384]{1,0:T(8,128)(2,1)S(1)} %collective-permute-done.28), channel_id=1, source_target_pairs={{0,8},{8,0},{16,24},{24,16},{1,9},{9,1},{17,25},{25,17},{2,10},{10... | collective-permute-start | bytes 1769480 | tf_op jit(solution)/shard_map/ppermute | solution.py:53
  109.7 2.7 %collective-permute-start.23 = (bf16[768,384]{1,0:T(8,128)(2,1)S(1)}, bf16[768,384]{1,0:T(8,128)(2,1)S(1)}, u32[]{:S(2)}, u32[]{:S(2)}) collective-permute-start(bf16[768,384]{1,0:T(8,128)(2,1)S(1)} %collective-permute-done.22.refs_2_), channel_id=1, source_target_pairs={{0,8},{8,0},{16,24},{24,16},{1,9},{9,1},{17,25},{25,17},{2,10},{10... | collective-permute-start | bytes 1769480 | tf_op jit(solution)/shard_map/ppermute | solution.py:53
  109.7 9.9 %collective-permute-start.33 = (bf16[768,384]{1,0:T(8,128)(2,1)S(1)}, bf16[768,384]{1,0:T(8,128)(2,1)S(1)}, u32[]{:S(2)}, u32[]{:S(2)}) collective-permute-start(bf16[768,384]{1,0:T(8,128)(2,1)S(1)} %collective-permute-done.30.refs_9_), channel_id=1, source_target_pairs={{0,2},{2,4},{4,6},{6,7},{7,5},{5,3},{3,1},{1,0},{8,9},{10,8},{12,1... | collective-permute-start | bytes 1769480 | tf_op jit(solution)/shard_map/ppermute | solution.py:50
  111.2 8.4 %collective-permute-start.32 = (bf16[768,384]{1,0:T(8,128)(2,1)S(1)}, bf16[768,384]{1,0:T(8,128)(2,1)S(1)}, u32[]{:S(2)}, u32[]{:S(2)}) collective-permute-start(bf16[768,384]{1,0:T(8,128)(2,1)S(1)} %collective-permute-done.31), channel_id=1, source_target_pairs={{0,8},{8,0},{16,24},{24,16},{1,9},{9,1},{17,25},{25,17},{2,10},{10... | collective-permute-start | bytes 1769480 | tf_op jit(solution)/shard_map/ppermute | solution.py:53
  112.4 7.2 %copy-start.1 = (bf16[768,384]{1,0:T(8,128)(2,1)S(1)}, bf16[768,384]{1,0:T(8,128)(2,1)}, u32[]{:S(2)}) copy-start(bf16[768,384]{1,0:T(8,128)(2,1)} %deriv_ref.1) | copy-start | bytes 1769476
  112.4 7.2 %copy-start.3 = (s32[24]{0:T(128)S(1)}, s32[24]{0:T(128)}, u32[]{:S(2)}) copy-start(s32[24]{0:T(128)} %band_ref.9) | copy-start | bytes 292
  112.4 7.2 %copy-start.4 = (s32[24]{0:T(128)S(1)}, s32[24]{0:T(128)}, u32[]{:S(2)}) copy-start(s32[24]{0:T(128)} %frag_ref.1) | copy-start | bytes 292

commit v7 on v6

--- a/solution.py
+++ b/solution.py
@@ -233,7 +233,9 @@
         owner = frag_ref[lax.axis_index("col") * plan.block_cols + j]
         line = jnp.broadcast_to(terms[:, j * BLK : (j + 1) * BLK], (count, BLK))
         sums = sums + jnp.where(fragment == owner, line, 0.0)
-    sums_ref[...] = sums
+    for device in range(plan.rows * plan.cols):
+        first = device % plan.cols * FRAG_DEV
+        sums_ref[device] = sums[first : first + FRAG_DEV, :]
 
 
 def body(ham, deriv, band, frag_of):
@@ -301,15 +303,13 @@
     places = near_places(plan, 0, plan.far)
     late = [shards[-1], far]
     total, right = call(bind(near_kernel, plan, places[:-1]), [total_type, column_type], [], column + shards[:-1])
-    energy_density, sums = call(
+    energy, sums = call(
         bind(energy_kernel, plan, places[-1:] + [(plan.far, True)]),
-        [block, jax.ShapeDtypeStruct((FRAG_DEV * plan.cols, BLK), jnp.float32)],
+        [block, jax.ShapeDtypeStruct((plan.rows * plan.cols, FRAG_DEV, BLK), jnp.float32)],
         [band, frag_of],
         [total, right, deriv] + late,
     )
-    sums = sums.reshape(1, plan.cols, FRAG_DEV, BLK)
-    sums = jnp.broadcast_to(sums, (plan.rows, plan.cols, FRAG_DEV, BLK))
-    sums = sums.reshape(plan.rows * plan.cols, FRAG_DEV, BLK)
+    (energy_density,) = call(copy_kernel, [block], [], [energy])
     pulay_terms = jnp.sum(lax.all_to_all(sums, AXES, 0, 0), axis=0)
     return (sign_iterate, energy_density, pulay_terms)
 

time: 135 us -> 135 us (level)
  blocking collectives: 11.8 us -> 0 us
  waiting for transfers between devices: 65.6 us -> 71.9 us
  starting transfers between devices: 34.5 us -> 39.3 us
    all_to_all x1 -> x0, blocking collectives: 11.8 us -> none  [body(): pulay_terms = jnp.sum(lax.all_to_all(sums, AXES, 0, 0), axis=0)]
    all_to_all x0 -> x1, waiting for transfers between devices: none -> 6.32 us  [body(): pulay_terms = jnp.sum(lax.all_to_all(sums, AXES, 0, 0), axis=0)]
    all_to_all x0 -> x1, starting transfers between devices: none -> 4.85 us  [body(): pulay_terms = jnp.sum(lax.all_to_all(sums, AXES, 0, 0), axis=0)]
    pallas_call x12 -> x13, Pallas kernels: 19.3 us -> 20 us  [call(): pl.pallas_call(kernel, out_shape=outs, in_specs=[smem] * len(scalars) + [...]
  transfers between devices with their start and end apart: 34 -> 35, of which waited for: 19 -> 20; matrix products, arithmetic and copies ran while one was open for 0% -> 0% of each run, Pallas kernels for 11% -> 11%
where the time goes in v7:
time: 135 us; the launch traced here: 134 us
  waiting for transfers between devices  71.9 us (53%)
  starting transfers between devices  39.3 us (29%)
  Pallas kernels  20 us (15%)
  local copies, waits for them, and re-layouts  1.73 us (1%)
    ppermute x14, waiting for transfers between devices, ring(): return lax.ppermute(value, AXES, pairs)  42.1 us
    ppermute x14, starting transfers between devices, ring(): return lax.ppermute(value, AXES, pairs)  24.7 us
    ppermute x20, waiting for transfers between devices, across(): lax.ppermute(value, 'row', [(i, i ^ other) for i in range(self.rows)])  23.5 us
    pallas_call x13, Pallas kernels, call(): pl.pallas_call(kernel, out_shape=outs, in_specs=[smem] * len(scalars) + [...  20 us
    ppermute x20, starting transfers between devices, across(): lax.ppermute(value, 'row', [(i, i ^ other) for i in range(self.rows)])  9.81 us
    all_to_all x1, waiting for transfers between devices, body(): pulay_terms = jnp.sum(lax.all_to_all(sums, AXES, 0, 0), axis=0)  6.32 us
    all_to_all x1, starting transfers between devices, body(): pulay_terms = jnp.sum(lax.all_to_all(sums, AXES, 0, 0), axis=0)  4.85 us
  transfers between devices with their start and end apart: 35, of which 20 were waited for; matrix products, arithmetic and copies ran while one was open for 0% of the time, Pallas kernels for 11%

profile of v7, /device:TPU:0, one launch (start us, length us, event | category | flops | bytes accessed | tf_op | source)
XLA Modules:
  0.0 134.4 jit_solution(12523193161674493041)
XLA Ops:
  0.6 0.5 collective-permute-start
  1.1 2.6 %collective-permute-start.3 = (bf16[768,384]{1,0:T(8,128)(2,1)}, bf16[768,384]{1,0:T(8,128)(2,1)S(1)}, u32[]{:S(2)}, u32[]{:S(2)}) collective-permute-start(bf16[768,384]{1,0:T(8,128)(2,1)} %refs_4_.1), channel_id=1, source_target_pairs={{0,2},{2,4},{4,6},{6,7},{7,5},{5,3},{3,1},{1,0},{8,9},{10,8},{12,1... | collective-permute-start | bytes 1769480 | tf_op jit(solution)/shard_map/ppermute | solution.py:50
  3.8 0.0 collective-permute-done.refs_1_
  3.8 2.1 %collective-permute-start.4 = (bf16[768,384]{1,0:T(8,128)(2,1)S(1)}, bf16[768,384]{1,0:T(8,128)(2,1)S(1)}, u32[]{:S(2)}, u32[]{:S(2)}) collective-permute-start(bf16[768,384]{1,0:T(8,128)(2,1)S(1)} %collective-permute-done.refs_1_), channel_id=1, source_target_pairs={{0,2},{2,4},{4,6},{6,7},{7,5},{5,3},{3,1},{1,0},{8,9},{10,8},{12,1... | collective-permute-start | bytes 1769480 | tf_op jit(solution)/shard_map/ppermute | solution.py:50
  5.9 5.9 %collective-permute-done.3.refs_5_ = bf16[768,384]{1,0:T(8,128)(2,1)S(1)} collective-permute-done((bf16[768,384]{1,0:T(8,128)(2,1)}, bf16[768,384]{1,0:T(8,128)(2,1)S(1)}, u32[]{:S(2)}, u32[]{:S(2)}) %collective-permute-start.3) | collective-permute-done | bytes 589856 | tf_op jit(solution)/shard_map/ppermute | solution.py:50
  11.8 2.1 %collective-permute-start.6 = (bf16[768,384]{1,0:T(8,128)(2,1)S(1)}, bf16[768,384]{1,0:T(8,128)(2,1)S(1)}, u32[]{:S(2)}, u32[]{:S(2)}) collective-permute-start(bf16[768,384]{1,0:T(8,128)(2,1)S(1)} %collective-permute-done.3.refs_5_), channel_id=1, source_target_pairs={{0,2},{2,4},{4,6},{6,7},{7,5},{5,3},{3,1},{1,0},{8,9},{10,8},{12,1... | collective-permute-start | bytes 1769480 | tf_op jit(solution)/shard_map/ppermute | solution.py:50
  13.9 1.5 %collective-permute-start.1 = (bf16[768,384]{1,0:T(8,128)(2,1)}, bf16[768,384]{1,0:T(8,128)(2,1)S(1)}, u32[]{:S(2)}, u32[]{:S(2)}) collective-permute-start(bf16[768,384]{1,0:T(8,128)(2,1)} %refs_4_.1), channel_id=1, source_target_pairs={{0,16},{8,24},{16,0},{24,8},{1,17},{9,25},{17,1},{25,9},{2,18},{10... | collective-permute-start | bytes 1769480 | tf_op jit(solution)/shard_map/ppermute | solution.py:53
  15.4 2.8 %collective-permute-done.4 = bf16[768,384]{1,0:T(8,128)(2,1)S(1)} collective-permute-done((bf16[768,384]{1,0:T(8,128)(2,1)S(1)}, bf16[768,384]{1,0:T(8,128)(2,1)S(1)}, u32[]{:S(2)}, u32[]{:S(2)}) %collective-permute-start.4) | collective-permute-done | bytes 589856 | tf_op jit(solution)/shard_map/ppermute | solution.py:50
  18.1 2.1 %collective-permute-start.7 = (bf16[768,384]{1,0:T(8,128)(2,1)S(1)}, bf16[768,384]{1,0:T(8,128)(2,1)S(1)}, u32[]{:S(2)}, u32[]{:S(2)}) collective-permute-start(bf16[768,384]{1,0:T(8,128)(2,1)S(1)} %collective-permute-done.4), channel_id=1, source_target_pairs={{0,2},{2,4},{4,6},{6,7},{7,5},{5,3},{3,1},{1,0},{8,9},{10,8},{12,1... | collective-permute-start | bytes 1769480 | tf_op jit(solution)/shard_map/ppermute | solution.py:50
  20.2 4.2 %collective-permute-done.6.refs_7_ = bf16[768,384]{1,0:T(8,128)(2,1)S(1)} collective-permute-done((bf16[768,384]{1,0:T(8,128)(2,1)S(1)}, bf16[768,384]{1,0:T(8,128)(2,1)S(1)}, u32[]{:S(2)}, u32[]{:S(2)}) %collective-permute-start.6) | collective-permute-done | bytes 589856 | tf_op jit(solution)/shard_map/ppermute | solution.py:50
  24.4 2.1 %collective-permute-start.9 = (bf16[768,384]{1,0:T(8,128)(2,1)S(1)}, bf16[768,384]{1,0:T(8,128)(2,1)S(1)}, u32[]{:S(2)}, u32[]{:S(2)}) collective-permute-start(bf16[768,384]{1,0:T(8,128)(2,1)S(1)} %collective-permute-done.6.refs_7_), channel_id=1, source_target_pairs={{0,2},{2,4},{4,6},{6,7},{7,5},{5,3},{3,1},{1,0},{8,9},{10,8},{12,1... | collective-permute-start | bytes 1769480 | tf_op jit(solution)/shard_map/ppermute | solution.py:50
  26.5 2.1 %collective-permute-done.1.refs_2_ = bf16[768,384]{1,0:T(8,128)(2,1)S(1)} collective-permute-done((bf16[768,384]{1,0:T(8,128)(2,1)}, bf16[768,384]{1,0:T(8,128)(2,1)S(1)}, u32[]{:S(2)}, u32[]{:S(2)}) %collective-permute-start.1) | collective-permute-done | bytes 589856 | tf_op jit(solution)/shard_map/ppermute | solution.py:53
  28.6 0.5 collective-permute-start.5
  29.1 1.7 %collective-permute-done.7 = bf16[768,384]{1,0:T(8,128)(2,1)S(1)} collective-permute-done((bf16[768,384]{1,0:T(8,128)(2,1)S(1)}, bf16[768,384]{1,0:T(8,128)(2,1)S(1)}, u32[]{:S(2)}, u32[]{:S(2)}) %collective-permute-start.7) | collective-permute-done | bytes 589856 | tf_op jit(solution)/shard_map/ppermute | solution.py:50
  30.8 1.3 collective-permute-start.10
  32.0 0.9 collective-permute-start.8
  32.9 4.2 %collective-permute-done.9.refs_9_ = bf16[768,384]{1,0:T(8,128)(2,1)S(1)} collective-permute-done((bf16[768,384]{1,0:T(8,128)(2,1)S(1)}, bf16[768,384]{1,0:T(8,128)(2,1)S(1)}, u32[]{:S(2)}, u32[]{:S(2)}) %collective-permute-start.9) | collective-permute-done | bytes 589856 | tf_op jit(solution)/shard_map/ppermute | solution.py:50
  37.1 2.1 %collective-permute-start.11 = (bf16[768,384]{1,0:T(8,128)(2,1)S(1)}, bf16[768,384]{1,0:T(8,128)(2,1)S(1)}, u32[]{:S(2)}, u32[]{:S(2)}) collective-permute-start(bf16[768,384]{1,0:T(8,128)(2,1)S(1)} %collective-permute-done.9.refs_9_), channel_id=1, source_target_pairs={{0,2},{2,4},{4,6},{6,7},{7,5},{5,3},{3,1},{1,0},{8,9},{10,8},{12,1... | collective-permute-start | bytes 1769480 | tf_op jit(solution)/shard_map/ppermute | solution.py:50
  39.2 4.0 %collective-permute-done.10.refs_10_ = bf16[768,384]{1,0:T(8,128)(2,1)S(1)} collective-permute-done((bf16[768,384]{1,0:T(8,128)(2,1)S(1)}, bf16[768,384]{1,0:T(8,128)(2,1)S(1)}, u32[]{:S(2)}, u32[]{:S(2)}) %collective-permute-start.10) | collective-permute-done | bytes 589856 | tf_op jit(solution)/shard_map/ppermute | solution.py:50
  43.2 0.0 collective-permute-done.8.refs_8_
  43.2 1.1 copy-done
  44.3 0.7 copy-done.2
  44.9 4.7 %shard_map.67 = (f32[768,384]{1,0:T(8,128)S(1)}, bf16[3072,384]{1,0:T(8,128)(2,1)S(1)}, bf16[768,3072]{1,0:T(8,128)(2,1)S(1)}) custom-call(s32[24]{0:T(128)S(1)} %copy-done.2, bf16[768,384]{1,0:T(8,128)(2,1)S(1)} %copy-done, bf16[768,384]{1,0:T(8,128)(2,1)S(1)} %collective-permute-done.refs_1_, bf16[768,384]{1,0:T(8,128)(2,1)S(1)} %collective-permute-done.1.refs_2_, ...), custom_call_target="tpu_custom_call" | custom-call | tf_op jit(solution)/shard_map/pallas_call | solution.py:97
  49.6 0.1 collective-permute-done.11.far_ref
  49.7 1.2 shard_map.68
  50.9 2.1 %collective-permute-start.15 = (bf16[384,384]{1,0:T(8,128)(2,1)S(1)}, bf16[384,384]{1,0:T(8,128)(2,1)S(1)}, u32[]{:S(2)}, u32[]{:S(2)}) collective-permute-start(bf16[384,384]{1,0:T(8,128)(2,1)S(1)} %get-tuple-element.24.refs_0_), channel_id=1, source_target_pairs={{0,16},{8,24},{16,0},{24,8},{1,17},{9,25},{17,1},{25,9},{2,18},{10... | collective-permute-start | bytes 884744 | tf_op jit(solution)/shard_map/ppermute | solution.py:53
  52.9 0.5 collective-permute-start.13
  53.5 0.1 collective-permute-start.12
  53.5 7.3 %collective-permute-done.15.refs_0_ = bf16[384,384]{1,0:T(8,128)(2,1)S(1)} collective-permute-done((bf16[384,384]{1,0:T(8,128)(2,1)S(1)}, bf16[384,384]{1,0:T(8,128)(2,1)S(1)}, u32[]{:S(2)}, u32[]{:S(2)}) %collective-permute-start.15) | collective-permute-done | bytes 294944 | tf_op jit(solution)/shard_map/ppermute | solution.py:53
  60.8 1.6 %shard_map.69.before_ref = f32[768,384]{1,0:T(8,128)S(1)} custom-call(bf16[768,3072]{1,0:T(8,128)(2,1)S(1)} %get-tuple-element.22.slab_ref, bf16[384,384]{1,0:T(8,128)(2,1)S(1)} %get-tuple-element.24.refs_0_, bf16[384,384]{1,0:T(8,128)(2,1)S(1)} %get-tuple-element.23.refs_1_, bf16[384,384]{1,0:T(8,128)(2,1)S(1)} %collective-permute-done.13.refs_2_, ...), custom_call_target="tpu_custom_call" | custom-call | tf_op jit(solution)/shard_map/pallas_call | solution.py:97
  62.4 3.9 %collective-permute-done.12.refs_0_ = bf16[384,384]{1,0:T(8,128)(2,1)S(1)} collective-permute-done((bf16[384,384]{1,0:T(8,128)(2,1)S(1)}, bf16[384,384]{1,0:T(8,128)(2,1)S(1)}, u32[]{:S(2)}, u32[]{:S(2)}) %collective-permute-start.12) | collective-permute-done | bytes 294944 | tf_op jit(solution)/shard_map/ppermute | solution.py:53
  66.4 0.9 shard_map.70.before_ref
  67.2 0.5 shard_map.71.total_ref
  67.8 0.2 collective-permute-done.17.refs_0_
  67.9 1.3 shard_map.72
  69.3 0.4 collective-permute-start.18
  69.7 1.8 %collective-permute-start.24 = (bf16[768,384]{1,0:T(8,128)(2,1)S(1)}, bf16[768,384]{1,0:T(8,128)(2,1)S(1)}, u32[]{:S(2)}, u32[]{:S(2)}) collective-permute-start(bf16[768,384]{1,0:T(8,128)(2,1)S(1)} %get-tuple-element.30.refs_0_.refs_4_), channel_id=1, source_target_pairs={{0,2},{2,4},{4,6},{6,7},{7,5},{5,3},{3,1},{1,0},{8,9},{10,8},{12,1... | collective-permute-start | bytes 1769480 | tf_op jit(solution)/shard_map/ppermute | solution.py:50
  71.5 1.5 %collective-permute-start.19 = (bf16[768,384]{1,0:T(8,128)(2,1)S(1)}, bf16[768,384]{1,0:T(8,128)(2,1)S(1)}, u32[]{:S(2)}, u32[]{:S(2)}) collective-permute-start(bf16[768,384]{1,0:T(8,128)(2,1)S(1)} %get-tuple-element.30.refs_0_.refs_4_), channel_id=1, source_target_pairs={{0,16},{8,24},{16,0},{24,8},{1,17},{9,25},{17,1},{25,9},{2,18},{10... | collective-permute-start | bytes 1769480 | tf_op jit(solution)/shard_map/ppermute | solution.py:53
  73.0 1.6 %collective-permute-start.25 = (bf16[768,384]{1,0:T(8,128)(2,1)S(1)}, bf16[768,384]{1,0:T(8,128)(2,1)S(1)}, u32[]{:S(2)}, u32[]{:S(2)}) collective-permute-start(bf16[768,384]{1,0:T(8,128)(2,1)S(1)} %collective-permute-done.18.refs_1_), channel_id=1, source_target_pairs={{0,2},{2,4},{4,6},{6,7},{7,5},{5,3},{3,1},{1,0},{8,9},{10,8},{12,1... | collective-permute-start | bytes 1769480 | tf_op jit(solution)/shard_map/ppermute | solution.py:50
  74.6 5.0 %collective-permute-done.24.refs_5_ = bf16[768,384]{1,0:T(8,128)(2,1)S(1)} collective-permute-done((bf16[768,384]{1,0:T(8,128)(2,1)S(1)}, bf16[768,384]{1,0:T(8,128)(2,1)S(1)}, u32[]{:S(2)}, u32[]{:S(2)}) %collective-permute-start.24) | collective-permute-done | bytes 589856 | tf_op jit(solution)/shard_map/ppermute | solution.py:50
  79.6 1.8 %collective-permute-start.27 = (bf16[768,384]{1,0:T(8,128)(2,1)S(1)}, bf16[768,384]{1,0:T(8,128)(2,1)S(1)}, u32[]{:S(2)}, u32[]{:S(2)}) collective-permute-start(bf16[768,384]{1,0:T(8,128)(2,1)S(1)} %collective-permute-done.24.refs_5_), channel_id=1, source_target_pairs={{0,2},{2,4},{4,6},{6,7},{7,5},{5,3},{3,1},{1,0},{8,9},{10,8},{12,1... | collective-permute-start | bytes 1769480 | tf_op jit(solution)/shard_map/ppermute | solution.py:50
  81.4 5.2 %collective-permute-done.19.refs_0_ = bf16[768,384]{1,0:T(8,128)(2,1)S(1)} collective-permute-done((bf16[768,384]{1,0:T(8,128)(2,1)S(1)}, bf16[768,384]{1,0:T(8,128)(2,1)S(1)}, u32[]{:S(2)}, u32[]{:S(2)}) %collective-permute-start.19) | collective-permute-done | bytes 589856 | tf_op jit(solution)/shard_map/ppermute | solution.py:53
  86.6 1.1 collective-permute-start.28
  87.7 1.4 %shard_map.74.before_ref = f32[768,384]{1,0:T(8,128)S(1)} custom-call(bf16[768,3072]{1,0:T(8,128)(2,1)S(1)} %get-tuple-element.22.slab_ref, bf16[768,384]{1,0:T(8,128)(2,1)S(1)} %get-tuple-element.30.refs_0_.refs_4_, bf16[768,384]{1,0:T(8,128)(2,1)S(1)} %collective-permute-done.18.refs_1_), custom_call_target="tpu_custom_call" | custom-call | tf_op jit(solution)/shard_map/pallas_call | solution.py:97
  89.1 0.8 shard_map.75.before_ref
  89.9 2.3 %collective-permute-done.27.refs_7_ = bf16[768,384]{1,0:T(8,128)(2,1)S(1)} collective-permute-done((bf16[768,384]{1,0:T(8,128)(2,1)S(1)}, bf16[768,384]{1,0:T(8,128)(2,1)S(1)}, u32[]{:S(2)}, u32[]{:S(2)}) %collective-permute-start.27) | collective-permute-done | bytes 589856 | tf_op jit(solution)/shard_map/ppermute | solution.py:50
  92.2 1.8 %collective-permute-start.30 = (bf16[768,384]{1,0:T(8,128)(2,1)S(1)}, bf16[768,384]{1,0:T(8,128)(2,1)S(1)}, u32[]{:S(2)}, u32[]{:S(2)}) collective-permute-start(bf16[768,384]{1,0:T(8,128)(2,1)S(1)} %collective-permute-done.27.refs_7_), channel_id=1, source_target_pairs={{0,2},{2,4},{4,6},{6,7},{7,5},{5,3},{3,1},{1,0},{8,9},{10,8},{12,1... | collective-permute-start | bytes 1769480 | tf_op jit(solution)/shard_map/ppermute | solution.py:50
  94.0 1.3 %shard_map.76.refs_0_ = bf16[768,384]{1,0:T(8,128)(2,1)S(1)} custom-call(s32[24]{0:T(128)S(1)} %copy-done.2, bf16[768,3072]{1,0:T(8,128)(2,1)S(1)} %get-tuple-element.22.slab_ref, f32[768,384]{1,0:T(8,128)S(1)} %shard_map.75.before_ref, bf16[768,384]{1,0:T(8,128)(2,1)S(1)} %collective-permute-done.20.refs_0_), custom_call_target="tpu_custom_call" | custom-call | tf_op jit(solution)/shard_map/pallas_call | solution.py:97
  95.4 1.5 %collective-permute-start.22 = (bf16[768,384]{1,0:T(8,128)(2,1)S(1)}, bf16[768,384]{1,0:T(8,128)(2,1)S(1)}, u32[]{:S(2)}, u32[]{:S(2)}) collective-permute-start(bf16[768,384]{1,0:T(8,128)(2,1)S(1)} %shard_map.76.refs_0_), channel_id=1, source_target_pairs={{0,16},{8,24},{16,0},{24,8},{1,17},{9,25},{17,1},{25,9},{2,18},{10... | collective-permute-start | bytes 1769480 | tf_op jit(solution)/shard_map/ppermute | solution.py:53
  96.9 1.6 %collective-permute-done.28 = bf16[768,384]{1,0:T(8,128)(2,1)S(1)} collective-permute-done((bf16[768,384]{1,0:T(8,128)(2,1)S(1)}, bf16[768,384]{1,0:T(8,128)(2,1)S(1)}, u32[]{:S(2)}, u32[]{:S(2)}) %collective-permute-start.28) | collective-permute-done | bytes 589856 | tf_op jit(solution)/shard_map/ppermute | solution.py:50
  98.5 1.8 %collective-permute-start.31 = (bf16[768,384]{1,0:T(8,128)(2,1)S(1)}, bf16[768,384]{1,0:T(8,128)(2,1)S(1)}, u32[]{:S(2)}, u32[]{:S(2)}) collective-permute-start(bf16[768,384]{1,0:T(8,128)(2,1)S(1)} %collective-permute-done.28), channel_id=1, source_target_pairs={{0,2},{2,4},{4,6},{6,7},{7,5},{5,3},{3,1},{1,0},{8,9},{10,8},{12,1... | collective-permute-start | bytes 1769480 | tf_op jit(solution)/shard_map/ppermute | solution.py:50
  100.4 4.5 %collective-permute-done.30.refs_9_ = bf16[768,384]{1,0:T(8,128)(2,1)S(1)} collective-permute-done((bf16[768,384]{1,0:T(8,128)(2,1)S(1)}, bf16[768,384]{1,0:T(8,128)(2,1)S(1)}, u32[]{:S(2)}, u32[]{:S(2)}) %collective-permute-start.30) | collective-permute-done | bytes 589856 | tf_op jit(solution)/shard_map/ppermute | solution.py:50
  104.9 4.8 %collective-permute-done.22.refs_2_ = bf16[768,384]{1,0:T(8,128)(2,1)S(1)} collective-permute-done((bf16[768,384]{1,0:T(8,128)(2,1)S(1)}, bf16[768,384]{1,0:T(8,128)(2,1)S(1)}, u32[]{:S(2)}, u32[]{:S(2)}) %collective-permute-start.22) | collective-permute-done | bytes 589856 | tf_op jit(solution)/shard_map/ppermute | solution.py:53
  109.7 0.3 collective-permute-start.33
  110.0 1.1 collective-permute-done.31
  111.2 0.3 collective-permute-start.32
  111.5 0.9 shard_map.73
  112.4 2.5 %shard_map.77 = (f32[768,384]{1,0:T(8,128)S(1)}, bf16[3072,384]{1,0:T(8,128)(2,1)S(1)}) custom-call(bf16[768,384]{1,0:T(8,128)(2,1)S(1)} %shard_map.76.refs_0_, bf16[768,384]{1,0:T(8,128)(2,1)S(1)} %collective-permute-done.21.refs_1_, bf16[768,384]{1,0:T(8,128)(2,1)S(1)} %collective-permute-done.22.refs_2_, ...), custom_call_target="tpu_custom_call" | custom-call | tf_op jit(solution)/shard_map/pallas_call | solution.py:97
  114.9 4.7 %collective-permute-done.33.refs_1_ = bf16[768,384]{1,0:T(8,128)(2,1)S(1)} collective-permute-done((bf16[768,384]{1,0:T(8,128)(2,1)S(1)}, bf16[768,384]{1,0:T(8,128)(2,1)S(1)}, u32[]{:S(2)}, u32[]{:S(2)}) %collective-permute-start.33) | collective-permute-done | bytes 589856 | tf_op jit(solution)/shard_map/ppermute | solution.py:50
  119.6 2.1 %shard_map.78 = (bf16[768,384]{1,0:T(8,128)(2,1)S(1)}, f32[32,2,128]{2,1,0:T(2,128)}) custom-call(s32[24]{0:T(128)S(1)} %copy-done.3, s32[24]{0:T(128)S(1)} %copy-done.4, f32[768,384]{1,0:T(8,128)S(1)} %get-tuple-element.31.total_ref, bf16[3072,384]{1,0:T(8,128)(2,1)S(1)} %get-tuple-element.32.right_ref, bf16[768,384]{1,0:T(8,128)(2,1)S(1)} %copy-done.1, ...), custom_call_target="tpu_custom_call" | custom-call | tf_op jit(solution)/shard_map/pallas_call | solution.py:97
  121.7 4.9 %all-to-all-start = ((f32[32,2,128]{2,1,0:T(2,128)}), f32[32,2,128]{2,1,0:T(2,128)S(1)}, u32[]{:S(2)}, u32[]{:S(2)}) async-start(f32[32,2,128]{2,1,0:T(2,128)} %get-tuple-element.34), calls=%async_computation | async-start | bytes 65536 | tf_op jit(solution)/shard_map/all_to_all | solution.py:313
  126.6 0.9 shard_map.79
  127.4 6.3 %all-to-all-done = f32[32,2,128]{2,1,0:T(2,128)S(1)} async-done(((f32[32,2,128]{2,1,0:T(2,128)}), f32[32,2,128]{2,1,0:T(2,128)S(1)}, u32[]{:S(2)}, u32[]{:S(2)}) %all-to-all-start) | async-done | bytes 32800 | tf_op jit(solution)/shard_map/all_to_all | solution.py:313
  133.8 0.6 reduce_sum.9
  (30 shorter events, 0.1 us)
Async XLA Ops:
  0.6 3.2 %collective-permute-start = (bf16[768,384]{1,0:T(8,128)(2,1)}, bf16[768,384]{1,0:T(8,128)(2,1)S(1)}, u32[]{:S(2)}, u32[]{:S(2)}) collective-permute-start(bf16[768,384]{1,0:T(8,128)(2,1)} %refs_4_.1), channel_id=1, source_target_pairs={{0,8},{8,0},{16,24},{24,16},{1,9},{9,1},{17,25},{25,17},{2,10},{10... | collective-permute-start | bytes 1769480 | tf_op jit(solution)/shard_map/ppermute | solution.py:53
  1.1 10.7 %collective-permute-start.3 = (bf16[768,384]{1,0:T(8,128)(2,1)}, bf16[768,384]{1,0:T(8,128)(2,1)S(1)}, u32[]{:S(2)}, u32[]{:S(2)}) collective-permute-start(bf16[768,384]{1,0:T(8,128)(2,1)} %refs_4_.1), channel_id=1, source_target_pairs={{0,2},{2,4},{4,6},{6,7},{7,5},{5,3},{3,1},{1,0},{8,9},{10,8},{12,1... | collective-permute-start | bytes 1769480 | tf_op jit(solution)/shard_map/ppermute | solution.py:50
  3.8 14.3 %collective-permute-start.4 = (bf16[768,384]{1,0:T(8,128)(2,1)S(1)}, bf16[768,384]{1,0:T(8,128)(2,1)S(1)}, u32[]{:S(2)}, u32[]{:S(2)}) collective-permute-start(bf16[768,384]{1,0:T(8,128)(2,1)S(1)} %collective-permute-done.refs_1_), channel_id=1, source_target_pairs={{0,2},{2,4},{4,6},{6,7},{7,5},{5,3},{3,1},{1,0},{8,9},{10,8},{12,1... | collective-permute-start | bytes 1769480 | tf_op jit(solution)/shard_map/ppermute | solution.py:50
  11.8 12.6 %collective-permute-start.6 = (bf16[768,384]{1,0:T(8,128)(2,1)S(1)}, bf16[768,384]{1,0:T(8,128)(2,1)S(1)}, u32[]{:S(2)}, u32[]{:S(2)}) collective-permute-start(bf16[768,384]{1,0:T(8,128)(2,1)S(1)} %collective-permute-done.3.refs_5_), channel_id=1, source_target_pairs={{0,2},{2,4},{4,6},{6,7},{7,5},{5,3},{3,1},{1,0},{8,9},{10,8},{12,1... | collective-permute-start | bytes 1769480 | tf_op jit(solution)/shard_map/ppermute | solution.py:50
  13.9 14.7 %collective-permute-start.1 = (bf16[768,384]{1,0:T(8,128)(2,1)}, bf16[768,384]{1,0:T(8,128)(2,1)S(1)}, u32[]{:S(2)}, u32[]{:S(2)}) collective-permute-start(bf16[768,384]{1,0:T(8,128)(2,1)} %refs_4_.1), channel_id=1, source_target_pairs={{0,16},{8,24},{16,0},{24,8},{1,17},{9,25},{17,1},{25,9},{2,18},{10... | collective-permute-start | bytes 1769480 | tf_op jit(solution)/shard_map/ppermute | solution.py:53
  18.1 12.6 %collective-permute-start.7 = (bf16[768,384]{1,0:T(8,128)(2,1)S(1)}, bf16[768,384]{1,0:T(8,128)(2,1)S(1)}, u32[]{:S(2)}, u32[]{:S(2)}) collective-permute-start(bf16[768,384]{1,0:T(8,128)(2,1)S(1)} %collective-permute-done.4), channel_id=1, source_target_pairs={{0,2},{2,4},{4,6},{6,7},{7,5},{5,3},{3,1},{1,0},{8,9},{10,8},{12,1... | collective-permute-start | bytes 1769480 | tf_op jit(solution)/shard_map/ppermute | solution.py:50
  24.4 12.6 %collective-permute-start.9 = (bf16[768,384]{1,0:T(8,128)(2,1)S(1)}, bf16[768,384]{1,0:T(8,128)(2,1)S(1)}, u32[]{:S(2)}, u32[]{:S(2)}) collective-permute-start(bf16[768,384]{1,0:T(8,128)(2,1)S(1)} %collective-permute-done.6.refs_7_), channel_id=1, source_target_pairs={{0,2},{2,4},{4,6},{6,7},{7,5},{5,3},{3,1},{1,0},{8,9},{10,8},{12,1... | collective-permute-start | bytes 1769480 | tf_op jit(solution)/shard_map/ppermute | solution.py:50
  28.6 10.6 %collective-permute-start.2 = (bf16[768,384]{1,0:T(8,128)(2,1)S(1)}, bf16[768,384]{1,0:T(8,128)(2,1)S(1)}, u32[]{:S(2)}, u32[]{:S(2)}) collective-permute-start(bf16[768,384]{1,0:T(8,128)(2,1)S(1)} %collective-permute-done.1.refs_2_), channel_id=1, source_target_pairs={{0,8},{8,0},{16,24},{24,16},{1,9},{9,1},{17,25},{25,17},{2,10},{10... | collective-permute-start | bytes 1769480 | tf_op jit(solution)/shard_map/ppermute | solution.py:53
  28.6 10.6 %collective-permute-start.5 = (bf16[768,384]{1,0:T(8,128)(2,1)S(1)}, bf16[768,384]{1,0:T(8,128)(2,1)S(1)}, u32[]{:S(2)}, u32[]{:S(2)}) collective-permute-start(bf16[768,384]{1,0:T(8,128)(2,1)S(1)} %collective-permute-done.4), channel_id=1, source_target_pairs={{0,8},{8,0},{16,24},{24,16},{1,9},{9,1},{17,25},{25,17},{2,10},{10... | collective-permute-start | bytes 1769480 | tf_op jit(solution)/shard_map/ppermute | solution.py:53
  30.8 12.4 %collective-permute-start.10 = (bf16[768,384]{1,0:T(8,128)(2,1)S(1)}, bf16[768,384]{1,0:T(8,128)(2,1)S(1)}, u32[]{:S(2)}, u32[]{:S(2)}) collective-permute-start(bf16[768,384]{1,0:T(8,128)(2,1)S(1)} %collective-permute-done.7), channel_id=1, source_target_pairs={{0,10},{2,12},{4,14},{6,15},{7,13},{5,11},{3,9},{1,8},{8,1},{10,0}... | collective-permute-start | bytes 1769480 | tf_op jit(solution)/shard_map/ppermute | solution.py:50
  32.0 11.2 %collective-permute-start.8 = (bf16[768,384]{1,0:T(8,128)(2,1)S(1)}, bf16[768,384]{1,0:T(8,128)(2,1)S(1)}, u32[]{:S(2)}, u32[]{:S(2)}) collective-permute-start(bf16[768,384]{1,0:T(8,128)(2,1)S(1)} %collective-permute-done.7), channel_id=1, source_target_pairs={{0,8},{8,0},{16,24},{24,16},{1,9},{9,1},{17,25},{25,17},{2,10},{10... | collective-permute-start | bytes 1769480 | tf_op jit(solution)/shard_map/ppermute | solution.py:53
  37.1 12.6 %collective-permute-start.11 = (bf16[768,384]{1,0:T(8,128)(2,1)S(1)}, bf16[768,384]{1,0:T(8,128)(2,1)S(1)}, u32[]{:S(2)}, u32[]{:S(2)}) collective-permute-start(bf16[768,384]{1,0:T(8,128)(2,1)S(1)} %collective-permute-done.9.refs_9_), channel_id=1, source_target_pairs={{0,2},{2,4},{4,6},{6,7},{7,5},{5,3},{3,1},{1,0},{8,9},{10,8},{12,1... | collective-permute-start | bytes 1769480 | tf_op jit(solution)/shard_map/ppermute | solution.py:50
  43.2 1.1 copy-start
  44.3 0.7 copy-start.2
  50.9 9.9 %collective-permute-start.15 = (bf16[384,384]{1,0:T(8,128)(2,1)S(1)}, bf16[384,384]{1,0:T(8,128)(2,1)S(1)}, u32[]{:S(2)}, u32[]{:S(2)}) collective-permute-start(bf16[384,384]{1,0:T(8,128)(2,1)S(1)} %get-tuple-element.24.refs_0_), channel_id=1, source_target_pairs={{0,16},{8,24},{16,0},{24,8},{1,17},{9,25},{17,1},{25,9},{2,18},{10... | collective-permute-start | bytes 884744 | tf_op jit(solution)/shard_map/ppermute | solution.py:53
  52.9 7.9 %collective-permute-start.14 = (bf16[384,384]{1,0:T(8,128)(2,1)S(1)}, bf16[384,384]{1,0:T(8,128)(2,1)S(1)}, u32[]{:S(2)}, u32[]{:S(2)}) collective-permute-start(bf16[384,384]{1,0:T(8,128)(2,1)S(1)} %get-tuple-element.23.refs_1_), channel_id=1, source_target_pairs={{0,8},{8,0},{16,24},{24,16},{1,9},{9,1},{17,25},{25,17},{2,10},{10... | collective-permute-start | bytes 884744 | tf_op jit(solution)/shard_map/ppermute | solution.py:53
  52.9 7.9 %collective-permute-start.13 = (bf16[384,384]{1,0:T(8,128)(2,1)S(1)}, bf16[384,384]{1,0:T(8,128)(2,1)S(1)}, u32[]{:S(2)}, u32[]{:S(2)}) collective-permute-start(bf16[384,384]{1,0:T(8,128)(2,1)S(1)} %get-tuple-element.24.refs_0_), channel_id=1, source_target_pairs={{0,8},{8,0},{16,24},{24,16},{1,9},{9,1},{17,25},{25,17},{2,10},{10... | collective-permute-start | bytes 884744 | tf_op jit(solution)/shard_map/ppermute | solution.py:53
  53.5 12.9 %collective-permute-start.12 = (bf16[384,384]{1,0:T(8,128)(2,1)S(1)}, bf16[384,384]{1,0:T(8,128)(2,1)S(1)}, u32[]{:S(2)}, u32[]{:S(2)}) collective-permute-start(bf16[384,384]{1,0:T(8,128)(2,1)S(1)} %get-tuple-element.23.refs_1_), channel_id=1, source_target_pairs={{0,16},{8,24},{16,0},{24,8},{1,17},{9,25},{17,1},{25,9},{2,18},{10... | collective-permute-start | bytes 884744 | tf_op jit(solution)/shard_map/ppermute | solution.py:53
  60.8 5.6 %collective-permute-start.16 = (bf16[384,384]{1,0:T(8,128)(2,1)S(1)}, bf16[384,384]{1,0:T(8,128)(2,1)S(1)}, u32[]{:S(2)}, u32[]{:S(2)}) collective-permute-start(bf16[384,384]{1,0:T(8,128)(2,1)S(1)} %collective-permute-done.15.refs_0_), channel_id=1, source_target_pairs={{0,8},{8,0},{16,24},{24,16},{1,9},{9,1},{17,25},{25,17},{2,10},{10... | collective-permute-start | bytes 884744 | tf_op jit(solution)/shard_map/ppermute | solution.py:53
  66.4 1.6 %collective-permute-start.17 = (bf16[384,384]{1,0:T(8,128)(2,1)S(1)}, bf16[384,384]{1,0:T(8,128)(2,1)S(1)}, u32[]{:S(2)}, u32[]{:S(2)}) collective-permute-start(bf16[384,384]{1,0:T(8,128)(2,1)S(1)} %collective-permute-done.12.refs_0_), channel_id=1, source_target_pairs={{0,8},{8,0},{16,24},{24,16},{1,9},{9,1},{17,25},{25,17},{2,10},{10... | collective-permute-start | bytes 884744 | tf_op jit(solution)/shard_map/ppermute | solution.py:53
  69.3 3.7 %collective-permute-start.18 = (bf16[768,384]{1,0:T(8,128)(2,1)S(1)}, bf16[768,384]{1,0:T(8,128)(2,1)S(1)}, u32[]{:S(2)}, u32[]{:S(2)}) collective-permute-start(bf16[768,384]{1,0:T(8,128)(2,1)S(1)} %get-tuple-element.30.refs_0_.refs_4_), channel_id=1, source_target_pairs={{0,8},{8,0},{16,24},{24,16},{1,9},{9,1},{17,25},{25,17},{2,10},{10... | collective-permute-start | bytes 1769480 | tf_op jit(solution)/shard_map/ppermute | solution.py:53
  69.7 9.9 %collective-permute-start.24 = (bf16[768,384]{1,0:T(8,128)(2,1)S(1)}, bf16[768,384]{1,0:T(8,128)(2,1)S(1)}, u32[]{:S(2)}, u32[]{:S(2)}) collective-permute-start(bf16[768,384]{1,0:T(8,128)(2,1)S(1)} %get-tuple-element.30.refs_0_.refs_4_), channel_id=1, source_target_pairs={{0,2},{2,4},{4,6},{6,7},{7,5},{5,3},{3,1},{1,0},{8,9},{10,8},{12,1... | collective-permute-start | bytes 1769480 | tf_op jit(solution)/shard_map/ppermute | solution.py:50
  71.5 15.1 %collective-permute-start.19 = (bf16[768,384]{1,0:T(8,128)(2,1)S(1)}, bf16[768,384]{1,0:T(8,128)(2,1)S(1)}, u32[]{:S(2)}, u32[]{:S(2)}) collective-permute-start(bf16[768,384]{1,0:T(8,128)(2,1)S(1)} %get-tuple-element.30.refs_0_.refs_4_), channel_id=1, source_target_pairs={{0,16},{8,24},{16,0},{24,8},{1,17},{9,25},{17,1},{25,9},{2,18},{10... | collective-permute-start | bytes 1769480 | tf_op jit(solution)/shard_map/ppermute | solution.py:53
  73.0 13.6 %collective-permute-start.25 = (bf16[768,384]{1,0:T(8,128)(2,1)S(1)}, bf16[768,384]{1,0:T(8,128)(2,1)S(1)}, u32[]{:S(2)}, u32[]{:S(2)}) collective-permute-start(bf16[768,384]{1,0:T(8,128)(2,1)S(1)} %collective-permute-done.18.refs_1_), channel_id=1, source_target_pairs={{0,2},{2,4},{4,6},{6,7},{7,5},{5,3},{3,1},{1,0},{8,9},{10,8},{12,1... | collective-permute-start | bytes 1769480 | tf_op jit(solution)/shard_map/ppermute | solution.py:50
  79.6 12.6 %collective-permute-start.27 = (bf16[768,384]{1,0:T(8,128)(2,1)S(1)}, bf16[768,384]{1,0:T(8,128)(2,1)S(1)}, u32[]{:S(2)}, u32[]{:S(2)}) collective-permute-start(bf16[768,384]{1,0:T(8,128)(2,1)S(1)} %collective-permute-done.24.refs_5_), channel_id=1, source_target_pairs={{0,2},{2,4},{4,6},{6,7},{7,5},{5,3},{3,1},{1,0},{8,9},{10,8},{12,1... | collective-permute-start | bytes 1769480 | tf_op jit(solution)/shard_map/ppermute | solution.py:50
  86.6 7.4 %collective-permute-start.20 = (bf16[768,384]{1,0:T(8,128)(2,1)S(1)}, bf16[768,384]{1,0:T(8,128)(2,1)S(1)}, u32[]{:S(2)}, u32[]{:S(2)}) collective-permute-start(bf16[768,384]{1,0:T(8,128)(2,1)S(1)} %collective-permute-done.19.refs_0_), channel_id=1, source_target_pairs={{0,8},{8,0},{16,24},{24,16},{1,9},{9,1},{17,25},{25,17},{2,10},{10... | collective-permute-start | bytes 1769480 | tf_op jit(solution)/shard_map/ppermute | solution.py:53
  86.6 11.9 %collective-permute-start.28 = (bf16[768,384]{1,0:T(8,128)(2,1)S(1)}, bf16[768,384]{1,0:T(8,128)(2,1)S(1)}, u32[]{:S(2)}, u32[]{:S(2)}) collective-permute-start(bf16[768,384]{1,0:T(8,128)(2,1)S(1)} %collective-permute-done.25), channel_id=1, source_target_pairs={{0,2},{2,4},{4,6},{6,7},{7,5},{5,3},{3,1},{1,0},{8,9},{10,8},{12,1... | collective-permute-start | bytes 1769480 | tf_op jit(solution)/shard_map/ppermute | solution.py:50
  92.2 12.6 %collective-permute-start.30 = (bf16[768,384]{1,0:T(8,128)(2,1)S(1)}, bf16[768,384]{1,0:T(8,128)(2,1)S(1)}, u32[]{:S(2)}, u32[]{:S(2)}) collective-permute-start(bf16[768,384]{1,0:T(8,128)(2,1)S(1)} %collective-permute-done.27.refs_7_), channel_id=1, source_target_pairs={{0,2},{2,4},{4,6},{6,7},{7,5},{5,3},{3,1},{1,0},{8,9},{10,8},{12,1... | collective-permute-start | bytes 1769480 | tf_op jit(solution)/shard_map/ppermute | solution.py:50
  95.4 14.3 %collective-permute-start.22 = (bf16[768,384]{1,0:T(8,128)(2,1)S(1)}, bf16[768,384]{1,0:T(8,128)(2,1)S(1)}, u32[]{:S(2)}, u32[]{:S(2)}) collective-permute-start(bf16[768,384]{1,0:T(8,128)(2,1)S(1)} %shard_map.76.refs_0_), channel_id=1, source_target_pairs={{0,16},{8,24},{16,0},{24,8},{1,17},{9,25},{17,1},{25,9},{2,18},{10... | collective-permute-start | bytes 1769480 | tf_op jit(solution)/shard_map/ppermute | solution.py:53
  96.9 12.8 %collective-permute-start.26 = (bf16[768,384]{1,0:T(8,128)(2,1)S(1)}, bf16[768,384]{1,0:T(8,128)(2,1)S(1)}, u32[]{:S(2)}, u32[]{:S(2)}) collective-permute-start(bf16[768,384]{1,0:T(8,128)(2,1)S(1)} %collective-permute-done.25), channel_id=1, source_target_pairs={{0,8},{8,0},{16,24},{24,16},{1,9},{9,1},{17,25},{25,17},{2,10},{10... | collective-permute-start | bytes 1769480 | tf_op jit(solution)/shard_map/ppermute | solution.py:53
  98.5 12.6 %collective-permute-start.31 = (bf16[768,384]{1,0:T(8,128)(2,1)S(1)}, bf16[768,384]{1,0:T(8,128)(2,1)S(1)}, u32[]{:S(2)}, u32[]{:S(2)}) collective-permute-start(bf16[768,384]{1,0:T(8,128)(2,1)S(1)} %collective-permute-done.28), channel_id=1, source_target_pairs={{0,2},{2,4},{4,6},{6,7},{7,5},{5,3},{3,1},{1,0},{8,9},{10,8},{12,1... | collective-permute-start | bytes 1769480 | tf_op jit(solution)/shard_map/ppermute | solution.py:50
  100.3 12.0 %collective-permute-start.21 = (bf16[768,384]{1,0:T(8,128)(2,1)S(1)}, bf16[768,384]{1,0:T(8,128)(2,1)S(1)}, u32[]{:S(2)}, u32[]{:S(2)}) collective-permute-start(bf16[768,384]{1,0:T(8,128)(2,1)S(1)} %shard_map.76.refs_0_), channel_id=1, source_target_pairs={{0,8},{8,0},{16,24},{24,16},{1,9},{9,1},{17,25},{25,17},{2,10},{10... | collective-permute-start | bytes 1769480 | tf_op jit(solution)/shard_map/ppermute | solution.py:53
  104.8 7.5 %collective-permute-start.29 = (bf16[768,384]{1,0:T(8,128)(2,1)S(1)}, bf16[768,384]{1,0:T(8,128)(2,1)S(1)}, u32[]{:S(2)}, u32[]{:S(2)}) collective-permute-start(bf16[768,384]{1,0:T(8,128)(2,1)S(1)} %collective-permute-done.28), channel_id=1, source_target_pairs={{0,8},{8,0},{16,24},{24,16},{1,9},{9,1},{17,25},{25,17},{2,10},{10... | collective-permute-start | bytes 1769480 | tf_op jit(solution)/shard_map/ppermute | solution.py:53
  109.7 2.7 %collective-permute-start.23 = (bf16[768,384]{1,0:T(8,128)(2,1)S(1)}, bf16[768,384]{1,0:T(8,128)(2,1)S(1)}, u32[]{:S(2)}, u32[]{:S(2)}) collective-permute-start(bf16[768,384]{1,0:T(8,128)(2,1)S(1)} %collective-permute-done.22.refs_2_), channel_id=1, source_target_pairs={{0,8},{8,0},{16,24},{24,16},{1,9},{9,1},{17,25},{25,17},{2,10},{10... | collective-permute-start | bytes 1769480 | tf_op jit(solution)/shard_map/ppermute | solution.py:53
  109.7 9.9 %collective-permute-start.33 = (bf16[768,384]{1,0:T(8,128)(2,1)S(1)}, bf16[768,384]{1,0:T(8,128)(2,1)S(1)}, u32[]{:S(2)}, u32[]{:S(2)}) collective-permute-start(bf16[768,384]{1,0:T(8,128)(2,1)S(1)} %collective-permute-done.30.refs_9_), channel_id=1, source_target_pairs={{0,2},{2,4},{4,6},{6,7},{7,5},{5,3},{3,1},{1,0},{8,9},{10,8},{12,1... | collective-permute-start | bytes 1769480 | tf_op jit(solution)/shard_map/ppermute | solution.py:50
  111.2 8.4 %collective-permute-start.32 = (bf16[768,384]{1,0:T(8,128)(2,1)S(1)}, bf16[768,384]{1,0:T(8,128)(2,1)S(1)}, u32[]{:S(2)}, u32[]{:S(2)}) collective-permute-start(bf16[768,384]{1,0:T(8,128)(2,1)S(1)} %collective-permute-done.31), channel_id=1, source_target_pairs={{0,8},{8,0},{16,24},{24,16},{1,9},{9,1},{17,25},{25,17},{2,10},{10... | collective-permute-start | bytes 1769480 | tf_op jit(solution)/shard_map/ppermute | solution.py:53
  112.4 7.2 %copy-start.1 = (bf16[768,384]{1,0:T(8,128)(2,1)S(1)}, bf16[768,384]{1,0:T(8,128)(2,1)}, u32[]{:S(2)}) copy-start(bf16[768,384]{1,0:T(8,128)(2,1)} %deriv_ref.1) | copy-start | bytes 1769476
  112.4 7.2 %copy-start.3 = (s32[24]{0:T(128)S(1)}, s32[24]{0:T(128)}, u32[]{:S(2)}) copy-start(s32[24]{0:T(128)} %band_ref.9) | copy-start | bytes 292
  112.4 7.2 %copy-start.4 = (s32[24]{0:T(128)S(1)}, s32[24]{0:T(128)}, u32[]{:S(2)}) copy-start(s32[24]{0:T(128)} %frag_ref.1) | copy-start | bytes 292
  121.7 12.0 %all-to-all-start = ((f32[32,2,128]{2,1,0:T(2,128)}), f32[32,2,128]{2,1,0:T(2,128)S(1)}, u32[]{:S(2)}, u32[]{:S(2)}) async-start(f32[32,2,128]{2,1,0:T(2,128)} %get-tuple-element.34), calls=%async_computation | async-start | bytes 65536 | tf_op jit(solution)/shard_map/all_to_all | solution.py:313
